TPU v7x, 32 devices: a whole 2x2x4 slice. The times are simulated.
32 devices in a mesh: section: 8 (over y, x, core), tensor: 4 (over z).
Axes of the slice: x: 2, y: 2, z: 4, core: 2. Of those that a mesh axis runs over, the one named last changes fastest.
Arguments:
- inputs: bfloat16 [4, 128, 16384], P(None, None, 'tensor'), may hold values from -6 to 6
- state: float32 [8, 128, 16, 16384], P('section', None, None, 'tensor'), may hold values from -4 to 4
- pool: float32 [8, 3, 16, 16384], P('section', None, None, 'tensor'), may hold values from -4 to 4
- x_weight: bfloat16 [8, 16384, 544], P('section', 'tensor'), may hold values from -0.046875 to 0.046875
- dt_weight: bfloat16 [8, 512, 16384], P('section', None, 'tensor'), may hold values from -0.25 to 0.25
- dt_bias: float32 [8, 16384], P('section', 'tensor'), may hold values from -4 to -1
- a_log: float32 [8, 16, 16384], P('section', None, 'tensor'), may hold values from 0 to 2.8
- skip: float32 [8, 16384], P('section', 'tensor'), may hold values from 0.5 to 1.5
- gain: float32 [8, 16384], P('section', 'tensor'), may hold values from 0.1 to 1.9
- gate_input: bfloat16 [8, 4, 128, 16384], P('section', None, None, 'tensor'), may hold values from -6 to 6
- swap_plan: int32 [3, 8, 3], replicated, may hold values from 0 to 127, as said below
- evict_plan: int32 [3, 8, 3], replicated, may hold values from 0 to 127, as said below
Outputs:
- mixer_out: bfloat16 [8, 4, 128, 16384], P('section', None, None, 'tensor')
- final_state: float32 [8, 128, 16, 16384], P('section', None, None, 'tensor')
- pool_out: float32 [8, 3, 16, 16384], P('section', None, None, 'tensor')
Inputs may be any that keep to these rules, and one draw needn't show every extreme that they name: `swap_plan`: row 0 names requests below 128, row 1 holders along section below 8, row 2 slots below 3. Within one layer the 3 requests are distinct and the 3 holders are distinct. `evict_plan`: row 0 names requests below 128, row 1 holders along section below 8, row 2 slots below 3. Within one layer the 3 requests are distinct and the 3 holders are distinct; no pair of holder and slot is named twice in the whole plan.
All inputs are finite; a program needn't handle non-finite values.
Results may differ from a plain program's by a relative error of at most 0.035.
Values may be sent and summed in bfloat16 or wider, within the bound.
No kernel may reach another device: no remote copies, remote signals or barrier semaphores. Data moves between devices by JAX's collectives and lax.ppermute only.
A program may use at most 192 MiB of HBM per device.

v0:
```python
import jax
import jax.numpy as jnp
from jax import lax
from jax.sharding import PartitionSpec as P

MICRO = 2


def from_behind(block, axis, distance):
    devices = range(lax.axis_size(axis))
    route = [(i - distance, i) for i in devices if i - distance in devices]
    return lax.ppermute(block, axis, route)


def shards(
    inputs,
    state,
    pool,
    x_weight,
    dt_weight,
    dt_bias,
    a_log,
    skip,
    gain,
    gate_input,
    swap_plan,
    evict_plan,
):
    section = lax.axis_index("section")
    holders = lax.axis_size("section")
    width = x_weight.shape[1] * lax.axis_size("tensor")
    rank = dt_weight.shape[1]
    states = a_log.shape[1]
    requests = state.shape[1]
    rows = requests // MICRO
    steps = inputs.shape[0]
    units = steps * MICRO
    turns = units + holders - 1
    hold = state[0]
    store = pool[0]
    own_swap = lax.dynamic_index_in_dim(swap_plan, section, 1, keepdims=False)
    matches = swap_plan[1] == section
    found = jnp.any(matches, axis=1)
    slot_of = jnp.sum(jnp.where(matches, swap_plan[2], 0), axis=1)
    picked = store[slot_of]
    outgoing = jnp.where(found[:, None, None], picked, 0.0)
    arrived = lax.all_to_all(outgoing, "section", split_axis=0, concat_axis=0, tiled=True)
    hold = hold.at[own_swap[0]].set(arrived[own_swap[1]])
    rates = jnp.exp(a_log[0])
    produced = jnp.zeros((steps, requests, x_weight.shape[1]), jnp.bfloat16)
    incoming = jnp.zeros((rows, x_weight.shape[1]), jnp.bfloat16)

    def turn(index, carry):
        hold, incoming, produced = carry
        unit = index - section
        valid = (unit >= 0) & (unit < units)
        clipped = jnp.clip(unit, 0, units - 1)
        step = clipped // MICRO
        first = clipped % MICRO * rows
        fresh = lax.dynamic_slice_in_dim(
            lax.dynamic_index_in_dim(inputs, step, 0, keepdims=False), first, rows, 0
        )
        stream = jnp.where(section == 0, fresh, incoming)
        widened = stream.astype(jnp.float32)
        scaled = (widened * gain[0]).astype(jnp.bfloat16)
        partial_proj = jnp.dot(scaled, x_weight[0], preferred_element_type=jnp.float32)
        squares, summed = lax.psum((jnp.sum(widened * widened, axis=1), partial_proj), "tensor")
        root = jnp.sqrt(squares[:, None] / width + 1e-05)
        proj = summed / root
        low = proj[:, :rank].astype(jnp.bfloat16)
        step_size = jax.nn.softplus(
            jnp.dot(low, dt_weight[0], preferred_element_type=jnp.float32) + dt_bias[0]
        )
        normed_f = scaled.astype(jnp.float32) / root
        older = lax.dynamic_slice_in_dim(hold, first, rows, 0)
        decay = jnp.exp(-step_size[:, None, :] * rates[None])
        newer = (
            decay * older + (step_size * normed_f)[:, None, :] * proj[:, rank : rank + states, None]
        )
        mixed = jnp.sum(newer * proj[:, rank + states :, None], axis=1) + skip[0] * normed_f
        gate_rows = lax.dynamic_slice_in_dim(
            lax.dynamic_index_in_dim(gate_input[0], step, 0, keepdims=False), first, rows, 0
        )
        result = (mixed * jax.nn.silu(gate_rows.astype(jnp.float32))).astype(jnp.bfloat16)
        hold = lax.dynamic_update_slice_in_dim(hold, jnp.where(valid, newer, older), first, 0)
        before = lax.dynamic_slice(produced, (step, first, 0), (1, rows, produced.shape[2]))
        produced = lax.dynamic_update_slice(
            produced, jnp.where(valid, result[None], before), (step, first, 0)
        )
        passed = (widened + result.astype(jnp.float32)).astype(jnp.bfloat16)
        incoming = from_behind(passed, "section", 1)
        return (hold, incoming, produced)

    hold, incoming, produced = lax.fori_loop(0, turns, turn, (hold, incoming, produced))
    evicted = lax.dynamic_index_in_dim(evict_plan, section, 1, keepdims=False)
    outgoing = (
        jnp.zeros((holders, states, hold.shape[2]), jnp.float32)
        .at[evicted[1]]
        .set(hold[evicted[0]])
    )
    returned = lax.all_to_all(
        outgoing.astype(jnp.bfloat16), "section", split_axis=0, concat_axis=0, tiled=True
    ).astype(outgoing.dtype)
    evict_match = evict_plan[1] == section
    has_entry = jnp.any(evict_match, axis=1)
    evict_slot = jnp.sum(jnp.where(evict_match, evict_plan[2], 0), axis=1)
    target = jnp.where(has_entry, evict_slot, store.shape[0])
    store_out = store.at[target].set(returned, mode="drop")
    return (produced[None], hold[None], store_out[None])


def solution(mesh):
    placed = (
        P(None, None, "tensor"),
        P("section", None, None, "tensor"),
        P("section", None, None, "tensor"),
        P("section", "tensor", None),
        P("section", None, "tensor"),
        P("section", "tensor"),
        P("section", None, "tensor"),
        P("section", "tensor"),
        P("section", "tensor"),
        P("section", None, None, "tensor"),
        P(),
        P(),
    )
    return jax.shard_map(
        shards,
        mesh=mesh,
        in_specs=placed,
        out_specs=(
            P("section", None, None, "tensor"),
            P("section", None, None, "tensor"),
            P("section", None, None, "tensor"),
        ),
        check_vma=False,
    )
```

profile of v0, /device:TPU:0, one launch (start us, length us, event | category | flops | bytes accessed | tf_op | source)
XLA Modules:
  0.0 1206.8 jit_solution(310315962109708705)
XLA Ops:
  8.3 23.0 %copy.35 = f32[1,128,16,4096]{3,2,1,0:T(8,128)} copy(f32[1,128,16,4096]{3,2,1,0:T(8,128)} %param.15) | data formatting | bytes 67108864
  33.7 5.2 all-to-all-start
  39.4 26.2 %all-to-all-done = f32[8,16,4096]{2,1,0:T(8,128)} async-done(((f32[8,16,4096]{2,1,0:T(8,128)}), f32[8,16,4096]{2,1,0:T(8,128)}, u32[]{:S(2)}, u32[]{:S(2)}) %all-to-all-start) | async-done | bytes 2097184 | tf_op jit(solution)/shard_map/all_to_all | solution.py:47
  73.1 1091.3 %while.20 = (s32[]{:T(128)}, f32[128,16,4096]{2,1,0:T(8,128)}, bf16[64,4096]{1,0:T(8,128)(2,1)S(1)}, bf16[4,128,4096]{2,1,0:T(8,128)(2,1)}, s32[]{:T(128)}, /*in...) while((s32[]{:T(128)}, f32[128,16,4096]{2,1,0:T(8,128)}, ...), condition=%wide.region_8.9_spmd, body=%wide.region_3.8_spmd.sunk | while | flops 593301632 | bytes 59149148 | solution.py:94
  74.6 4.4 fusion.37
  79.1 12.5 %psum.33 = f32[64]{0:T(128)S(1)} all-reduce(f32[64]{0:T(128)S(1)} %get-tuple-element.514), channel_id=1, replica_groups=mesh['section'=8,'tensor'=4] {'tensor'}, use_global_device_ids=true, to_apply=%region_6.6 | all-reduce | flops 64 | bytes 512 | tf_op jit(solution)/shard_map/while/body/eval_jaxpr/psum | solution.py:67
  91.6 22.2 %all-reduce.2.cloned.1.call-done = f32[64,544]{1,0:T(8,128)} async-done(((f32[64,544]{1,0:T(8,128)}), f32[64,544]{1,0:T(8,128)}) %all-reduce.2.cloned.1.call-update) | async-done | bytes 139280 | tf_op jit(solution)/shard_map/while/body/eval_jaxpr/psum | solution.py:67
  118.4 14.9 %multiply_reduce_fusion.2 = (f32[64,4096]{1,0:T(8,128)S(1)}, f32[128,16,4096]{2,1,0:T(8,128)}) fusion(f32[128,16,4096]{2,1,0:T(8,128)} %get-tuple-element.548, s32[]{:T(128)S(6)} %select_n.300, f32[64,16]{1,0:T(8,128)S(1)} %get-tuple-element.515, f32[64,16]{1,0:T(8,128)S(1)} %get-tuple-element.516, f32[64,4096]{1,0:T(8,128)S(1)} %get-tuple-element.517, ...), kind=kLoop, calls=%fused_computation.6.clone.1 | loop fusion | flops 29097984 | bytes 36970500 | tf_op jit(solution)/shard_map/while/body/eval_jaxpr/reduce_sum | solution.py:80
  140.3 4.4 fusion.37
  144.8 10.5 psum.33
  155.3 31.7 %all-reduce.2.cloned.1.call-done = f32[64,544]{1,0:T(8,128)} async-done(((f32[64,544]{1,0:T(8,128)}), f32[64,544]{1,0:T(8,128)}) %all-reduce.2.cloned.1.call-update) | async-done | bytes 139280 | tf_op jit(solution)/shard_map/while/body/eval_jaxpr/psum | solution.py:67
  191.7 14.9 %multiply_reduce_fusion.2 = (f32[64,4096]{1,0:T(8,128)S(1)}, f32[128,16,4096]{2,1,0:T(8,128)}) fusion(f32[128,16,4096]{2,1,0:T(8,128)} %get-tuple-element.548, s32[]{:T(128)S(6)} %select_n.300, f32[64,16]{1,0:T(8,128)S(1)} %get-tuple-element.515, f32[64,16]{1,0:T(8,128)S(1)} %get-tuple-element.516, f32[64,4096]{1,0:T(8,128)S(1)} %get-tuple-element.517, ...), kind=kLoop, calls=%fused_computation.6.clone.1 | loop fusion | flops 29097984 | bytes 36970500 | tf_op jit(solution)/shard_map/while/body/eval_jaxpr/reduce_sum | solution.py:80
  213.6 4.4 fusion.37
  218.1 10.5 psum.33
  228.6 31.7 %all-reduce.2.cloned.1.call-done = f32[64,544]{1,0:T(8,128)} async-done(((f32[64,544]{1,0:T(8,128)}), f32[64,544]{1,0:T(8,128)}) %all-reduce.2.cloned.1.call-update) | async-done | bytes 139280 | tf_op jit(solution)/shard_map/while/body/eval_jaxpr/psum | solution.py:67
  265.0 14.9 %multiply_reduce_fusion.2 = (f32[64,4096]{1,0:T(8,128)S(1)}, f32[128,16,4096]{2,1,0:T(8,128)}) fusion(f32[128,16,4096]{2,1,0:T(8,128)} %get-tuple-element.548, s32[]{:T(128)S(6)} %select_n.300, f32[64,16]{1,0:T(8,128)S(1)} %get-tuple-element.515, f32[64,16]{1,0:T(8,128)S(1)} %get-tuple-element.516, f32[64,4096]{1,0:T(8,128)S(1)} %get-tuple-element.517, ...), kind=kLoop, calls=%fused_computation.6.clone.1 | loop fusion | flops 29097984 | bytes 36970500 | tf_op jit(solution)/shard_map/while/body/eval_jaxpr/reduce_sum | solution.py:80
  286.9 4.4 fusion.37
  291.4 10.5 psum.33
  301.9 31.7 %all-reduce.2.cloned.1.call-done = f32[64,544]{1,0:T(8,128)} async-done(((f32[64,544]{1,0:T(8,128)}), f32[64,544]{1,0:T(8,128)}) %all-reduce.2.cloned.1.call-update) | async-done | bytes 139280 | tf_op jit(solution)/shard_map/while/body/eval_jaxpr/psum | solution.py:67
  338.2 14.9 %multiply_reduce_fusion.2 = (f32[64,4096]{1,0:T(8,128)S(1)}, f32[128,16,4096]{2,1,0:T(8,128)}) fusion(f32[128,16,4096]{2,1,0:T(8,128)} %get-tuple-element.548, s32[]{:T(128)S(6)} %select_n.300, f32[64,16]{1,0:T(8,128)S(1)} %get-tuple-element.515, f32[64,16]{1,0:T(8,128)S(1)} %get-tuple-element.516, f32[64,4096]{1,0:T(8,128)S(1)} %get-tuple-element.517, ...), kind=kLoop, calls=%fused_computation.6.clone.1 | loop fusion | flops 29097984 | bytes 36970500 | tf_op jit(solution)/shard_map/while/body/eval_jaxpr/reduce_sum | solution.py:80
  364.6 10.5 psum.33
  375.1 31.7 %all-reduce.2.cloned.1.call-done = f32[64,544]{1,0:T(8,128)} async-done(((f32[64,544]{1,0:T(8,128)}), f32[64,544]{1,0:T(8,128)}) %all-reduce.2.cloned.1.call-update) | async-done | bytes 139280 | tf_op jit(solution)/shard_map/while/body/eval_jaxpr/psum | solution.py:67
  411.5 14.9 %multiply_reduce_fusion.2 = (f32[64,4096]{1,0:T(8,128)S(1)}, f32[128,16,4096]{2,1,0:T(8,128)}) fusion(f32[128,16,4096]{2,1,0:T(8,128)} %get-tuple-element.548, s32[]{:T(128)S(6)} %select_n.300, f32[64,16]{1,0:T(8,128)S(1)} %get-tuple-element.515, f32[64,16]{1,0:T(8,128)S(1)} %get-tuple-element.516, f32[64,4096]{1,0:T(8,128)S(1)} %get-tuple-element.517, ...), kind=kLoop, calls=%fused_computation.6.clone.1 | loop fusion | flops 29097984 | bytes 36970500 | tf_op jit(solution)/shard_map/while/body/eval_jaxpr/reduce_sum | solution.py:80
  433.4 4.4 fusion.37
  437.9 10.5 psum.33
  448.4 31.7 %all-reduce.2.cloned.1.call-done = f32[64,544]{1,0:T(8,128)} async-done(((f32[64,544]{1,0:T(8,128)}), f32[64,544]{1,0:T(8,128)}) %all-reduce.2.cloned.1.call-update) | async-done | bytes 139280 | tf_op jit(solution)/shard_map/while/body/eval_jaxpr/psum | solution.py:67
  484.8 14.9 %multiply_reduce_fusion.2 = (f32[64,4096]{1,0:T(8,128)S(1)}, f32[128,16,4096]{2,1,0:T(8,128)}) fusion(f32[128,16,4096]{2,1,0:T(8,128)} %get-tuple-element.548, s32[]{:T(128)S(6)} %select_n.300, f32[64,16]{1,0:T(8,128)S(1)} %get-tuple-element.515, f32[64,16]{1,0:T(8,128)S(1)} %get-tuple-element.516, f32[64,4096]{1,0:T(8,128)S(1)} %get-tuple-element.517, ...), kind=kLoop, calls=%fused_computation.6.clone.1 | loop fusion | flops 29097984 | bytes 36970500 | tf_op jit(solution)/shard_map/while/body/eval_jaxpr/reduce_sum | solution.py:80
  511.2 10.5 psum.33
  521.7 31.7 %all-reduce.2.cloned.1.call-done = f32[64,544]{1,0:T(8,128)} async-done(((f32[64,544]{1,0:T(8,128)}), f32[64,544]{1,0:T(8,128)}) %all-reduce.2.cloned.1.call-update) | async-done | bytes 139280 | tf_op jit(solution)/shard_map/while/body/eval_jaxpr/psum | solution.py:67
  558.1 14.9 %multiply_reduce_fusion.2 = (f32[64,4096]{1,0:T(8,128)S(1)}, f32[128,16,4096]{2,1,0:T(8,128)}) fusion(f32[128,16,4096]{2,1,0:T(8,128)} %get-tuple-element.548, s32[]{:T(128)S(6)} %select_n.300, f32[64,16]{1,0:T(8,128)S(1)} %get-tuple-element.515, f32[64,16]{1,0:T(8,128)S(1)} %get-tuple-element.516, f32[64,4096]{1,0:T(8,128)S(1)} %get-tuple-element.517, ...), kind=kLoop, calls=%fused_computation.6.clone.1 | loop fusion | flops 29097984 | bytes 36970500 | tf_op jit(solution)/shard_map/while/body/eval_jaxpr/reduce_sum | solution.py:80
  580.0 4.4 fusion.37
  584.4 10.5 psum.33
  594.9 31.7 %all-reduce.2.cloned.1.call-done = f32[64,544]{1,0:T(8,128)} async-done(((f32[64,544]{1,0:T(8,128)}), f32[64,544]{1,0:T(8,128)}) %all-reduce.2.cloned.1.call-update) | async-done | bytes 139280 | tf_op jit(solution)/shard_map/while/body/eval_jaxpr/psum | solution.py:67
  631.3 14.9 %multiply_reduce_fusion.2 = (f32[64,4096]{1,0:T(8,128)S(1)}, f32[128,16,4096]{2,1,0:T(8,128)}) fusion(f32[128,16,4096]{2,1,0:T(8,128)} %get-tuple-element.548, s32[]{:T(128)S(6)} %select_n.300, f32[64,16]{1,0:T(8,128)S(1)} %get-tuple-element.515, f32[64,16]{1,0:T(8,128)S(1)} %get-tuple-element.516, f32[64,4096]{1,0:T(8,128)S(1)} %get-tuple-element.517, ...), kind=kLoop, calls=%fused_computation.6.clone.1 | loop fusion | flops 29097984 | bytes 36970500 | tf_op jit(solution)/shard_map/while/body/eval_jaxpr/reduce_sum | solution.py:80
  653.2 4.4 fusion.37
  657.7 10.5 psum.33
  668.2 31.7 %all-reduce.2.cloned.1.call-done = f32[64,544]{1,0:T(8,128)} async-done(((f32[64,544]{1,0:T(8,128)}), f32[64,544]{1,0:T(8,128)}) %all-reduce.2.cloned.1.call-update) | async-done | bytes 139280 | tf_op jit(solution)/shard_map/while/body/eval_jaxpr/psum | solution.py:67
  704.5 14.9 %multiply_reduce_fusion.2 = (f32[64,4096]{1,0:T(8,128)S(1)}, f32[128,16,4096]{2,1,0:T(8,128)}) fusion(f32[128,16,4096]{2,1,0:T(8,128)} %get-tuple-element.548, s32[]{:T(128)S(6)} %select_n.300, f32[64,16]{1,0:T(8,128)S(1)} %get-tuple-element.515, f32[64,16]{1,0:T(8,128)S(1)} %get-tuple-element.516, f32[64,4096]{1,0:T(8,128)S(1)} %get-tuple-element.517, ...), kind=kLoop, calls=%fused_computation.6.clone.1 | loop fusion | flops 29097984 | bytes 36970500 | tf_op jit(solution)/shard_map/while/body/eval_jaxpr/reduce_sum | solution.py:80
  726.4 4.4 fusion.37
  730.9 10.5 psum.33
  741.4 31.7 %all-reduce.2.cloned.1.call-done = f32[64,544]{1,0:T(8,128)} async-done(((f32[64,544]{1,0:T(8,128)}), f32[64,544]{1,0:T(8,128)}) %all-reduce.2.cloned.1.call-update) | async-done | bytes 139280 | tf_op jit(solution)/shard_map/while/body/eval_jaxpr/psum | solution.py:67
  777.8 14.9 %multiply_reduce_fusion.2 = (f32[64,4096]{1,0:T(8,128)S(1)}, f32[128,16,4096]{2,1,0:T(8,128)}) fusion(f32[128,16,4096]{2,1,0:T(8,128)} %get-tuple-element.548, s32[]{:T(128)S(6)} %select_n.300, f32[64,16]{1,0:T(8,128)S(1)} %get-tuple-element.515, f32[64,16]{1,0:T(8,128)S(1)} %get-tuple-element.516, f32[64,4096]{1,0:T(8,128)S(1)} %get-tuple-element.517, ...), kind=kLoop, calls=%fused_computation.6.clone.1 | loop fusion | flops 29097984 | bytes 36970500 | tf_op jit(solution)/shard_map/while/body/eval_jaxpr/reduce_sum | solution.py:80
  799.7 4.4 fusion.37
  804.1 10.5 psum.33
  814.6 31.7 %all-reduce.2.cloned.1.call-done = f32[64,544]{1,0:T(8,128)} async-done(((f32[64,544]{1,0:T(8,128)}), f32[64,544]{1,0:T(8,128)}) %all-reduce.2.cloned.1.call-update) | async-done | bytes 139280 | tf_op jit(solution)/shard_map/while/body/eval_jaxpr/psum | solution.py:67
  851.0 14.9 %multiply_reduce_fusion.2 = (f32[64,4096]{1,0:T(8,128)S(1)}, f32[128,16,4096]{2,1,0:T(8,128)}) fusion(f32[128,16,4096]{2,1,0:T(8,128)} %get-tuple-element.548, s32[]{:T(128)S(6)} %select_n.300, f32[64,16]{1,0:T(8,128)S(1)} %get-tuple-element.515, f32[64,16]{1,0:T(8,128)S(1)} %get-tuple-element.516, f32[64,4096]{1,0:T(8,128)S(1)} %get-tuple-element.517, ...), kind=kLoop, calls=%fused_computation.6.clone.1 | loop fusion | flops 29097984 | bytes 36970500 | tf_op jit(solution)/shard_map/while/body/eval_jaxpr/reduce_sum | solution.py:80
  872.9 4.4 fusion.37
  877.3 10.5 psum.33
  887.8 31.7 %all-reduce.2.cloned.1.call-done = f32[64,544]{1,0:T(8,128)} async-done(((f32[64,544]{1,0:T(8,128)}), f32[64,544]{1,0:T(8,128)}) %all-reduce.2.cloned.1.call-update) | async-done | bytes 139280 | tf_op jit(solution)/shard_map/while/body/eval_jaxpr/psum | solution.py:67
  924.2 14.9 %multiply_reduce_fusion.2 = (f32[64,4096]{1,0:T(8,128)S(1)}, f32[128,16,4096]{2,1,0:T(8,128)}) fusion(f32[128,16,4096]{2,1,0:T(8,128)} %get-tuple-element.548, s32[]{:T(128)S(6)} %select_n.300, f32[64,16]{1,0:T(8,128)S(1)} %get-tuple-element.515, f32[64,16]{1,0:T(8,128)S(1)} %get-tuple-element.516, f32[64,4096]{1,0:T(8,128)S(1)} %get-tuple-element.517, ...), kind=kLoop, calls=%fused_computation.6.clone.1 | loop fusion | flops 29097984 | bytes 36970500 | tf_op jit(solution)/shard_map/while/body/eval_jaxpr/reduce_sum | solution.py:80
  946.1 4.4 fusion.37
  950.6 10.5 psum.33
  961.1 31.7 %all-reduce.2.cloned.1.call-done = f32[64,544]{1,0:T(8,128)} async-done(((f32[64,544]{1,0:T(8,128)}), f32[64,544]{1,0:T(8,128)}) %all-reduce.2.cloned.1.call-update) | async-done | bytes 139280 | tf_op jit(solution)/shard_map/while/body/eval_jaxpr/psum | solution.py:67
  997.4 14.9 %multiply_reduce_fusion.2 = (f32[64,4096]{1,0:T(8,128)S(1)}, f32[128,16,4096]{2,1,0:T(8,128)}) fusion(f32[128,16,4096]{2,1,0:T(8,128)} %get-tuple-element.548, s32[]{:T(128)S(6)} %select_n.300, f32[64,16]{1,0:T(8,128)S(1)} %get-tuple-element.515, f32[64,16]{1,0:T(8,128)S(1)} %get-tuple-element.516, f32[64,4096]{1,0:T(8,128)S(1)} %get-tuple-element.517, ...), kind=kLoop, calls=%fused_computation.6.clone.1 | loop fusion | flops 29097984 | bytes 36970500 | tf_op jit(solution)/shard_map/while/body/eval_jaxpr/reduce_sum | solution.py:80
  1019.3 4.4 fusion.37
  1023.8 10.5 psum.33
  1034.3 31.7 %all-reduce.2.cloned.1.call-done = f32[64,544]{1,0:T(8,128)} async-done(((f32[64,544]{1,0:T(8,128)}), f32[64,544]{1,0:T(8,128)}) %all-reduce.2.cloned.1.call-update) | async-done | bytes 139280 | tf_op jit(solution)/shard_map/while/body/eval_jaxpr/psum | solution.py:67
  1070.7 14.9 %multiply_reduce_fusion.2 = (f32[64,4096]{1,0:T(8,128)S(1)}, f32[128,16,4096]{2,1,0:T(8,128)}) fusion(f32[128,16,4096]{2,1,0:T(8,128)} %get-tuple-element.548, s32[]{:T(128)S(6)} %select_n.300, f32[64,16]{1,0:T(8,128)S(1)} %get-tuple-element.515, f32[64,16]{1,0:T(8,128)S(1)} %get-tuple-element.516, f32[64,4096]{1,0:T(8,128)S(1)} %get-tuple-element.517, ...), kind=kLoop, calls=%fused_computation.6.clone.1 | loop fusion | flops 29097984 | bytes 36970500 | tf_op jit(solution)/shard_map/while/body/eval_jaxpr/reduce_sum | solution.py:80
  1092.6 4.4 fusion.37
  1097.0 10.5 psum.33
  1107.5 31.7 %all-reduce.2.cloned.1.call-done = f32[64,544]{1,0:T(8,128)} async-done(((f32[64,544]{1,0:T(8,128)}), f32[64,544]{1,0:T(8,128)}) %all-reduce.2.cloned.1.call-update) | async-done | bytes 139280 | tf_op jit(solution)/shard_map/while/body/eval_jaxpr/psum | solution.py:67
  1143.9 14.9 %multiply_reduce_fusion.2 = (f32[64,4096]{1,0:T(8,128)S(1)}, f32[128,16,4096]{2,1,0:T(8,128)}) fusion(f32[128,16,4096]{2,1,0:T(8,128)} %get-tuple-element.548, s32[]{:T(128)S(6)} %select_n.300, f32[64,16]{1,0:T(8,128)S(1)} %get-tuple-element.515, f32[64,16]{1,0:T(8,128)S(1)} %get-tuple-element.516, f32[64,4096]{1,0:T(8,128)S(1)} %get-tuple-element.517, ...), kind=kLoop, calls=%fused_computation.6.clone.1 | loop fusion | flops 29097984 | bytes 36970500 | tf_op jit(solution)/shard_map/while/body/eval_jaxpr/reduce_sum | solution.py:80
  1170.2 11.3 all-to-all-start.1
  1181.5 15.5 %all-to-all-done.1 = bf16[8,16,4096]{2,1,0:T(8,128)(2,1)} async-done(((bf16[8,16,4096]{2,1,0:T(8,128)(2,1)}), bf16[8,16,4096]{2,1,0:T(8,128)(2,1)}, u32[]{:S(2)}, u32[]{:S(2)}) %all-to-all-start.1) | async-done | bytes 1048608 | tf_op jit(solution)/shard_map/all_to_all | solution.py:101
  (208 shorter events, 203.7 us)
Async XLA Ops:
  8.3 23.0 %copy-start.4 = (s32[3,8,3]{1,2,0:T(4,128)S(1)}, s32[3,8,3]{1,2,0:T(4,128)}, u32[]{:S(2)}) copy-start(s32[3,8,3]{1,2,0:T(4,128)} %param.24) | copy-start | bytes 868
  32.1 7.0 copy-start.5
  32.1 7.3 copy-start.3
  33.7 31.9 %all-to-all-start = ((f32[8,16,4096]{2,1,0:T(8,128)}), f32[8,16,4096]{2,1,0:T(8,128)}, u32[]{:S(2)}, u32[]{:S(2)}) async-start(f32[8,16,4096]{2,1,0:T(8,128)} %broadcast_select_fusion), calls=%async_computation | async-start | bytes 4194304 | tf_op jit(solution)/shard_map/all_to_all | solution.py:47
  39.4 33.6 %copy-start.1 = (f32[1,4096]{1,0:T(1,128)S(1)}, f32[1,4096]{1,0:T(1,128)}, u32[]{:S(2)}) copy-start(f32[1,4096]{1,0:T(1,128)} %param.22) | copy-start | bytes 49156
  39.4 33.6 %copy-start.2 = (f32[1,4096]{1,0:T(1,128)S(1)}, f32[1,4096]{1,0:T(1,128)}, u32[]{:S(2)}) copy-start(f32[1,4096]{1,0:T(1,128)} %param.21) | copy-start | bytes 49156
  39.4 33.6 %copy-start.6 = (f32[1,4096]{1,0:T(1,128)S(1)}, f32[1,4096]{1,0:T(1,128)}, u32[]{:S(2)}) copy-start(f32[1,4096]{1,0:T(1,128)} %param.19) | copy-start | bytes 49156
  73.1 40.7 %all-reduce.2.cloned.1.call-start = ((), (), s32[]{:S(2)}) async-start(), calls=%async_computation.2 | async-start | bytes 327680 | tf_op jit(solution)/shard_map/while/body/eval_jaxpr/psum | solution.py:67
  136.1 2.8 collective-permute-start
  138.9 48.1 %all-reduce.2.cloned.1.call-start = ((), (), s32[]{:S(2)}) async-start(), calls=%async_computation.2 | async-start | bytes 327680 | tf_op jit(solution)/shard_map/while/body/eval_jaxpr/psum | solution.py:67
  209.4 2.8 collective-permute-start
  212.2 48.1 %all-reduce.2.cloned.1.call-start = ((), (), s32[]{:S(2)}) async-start(), calls=%async_computation.2 | async-start | bytes 327680 | tf_op jit(solution)/shard_map/while/body/eval_jaxpr/psum | solution.py:67
  282.7 2.8 collective-permute-start
  285.5 48.1 %all-reduce.2.cloned.1.call-start = ((), (), s32[]{:S(2)}) async-start(), calls=%async_computation.2 | async-start | bytes 327680 | tf_op jit(solution)/shard_map/while/body/eval_jaxpr/psum | solution.py:67
  355.9 2.8 collective-permute-start
  358.7 48.1 %all-reduce.2.cloned.1.call-start = ((), (), s32[]{:S(2)}) async-start(), calls=%async_computation.2 | async-start | bytes 327680 | tf_op jit(solution)/shard_map/while/body/eval_jaxpr/psum | solution.py:67
  429.2 2.8 collective-permute-start
  432.0 48.1 %all-reduce.2.cloned.1.call-start = ((), (), s32[]{:S(2)}) async-start(), calls=%async_computation.2 | async-start | bytes 327680 | tf_op jit(solution)/shard_map/while/body/eval_jaxpr/psum | solution.py:67
  502.5 2.8 collective-permute-start
  505.3 48.1 %all-reduce.2.cloned.1.call-start = ((), (), s32[]{:S(2)}) async-start(), calls=%async_computation.2 | async-start | bytes 327680 | tf_op jit(solution)/shard_map/while/body/eval_jaxpr/psum | solution.py:67
  575.8 2.8 collective-permute-start
  578.6 48.1 %all-reduce.2.cloned.1.call-start = ((), (), s32[]{:S(2)}) async-start(), calls=%async_computation.2 | async-start | bytes 327680 | tf_op jit(solution)/shard_map/while/body/eval_jaxpr/psum | solution.py:67
  649.0 2.8 collective-permute-start
  651.8 48.0 %all-reduce.2.cloned.1.call-start = ((), (), s32[]{:S(2)}) async-start(), calls=%async_computation.2 | async-start | bytes 327680 | tf_op jit(solution)/shard_map/while/body/eval_jaxpr/psum | solution.py:67
  722.2 2.8 collective-permute-start
  725.0 48.1 %all-reduce.2.cloned.1.call-start = ((), (), s32[]{:S(2)}) async-start(), calls=%async_computation.2 | async-start | bytes 327680 | tf_op jit(solution)/shard_map/while/body/eval_jaxpr/psum | solution.py:67
  795.4 2.8 collective-permute-start
  798.2 48.0 %all-reduce.2.cloned.1.call-start = ((), (), s32[]{:S(2)}) async-start(), calls=%async_computation.2 | async-start | bytes 327680 | tf_op jit(solution)/shard_map/while/body/eval_jaxpr/psum | solution.py:67
  868.6 2.8 collective-permute-start
  871.4 48.1 %all-reduce.2.cloned.1.call-start = ((), (), s32[]{:S(2)}) async-start(), calls=%async_computation.2 | async-start | bytes 327680 | tf_op jit(solution)/shard_map/while/body/eval_jaxpr/psum | solution.py:67
  941.9 2.8 collective-permute-start
  944.7 48.0 %all-reduce.2.cloned.1.call-start = ((), (), s32[]{:S(2)}) async-start(), calls=%async_computation.2 | async-start | bytes 327680 | tf_op jit(solution)/shard_map/while/body/eval_jaxpr/psum | solution.py:67
  1015.1 2.8 collective-permute-start
  1017.9 48.1 %all-reduce.2.cloned.1.call-start = ((), (), s32[]{:S(2)}) async-start(), calls=%async_computation.2 | async-start | bytes 327680 | tf_op jit(solution)/shard_map/while/body/eval_jaxpr/psum | solution.py:67
  1088.3 2.8 collective-permute-start
  1091.1 48.1 %all-reduce.2.cloned.1.call-start = ((), (), s32[]{:S(2)}) async-start(), calls=%async_computation.2 | async-start | bytes 327680 | tf_op jit(solution)/shard_map/while/body/eval_jaxpr/psum | solution.py:67
  1161.6 2.8 collective-permute-start
  1170.2 26.9 %all-to-all-start.1 = ((bf16[8,16,4096]{2,1,0:T(8,128)(2,1)}), bf16[8,16,4096]{2,1,0:T(8,128)(2,1)}, u32[]{:S(2)}, u32[]{:S(2)}) async-start(bf16[8,16,4096]{2,1,0:T(8,128)(2,1)} %convert_element_type.95), calls=%async_computation.1 | async-start | bytes 2097152 | tf_op jit(solution)/shard_map/all_to_all | solution.py:101
  1199.4 0.9 copy-start
Sparse Core Ops, SparseCore 0:
  79.2 34.5 all-reduce.1
  144.9 42.0 all-reduce.1
  218.2 42.0 all-reduce.1
  291.5 42.0 all-reduce.1
  364.7 42.0 all-reduce.1
  438.0 42.0 all-reduce.1
  511.3 42.0 all-reduce.1
  584.6 42.0 all-reduce.1
  657.8 42.0 all-reduce.1
  731.0 42.0 all-reduce.1
  804.2 42.0 all-reduce.1
  877.4 42.0 all-reduce.1
  950.7 42.0 all-reduce.1
  1023.9 42.0 all-reduce.1
  1097.1 42.0 all-reduce.1
where the time goes:
time: 1210 us
  waiting for transfers between devices  530 us (44%)
  other arithmetic  306 us (25%)
  blocking collectives  159 us (13%)
  matrix products  120 us (10%)
  local copies, waits for them, and re-layouts  40.3 us (3%)
  starting transfers between devices  36.4 us (3%)
  between operations  13.9 us (1%)
    psum x15, waiting for transfers between devices, turn(): lax.psum((jnp.sum(widened * widened, axis=1), partial_proj), 'tensor')  466 us
    reduce_sum x15, other arithmetic, turn(): jnp.sum(newer * proj[:, rank + states:, None], axis=1) + skip[0] * normed_f  224 us
    psum x15, blocking collectives, turn(): lax.psum((jnp.sum(widened * widened, axis=1), partial_proj), 'tensor')  159 us
    dot_general x15, matrix products, turn(): jnp.dot(scaled, x_weight[0], preferred_element_type=jnp.float32)  66.6 us
    dot_general x15, matrix products, turn(): jnp.dot(low, dt_weight[0], preferred_element_type=jnp.float32) + dt_bias[0]  53.6 us
    dynamic_update_slice x15, other arithmetic, turn(): lax.dynamic_update_slice(produced, jnp.where(valid, result[None], before)...  39.2 us
    all_to_all x1, waiting for transfers between devices, shards(): lax.all_to_all(outgoing, 'section', split_axis=0, concat_axis=0, tiled=True)  26.2 us
    unnamed x16, local copies, waits for them, and re-layouts  25.1 us
  transfers between devices with their start and end apart: 32, of which 32 were waited for; matrix products, arithmetic and copies ran while one was open for 0% of the time, Pallas kernels for 0%

commit v1 on v0

v1 whole, which is shorter than its diff:
```python
import functools

import jax
import jax.numpy as jnp
from jax import lax
from jax.experimental import pallas as pl
from jax.experimental.pallas import tpu as pltpu
from jax.sharding import PartitionSpec as P

ROWS = 16
LANES = 128
COLS = 512
DEPTH = 1024
ANY = pl.BlockSpec(memory_space=pl.ANY)
VMEM = pl.BlockSpec(memory_space=pltpu.VMEM)
SMEM = pl.BlockSpec(memory_space=pltpu.SMEM)
LOG2E = 1.4426950408889634


def project_kernel(meta, arrived, inputs, gain, weight, out, stream, held, stream_sem, weight_sem):
    steps, rows, channels = stream.shape
    rank = out.shape[2] - LANES
    extra = weight.shape[1] - rank
    depth = min(DEPTH, channels)
    parts = channels // depth

    @pl.when(meta[1] == 1)
    def _():
        first = pl.multiple_of(meta[0], ROWS)
        fetch = [
            pltpu.make_async_copy(
                weight.at[0, :, pl.ds(k * depth, depth)],
                held.at[:, pl.ds(k * depth, depth)],
                weight_sem.at[k],
            )
            for k in range(parts)
        ]

        @pl.when(meta[2] == 0)
        def _():
            pltpu.make_async_copy(inputs.at[:, pl.ds(first, rows)], stream, stream_sem).start()

        @pl.when(meta[2] > 0)
        def _():
            pltpu.make_async_copy(arrived, stream, stream_sem).start()

        for copy in fetch:
            copy.start()
        pltpu.make_async_copy(arrived, stream, stream_sem).wait()
        total = jnp.zeros((steps * rows, rank + extra), jnp.float32)
        squares = jnp.zeros((steps * rows, 1), jnp.float32)
        for k in range(parts):
            part = pl.ds(k * depth, depth)
            wide = stream[:, :, part].astype(jnp.float32).reshape(steps * rows, depth)
            squares += jnp.sum(wide * wide, axis=1, keepdims=True)
            scaled = (wide * gain[:, part]).astype(jnp.bfloat16)
            fetch[k].wait()
            total += lax.dot_general(
                scaled,
                held[:, part],
                (((1,), (1,)), ((), ())),
                preferred_element_type=jnp.float32,
            )
        lane = lax.broadcasted_iota(jnp.int32, (steps * rows, LANES), 1)
        high = squares.astype(jnp.bfloat16).astype(jnp.float32)
        low = total[:, :rank].astype(jnp.bfloat16)
        tail = jnp.concatenate(
            [total[:, rank:], jnp.zeros((steps * rows, LANES - extra), jnp.float32)], axis=1
        )
        tail = jnp.where(lane == extra, high, jnp.where(lane == extra + 1, squares - high, tail))
        tail = tail.astype(jnp.bfloat16)
        for copy in range(out.shape[0]):
            out[copy, :, :rank] = low
            out[copy, :, rank:] = tail


def softplus(value):
    small = jnp.exp(-jnp.abs(value))
    return jnp.maximum(value, 0.0) + jnp.where(
        small < 1e-3, small - 0.5 * small * small, jnp.log(1.0 + small)
    )


def mix_kernel(
    width,
    layers,
    meta,
    plan,
    summands,
    arrived,
    inputs,
    state,
    landed,
    dt_weight,
    dt_bias,
    rates,
    skip,
    gain,
    gate,
    final_in,
    mixed_in,
    leaving_in,
    onward,
    final,
    mixed,
    leaving,
    stream,
    gates,
    result,
    hold,
    held,
    going,
    sizes,
    drives,
    totals,
    spread,
    sems,
    state_sem,
    weight_sem,
    final_sem,
    mixed_sem,
    going_sem,
):
    steps, rows, channels = stream.shape
    units = steps * rows
    rank = held.shape[0]
    states = rates.shape[0]
    swaps = going.shape[0]
    cols = min(COLS, channels)
    parts = channels // cols
    strips = cols // LANES
    flat = hold.reshape(channels // LANES * rows * states, LANES)

    @pl.when(meta[1] == 1)
    def _():
        first = pl.multiple_of(meta[0], ROWS)
        layer = meta[2]

        def planned(which, row, k):
            return plan[((which * 3 + row) * layers + layer) * swaps + k]

        @pl.when(layer == 0)
        def _():
            pltpu.make_async_copy(inputs.at[:, pl.ds(first, rows)], stream, sems.at[0]).start()

        @pl.when(layer > 0)
        def _():
            pltpu.make_async_copy(arrived, stream, sems.at[0]).start()

        gate_copy = pltpu.make_async_copy(gate.at[0, :, pl.ds(first, rows)], gates, sems.at[1])

        def at(j):
            return pl.ds(pl.multiple_of(j * cols, cols), cols)

        def weight_copy(j):
            return pltpu.make_async_copy(
                dt_weight.at[0, :, at(j)], held.at[:, at(j)], weight_sem.at[j]
            )

        def strip_at(c):
            return pl.ds(pl.multiple_of(c * LANES, LANES), LANES)

        def state_copy(c):
            return pltpu.make_async_copy(
                state.at[0, pl.ds(first, rows), :, strip_at(c)], hold.at[c], state_sem.at[c]
            )

        def final_copy(c):
            return pltpu.make_async_copy(
                hold.at[c], final.at[0, pl.ds(first, rows), :, strip_at(c)], final_sem.at[c]
            )

        def mixed_copy(j):
            return pltpu.make_async_copy(
                result.at[:, :, at(j)], mixed.at[0, :, pl.ds(first, rows), at(j)], mixed_sem.at[j]
            )

        def going_copy(k):
            return pltpu.make_async_copy(
                going.at[k], leaving.at[planned(1, 1, k)], going_sem.at[k]
            )

        for j in range(parts):
            weight_copy(j).start()
            for c in range(strips):
                state_copy(j * strips + c).start()
            if j == 0:
                gate_copy.start()

        total = jnp.sum(summands[...].astype(jnp.float32), axis=0)
        tail = total[:, rank:]
        squares = tail[:, 2 * states : 2 * states + 1] + tail[:, 2 * states + 1 : 2 * states + 2]
        inverse = 1.0 / jnp.sqrt(squares / width + 1e-05)
        low = (total[:, :rank] * inverse).astype(jnp.bfloat16)
        tail = tail * inverse
        for t in range(steps):
            for k in range(2 * states):
                column = tail[t * rows : (t + 1) * rows, k : k + 1]
                spread[t, k] = jnp.broadcast_to(column, (rows, LANES)).astype(jnp.bfloat16)
        pltpu.make_async_copy(arrived, stream, sems.at[0]).wait()
        gate_copy.wait()

        def part(j, carry):
            here = at(j)
            weight_copy(j).wait()
            size = softplus(
                jnp.dot(low, held[:, here], preferred_element_type=jnp.float32) + dt_bias[:, here]
            )
            wide = stream[:, :, here].astype(jnp.float32).reshape(units, cols)
            scaled = (wide * gain[:, here]).astype(jnp.bfloat16).astype(jnp.float32)
            normed = scaled * inverse
            sizes[...] = size.astype(jnp.bfloat16).reshape(steps, rows, cols)
            drives[...] = (size * normed).astype(jnp.bfloat16).reshape(steps, rows, cols)
            for c in range(strips):
                state_copy(j * strips + c).wait()
            for k in range(swaps):
                place = planned(0, 0, k) - first

                @pl.when((place >= 0) & (place < rows))
                def _():
                    for c in range(strips):
                        g = j * strips + c
                        hold[g, place] = landed[planned(0, 1, k), :, strip_at(g)].astype(
                            jnp.float32
                        )

            def strip(c, carry):
                inside = strip_at(c)
                lanes = strip_at(j * strips + c)
                base = (j * strips + c) * rows * states
                size = [sizes[t, :, inside] for t in range(steps)]
                drive = [drives[t, :, inside] for t in range(steps)]
                summed = [None] * steps
                group = [None] * steps
                for n in range(states):
                    rate = rates[n, :, lanes]
                    row = pl.ds(base + n, rows, stride=states)
                    h = flat[row, :].astype(jnp.bfloat16)
                    for t in range(steps):
                        h = jnp.exp2(size[t] * rate) * h + drive[t] * spread[t, n]
                        term = h * spread[t, states + n]
                        group[t] = term if n % 4 == 0 else group[t] + term
                        if n % 4 == 3:
                            term = group[t].astype(jnp.float32)
                            summed[t] = term if summed[t] is None else summed[t] + term
                    flat[row, :] = h.astype(jnp.float32)
                for t in range(steps):
                    totals[t * rows : (t + 1) * rows, inside] = summed[t]
                return carry

            lax.fori_loop(0, strips, strip, 0)
            for c in range(strips):
                final_copy(j * strips + c).start()
            for k in range(swaps):
                place = planned(1, 0, k) - first

                @pl.when((place >= 0) & (place < rows))
                def _():
                    for c in range(strips):
                        g = j * strips + c
                        going[k, :, strip_at(g)] = hold[g, place].astype(jnp.bfloat16)

            opened = gates[:, :, here].astype(jnp.float32).reshape(units, cols)
            value = (totals[...] + skip[:, here] * normed) * (opened * jax.nn.sigmoid(opened))
            value = value.astype(jnp.bfloat16)
            result[:, :, here] = value.reshape(steps, rows, cols)
            passed = (wide + value.astype(jnp.float32)).astype(jnp.bfloat16)
            onward[:, :, here] = passed.reshape(steps, rows, cols)
            mixed_copy(j).start()
            return carry

        lax.fori_loop(0, parts, part, 0)
        for k in range(swaps):
            place = planned(1, 0, k) - first

            @pl.when((place >= 0) & (place < rows))
            def _():
                going_copy(k).start()
                going_copy(k).wait()

        for j in range(parts):
            mixed_copy(j).wait()
        for c in range(parts * strips):
            final_copy(c).wait()


def pick_kernel(meta, plan, store, out):
    layers = out.shape[0]
    swaps = plan.shape[0] // (6 * layers)
    for layer in range(layers):
        slot = 0
        for k in range(swaps):
            asked = plan[(layers + layer) * swaps + k] == meta[0]
            slot = jnp.where(asked, plan[(2 * layers + layer) * swaps + k], slot)
        out[layer] = store[0, slot].astype(out.dtype)


def keep_kernel(meta, plan, store, returned, out):
    layers = returned.shape[0]
    swaps = plan.shape[0] // (6 * layers)
    for slot in range(store.shape[1]):
        source = -1
        for layer in range(layers):
            for k in range(swaps):
                named = (plan[(4 * layers + layer) * swaps + k] == meta[0]) & (
                    plan[(5 * layers + layer) * swaps + k] == slot
                )
                source = jnp.where(named, layer, source)

        @pl.when(source >= 0)
        def _():
            out[0, slot] = returned[source].astype(out.dtype)

        @pl.when(source < 0)
        def _():
            out[0, slot] = store[0, slot]


def leave(*refs):
    pass


def empty(shapes):
    return pl.pallas_call(leave, out_shape=shapes, out_specs=[ANY] * len(shapes))()


def shards(
    inputs,
    state,
    pool,
    x_weight,
    dt_weight,
    dt_bias,
    a_log,
    skip,
    gain,
    gate_input,
    swap_plan,
    evict_plan,
):
    section = lax.axis_index("section")
    holders = lax.axis_size("section")
    peers = lax.axis_size("tensor")
    channels = x_weight.shape[1]
    width = channels * peers
    rank = dt_weight.shape[1]
    states = a_log.shape[1]
    requests = state.shape[1]
    steps = inputs.shape[0]
    swaps = swap_plan.shape[2]
    units = requests // ROWS
    turns = units + holders - 1
    plan = jnp.concatenate([swap_plan.reshape(-1), evict_plan.reshape(-1)])
    weight = jnp.swapaxes(x_weight, 1, 2)
    rates = jnp.broadcast_to(
        (-LOG2E * jnp.exp(a_log[0])).astype(jnp.bfloat16)[:, None], (states, ROWS, channels)
    )
    place = section.astype(jnp.int32)[None]
    route = [(i, i + 1) for i in range(holders - 1)]

    stream_shape = jax.ShapeDtypeStruct((steps, ROWS, channels), jnp.bfloat16)
    partial_shape = jax.ShapeDtypeStruct((peers, steps * ROWS, rank + LANES), jnp.bfloat16)
    state_shape = jax.ShapeDtypeStruct(state.shape, state.dtype)
    mixed_shape = jax.ShapeDtypeStruct(gate_input.shape, gate_input.dtype)
    moved_shape = jax.ShapeDtypeStruct((holders, states, channels), jnp.bfloat16)

    def meta_of(turn):
        unit = turn - section
        valid = (unit >= 0) & (unit < units)
        first = jnp.clip(unit, 0, units - 1) * ROWS
        return jnp.stack([first, valid, section]).astype(jnp.int32)

    def project(meta, arrived):
        depth = min(DEPTH, channels)
        return pl.pallas_call(
            project_kernel,
            out_shape=partial_shape,
            in_specs=[SMEM, ANY, ANY, VMEM, ANY],
            out_specs=VMEM,
            scratch_shapes=[
                pltpu.VMEM(stream_shape.shape, jnp.bfloat16),
                pltpu.VMEM(weight.shape[1:], jnp.bfloat16),
                pltpu.SemaphoreType.DMA,
                pltpu.SemaphoreType.DMA((channels // depth,)),
            ],
            compiler_params=pltpu.CompilerParams(vmem_limit_bytes=24 * 2**20),
            cost_estimate=pl.CostEstimate(
                flops=2 * steps * ROWS * channels * (rank + LANES),
                bytes_accessed=2 * channels * (rank + LANES),
                transcendentals=0,
            ),
            name="project",
        )(meta, arrived, inputs, gain, weight)

    def mix(meta, summands, arrived, final, mixed, leaving):
        cols = min(COLS, channels)
        parts = channels // cols
        rows = steps * ROWS
        return pl.pallas_call(
            functools.partial(mix_kernel, width, holders),
            out_shape=[stream_shape, state_shape, mixed_shape, moved_shape],
            in_specs=[SMEM, SMEM, VMEM, ANY, ANY, ANY, VMEM, ANY, VMEM, VMEM, VMEM, VMEM]
            + [ANY] * 4,
            out_specs=[VMEM, ANY, ANY, ANY],
            scratch_shapes=[
                pltpu.VMEM(stream_shape.shape, jnp.bfloat16),
                pltpu.VMEM(stream_shape.shape, jnp.bfloat16),
                pltpu.VMEM(stream_shape.shape, jnp.bfloat16),
                pltpu.VMEM((channels // LANES, ROWS, states, LANES), jnp.float32),
                pltpu.VMEM((rank, channels), jnp.bfloat16),
                pltpu.VMEM((swaps, states, channels), jnp.bfloat16),
                pltpu.VMEM((steps, ROWS, cols), jnp.bfloat16),
                pltpu.VMEM((steps, ROWS, cols), jnp.bfloat16),
                pltpu.VMEM((rows, cols), jnp.float32),
                pltpu.VMEM((steps, 2 * states, ROWS, LANES), jnp.bfloat16),
                pltpu.SemaphoreType.DMA((2,)),
                pltpu.SemaphoreType.DMA((channels // LANES,)),
                pltpu.SemaphoreType.DMA((parts,)),
                pltpu.SemaphoreType.DMA((channels // LANES,)),
                pltpu.SemaphoreType.DMA((parts,)),
                pltpu.SemaphoreType.DMA((swaps,)),
            ],
            input_output_aliases={13: 1, 14: 2, 15: 3},
            compiler_params=pltpu.CompilerParams(vmem_limit_bytes=24 * 2**20),
            cost_estimate=pl.CostEstimate(
                flops=2 * rows * channels * rank + 8 * rows * states * channels,
                bytes_accessed=2 * channels * rank + 8 * ROWS * states * channels,
                transcendentals=rows * states * channels,
            ),
            name="mix",
        )(
            meta,
            plan,
            summands,
            arrived,
            inputs,
            state,
            landed,
            dt_weight,
            dt_bias,
            rates,
            skip,
            gain,
            gate_input,
            final,
            mixed,
            leaving,
        )

    def exchange(partial):
        return lax.all_to_all(partial, "tensor", split_axis=0, concat_axis=0, tiled=True)

    def swap(block):
        return lax.all_to_all(block, "section", split_axis=0, concat_axis=0, tiled=True)

    def turn(index, carry):
        summands, stream, *kept = carry
        sent, *kept = mix(meta_of(index), summands, stream, *kept)
        stream = lax.ppermute(sent, "section", route)
        summands = exchange(project(meta_of(index + 1), stream))
        return summands, stream, *kept

    picked = pl.pallas_call(
        pick_kernel, out_shape=moved_shape, in_specs=[SMEM, SMEM, VMEM], out_specs=VMEM, name="pick"
    )(place, plan, pool)
    landed = swap(picked)
    kept = empty([state_shape, mixed_shape, moved_shape])
    stream = jnp.zeros(stream_shape.shape, jnp.bfloat16)
    summands = exchange(project(meta_of(0), stream))
    summands, stream, *kept = lax.fori_loop(0, turns - 1, turn, (summands, stream, *kept))
    _, final, mixed, leaving = mix(meta_of(turns - 1), summands, stream, *kept)
    stored = pl.pallas_call(
        keep_kernel,
        out_shape=jax.ShapeDtypeStruct(pool.shape, pool.dtype),
        in_specs=[SMEM, SMEM, VMEM, VMEM],
        out_specs=VMEM,
        name="keep",
    )(place, plan, pool, swap(leaving))
    return (mixed, final, stored)


def solution(mesh):
    placed = (
        P(None, None, "tensor"),
        P("section", None, None, "tensor"),
        P("section", None, None, "tensor"),
        P("section", "tensor", None),
        P("section", None, "tensor"),
        P("section", "tensor"),
        P("section", None, "tensor"),
        P("section", "tensor"),
        P("section", "tensor"),
        P("section", None, None, "tensor"),
        P(),
        P(),
    )
    return jax.shard_map(
        shards,
        mesh=mesh,
        in_specs=placed,
        out_specs=(
            P("section", None, None, "tensor"),
            P("section", None, None, "tensor"),
            P("section", None, None, "tensor"),
        ),
        check_vma=False,
    )
```

time: 1210 us -> 620 us (0.51)
  waiting for transfers between devices: 530 us -> 39.3 us
  other arithmetic: 306 us -> 2.39 us
  Pallas kernels: 0 us -> 172 us
  matrix products: 120 us -> 0 us
  starting transfers between devices: 36.4 us -> 155 us
  blocking collectives: 159 us -> 240 us
  local copies, waits for them, and re-layouts: 40.3 us -> 8.73 us
  between operations: 13.9 us -> 0.76 us
    psum x15 -> x0, waiting for transfers between devices: 466 us -> none  [turn(): lax.psum((jnp.sum(widened * widened, axis=1), partial_proj), 'tensor')]
    reduce_sum x32 -> x0, other arithmetic: 245 us -> none  [the longest x15 224 us: turn(): jnp.sum(newer * proj[:, rank + states:, None], axis=1) + skip[0] * normed_f]
    all_to_all x0 -> x15, blocking collectives: none -> 240 us  [the longest x14 153 us: exchange(): lax.all_to_all(partial, 'tensor', split_axis=0, concat_axis=0, tiled=True)]
    pallas_call x0 -> x33, Pallas kernels: none -> 172 us  [the longest x15 130 us: mix(): pl.pallas_call(functools.partial(mix_kernel, width, holders), out_shape=[...]
    psum x15 -> x0, blocking collectives: 159 us -> none  [turn(): lax.psum((jnp.sum(widened * widened, axis=1), partial_proj), 'tensor')]
    ppermute x15 -> x14, starting transfers between devices: 19.8 us -> 145 us  [turn(): stream = lax.ppermute(sent, 'section', route)]
    dot_general x30 -> x0, matrix products: 120 us -> none  [the longest x15 66.6 us: turn(): jnp.dot(scaled, x_weight[0], preferred_element_type=jnp.float32)]
    dynamic_update_slice x15 -> x0, other arithmetic: 39.2 us -> none  [turn(): lax.dynamic_update_slice(produced, jnp.where(valid, result[None], before)...]
  transfers between devices with their start and end apart: 32 -> 16, of which waited for: 32 -> 16; matrix products, arithmetic and copies ran while one was open for 0% -> 0% of each run, Pallas kernels for 0% -> 0%
where the time goes in v1:
time: 620 us; the launch traced here: 619 us
  blocking collectives  240 us (39%)
  Pallas kernels  172 us (28%)
  starting transfers between devices  155 us (25%)
  waiting for transfers between devices  39.3 us (6%)
  local copies, waits for them, and re-layouts  8.73 us (1%)
    all_to_all x14, blocking collectives, exchange(): lax.all_to_all(partial, 'tensor', split_axis=0, concat_axis=0, tiled=True)  153 us
    ppermute x14, starting transfers between devices, turn(): stream = lax.ppermute(sent, 'section', route)  145 us
    pallas_call x15, Pallas kernels, mix(): pl.pallas_call(functools.partial(mix_kernel, width, holders), out_shape=[...  130 us
    all_to_all x1, blocking collectives, swap(): lax.all_to_all(block, 'section', split_axis=0, concat_axis=0, tiled=True)  86.4 us
    pallas_call x15, Pallas kernels, project(): pl.pallas_call(project_kernel, out_shape=partial_shape, in_specs=[SMEM, A...  37.1 us
    ppermute x14, waiting for transfers between devices, turn(): stream = lax.ppermute(sent, 'section', route)  19.5 us
    all_to_all x1, waiting for transfers between devices, swap(): lax.all_to_all(block, 'section', split_axis=0, concat_axis=0, tiled=True)  15.2 us
  transfers between devices with their start and end apart: 16, of which 16 were waited for; matrix products, arithmetic and copies ran while one was open for 0% of the time, Pallas kernels for 0%

profile of v1, /device:TPU:0, one launch (start us, length us, event | category | flops | bytes accessed | tf_op | source)
XLA Modules:
  0.0 618.7 jit_solution(11278551631121604927)
XLA Ops:
  0.8 4.9 project.6
  5.8 6.5 %all-to-all-start.1 = ((bf16[4,64,640]{2,1,0:T(8,128)(2,1)}), bf16[4,64,640]{2,1,0:T(8,128)(2,1)S(1)}, u32[]{:S(2)}, u32[]{:S(2)}) async-start(bf16[4,64,640]{2,1,0:T(8,128)(2,1)} %project.6), calls=%async_computation.1 | async-start | bytes 655360 | tf_op jit(solution)/shard_map/all_to_all | solution.py:451
  12.7 2.2 pick.1
  14.9 4.6 all-to-all-done.1
  19.5 3.6 all-to-all-start.2
  23.2 15.2 %all-to-all-done.2.landed = bf16[8,16,4096]{2,1,0:T(8,128)(2,1)S(1)} async-done(((bf16[8,16,4096]{2,1,0:T(8,128)(2,1)}), bf16[8,16,4096]{2,1,0:T(8,128)(2,1)S(1)}, u32[]{:S(2)}, u32[]{:S(2)}) %all-to-all-start.2) | async-done | bytes 1048608 | tf_op jit(solution)/shard_map/all_to_all | solution.py:454
  38.4 488.9 %while.22 = (s32[]{:T(128)}, bf16[4,64,640]{2,1,0:T(8,128)(2,1)S(1)}, bf16[4,16,4096]{2,1,0:T(8,128)(2,1)S(1)}, f32[1,128,16,4096]{3,2,1,0:T(8,128)}, bf16[1,4,1...) while((s32[]{:T(128)}, ...), condition=%wide.region_1.2_spmd.clone, body=%wide.region_0.1_spmd.clone.sunk | while | flops 637534208 | bytes 23855600 | solution.py:470
  39.1 15.0 %mix.7 = (bf16[4,16,4096]{2,1,0:T(8,128)(2,1)S(1)}, f32[1,128,16,4096]{3,2,1,0:T(8,128)}, bf16[1,4,128,4096]{3,2,1,0:T(8,128)(2,1)}, bf16[8,16,4096]{2,1,0:T(8,128)(2,1)S(1)}) custom-call(s32[3]{0:T(128)S(1)} %add_add_fusion.7.meta, s32[144]{0:T(256)S(1)} %get-tuple-element.535.plan, ...), custom_call_target="tpu_custom_call", output_to_operand_aliasing={{1}: (13, {}), {2}: (14, {}), {3}: (15, {})} | custom-call | flops 301989888 | bytes 12582912 | tf_op jit(solution)/shard_map/while/body/eval_jaxpr/mix/pallas_call | solution.py:399
  55.5 1.4 collective-permute-done.arrived
  56.9 4.0 project.7
  61.0 14.1 %all_to_all.27 = bf16[4,64,640]{2,1,0:T(8,128)(2,1)S(1)} all-to-all(bf16[4,64,640]{2,1,0:T(8,128)(2,1)S(1)} %project.7), channel_id=1, replica_groups=mesh['section'=8,'tensor'=4] {'tensor'}, dimensions={0} | all-to-all | bytes 655360 | tf_op jit(solution)/shard_map/while/body/eval_jaxpr/all_to_all | solution.py:451
  75.7 15.0 %mix.7 = (bf16[4,16,4096]{2,1,0:T(8,128)(2,1)S(1)}, f32[1,128,16,4096]{3,2,1,0:T(8,128)}, bf16[1,4,128,4096]{3,2,1,0:T(8,128)(2,1)}, bf16[8,16,4096]{2,1,0:T(8,128)(2,1)S(1)}) custom-call(s32[3]{0:T(128)S(1)} %add_add_fusion.7.meta, s32[144]{0:T(256)S(1)} %get-tuple-element.535.plan, ...), custom_call_target="tpu_custom_call", output_to_operand_aliasing={{1}: (13, {}), {2}: (14, {}), {3}: (15, {})} | custom-call | flops 301989888 | bytes 12582912 | tf_op jit(solution)/shard_map/while/body/eval_jaxpr/mix/pallas_call | solution.py:399
  92.2 1.4 collective-permute-done.arrived
  93.6 4.0 project.7
  97.6 11.1 %all_to_all.27 = bf16[4,64,640]{2,1,0:T(8,128)(2,1)S(1)} all-to-all(bf16[4,64,640]{2,1,0:T(8,128)(2,1)S(1)} %project.7), channel_id=1, replica_groups=mesh['section'=8,'tensor'=4] {'tensor'}, dimensions={0} | all-to-all | bytes 655360 | tf_op jit(solution)/shard_map/while/body/eval_jaxpr/all_to_all | solution.py:451
  109.3 15.0 %mix.7 = (bf16[4,16,4096]{2,1,0:T(8,128)(2,1)S(1)}, f32[1,128,16,4096]{3,2,1,0:T(8,128)}, bf16[1,4,128,4096]{3,2,1,0:T(8,128)(2,1)}, bf16[8,16,4096]{2,1,0:T(8,128)(2,1)S(1)}) custom-call(s32[3]{0:T(128)S(1)} %add_add_fusion.7.meta, s32[144]{0:T(256)S(1)} %get-tuple-element.535.plan, ...), custom_call_target="tpu_custom_call", output_to_operand_aliasing={{1}: (13, {}), {2}: (14, {}), {3}: (15, {})} | custom-call | flops 301989888 | bytes 12582912 | tf_op jit(solution)/shard_map/while/body/eval_jaxpr/mix/pallas_call | solution.py:399
  124.3 5.3 collective-permute-start
  129.7 1.4 collective-permute-done.arrived
  131.1 4.0 project.7
  135.1 10.4 %all_to_all.27 = bf16[4,64,640]{2,1,0:T(8,128)(2,1)S(1)} all-to-all(bf16[4,64,640]{2,1,0:T(8,128)(2,1)S(1)} %project.7), channel_id=1, replica_groups=mesh['section'=8,'tensor'=4] {'tensor'}, dimensions={0} | all-to-all | bytes 655360 | tf_op jit(solution)/shard_map/while/body/eval_jaxpr/all_to_all | solution.py:451
  146.2 15.1 %mix.7 = (bf16[4,16,4096]{2,1,0:T(8,128)(2,1)S(1)}, f32[1,128,16,4096]{3,2,1,0:T(8,128)}, bf16[1,4,128,4096]{3,2,1,0:T(8,128)(2,1)}, bf16[8,16,4096]{2,1,0:T(8,128)(2,1)S(1)}) custom-call(s32[3]{0:T(128)S(1)} %add_add_fusion.7.meta, s32[144]{0:T(256)S(1)} %get-tuple-element.535.plan, ...), custom_call_target="tpu_custom_call", output_to_operand_aliasing={{1}: (13, {}), {2}: (14, {}), {3}: (15, {})} | custom-call | flops 301989888 | bytes 12582912 | tf_op jit(solution)/shard_map/while/body/eval_jaxpr/mix/pallas_call | solution.py:399
  161.3 8.5 %collective-permute-start = (bf16[4,16,4096]{2,1,0:T(8,128)(2,1)S(1)}, bf16[4,16,4096]{2,1,0:T(8,128)(2,1)S(1)}, u32[]{:S(2)}, u32[]{:S(2)}) collective-permute-start(bf16[4,16,4096]{2,1,0:T(8,128)(2,1)S(1)} %get-tuple-element.478), channel_id=1, source_target_pairs={{0,4},{4,8},{8,12},{12,16},{16,20},{20,24},{24,28},{1,5},{5,9},{9,... | collective-permute-start | bytes 1572872 | tf_op jit(solution)/shard_map/while/body/eval_jaxpr/ppermute | solution.py:459
  169.9 1.4 collective-permute-done.arrived
  171.3 4.0 project.7
  175.3 10.7 %all_to_all.27 = bf16[4,64,640]{2,1,0:T(8,128)(2,1)S(1)} all-to-all(bf16[4,64,640]{2,1,0:T(8,128)(2,1)S(1)} %project.7), channel_id=1, replica_groups=mesh['section'=8,'tensor'=4] {'tensor'}, dimensions={0} | all-to-all | bytes 655360 | tf_op jit(solution)/shard_map/while/body/eval_jaxpr/all_to_all | solution.py:451
  186.7 15.0 %mix.7 = (bf16[4,16,4096]{2,1,0:T(8,128)(2,1)S(1)}, f32[1,128,16,4096]{3,2,1,0:T(8,128)}, bf16[1,4,128,4096]{3,2,1,0:T(8,128)(2,1)}, bf16[8,16,4096]{2,1,0:T(8,128)(2,1)S(1)}) custom-call(s32[3]{0:T(128)S(1)} %add_add_fusion.7.meta, s32[144]{0:T(256)S(1)} %get-tuple-element.535.plan, ...), custom_call_target="tpu_custom_call", output_to_operand_aliasing={{1}: (13, {}), {2}: (14, {}), {3}: (15, {})} | custom-call | flops 301989888 | bytes 12582912 | tf_op jit(solution)/shard_map/while/body/eval_jaxpr/mix/pallas_call | solution.py:399
  201.7 8.7 %collective-permute-start = (bf16[4,16,4096]{2,1,0:T(8,128)(2,1)S(1)}, bf16[4,16,4096]{2,1,0:T(8,128)(2,1)S(1)}, u32[]{:S(2)}, u32[]{:S(2)}) collective-permute-start(bf16[4,16,4096]{2,1,0:T(8,128)(2,1)S(1)} %get-tuple-element.478), channel_id=1, source_target_pairs={{0,4},{4,8},{8,12},{12,16},{16,20},{20,24},{24,28},{1,5},{5,9},{9,... | collective-permute-start | bytes 1572872 | tf_op jit(solution)/shard_map/while/body/eval_jaxpr/ppermute | solution.py:459
  210.4 1.4 collective-permute-done.arrived
  211.8 4.0 project.7
  215.8 10.7 %all_to_all.27 = bf16[4,64,640]{2,1,0:T(8,128)(2,1)S(1)} all-to-all(bf16[4,64,640]{2,1,0:T(8,128)(2,1)S(1)} %project.7), channel_id=1, replica_groups=mesh['section'=8,'tensor'=4] {'tensor'}, dimensions={0} | all-to-all | bytes 655360 | tf_op jit(solution)/shard_map/while/body/eval_jaxpr/all_to_all | solution.py:451
  227.2 15.1 %mix.7 = (bf16[4,16,4096]{2,1,0:T(8,128)(2,1)S(1)}, f32[1,128,16,4096]{3,2,1,0:T(8,128)}, bf16[1,4,128,4096]{3,2,1,0:T(8,128)(2,1)}, bf16[8,16,4096]{2,1,0:T(8,128)(2,1)S(1)}) custom-call(s32[3]{0:T(128)S(1)} %add_add_fusion.7.meta, s32[144]{0:T(256)S(1)} %get-tuple-element.535.plan, ...), custom_call_target="tpu_custom_call", output_to_operand_aliasing={{1}: (13, {}), {2}: (14, {}), {3}: (15, {})} | custom-call | flops 301989888 | bytes 12582912 | tf_op jit(solution)/shard_map/while/body/eval_jaxpr/mix/pallas_call | solution.py:399
  242.3 8.7 %collective-permute-start = (bf16[4,16,4096]{2,1,0:T(8,128)(2,1)S(1)}, bf16[4,16,4096]{2,1,0:T(8,128)(2,1)S(1)}, u32[]{:S(2)}, u32[]{:S(2)}) collective-permute-start(bf16[4,16,4096]{2,1,0:T(8,128)(2,1)S(1)} %get-tuple-element.478), channel_id=1, source_target_pairs={{0,4},{4,8},{8,12},{12,16},{16,20},{20,24},{24,28},{1,5},{5,9},{9,... | collective-permute-start | bytes 1572872 | tf_op jit(solution)/shard_map/while/body/eval_jaxpr/ppermute | solution.py:459
  251.1 1.4 collective-permute-done.arrived
  252.5 4.0 project.7
  256.5 10.7 %all_to_all.27 = bf16[4,64,640]{2,1,0:T(8,128)(2,1)S(1)} all-to-all(bf16[4,64,640]{2,1,0:T(8,128)(2,1)S(1)} %project.7), channel_id=1, replica_groups=mesh['section'=8,'tensor'=4] {'tensor'}, dimensions={0} | all-to-all | bytes 655360 | tf_op jit(solution)/shard_map/while/body/eval_jaxpr/all_to_all | solution.py:451
  267.9 15.0 %mix.7 = (bf16[4,16,4096]{2,1,0:T(8,128)(2,1)S(1)}, f32[1,128,16,4096]{3,2,1,0:T(8,128)}, bf16[1,4,128,4096]{3,2,1,0:T(8,128)(2,1)}, bf16[8,16,4096]{2,1,0:T(8,128)(2,1)S(1)}) custom-call(s32[3]{0:T(128)S(1)} %add_add_fusion.7.meta, s32[144]{0:T(256)S(1)} %get-tuple-element.535.plan, ...), custom_call_target="tpu_custom_call", output_to_operand_aliasing={{1}: (13, {}), {2}: (14, {}), {3}: (15, {})} | custom-call | flops 301989888 | bytes 12582912 | tf_op jit(solution)/shard_map/while/body/eval_jaxpr/mix/pallas_call | solution.py:399
  282.9 8.8 %collective-permute-start = (bf16[4,16,4096]{2,1,0:T(8,128)(2,1)S(1)}, bf16[4,16,4096]{2,1,0:T(8,128)(2,1)S(1)}, u32[]{:S(2)}, u32[]{:S(2)}) collective-permute-start(bf16[4,16,4096]{2,1,0:T(8,128)(2,1)S(1)} %get-tuple-element.478), channel_id=1, source_target_pairs={{0,4},{4,8},{8,12},{12,16},{16,20},{20,24},{24,28},{1,5},{5,9},{9,... | collective-permute-start | bytes 1572872 | tf_op jit(solution)/shard_map/while/body/eval_jaxpr/ppermute | solution.py:459
  293.2 4.0 project.7
  297.2 10.7 %all_to_all.27 = bf16[4,64,640]{2,1,0:T(8,128)(2,1)S(1)} all-to-all(bf16[4,64,640]{2,1,0:T(8,128)(2,1)S(1)} %project.7), channel_id=1, replica_groups=mesh['section'=8,'tensor'=4] {'tensor'}, dimensions={0} | all-to-all | bytes 655360 | tf_op jit(solution)/shard_map/while/body/eval_jaxpr/all_to_all | solution.py:451
  308.6 15.1 %mix.7 = (bf16[4,16,4096]{2,1,0:T(8,128)(2,1)S(1)}, f32[1,128,16,4096]{3,2,1,0:T(8,128)}, bf16[1,4,128,4096]{3,2,1,0:T(8,128)(2,1)}, bf16[8,16,4096]{2,1,0:T(8,128)(2,1)S(1)}) custom-call(s32[3]{0:T(128)S(1)} %add_add_fusion.7.meta, s32[144]{0:T(256)S(1)} %get-tuple-element.535.plan, ...), custom_call_target="tpu_custom_call", output_to_operand_aliasing={{1}: (13, {}), {2}: (14, {}), {3}: (15, {})} | custom-call | flops 301989888 | bytes 12582912 | tf_op jit(solution)/shard_map/while/body/eval_jaxpr/mix/pallas_call | solution.py:399
  323.7 8.5 %collective-permute-start = (bf16[4,16,4096]{2,1,0:T(8,128)(2,1)S(1)}, bf16[4,16,4096]{2,1,0:T(8,128)(2,1)S(1)}, u32[]{:S(2)}, u32[]{:S(2)}) collective-permute-start(bf16[4,16,4096]{2,1,0:T(8,128)(2,1)S(1)} %get-tuple-element.478), channel_id=1, source_target_pairs={{0,4},{4,8},{8,12},{12,16},{16,20},{20,24},{24,28},{1,5},{5,9},{9,... | collective-permute-start | bytes 1572872 | tf_op jit(solution)/shard_map/while/body/eval_jaxpr/ppermute | solution.py:459
  332.3 1.4 collective-permute-done.arrived
  334.3 10.7 %all_to_all.27 = bf16[4,64,640]{2,1,0:T(8,128)(2,1)S(1)} all-to-all(bf16[4,64,640]{2,1,0:T(8,128)(2,1)S(1)} %project.7), channel_id=1, replica_groups=mesh['section'=8,'tensor'=4] {'tensor'}, dimensions={0} | all-to-all | bytes 655360 | tf_op jit(solution)/shard_map/while/body/eval_jaxpr/all_to_all | solution.py:451
  347.0 25.8 %collective-permute-start = (bf16[4,16,4096]{2,1,0:T(8,128)(2,1)S(1)}, bf16[4,16,4096]{2,1,0:T(8,128)(2,1)S(1)}, u32[]{:S(2)}, u32[]{:S(2)}) collective-permute-start(bf16[4,16,4096]{2,1,0:T(8,128)(2,1)S(1)} %get-tuple-element.478), channel_id=1, source_target_pairs={{0,4},{4,8},{8,12},{12,16},{16,20},{20,24},{24,28},{1,5},{5,9},{9,... | collective-permute-start | bytes 1572872 | tf_op jit(solution)/shard_map/while/body/eval_jaxpr/ppermute | solution.py:459
  372.9 1.4 collective-permute-done.arrived
  374.9 10.7 %all_to_all.27 = bf16[4,64,640]{2,1,0:T(8,128)(2,1)S(1)} all-to-all(bf16[4,64,640]{2,1,0:T(8,128)(2,1)S(1)} %project.7), channel_id=1, replica_groups=mesh['section'=8,'tensor'=4] {'tensor'}, dimensions={0} | all-to-all | bytes 655360 | tf_op jit(solution)/shard_map/while/body/eval_jaxpr/all_to_all | solution.py:451
  387.6 8.7 %collective-permute-start = (bf16[4,16,4096]{2,1,0:T(8,128)(2,1)S(1)}, bf16[4,16,4096]{2,1,0:T(8,128)(2,1)S(1)}, u32[]{:S(2)}, u32[]{:S(2)}) collective-permute-start(bf16[4,16,4096]{2,1,0:T(8,128)(2,1)S(1)} %get-tuple-element.478), channel_id=1, source_target_pairs={{0,4},{4,8},{8,12},{12,16},{16,20},{20,24},{24,28},{1,5},{5,9},{9,... | collective-permute-start | bytes 1572872 | tf_op jit(solution)/shard_map/while/body/eval_jaxpr/ppermute | solution.py:459
  396.4 1.4 collective-permute-done.arrived
  398.4 10.7 %all_to_all.27 = bf16[4,64,640]{2,1,0:T(8,128)(2,1)S(1)} all-to-all(bf16[4,64,640]{2,1,0:T(8,128)(2,1)S(1)} %project.7), channel_id=1, replica_groups=mesh['section'=8,'tensor'=4] {'tensor'}, dimensions={0} | all-to-all | bytes 655360 | tf_op jit(solution)/shard_map/while/body/eval_jaxpr/all_to_all | solution.py:451
  411.1 25.9 %collective-permute-start = (bf16[4,16,4096]{2,1,0:T(8,128)(2,1)S(1)}, bf16[4,16,4096]{2,1,0:T(8,128)(2,1)S(1)}, u32[]{:S(2)}, u32[]{:S(2)}) collective-permute-start(bf16[4,16,4096]{2,1,0:T(8,128)(2,1)S(1)} %get-tuple-element.478), channel_id=1, source_target_pairs={{0,4},{4,8},{8,12},{12,16},{16,20},{20,24},{24,28},{1,5},{5,9},{9,... | collective-permute-start | bytes 1572872 | tf_op jit(solution)/shard_map/while/body/eval_jaxpr/ppermute | solution.py:459
  437.1 1.4 collective-permute-done.arrived
  439.1 10.7 %all_to_all.27 = bf16[4,64,640]{2,1,0:T(8,128)(2,1)S(1)} all-to-all(bf16[4,64,640]{2,1,0:T(8,128)(2,1)S(1)} %project.7), channel_id=1, replica_groups=mesh['section'=8,'tensor'=4] {'tensor'}, dimensions={0} | all-to-all | bytes 655360 | tf_op jit(solution)/shard_map/while/body/eval_jaxpr/all_to_all | solution.py:451
  451.8 9.8 %collective-permute-start = (bf16[4,16,4096]{2,1,0:T(8,128)(2,1)S(1)}, bf16[4,16,4096]{2,1,0:T(8,128)(2,1)S(1)}, u32[]{:S(2)}, u32[]{:S(2)}) collective-permute-start(bf16[4,16,4096]{2,1,0:T(8,128)(2,1)S(1)} %get-tuple-element.478), channel_id=1, source_target_pairs={{0,4},{4,8},{8,12},{12,16},{16,20},{20,24},{24,28},{1,5},{5,9},{9,... | collective-permute-start | bytes 1572872 | tf_op jit(solution)/shard_map/while/body/eval_jaxpr/ppermute | solution.py:459
  461.6 1.4 collective-permute-done.arrived
  463.6 10.7 %all_to_all.27 = bf16[4,64,640]{2,1,0:T(8,128)(2,1)S(1)} all-to-all(bf16[4,64,640]{2,1,0:T(8,128)(2,1)S(1)} %project.7), channel_id=1, replica_groups=mesh['section'=8,'tensor'=4] {'tensor'}, dimensions={0} | all-to-all | bytes 655360 | tf_op jit(solution)/shard_map/while/body/eval_jaxpr/all_to_all | solution.py:451
  476.3 14.6 %collective-permute-start = (bf16[4,16,4096]{2,1,0:T(8,128)(2,1)S(1)}, bf16[4,16,4096]{2,1,0:T(8,128)(2,1)S(1)}, u32[]{:S(2)}, u32[]{:S(2)}) collective-permute-start(bf16[4,16,4096]{2,1,0:T(8,128)(2,1)S(1)} %get-tuple-element.478), channel_id=1, source_target_pairs={{0,4},{4,8},{8,12},{12,16},{16,20},{20,24},{24,28},{1,5},{5,9},{9,... | collective-permute-start | bytes 1572872 | tf_op jit(solution)/shard_map/while/body/eval_jaxpr/ppermute | solution.py:459
  491.1 1.4 collective-permute-done.arrived
  493.1 10.7 %all_to_all.27 = bf16[4,64,640]{2,1,0:T(8,128)(2,1)S(1)} all-to-all(bf16[4,64,640]{2,1,0:T(8,128)(2,1)S(1)} %project.7), channel_id=1, replica_groups=mesh['section'=8,'tensor'=4] {'tensor'}, dimensions={0} | all-to-all | bytes 655360 | tf_op jit(solution)/shard_map/while/body/eval_jaxpr/all_to_all | solution.py:451
  505.8 8.8 %collective-permute-start = (bf16[4,16,4096]{2,1,0:T(8,128)(2,1)S(1)}, bf16[4,16,4096]{2,1,0:T(8,128)(2,1)S(1)}, u32[]{:S(2)}, u32[]{:S(2)}) collective-permute-start(bf16[4,16,4096]{2,1,0:T(8,128)(2,1)S(1)} %get-tuple-element.478), channel_id=1, source_target_pairs={{0,4},{4,8},{8,12},{12,16},{16,20},{20,24},{24,28},{1,5},{5,9},{9,... | collective-permute-start | bytes 1572872 | tf_op jit(solution)/shard_map/while/body/eval_jaxpr/ppermute | solution.py:459
  514.7 1.4 collective-permute-done.arrived
  516.7 10.7 %all_to_all.27 = bf16[4,64,640]{2,1,0:T(8,128)(2,1)S(1)} all-to-all(bf16[4,64,640]{2,1,0:T(8,128)(2,1)S(1)} %project.7), channel_id=1, replica_groups=mesh['section'=8,'tensor'=4] {'tensor'}, dimensions={0} | all-to-all | bytes 655360 | tf_op jit(solution)/shard_map/while/body/eval_jaxpr/all_to_all | solution.py:451
  527.6 2.1 mix.6
  529.8 86.4 %all_to_all.26.returned = bf16[8,16,4096]{2,1,0:T(8,128)(2,1)} all-to-all(bf16[8,16,4096]{2,1,0:T(8,128)(2,1)S(1)} %get-tuple-element.285), channel_id=1, replica_groups=mesh['section'=8,'tensor'=4] {'section'}, dimensions={0} | all-to-all | bytes 2097152 | tf_op jit(solution)/shard_map/all_to_all | solution.py:454
  616.2 2.6 keep.1
  (137 shorter events, 27.2 us)
Async XLA Ops:
  0.8 11.5 %copy-start.6 = (s32[3,8,3]{1,2,0:T(4,128)S(1)}, s32[3,8,3]{1,2,0:T(4,128)}, u32[]{:S(2)}) copy-start(s32[3,8,3]{1,2,0:T(4,128)} %param.24) | copy-start | bytes 868
  0.8 11.6 %copy-start.7 = (s32[3,8,3]{1,2,0:T(4,128)S(1)}, s32[3,8,3]{1,2,0:T(4,128)}, u32[]{:S(2)}) copy-start(s32[3,8,3]{1,2,0:T(4,128)} %param.25) | copy-start | bytes 868
  5.7 17.5 %copy-start.5 = (f32[1,16,4096]{2,1,0:T(8,128)S(1)}, f32[1,16,4096]{2,1,0:T(8,128)}, u32[]{:S(2)}) copy-start(f32[1,16,4096]{2,1,0:T(8,128)} %param.20) | copy-start | bytes 786436
  5.7 32.7 %copy-start.2 = (f32[1,4096]{1,0:T(1,128)S(1)}, f32[1,4096]{1,0:T(1,128)}, u32[]{:S(2)}) copy-start(f32[1,4096]{1,0:T(1,128)} %gain.3) | copy-start | bytes 49156
  5.7 32.7 %copy-start.3 = (f32[1,4096]{1,0:T(1,128)S(1)}, f32[1,4096]{1,0:T(1,128)}, u32[]{:S(2)}) copy-start(f32[1,4096]{1,0:T(1,128)} %dt_bias.1) | copy-start | bytes 49156
  5.8 32.7 %copy-start.4 = (f32[1,4096]{1,0:T(1,128)S(1)}, f32[1,4096]{1,0:T(1,128)}, u32[]{:S(2)}) copy-start(f32[1,4096]{1,0:T(1,128)} %skip.1) | copy-start | bytes 49156
  5.8 13.8 %all-to-all-start.1 = ((bf16[4,64,640]{2,1,0:T(8,128)(2,1)}), bf16[4,64,640]{2,1,0:T(8,128)(2,1)S(1)}, u32[]{:S(2)}, u32[]{:S(2)}) async-start(bf16[4,64,640]{2,1,0:T(8,128)(2,1)} %project.6), calls=%async_computation.1 | async-start | bytes 655360 | tf_op jit(solution)/shard_map/all_to_all | solution.py:451
  19.5 18.9 %all-to-all-start.2 = ((bf16[8,16,4096]{2,1,0:T(8,128)(2,1)}), bf16[8,16,4096]{2,1,0:T(8,128)(2,1)S(1)}, u32[]{:S(2)}, u32[]{:S(2)}) async-start(bf16[8,16,4096]{2,1,0:T(8,128)(2,1)} %pick.1), calls=%async_computation.2 | async-start | bytes 2097152 | tf_op jit(solution)/shard_map/all_to_all | solution.py:454
  38.5 0.7 copy-start
  54.1 2.8 collective-permute-start
  56.9 18.1 %copy-start.1 = (bf16[16,4096]{1,0:T(8,128)(2,1)S(1)}, bf16[16,4096]{1,0:T(8,128)(2,1)}, u32[]{:S(2)}) copy-start(bf16[16,4096]{1,0:T(8,128)(2,1)} %copy-done) | copy-start | bytes 393220 | tf_op jit(solution)/shard_map/while
  75.1 0.7 copy-start
  90.7 2.8 collective-permute-start
  93.6 15.1 %copy-start.1 = (bf16[16,4096]{1,0:T(8,128)(2,1)S(1)}, bf16[16,4096]{1,0:T(8,128)(2,1)}, u32[]{:S(2)}) copy-start(bf16[16,4096]{1,0:T(8,128)(2,1)} %copy-done) | copy-start | bytes 393220 | tf_op jit(solution)/shard_map/while
  108.7 0.7 copy-start
  124.3 6.8 %collective-permute-start = (bf16[4,16,4096]{2,1,0:T(8,128)(2,1)S(1)}, bf16[4,16,4096]{2,1,0:T(8,128)(2,1)S(1)}, u32[]{:S(2)}, u32[]{:S(2)}) collective-permute-start(bf16[4,16,4096]{2,1,0:T(8,128)(2,1)S(1)} %get-tuple-element.478), channel_id=1, source_target_pairs={{0,4},{4,8},{8,12},{12,16},{16,20},{20,24},{24,28},{1,5},{5,9},{9,... | collective-permute-start | bytes 1572872 | tf_op jit(solution)/shard_map/while/body/eval_jaxpr/ppermute | solution.py:459
  131.1 14.4 %copy-start.1 = (bf16[16,4096]{1,0:T(8,128)(2,1)S(1)}, bf16[16,4096]{1,0:T(8,128)(2,1)}, u32[]{:S(2)}) copy-start(bf16[16,4096]{1,0:T(8,128)(2,1)} %copy-done) | copy-start | bytes 393220 | tf_op jit(solution)/shard_map/while
  145.5 0.7 copy-start
  161.3 10.0 %collective-permute-start = (bf16[4,16,4096]{2,1,0:T(8,128)(2,1)S(1)}, bf16[4,16,4096]{2,1,0:T(8,128)(2,1)S(1)}, u32[]{:S(2)}, u32[]{:S(2)}) collective-permute-start(bf16[4,16,4096]{2,1,0:T(8,128)(2,1)S(1)} %get-tuple-element.478), channel_id=1, source_target_pairs={{0,4},{4,8},{8,12},{12,16},{16,20},{20,24},{24,28},{1,5},{5,9},{9,... | collective-permute-start | bytes 1572872 | tf_op jit(solution)/shard_map/while/body/eval_jaxpr/ppermute | solution.py:459
  171.3 14.7 %copy-start.1 = (bf16[16,4096]{1,0:T(8,128)(2,1)S(1)}, bf16[16,4096]{1,0:T(8,128)(2,1)}, u32[]{:S(2)}) copy-start(bf16[16,4096]{1,0:T(8,128)(2,1)} %copy-done) | copy-start | bytes 393220 | tf_op jit(solution)/shard_map/while
  186.0 0.7 copy-start
  201.7 10.2 %collective-permute-start = (bf16[4,16,4096]{2,1,0:T(8,128)(2,1)S(1)}, bf16[4,16,4096]{2,1,0:T(8,128)(2,1)S(1)}, u32[]{:S(2)}, u32[]{:S(2)}) collective-permute-start(bf16[4,16,4096]{2,1,0:T(8,128)(2,1)S(1)} %get-tuple-element.478), channel_id=1, source_target_pairs={{0,4},{4,8},{8,12},{12,16},{16,20},{20,24},{24,28},{1,5},{5,9},{9,... | collective-permute-start | bytes 1572872 | tf_op jit(solution)/shard_map/while/body/eval_jaxpr/ppermute | solution.py:459
  211.8 14.7 %copy-start.1 = (bf16[16,4096]{1,0:T(8,128)(2,1)S(1)}, bf16[16,4096]{1,0:T(8,128)(2,1)}, u32[]{:S(2)}) copy-start(bf16[16,4096]{1,0:T(8,128)(2,1)} %copy-done) | copy-start | bytes 393220 | tf_op jit(solution)/shard_map/while
  226.6 0.7 copy-start
  242.3 10.2 %collective-permute-start = (bf16[4,16,4096]{2,1,0:T(8,128)(2,1)S(1)}, bf16[4,16,4096]{2,1,0:T(8,128)(2,1)S(1)}, u32[]{:S(2)}, u32[]{:S(2)}) collective-permute-start(bf16[4,16,4096]{2,1,0:T(8,128)(2,1)S(1)} %get-tuple-element.478), channel_id=1, source_target_pairs={{0,4},{4,8},{8,12},{12,16},{16,20},{20,24},{24,28},{1,5},{5,9},{9,... | collective-permute-start | bytes 1572872 | tf_op jit(solution)/shard_map/while/body/eval_jaxpr/ppermute | solution.py:459
  252.5 14.7 %copy-start.1 = (bf16[16,4096]{1,0:T(8,128)(2,1)S(1)}, bf16[16,4096]{1,0:T(8,128)(2,1)}, u32[]{:S(2)}) copy-start(bf16[16,4096]{1,0:T(8,128)(2,1)} %copy-done) | copy-start | bytes 393220 | tf_op jit(solution)/shard_map/while
  267.2 0.7 copy-start
  282.9 10.3 %collective-permute-start = (bf16[4,16,4096]{2,1,0:T(8,128)(2,1)S(1)}, bf16[4,16,4096]{2,1,0:T(8,128)(2,1)S(1)}, u32[]{:S(2)}, u32[]{:S(2)}) collective-permute-start(bf16[4,16,4096]{2,1,0:T(8,128)(2,1)S(1)} %get-tuple-element.478), channel_id=1, source_target_pairs={{0,4},{4,8},{8,12},{12,16},{16,20},{20,24},{24,28},{1,5},{5,9},{9,... | collective-permute-start | bytes 1572872 | tf_op jit(solution)/shard_map/while/body/eval_jaxpr/ppermute | solution.py:459
  293.2 14.7 %copy-start.1 = (bf16[16,4096]{1,0:T(8,128)(2,1)S(1)}, bf16[16,4096]{1,0:T(8,128)(2,1)}, u32[]{:S(2)}) copy-start(bf16[16,4096]{1,0:T(8,128)(2,1)} %copy-done) | copy-start | bytes 393220 | tf_op jit(solution)/shard_map/while
  307.9 0.7 copy-start
  323.7 10.0 %collective-permute-start = (bf16[4,16,4096]{2,1,0:T(8,128)(2,1)S(1)}, bf16[4,16,4096]{2,1,0:T(8,128)(2,1)S(1)}, u32[]{:S(2)}, u32[]{:S(2)}) collective-permute-start(bf16[4,16,4096]{2,1,0:T(8,128)(2,1)S(1)} %get-tuple-element.478), channel_id=1, source_target_pairs={{0,4},{4,8},{8,12},{12,16},{16,20},{20,24},{24,28},{1,5},{5,9},{9,... | collective-permute-start | bytes 1572872 | tf_op jit(solution)/shard_map/while/body/eval_jaxpr/ppermute | solution.py:459
  333.7 11.3 %copy-start.1 = (bf16[16,4096]{1,0:T(8,128)(2,1)S(1)}, bf16[16,4096]{1,0:T(8,128)(2,1)}, u32[]{:S(2)}) copy-start(bf16[16,4096]{1,0:T(8,128)(2,1)} %copy-done) | copy-start | bytes 393220 | tf_op jit(solution)/shard_map/while
  345.0 0.7 copy-start
  347.0 27.3 %collective-permute-start = (bf16[4,16,4096]{2,1,0:T(8,128)(2,1)S(1)}, bf16[4,16,4096]{2,1,0:T(8,128)(2,1)S(1)}, u32[]{:S(2)}, u32[]{:S(2)}) collective-permute-start(bf16[4,16,4096]{2,1,0:T(8,128)(2,1)S(1)} %get-tuple-element.478), channel_id=1, source_target_pairs={{0,4},{4,8},{8,12},{12,16},{16,20},{20,24},{24,28},{1,5},{5,9},{9,... | collective-permute-start | bytes 1572872 | tf_op jit(solution)/shard_map/while/body/eval_jaxpr/ppermute | solution.py:459
  374.3 11.3 %copy-start.1 = (bf16[16,4096]{1,0:T(8,128)(2,1)S(1)}, bf16[16,4096]{1,0:T(8,128)(2,1)}, u32[]{:S(2)}) copy-start(bf16[16,4096]{1,0:T(8,128)(2,1)} %copy-done) | copy-start | bytes 393220 | tf_op jit(solution)/shard_map/while
  385.6 0.7 copy-start
  387.6 10.2 %collective-permute-start = (bf16[4,16,4096]{2,1,0:T(8,128)(2,1)S(1)}, bf16[4,16,4096]{2,1,0:T(8,128)(2,1)S(1)}, u32[]{:S(2)}, u32[]{:S(2)}) collective-permute-start(bf16[4,16,4096]{2,1,0:T(8,128)(2,1)S(1)} %get-tuple-element.478), channel_id=1, source_target_pairs={{0,4},{4,8},{8,12},{12,16},{16,20},{20,24},{24,28},{1,5},{5,9},{9,... | collective-permute-start | bytes 1572872 | tf_op jit(solution)/shard_map/while/body/eval_jaxpr/ppermute | solution.py:459
  397.8 11.3 %copy-start.1 = (bf16[16,4096]{1,0:T(8,128)(2,1)S(1)}, bf16[16,4096]{1,0:T(8,128)(2,1)}, u32[]{:S(2)}) copy-start(bf16[16,4096]{1,0:T(8,128)(2,1)} %copy-done) | copy-start | bytes 393220 | tf_op jit(solution)/shard_map/while
  409.1 0.7 copy-start
  411.1 27.4 %collective-permute-start = (bf16[4,16,4096]{2,1,0:T(8,128)(2,1)S(1)}, bf16[4,16,4096]{2,1,0:T(8,128)(2,1)S(1)}, u32[]{:S(2)}, u32[]{:S(2)}) collective-permute-start(bf16[4,16,4096]{2,1,0:T(8,128)(2,1)S(1)} %get-tuple-element.478), channel_id=1, source_target_pairs={{0,4},{4,8},{8,12},{12,16},{16,20},{20,24},{24,28},{1,5},{5,9},{9,... | collective-permute-start | bytes 1572872 | tf_op jit(solution)/shard_map/while/body/eval_jaxpr/ppermute | solution.py:459
  438.5 11.3 %copy-start.1 = (bf16[16,4096]{1,0:T(8,128)(2,1)S(1)}, bf16[16,4096]{1,0:T(8,128)(2,1)}, u32[]{:S(2)}) copy-start(bf16[16,4096]{1,0:T(8,128)(2,1)} %copy-done) | copy-start | bytes 393220 | tf_op jit(solution)/shard_map/while
  449.8 0.7 copy-start
  451.8 11.2 %collective-permute-start = (bf16[4,16,4096]{2,1,0:T(8,128)(2,1)S(1)}, bf16[4,16,4096]{2,1,0:T(8,128)(2,1)S(1)}, u32[]{:S(2)}, u32[]{:S(2)}) collective-permute-start(bf16[4,16,4096]{2,1,0:T(8,128)(2,1)S(1)} %get-tuple-element.478), channel_id=1, source_target_pairs={{0,4},{4,8},{8,12},{12,16},{16,20},{20,24},{24,28},{1,5},{5,9},{9,... | collective-permute-start | bytes 1572872 | tf_op jit(solution)/shard_map/while/body/eval_jaxpr/ppermute | solution.py:459
  463.0 11.3 %copy-start.1 = (bf16[16,4096]{1,0:T(8,128)(2,1)S(1)}, bf16[16,4096]{1,0:T(8,128)(2,1)}, u32[]{:S(2)}) copy-start(bf16[16,4096]{1,0:T(8,128)(2,1)} %copy-done) | copy-start | bytes 393220 | tf_op jit(solution)/shard_map/while
  474.3 0.7 copy-start
  476.3 16.1 %collective-permute-start = (bf16[4,16,4096]{2,1,0:T(8,128)(2,1)S(1)}, bf16[4,16,4096]{2,1,0:T(8,128)(2,1)S(1)}, u32[]{:S(2)}, u32[]{:S(2)}) collective-permute-start(bf16[4,16,4096]{2,1,0:T(8,128)(2,1)S(1)} %get-tuple-element.478), channel_id=1, source_target_pairs={{0,4},{4,8},{8,12},{12,16},{16,20},{20,24},{24,28},{1,5},{5,9},{9,... | collective-permute-start | bytes 1572872 | tf_op jit(solution)/shard_map/while/body/eval_jaxpr/ppermute | solution.py:459
  492.5 11.3 %copy-start.1 = (bf16[16,4096]{1,0:T(8,128)(2,1)S(1)}, bf16[16,4096]{1,0:T(8,128)(2,1)}, u32[]{:S(2)}) copy-start(bf16[16,4096]{1,0:T(8,128)(2,1)} %copy-done) | copy-start | bytes 393220 | tf_op jit(solution)/shard_map/while
  503.8 0.7 copy-start
  505.8 10.3 %collective-permute-start = (bf16[4,16,4096]{2,1,0:T(8,128)(2,1)S(1)}, bf16[4,16,4096]{2,1,0:T(8,128)(2,1)S(1)}, u32[]{:S(2)}, u32[]{:S(2)}) collective-permute-start(bf16[4,16,4096]{2,1,0:T(8,128)(2,1)S(1)} %get-tuple-element.478), channel_id=1, source_target_pairs={{0,4},{4,8},{8,12},{12,16},{16,20},{20,24},{24,28},{1,5},{5,9},{9,... | collective-permute-start | bytes 1572872 | tf_op jit(solution)/shard_map/while/body/eval_jaxpr/ppermute | solution.py:459
  516.1 11.3 %copy-start.1 = (bf16[16,4096]{1,0:T(8,128)(2,1)S(1)}, bf16[16,4096]{1,0:T(8,128)(2,1)}, u32[]{:S(2)}) copy-start(bf16[16,4096]{1,0:T(8,128)(2,1)} %copy-done) | copy-start | bytes 393220 | tf_op jit(solution)/shard_map/while

commit v2 on v0

v2 whole, which is shorter than its diff:
```python
import functools

import jax
import jax.numpy as jnp
from jax import lax
from jax.experimental import pallas as pl
from jax.experimental.pallas import tpu as pltpu
from jax.sharding import PartitionSpec as P

ROWS = 16
LANES = 128
COLS = 512
DEPTH = 1024
ANY = pl.BlockSpec(memory_space=pl.ANY)
HBM = pl.BlockSpec(memory_space=pltpu.HBM)
VMEM = pl.BlockSpec(memory_space=pltpu.VMEM)
SMEM = pl.BlockSpec(memory_space=pltpu.SMEM)
LOG2E = 1.4426950408889634


def softplus(value):
    small = jnp.exp(-jnp.abs(value))
    return jnp.maximum(value, 0.0) + jnp.where(
        small < 1e-3, small - 0.5 * small * small, jnp.log(1.0 + small)
    )


def finish(total, squares, rank):
    rows, width = total.shape
    extra = width - rank
    lane = lax.broadcasted_iota(jnp.int32, (rows, LANES), 1)
    high = squares.astype(jnp.bfloat16).astype(jnp.float32)
    tail = jnp.concatenate(
        [total[:, rank:], jnp.zeros((rows, LANES - extra), jnp.float32)], axis=1
    )
    tail = jnp.where(lane == extra, high, jnp.where(lane == extra + 1, squares - high, tail))
    return total[:, :rank].astype(jnp.bfloat16), tail.astype(jnp.bfloat16)


def open_kernel(meta, inputs, weight, gain, first, rest, block, held, total, sums, sems):
    steps, requests, channels = block.shape
    rank = first.shape[1] - LANES
    depth = min(DEPTH, channels)
    parts = channels // depth

    @pl.when(meta[0] == 0)
    def _():
        copies = []
        for k in range(parts):
            span = pl.ds(k * depth, depth)
            copies.append(
                (
                    pltpu.make_async_copy(weight.at[:, span], held.at[:, span], sems.at[0, k]),
                    pltpu.make_async_copy(
                        inputs.at[:, :, span], block.at[:, :, span], sems.at[1, k]
                    ),
                )
            )
            for copy in copies[-1]:
                copy.start()
        for k in range(parts):
            span = pl.ds(k * depth, depth)
            for copy in copies[k]:
                copy.wait()
            for t in range(steps):
                here = pl.ds(t * requests, requests)
                wide = block[t, :, span].astype(jnp.float32)
                squares = jnp.sum(wide * wide, axis=1, keepdims=True)
                product = lax.dot_general(
                    (wide * gain[:, span]).astype(jnp.bfloat16),
                    held[:, span],
                    (((1,), (1,)), ((), ())),
                    preferred_element_type=jnp.float32,
                )
                squares = jnp.broadcast_to(squares, (requests, LANES))
                total[here, :] = product if k == 0 else total[here, :] + product
                sums[here, :] = squares if k == 0 else sums[here, :] + squares
        for t in range(steps):
            here = pl.ds(t * requests, requests)
            low, tail = finish(total[here, :], sums[here, :1], rank)
            for unit in range(requests // ROWS):
                out = first if unit == 0 else rest
                start = max(unit - 1, 0) * steps * ROWS + t * ROWS
                out[start : start + ROWS, :rank] = low[unit * ROWS : (unit + 1) * ROWS]
                out[start : start + ROWS, rank:] = tail[unit * ROWS : (unit + 1) * ROWS]


def step_kernel(width, layers, peers, *refs):
    meta, plan, arrived = refs[:3]
    near, *others = refs[3 : 3 + peers]
    opening = refs[3 + peers : 3 + 2 * peers]
    (
        inputs,
        state,
        landed,
        dt_weight,
        dt_bias,
        rates,
        skip,
        gain,
        next_gain,
        gate,
        even_weight,
        odd_weight,
        final_in,
        mixed_in,
        leaving_in,
        onward,
        partial,
        final,
        mixed,
        leaving,
        stream,
        terms,
        gates,
        result,
        hold,
        held,
        weight,
        coming,
        going,
        size_rows,
        drive_rows,
        product,
        spread_in,
        spread_out,
        stream_sem,
        term_sem,
        gate_sem,
        state_sem,
        held_sem,
        weight_sem,
        final_sem,
        mixed_sem,
        coming_sem,
        going_sem,
    ) = refs[3 + 2 * peers :]
    steps, rows, channels = gates.shape
    units = steps * rows
    rank = dt_weight.shape[1]
    states = rates.shape[0]
    swaps = going.shape[0]
    cols = min(COLS, channels)
    parts = channels // cols
    depth = min(DEPTH, channels)
    layer = meta[2]

    @pl.when(meta[0] == 1)
    def _():
        first = pl.multiple_of(meta[1], ROWS)
        offset = pl.multiple_of(meta[3], ROWS)

        def planned(which, row, k):
            return plan[((which * 3 + row) * layers + layer) * swaps + k]

        def at(j):
            return pl.ds(pl.multiple_of(j * cols, cols), cols)

        gate_copy = pltpu.make_async_copy(gate.at[0, :, pl.ds(first, rows)], gates, gate_sem)

        def stream_copy(t, fresh):
            if fresh:
                source = inputs.at[t, pl.ds(first, rows)]
            else:
                source = arrived.at[pl.ds(t * rows, rows)]
            return pltpu.make_async_copy(
                source, stream.at[pl.ds(t * rows, rows)], stream_sem.at[t]
            )

        def term_copy(k, fresh):
            if fresh:
                source = opening[k].at[pl.ds(offset, units)]
            else:
                source = others[k - 1] if k else near
            return pltpu.make_async_copy(source, terms.at[k], term_sem.at[k])

        def held_copy(j):
            return pltpu.make_async_copy(
                dt_weight.at[0, :, at(j)], held.at[:, at(j)], held_sem.at[j]
            )

        def weight_copy(k, odd):
            span = pl.ds(k * depth, depth)
            source = odd_weight if odd else even_weight
            return pltpu.make_async_copy(
                source.at[:, span], weight.at[:, span], weight_sem.at[k]
            )

        def state_copy(j):
            return pltpu.make_async_copy(
                state.at[0, pl.ds(first, rows), :, at(j)], hold.at[:, :, at(j)], state_sem.at[j]
            )

        def final_copy(j):
            return pltpu.make_async_copy(
                hold.at[:, :, at(j)], final.at[0, pl.ds(first, rows), :, at(j)], final_sem.at[j]
            )

        def mixed_copy(j):
            return pltpu.make_async_copy(
                result.at[:, :, at(j)], mixed.at[0, :, pl.ds(first, rows), at(j)], mixed_sem.at[j]
            )

        def coming_copy(k):
            return pltpu.make_async_copy(
                landed.at[planned(0, 1, k)], coming.at[k], coming_sem.at[k]
            )

        def going_copy(k):
            return pltpu.make_async_copy(
                going.at[k], leaving.at[planned(1, 1, k)], going_sem.at[k]
            )

        def inside(which, k):
            place = planned(which, 0, k) - first
            return (place >= 0) & (place < rows)

        @pl.when(layer == 0)
        def _():
            for k in range(peers):
                term_copy(k, True).start()
            for t in range(steps):
                stream_copy(t, True).start()

        @pl.when(layer > 0)
        def _():
            for k in range(peers):
                term_copy(k, False).start()
            for t in range(steps):
                stream_copy(t, False).start()

        gate_copy.start()
        for k in range(swaps):

            @pl.when(inside(0, k))
            def _():
                coming_copy(k).start()

        for j in range(parts):
            held_copy(j).start()
            state_copy(j).start()

        @pl.when(layer % 2 == 0)
        def _():
            for k in range(channels // depth):
                weight_copy(k, False).start()

        @pl.when(layer % 2 == 1)
        def _():
            for k in range(channels // depth):
                weight_copy(k, True).start()

        for k in range(peers):
            term_copy(k, False).wait()
        total = jnp.sum(terms[...].astype(jnp.float32), axis=0)
        tail = total[:, rank:]
        squares = tail[:, 2 * states : 2 * states + 1] + tail[:, 2 * states + 1 : 2 * states + 2]
        inverse = 1.0 / jnp.sqrt(squares / width + 1e-05)
        low = (total[:, :rank] * inverse).astype(jnp.bfloat16)
        turned = (tail * inverse).T
        for row in range(units):
            column = turned[: 2 * states, row : row + 1]
            wide = jnp.broadcast_to(column, (2 * states, LANES)).astype(jnp.bfloat16)
            spread_in[row] = wide[:states]
            spread_out[row] = wide[states:]
        gather = (
            lax.broadcasted_iota(jnp.int32, (rows, rows * states), 1) // states
            == lax.broadcasted_iota(jnp.int32, (rows, rows * states), 0)
        ).astype(jnp.bfloat16)
        for k in range(swaps):

            @pl.when(inside(0, k))
            def _():
                coming_copy(k).wait()

        for t in range(steps):
            stream_copy(t, False).wait()
        gate_copy.wait()

        def part(j, carry):
            here = at(j)
            held_copy(j).wait()
            size = softplus(
                jnp.dot(low, held[:, here], preferred_element_type=jnp.float32) + dt_bias[:, here]
            )
            wide = stream[:, here].astype(jnp.float32)
            normed = wide * gain[:, here] * inverse
            size_rows[...] = size
            drive_rows[...] = size * normed
            state_copy(j).wait()
            for k in range(swaps):
                place = planned(0, 0, k) - first

                @pl.when((place >= 0) & (place < rows))
                def _():
                    hold[place, :, here] = coming[k, :, here].astype(jnp.float32)

            rate = rates[:, here]
            for r in range(rows):
                h = hold[r, :, here].astype(jnp.bfloat16)
                for t in range(steps):
                    row = t * rows + r
                    size_row = jnp.broadcast_to(
                        size_rows[row : row + 1, :], (states, cols)
                    ).astype(jnp.bfloat16)
                    drive_row = jnp.broadcast_to(
                        drive_rows[row : row + 1, :], (states, cols)
                    ).astype(jnp.bfloat16)
                    b = jnp.concatenate([spread_in[row]] * (cols // LANES), axis=1)
                    c = jnp.concatenate([spread_out[row]] * (cols // LANES), axis=1)
                    h = jnp.exp2(size_row * rate) * h + drive_row * b
                    product[t, r * states : (r + 1) * states, :] = h * c
                hold[r, :, here] = h.astype(jnp.float32)
            final_copy(j).start()
            for k in range(swaps):
                place = planned(1, 0, k) - first

                @pl.when((place >= 0) & (place < rows))
                def _():
                    going[k, :, here] = hold[place, :, here].astype(jnp.bfloat16)

            summed = jnp.concatenate(
                [
                    jnp.dot(gather, product[t], preferred_element_type=jnp.float32)
                    for t in range(steps)
                ],
                axis=0,
            )
            opened = gates[:, :, here].astype(jnp.float32).reshape(units, cols)
            value = (summed + skip[:, here] * normed) * (opened * jax.nn.sigmoid(opened))
            value = value.astype(jnp.bfloat16)
            result[:, :, here] = value.reshape(steps, rows, cols)
            mixed_copy(j).start()

            onward[:, here] = (wide + value.astype(jnp.float32)).astype(jnp.bfloat16)
            return carry

        lax.fori_loop(0, parts, part, 0)
        for k in range(swaps):
            place = planned(1, 0, k) - first

            @pl.when((place >= 0) & (place < rows))
            def _():
                going_copy(k).start()
                going_copy(k).wait()

        total = jnp.zeros((units, weight.shape[0]), jnp.float32)
        squares = jnp.zeros((units, 1), jnp.float32)
        for k in range(channels // depth):
            span = pl.ds(k * depth, depth)
            wide = onward[:, span].astype(jnp.float32)
            squares += jnp.sum(wide * wide, axis=1, keepdims=True)
            scaled = (wide * next_gain[:, span]).astype(jnp.bfloat16)
            weight_copy(k, False).wait()
            total += lax.dot_general(
                scaled,
                weight[:, span],
                (((1,), (1,)), ((), ())),
                preferred_element_type=jnp.float32,
            )
        low, tail = finish(total, squares, rank)
        partial[:, :rank] = low
        partial[:, rank:] = tail
        for j in range(parts):
            mixed_copy(j).wait()
            final_copy(j).wait()


def pick_kernel(meta, plan, store, out):
    layers = out.shape[0]
    swaps = plan.shape[0] // (6 * layers)
    for layer in range(layers):
        slot = 0
        for k in range(swaps):
            asked = plan[(layers + layer) * swaps + k] == meta[0]
            slot = jnp.where(asked, plan[(2 * layers + layer) * swaps + k], slot)
        out[layer] = store[0, slot].astype(out.dtype)


def keep_kernel(meta, plan, store, returned, out):
    layers = returned.shape[0]
    swaps = plan.shape[0] // (6 * layers)
    for slot in range(store.shape[1]):
        source = -1
        for layer in range(layers):
            for k in range(swaps):
                named = (plan[(4 * layers + layer) * swaps + k] == meta[0]) & (
                    plan[(5 * layers + layer) * swaps + k] == slot
                )
                source = jnp.where(named, layer, source)

        @pl.when(source >= 0)
        def _():
            out[0, slot] = returned[source].astype(out.dtype)

        @pl.when(source < 0)
        def _():
            out[0, slot] = store[0, slot]


def leave(*refs):
    pass


def empty(shapes):
    return pl.pallas_call(leave, out_shape=shapes, out_specs=[HBM] * len(shapes))()


def shards(
    inputs,
    state,
    pool,
    x_weight,
    dt_weight,
    dt_bias,
    a_log,
    skip,
    gain,
    gate_input,
    swap_plan,
    evict_plan,
):
    section = lax.axis_index("section")
    holders = lax.axis_size("section")
    peers = lax.axis_size("tensor")
    channels = x_weight.shape[1]
    width = channels * peers
    rank = dt_weight.shape[1]
    states = a_log.shape[1]
    requests = state.shape[1]
    steps = inputs.shape[0]
    swaps = swap_plan.shape[2]
    units = requests // ROWS
    rows = steps * ROWS
    cols = min(COLS, channels)
    parts = channels // cols
    turns = units + holders - 1
    plan = jnp.concatenate([swap_plan.reshape(-1), evict_plan.reshape(-1)])
    weight = jnp.swapaxes(x_weight[0], 0, 1)
    even = [(i + 1, i) for i in range(0, holders - 1, 2)]
    odd = [(i + 1, i) for i in range(1, holders - 1, 2)]
    odd_weight = lax.ppermute(weight, "section", odd)
    even_weight = lax.ppermute(weight, "section", even)
    next_gain = lax.ppermute(gain, "section", even + odd)
    rates = (-LOG2E * jnp.exp(a_log[0])).astype(jnp.bfloat16)
    place = section.astype(jnp.int32)[None]
    onto = [(i, i + 1) for i in range(holders - 1)]

    block_shape = jax.ShapeDtypeStruct((rows, channels), jnp.bfloat16)
    partial_shape = jax.ShapeDtypeStruct((rows, rank + LANES), jnp.bfloat16)
    rest_shape = jax.ShapeDtypeStruct(((units - 1) * rows, rank + LANES), jnp.bfloat16)
    stream_shape = (steps, ROWS, channels)
    state_shape = jax.ShapeDtypeStruct(state.shape, state.dtype)
    mixed_shape = jax.ShapeDtypeStruct(gate_input.shape, gate_input.dtype)
    moved_shape = jax.ShapeDtypeStruct((holders, states, channels), jnp.bfloat16)
    depth = min(DEPTH, channels)

    def meta_of(turn):
        unit = turn - section
        valid = (unit >= 0) & (unit < units)
        unit = jnp.clip(unit, 0, units - 1)
        return jnp.stack(
            [valid, unit * ROWS, section, jnp.maximum(unit - 1, 0) * rows]
        ).astype(jnp.int32)

    def around(block):
        size = range(peers)
        return [block] + [
            lax.ppermute(block, "tensor", [(i, (i + shift) % peers) for i in size])
            for shift in range(1, peers)
        ]

    def step(meta, blocks, opening, weights, final, mixed, leaving):
        given = 3 + 2 * peers
        return pl.pallas_call(
            functools.partial(step_kernel, width, holders, peers),
            out_shape=[block_shape, partial_shape, state_shape, mixed_shape, moved_shape],
            in_specs=[SMEM, SMEM]
            + [ANY] * (2 * peers + 1)
            + [HBM, HBM, ANY, ANY]
            + [VMEM] * 5
            + [HBM, ANY, ANY]
            + [HBM] * 3,
            out_specs=[VMEM, VMEM, HBM, HBM, HBM],
            scratch_shapes=[
                pltpu.VMEM(block_shape.shape, jnp.bfloat16),
                pltpu.VMEM((peers, *partial_shape.shape), jnp.bfloat16),
                pltpu.VMEM(stream_shape, jnp.bfloat16),
                pltpu.VMEM(stream_shape, jnp.bfloat16),
                pltpu.VMEM((ROWS, states, channels), jnp.float32),
                pltpu.VMEM((rank, channels), jnp.bfloat16),
                pltpu.VMEM(weight.shape, jnp.bfloat16),
                pltpu.VMEM((swaps, states, channels), jnp.bfloat16),
                pltpu.VMEM((swaps, states, channels), jnp.bfloat16),
                pltpu.VMEM((rows, cols), jnp.float32),
                pltpu.VMEM((rows, cols), jnp.float32),
                pltpu.VMEM((steps, ROWS * states, cols), jnp.bfloat16),
                pltpu.VMEM((rows, states, LANES), jnp.bfloat16),
                pltpu.VMEM((rows, states, LANES), jnp.bfloat16),
                pltpu.SemaphoreType.DMA((steps,)),
                pltpu.SemaphoreType.DMA((peers,)),
                pltpu.SemaphoreType.DMA,
                pltpu.SemaphoreType.DMA((parts,)),
                pltpu.SemaphoreType.DMA((parts,)),
                pltpu.SemaphoreType.DMA((channels // depth,)),
                pltpu.SemaphoreType.DMA((parts,)),
                pltpu.SemaphoreType.DMA((parts,)),
                pltpu.SemaphoreType.DMA((swaps,)),
                pltpu.SemaphoreType.DMA((swaps,)),
            ],
            input_output_aliases={given + 12 + k: 2 + k for k in range(3)},
            compiler_params=pltpu.CompilerParams(vmem_limit_bytes=28 * 2**20),
            cost_estimate=pl.CostEstimate(
                flops=4 * rows * channels * (rank + LANES) + 8 * rows * states * channels,
                bytes_accessed=4 * channels * rank + 8 * ROWS * states * channels,
                transcendentals=rows * states * channels,
            ),
            name="step",
        )(
            meta,
            plan,
            *blocks,
            *opening,
            inputs,
            state,
            landed,
            dt_weight,
            dt_bias,
            rates,
            skip,
            gain,
            next_gain,
            gate_input,
            *weights,
            final,
            mixed,
            leaving,
        )

    def send(block, partial):
        near = lax.ppermute(partial, "section", onto)
        arrived = lax.ppermute(block, "section", onto)
        return [arrived, *around(near)]

    def swap(block):
        return lax.all_to_all(block, "section", split_axis=0, concat_axis=0, tiled=True)

    def turn(index, carry):
        blocks, kept = carry
        block, partial, *kept = step(
            meta_of(index), blocks, rest, (even_weight, odd_weight), *kept
        )
        return send(block, partial), kept

    picked = pl.pallas_call(
        pick_kernel, out_shape=moved_shape, in_specs=[SMEM, SMEM, VMEM], out_specs=VMEM, name="pick"
    )(place, plan, pool)
    first, rest = pl.pallas_call(
        open_kernel,
        out_shape=[partial_shape, rest_shape],
        in_specs=[SMEM, HBM, HBM, VMEM],
        out_specs=[VMEM, VMEM],
        scratch_shapes=[
            pltpu.VMEM(inputs.shape, jnp.bfloat16),
            pltpu.VMEM(weight.shape, jnp.bfloat16),
            pltpu.VMEM((steps * requests, weight.shape[0]), jnp.float32),
            pltpu.VMEM((steps * requests, LANES), jnp.float32),
            pltpu.SemaphoreType.DMA((2, channels // depth)),
        ],
        compiler_params=pltpu.CompilerParams(vmem_limit_bytes=28 * 2**20),
        name="open",
    )(place, inputs, weight, gain)
    landed = swap(picked)
    first = around(first)
    rest = around(rest)
    *kept, block = empty([state_shape, mixed_shape, moved_shape, block_shape])
    blocks = [block, *first]
    block, partial, *kept = step(meta_of(0), blocks, first, (even_weight, even_weight), *kept)
    blocks, kept = lax.fori_loop(1, turns - 1, turn, (send(block, partial), kept))
    _, _, final, mixed, leaving = step(
        meta_of(turns - 1), blocks, rest, (even_weight, odd_weight), *kept
    )
    stored = pl.pallas_call(
        keep_kernel,
        out_shape=jax.ShapeDtypeStruct(pool.shape, pool.dtype),
        in_specs=[SMEM, SMEM, VMEM, VMEM],
        out_specs=VMEM,
        name="keep",
    )(place, plan, pool, swap(leaving))
    return (mixed, final, stored)


def solution(mesh):
    placed = (
        P(None, None, "tensor"),
        P("section", None, None, "tensor"),
        P("section", None, None, "tensor"),
        P("section", "tensor", None),
        P("section", None, "tensor"),
        P("section", "tensor"),
        P("section", None, "tensor"),
        P("section", "tensor"),
        P("section", "tensor"),
        P("section", None, None, "tensor"),
        P(),
        P(),
    )
    return jax.shard_map(
        shards,
        mesh=mesh,
        in_specs=placed,
        out_specs=(
            P("section", None, None, "tensor"),
            P("section", None, None, "tensor"),
            P("section", None, None, "tensor"),
        ),
        check_vma=False,
    )
```

time: 1210 us -> 556 us (0.46)
  waiting for transfers between devices: 530 us -> 110 us
  other arithmetic: 306 us -> 1.26 us
  starting transfers between devices: 36.4 us -> 271 us
  Pallas kernels: 0 us -> 123 us
  matrix products: 120 us -> 0 us
  blocking collectives: 159 us -> 44.6 us
  local copies, waits for them, and re-layouts: 40.3 us -> 3.69 us
  between operations: 13.9 us -> 0.82 us
    psum x15 -> x0, waiting for transfers between devices: 466 us -> none  [turn(): lax.psum((jnp.sum(widened * widened, axis=1), partial_proj), 'tensor')]
    ppermute x15 -> x79, starting transfers between devices: 19.8 us -> 268 us  [the longest x14 97.7 us: send(): near = lax.ppermute(partial, 'section', onto)]
    reduce_sum x32 -> x0, other arithmetic: 245 us -> none  [the longest x15 224 us: turn(): jnp.sum(newer * proj[:, rank + states:, None], axis=1) + skip[0] * normed_f]
    psum x15 -> x0, blocking collectives: 159 us -> none  [turn(): lax.psum((jnp.sum(widened * widened, axis=1), partial_proj), 'tensor')]
    pallas_call x0 -> x19, Pallas kernels: none -> 123 us  [the longest x15 108 us: step(): pl.pallas_call(functools.partial(step_kernel, width, holders, peers), out...]
    dot_general x30 -> x0, matrix products: 120 us -> none  [the longest x15 66.6 us: turn(): jnp.dot(scaled, x_weight[0], preferred_element_type=jnp.float32)]
    ppermute x15 -> x79, waiting for transfers between devices: 22.2 us -> 77 us  [the longest x48 64.4 us: around(): lax.ppermute(block, 'tensor', [(i, (i + shift) % peers) for i in size])]
    all_to_all x0 -> x1, blocking collectives: none -> 44.6 us  [swap(): lax.all_to_all(block, 'section', split_axis=0, concat_axis=0, tiled=True)]
  transfers between devices with their start and end apart: 32 -> 80, of which waited for: 32 -> 57; matrix products, arithmetic and copies ran while one was open for 0% -> 0% of each run, Pallas kernels for 0% -> 5%
where the time goes in v2:
time: 556 us; the launch traced here: 555 us
  starting transfers between devices  271 us (49%)
  Pallas kernels  123 us (22%)
  waiting for transfers between devices  110 us (20%)
  blocking collectives  44.6 us (8%)
    pallas_call x15, Pallas kernels, step(): pl.pallas_call(functools.partial(step_kernel, width, holders, peers), out...  108 us
    ppermute x14, starting transfers between devices, send(): near = lax.ppermute(partial, 'section', onto)  97.7 us
    ppermute x14, starting transfers between devices, send(): arrived = lax.ppermute(block, 'section', onto)  91.1 us
    ppermute x48, starting transfers between devices, around(): lax.ppermute(block, 'tensor', [(i, (i + shift) % peers) for i in size])  73.5 us
    ppermute x48, waiting for transfers between devices, around(): lax.ppermute(block, 'tensor', [(i, (i + shift) % peers) for i in size])  64.4 us
    all_to_all x1, blocking collectives, swap(): lax.all_to_all(block, 'section', split_axis=0, concat_axis=0, tiled=True)  44.6 us
    all_to_all x1, waiting for transfers between devices, swap(): lax.all_to_all(block, 'section', split_axis=0, concat_axis=0, tiled=True)  33.3 us
    ppermute x14, waiting for transfers between devices, send(): near = lax.ppermute(partial, 'section', onto)  12.6 us
  transfers between devices with their start and end apart: 80, of which 57 were waited for; matrix products, arithmetic and copies ran while one was open for 0% of the time, Pallas kernels for 5%

profile of v2, /device:TPU:0, one launch (start us, length us, event | category | flops | bytes accessed | tf_op | source)
XLA Modules:
  0.0 555.0 jit_solution(2049914533567102166)
XLA Ops:
  1.9 2.8 collective-permute-start.18
  6.0 2.3 copy-done
  8.3 10.5 %open.1 = (bf16[64,640]{1,0:T(8,128)(2,1)S(1)}, bf16[448,640]{1,0:T(8,128)(2,1)}) custom-call(s32[1]{0:T(128)} %bitcast.6.meta, bf16[4,128,4096]{2,1,0:T(8,128)(2,1)} %refs_11_.3, bf16[544,4096]{1,0:T(8,128)(2,1)S(1)} %bitcast.26, f32[1,4096]{1,0:T(1,128)} %refs_18_.3), custom_call_target="tpu_custom_call" | custom-call | tf_op jit(solution)/shard_map/open/pallas_call | solution.py:558
  18.8 3.1 collective-permute-start.5
  24.5 3.6 all-to-all-start
  28.1 2.7 collective-permute-start.6
  32.9 2.7 collective-permute-done.6.refs_5_.refs_9_
  38.6 33.3 %all-to-all-done.refs_13_ = bf16[8,16,4096]{2,1,0:T(8,128)(2,1)S(1)} async-done(((bf16[8,16,4096]{2,1,0:T(8,128)(2,1)}), bf16[8,16,4096]{2,1,0:T(8,128)(2,1)S(1)}, u32[]{:S(2)}, u32[]{:S(2)}) %all-to-all-start) | async-done | bytes 1048608 | tf_op jit(solution)/shard_map/all_to_all | solution.py:546
  73.0 12.5 %step.10 = (bf16[64,4096]{1,0:T(8,128)(2,1)S(1)}, bf16[64,640]{1,0:T(8,128)(2,1)S(1)}, f32[1,128,16,4096]{3,2,1,0:T(8,128)}, bf16[1,4,128,4096]{3,2,1,0:T(8,128)(2,1)}, bf16[8,16,4096]{2,1,0:T(8,128)(2,1)S(1)}) custom-call(s32[4]{0:T(128)S(1)} %pad_add_fusion.3.refs_0_, ...), custom_call_target="tpu_custom_call", output_to_operand_aliasing={{2}: (23, {}), {3}: (24, {}), {4}: (25, {})} | custom-call | flops 704643072 | bytes 16777216 | tf_op jit(solution)/shard_map/step/pallas_call | solution.py:475
  91.4 2.6 collective-permute-start.13
  96.5 3.6 collective-permute-done.13
  100.1 405.9 %while.29 = (s32[]{:T(128)}, bf16[64,4096]{1,0:T(8,128)(2,1)}, bf16[64,640]{1,0:T(8,128)(2,1)S(1)}, bf16[64,640]{1,0:T(8,128)(2,1)S(1)}, bf16[64,640]{1,0:T(8,12...) while((s32[]{:T(128)}, bf16[64,4096]{1,0:T(8,128)(2,1)}, ...), condition=%wide.region_1.2_spmd, body=%wide.region_0.1_spmd.sunk | while | flops 704643072 | bytes 20185724 | solution.py:579
  100.2 12.4 %step.12 = (bf16[64,4096]{1,0:T(8,128)(2,1)S(1)}, bf16[64,640]{1,0:T(8,128)(2,1)S(1)}, f32[1,128,16,4096]{3,2,1,0:T(8,128)}, bf16[1,4,128,4096]{3,2,1,0:T(8,128)(2,1)}, bf16[8,16,4096]{2,1,0:T(8,128)(2,1)S(1)}) custom-call(s32[4]{0:T(128)S(1)} %pad_add_fusion.5.refs_0_, ...), custom_call_target="tpu_custom_call", output_to_operand_aliasing={{2}: (23, {}), {3}: (24, {}), {4}: (25, {})} | custom-call | flops 704643072 | bytes 16777216 | tf_op jit(solution)/shard_map/while/body/eval_jaxpr/step/pallas_call | solution.py:475
  112.5 7.5 %collective-permute-start = (bf16[64,4096]{1,0:T(8,128)(2,1)S(1)}, bf16[64,4096]{1,0:T(8,128)(2,1)}, u32[]{:S(2)}, u32[]{:S(2)}) collective-permute-start(bf16[64,4096]{1,0:T(8,128)(2,1)S(1)} %get-tuple-element.846), channel_id=1, source_target_pairs={{0,4},{4,8},{8,12},{12,16},{16,20},{20,24},{24,28},{1,5},{5,9},{9,... | collective-permute-start | bytes 1572872 | tf_op jit(solution)/shard_map/while/body/eval_jaxpr/ppermute | solution.py:542
  120.0 12.5 %collective-permute-start.1 = (bf16[64,640]{1,0:T(8,128)(2,1)S(1)}, bf16[64,640]{1,0:T(8,128)(2,1)S(1)}, u32[]{:S(2)}, u32[]{:S(2)}) collective-permute-start(bf16[64,640]{1,0:T(8,128)(2,1)S(1)} %get-tuple-element.847), channel_id=1, source_target_pairs={{0,4},{4,8},{8,12},{12,16},{16,20},{20,24},{24,28},{1,5},{5,9},{9,... | collective-permute-start | bytes 245768 | tf_op jit(solution)/shard_map/while/body/eval_jaxpr/ppermute | solution.py:541
  133.5 2.7 collective-permute-start.2
  139.7 2.3 collective-permute-done.3
  142.5 12.6 %step.12 = (bf16[64,4096]{1,0:T(8,128)(2,1)S(1)}, bf16[64,640]{1,0:T(8,128)(2,1)S(1)}, f32[1,128,16,4096]{3,2,1,0:T(8,128)}, bf16[1,4,128,4096]{3,2,1,0:T(8,128)(2,1)}, bf16[8,16,4096]{2,1,0:T(8,128)(2,1)S(1)}) custom-call(s32[4]{0:T(128)S(1)} %pad_add_fusion.5.refs_0_, ...), custom_call_target="tpu_custom_call", output_to_operand_aliasing={{2}: (23, {}), {3}: (24, {}), {4}: (25, {})} | custom-call | flops 704643072 | bytes 16777216 | tf_op jit(solution)/shard_map/while/body/eval_jaxpr/step/pallas_call | solution.py:475
  155.1 5.5 collective-permute-start
  160.6 6.7 %collective-permute-start.1 = (bf16[64,640]{1,0:T(8,128)(2,1)S(1)}, bf16[64,640]{1,0:T(8,128)(2,1)S(1)}, u32[]{:S(2)}, u32[]{:S(2)}) collective-permute-start(bf16[64,640]{1,0:T(8,128)(2,1)S(1)} %get-tuple-element.847), channel_id=1, source_target_pairs={{0,4},{4,8},{8,12},{12,16},{16,20},{20,24},{24,28},{1,5},{5,9},{9,... | collective-permute-start | bytes 245768 | tf_op jit(solution)/shard_map/while/body/eval_jaxpr/ppermute | solution.py:541
  168.2 2.2 collective-permute-start.2
  176.7 12.4 %step.12 = (bf16[64,4096]{1,0:T(8,128)(2,1)S(1)}, bf16[64,640]{1,0:T(8,128)(2,1)S(1)}, f32[1,128,16,4096]{3,2,1,0:T(8,128)}, bf16[1,4,128,4096]{3,2,1,0:T(8,128)(2,1)}, bf16[8,16,4096]{2,1,0:T(8,128)(2,1)S(1)}) custom-call(s32[4]{0:T(128)S(1)} %pad_add_fusion.5.refs_0_, ...), custom_call_target="tpu_custom_call", output_to_operand_aliasing={{2}: (23, {}), {3}: (24, {}), {4}: (25, {})} | custom-call | flops 704643072 | bytes 16777216 | tf_op jit(solution)/shard_map/while/body/eval_jaxpr/step/pallas_call | solution.py:475
  189.1 5.9 %collective-permute-start = (bf16[64,4096]{1,0:T(8,128)(2,1)S(1)}, bf16[64,4096]{1,0:T(8,128)(2,1)}, u32[]{:S(2)}, u32[]{:S(2)}) collective-permute-start(bf16[64,4096]{1,0:T(8,128)(2,1)S(1)} %get-tuple-element.846), channel_id=1, source_target_pairs={{0,4},{4,8},{8,12},{12,16},{16,20},{20,24},{24,28},{1,5},{5,9},{9,... | collective-permute-start | bytes 1572872 | tf_op jit(solution)/shard_map/while/body/eval_jaxpr/ppermute | solution.py:542
  195.0 4.8 collective-permute-start.1
  204.7 2.3 collective-permute-done.2
  209.0 12.4 %step.12 = (bf16[64,4096]{1,0:T(8,128)(2,1)S(1)}, bf16[64,640]{1,0:T(8,128)(2,1)S(1)}, f32[1,128,16,4096]{3,2,1,0:T(8,128)}, bf16[1,4,128,4096]{3,2,1,0:T(8,128)(2,1)}, bf16[8,16,4096]{2,1,0:T(8,128)(2,1)S(1)}) custom-call(s32[4]{0:T(128)S(1)} %pad_add_fusion.5.refs_0_, ...), custom_call_target="tpu_custom_call", output_to_operand_aliasing={{2}: (23, {}), {3}: (24, {}), {4}: (25, {})} | custom-call | flops 704643072 | bytes 16777216 | tf_op jit(solution)/shard_map/while/body/eval_jaxpr/step/pallas_call | solution.py:475
  221.4 6.0 %collective-permute-start = (bf16[64,4096]{1,0:T(8,128)(2,1)S(1)}, bf16[64,4096]{1,0:T(8,128)(2,1)}, u32[]{:S(2)}, u32[]{:S(2)}) collective-permute-start(bf16[64,4096]{1,0:T(8,128)(2,1)S(1)} %get-tuple-element.846), channel_id=1, source_target_pairs={{0,4},{4,8},{8,12},{12,16},{16,20},{20,24},{24,28},{1,5},{5,9},{9,... | collective-permute-start | bytes 1572872 | tf_op jit(solution)/shard_map/while/body/eval_jaxpr/ppermute | solution.py:542
  227.4 4.7 collective-permute-start.1
  236.8 2.5 collective-permute-done.2
  241.5 12.4 %step.12 = (bf16[64,4096]{1,0:T(8,128)(2,1)S(1)}, bf16[64,640]{1,0:T(8,128)(2,1)S(1)}, f32[1,128,16,4096]{3,2,1,0:T(8,128)}, bf16[1,4,128,4096]{3,2,1,0:T(8,128)(2,1)}, bf16[8,16,4096]{2,1,0:T(8,128)(2,1)S(1)}) custom-call(s32[4]{0:T(128)S(1)} %pad_add_fusion.5.refs_0_, ...), custom_call_target="tpu_custom_call", output_to_operand_aliasing={{2}: (23, {}), {3}: (24, {}), {4}: (25, {})} | custom-call | flops 704643072 | bytes 16777216 | tf_op jit(solution)/shard_map/while/body/eval_jaxpr/step/pallas_call | solution.py:475
  253.9 5.8 %collective-permute-start = (bf16[64,4096]{1,0:T(8,128)(2,1)S(1)}, bf16[64,4096]{1,0:T(8,128)(2,1)}, u32[]{:S(2)}, u32[]{:S(2)}) collective-permute-start(bf16[64,4096]{1,0:T(8,128)(2,1)S(1)} %get-tuple-element.846), channel_id=1, source_target_pairs={{0,4},{4,8},{8,12},{12,16},{16,20},{20,24},{24,28},{1,5},{5,9},{9,... | collective-permute-start | bytes 1572872 | tf_op jit(solution)/shard_map/while/body/eval_jaxpr/ppermute | solution.py:542
  259.7 4.9 collective-permute-start.1
  269.3 2.5 collective-permute-done.2
  273.7 12.5 %step.12 = (bf16[64,4096]{1,0:T(8,128)(2,1)S(1)}, bf16[64,640]{1,0:T(8,128)(2,1)S(1)}, f32[1,128,16,4096]{3,2,1,0:T(8,128)}, bf16[1,4,128,4096]{3,2,1,0:T(8,128)(2,1)}, bf16[8,16,4096]{2,1,0:T(8,128)(2,1)S(1)}) custom-call(s32[4]{0:T(128)S(1)} %pad_add_fusion.5.refs_0_, ...), custom_call_target="tpu_custom_call", output_to_operand_aliasing={{2}: (23, {}), {3}: (24, {}), {4}: (25, {})} | custom-call | flops 704643072 | bytes 16777216 | tf_op jit(solution)/shard_map/while/body/eval_jaxpr/step/pallas_call | solution.py:475
  286.3 5.8 %collective-permute-start = (bf16[64,4096]{1,0:T(8,128)(2,1)S(1)}, bf16[64,4096]{1,0:T(8,128)(2,1)}, u32[]{:S(2)}, u32[]{:S(2)}) collective-permute-start(bf16[64,4096]{1,0:T(8,128)(2,1)S(1)} %get-tuple-element.846), channel_id=1, source_target_pairs={{0,4},{4,8},{8,12},{12,16},{16,20},{20,24},{24,28},{1,5},{5,9},{9,... | collective-permute-start | bytes 1572872 | tf_op jit(solution)/shard_map/while/body/eval_jaxpr/ppermute | solution.py:542
  292.1 4.9 collective-permute-start.1
  301.7 2.5 collective-permute-done.2
  306.5 12.6 %step.12 = (bf16[64,4096]{1,0:T(8,128)(2,1)S(1)}, bf16[64,640]{1,0:T(8,128)(2,1)S(1)}, f32[1,128,16,4096]{3,2,1,0:T(8,128)}, bf16[1,4,128,4096]{3,2,1,0:T(8,128)(2,1)}, bf16[8,16,4096]{2,1,0:T(8,128)(2,1)S(1)}) custom-call(s32[4]{0:T(128)S(1)} %pad_add_fusion.5.refs_0_, ...), custom_call_target="tpu_custom_call", output_to_operand_aliasing={{2}: (23, {}), {3}: (24, {}), {4}: (25, {})} | custom-call | flops 704643072 | bytes 16777216 | tf_op jit(solution)/shard_map/while/body/eval_jaxpr/step/pallas_call | solution.py:475
  319.0 5.6 %collective-permute-start = (bf16[64,4096]{1,0:T(8,128)(2,1)S(1)}, bf16[64,4096]{1,0:T(8,128)(2,1)}, u32[]{:S(2)}, u32[]{:S(2)}) collective-permute-start(bf16[64,4096]{1,0:T(8,128)(2,1)S(1)} %get-tuple-element.846), channel_id=1, source_target_pairs={{0,4},{4,8},{8,12},{12,16},{16,20},{20,24},{24,28},{1,5},{5,9},{9,... | collective-permute-start | bytes 1572872 | tf_op jit(solution)/shard_map/while/body/eval_jaxpr/ppermute | solution.py:542
  324.6 5.1 collective-permute-start.1
  334.4 2.5 collective-permute-done.2
  339.9 17.6 %collective-permute-start = (bf16[64,4096]{1,0:T(8,128)(2,1)S(1)}, bf16[64,4096]{1,0:T(8,128)(2,1)}, u32[]{:S(2)}, u32[]{:S(2)}) collective-permute-start(bf16[64,4096]{1,0:T(8,128)(2,1)S(1)} %get-tuple-element.846), channel_id=1, source_target_pairs={{0,4},{4,8},{8,12},{12,16},{16,20},{20,24},{24,28},{1,5},{5,9},{9,... | collective-permute-start | bytes 1572872 | tf_op jit(solution)/shard_map/while/body/eval_jaxpr/ppermute | solution.py:542
  357.5 4.5 collective-permute-start.1
  366.7 2.5 collective-permute-done.2
  372.5 5.5 collective-permute-start
  378.0 16.7 %collective-permute-start.1 = (bf16[64,640]{1,0:T(8,128)(2,1)S(1)}, bf16[64,640]{1,0:T(8,128)(2,1)S(1)}, u32[]{:S(2)}, u32[]{:S(2)}) collective-permute-start(bf16[64,640]{1,0:T(8,128)(2,1)S(1)} %get-tuple-element.847), channel_id=1, source_target_pairs={{0,4},{4,8},{8,12},{12,16},{16,20},{20,24},{24,28},{1,5},{5,9},{9,... | collective-permute-start | bytes 245768 | tf_op jit(solution)/shard_map/while/body/eval_jaxpr/ppermute | solution.py:541
  399.4 2.5 collective-permute-done.2
  404.9 5.8 %collective-permute-start = (bf16[64,4096]{1,0:T(8,128)(2,1)S(1)}, bf16[64,4096]{1,0:T(8,128)(2,1)}, u32[]{:S(2)}, u32[]{:S(2)}) collective-permute-start(bf16[64,4096]{1,0:T(8,128)(2,1)S(1)} %get-tuple-element.846), channel_id=1, source_target_pairs={{0,4},{4,8},{8,12},{12,16},{16,20},{20,24},{24,28},{1,5},{5,9},{9,... | collective-permute-start | bytes 1572872 | tf_op jit(solution)/shard_map/while/body/eval_jaxpr/ppermute | solution.py:542
  410.8 4.7 collective-permute-start.1
  420.1 2.5 collective-permute-done.2
  425.9 7.0 %collective-permute-start = (bf16[64,4096]{1,0:T(8,128)(2,1)S(1)}, bf16[64,4096]{1,0:T(8,128)(2,1)}, u32[]{:S(2)}, u32[]{:S(2)}) collective-permute-start(bf16[64,4096]{1,0:T(8,128)(2,1)S(1)} %get-tuple-element.846), channel_id=1, source_target_pairs={{0,4},{4,8},{8,12},{12,16},{16,20},{20,24},{24,28},{1,5},{5,9},{9,... | collective-permute-start | bytes 1572872 | tf_op jit(solution)/shard_map/while/body/eval_jaxpr/ppermute | solution.py:542
  432.9 6.7 %collective-permute-start.1 = (bf16[64,640]{1,0:T(8,128)(2,1)S(1)}, bf16[64,640]{1,0:T(8,128)(2,1)S(1)}, u32[]{:S(2)}, u32[]{:S(2)}) collective-permute-start(bf16[64,640]{1,0:T(8,128)(2,1)S(1)} %get-tuple-element.847), channel_id=1, source_target_pairs={{0,4},{4,8},{8,12},{12,16},{16,20},{20,24},{24,28},{1,5},{5,9},{9,... | collective-permute-start | bytes 245768 | tf_op jit(solution)/shard_map/while/body/eval_jaxpr/ppermute | solution.py:541
  440.5 3.4 collective-permute-start.2
  444.0 2.4 collective-permute-start.3
  452.0 5.9 %collective-permute-start = (bf16[64,4096]{1,0:T(8,128)(2,1)S(1)}, bf16[64,4096]{1,0:T(8,128)(2,1)}, u32[]{:S(2)}, u32[]{:S(2)}) collective-permute-start(bf16[64,4096]{1,0:T(8,128)(2,1)S(1)} %get-tuple-element.846), channel_id=1, source_target_pairs={{0,4},{4,8},{8,12},{12,16},{16,20},{20,24},{24,28},{1,5},{5,9},{9,... | collective-permute-start | bytes 1572872 | tf_op jit(solution)/shard_map/while/body/eval_jaxpr/ppermute | solution.py:542
  457.9 15.3 %collective-permute-start.1 = (bf16[64,640]{1,0:T(8,128)(2,1)S(1)}, bf16[64,640]{1,0:T(8,128)(2,1)S(1)}, u32[]{:S(2)}, u32[]{:S(2)}) collective-permute-start(bf16[64,640]{1,0:T(8,128)(2,1)S(1)} %get-tuple-element.847), channel_id=1, source_target_pairs={{0,4},{4,8},{8,12},{12,16},{16,20},{20,24},{24,28},{1,5},{5,9},{9,... | collective-permute-start | bytes 245768 | tf_op jit(solution)/shard_map/while/body/eval_jaxpr/ppermute | solution.py:541
  474.2 2.9 collective-permute-start.2
  480.4 2.5 collective-permute-done.3
  484.8 5.1 collective-permute-start
  489.9 5.0 collective-permute-start.1
  495.9 3.1 collective-permute-start.2
  499.0 2.5 collective-permute-start.3
  507.8 44.6 %all_to_all.10.returned = bf16[8,16,4096]{2,1,0:T(8,128)(2,1)} all-to-all(bf16[8,16,4096]{2,1,0:T(8,128)(2,1)S(1)} %get-tuple-element.623), channel_id=1, replica_groups=mesh['section'=8,'tensor'=4] {'section'}, dimensions={0} | all-to-all | bytes 2097152 | tf_op jit(solution)/shard_map/all_to_all | solution.py:546
  552.4 2.6 keep.1
  (154 shorter events, 110.9 us)
Async XLA Ops:
  0.6 71.3 %collective-permute-start.9 = (bf16[544,4096]{1,0:T(8,128)(2,1)}, bf16[544,4096]{1,0:T(8,128)(2,1)}, u32[]{:S(2)}, u32[]{:S(2)}) collective-permute-start(bf16[544,4096]{1,0:T(8,128)(2,1)} %bitcast.24), channel_id=1, source_target_pairs={{4,0},{12,8},{20,16},{28,24},{5,1},{13,9},{21,17},{29,25},{6,2},{1... | collective-permute-start | bytes 13369352 | tf_op jit(solution)/shard_map/ppermute | solution.py:443
  1.9 93.5 %collective-permute-start.18 = (bf16[544,4096]{1,0:T(8,128)(2,1)}, bf16[544,4096]{1,0:T(8,128)(2,1)}, u32[]{:S(2)}, u32[]{:S(2)}) collective-permute-start(bf16[544,4096]{1,0:T(8,128)(2,1)} %bitcast.25), channel_id=1, source_target_pairs={{8,4},{16,12},{24,20},{9,5},{17,13},{25,21},{10,6},{18,14},{26,22}... | collective-permute-start | bytes 13369352 | tf_op jit(solution)/shard_map/ppermute | solution.py:442
  4.7 26.0 %collective-permute-start.8 = (f32[1,4096]{1,0:T(1,128)}, f32[1,4096]{1,0:T(1,128)S(1)}, u32[]{:S(2)}, u32[]{:S(2)}) collective-permute-start(f32[1,4096]{1,0:T(1,128)} %refs_18_.3), channel_id=1, source_target_pairs={{4,0},{12,8},{20,16},{28,24},{8,4},{16,12},{24,20},{5,1},{13,9},{2... | collective-permute-start | bytes 49160 | tf_op jit(solution)/shard_map/ppermute | solution.py:444
  18.8 13.3 %collective-permute-start.5 = (bf16[64,640]{1,0:T(8,128)(2,1)S(1)}, bf16[64,640]{1,0:T(8,128)(2,1)S(1)}, u32[]{:S(2)}, u32[]{:S(2)}) collective-permute-start(bf16[64,640]{1,0:T(8,128)(2,1)S(1)} %get-tuple-element.603.refs_3_.refs_7_), channel_id=1, source_target_pairs={{0,1},{1,2},{2,3},{3,0},{4,5},{5,6},{6,7},{7,4},{8,9},{9,10},{10,1... | collective-permute-start | bytes 245768 | tf_op jit(solution)/shard_map/ppermute | solution.py:469
  24.5 47.4 %all-to-all-start = ((bf16[8,16,4096]{2,1,0:T(8,128)(2,1)}), bf16[8,16,4096]{2,1,0:T(8,128)(2,1)S(1)}, u32[]{:S(2)}, u32[]{:S(2)}) async-start(bf16[8,16,4096]{2,1,0:T(8,128)(2,1)} %pick.1), calls=%async_computation | async-start | bytes 2097152 | tf_op jit(solution)/shard_map/all_to_all | solution.py:546
  28.1 7.5 %collective-permute-start.6 = (bf16[64,640]{1,0:T(8,128)(2,1)S(1)}, bf16[64,640]{1,0:T(8,128)(2,1)S(1)}, u32[]{:S(2)}, u32[]{:S(2)}) collective-permute-start(bf16[64,640]{1,0:T(8,128)(2,1)S(1)} %get-tuple-element.603.refs_3_.refs_7_), channel_id=1, source_target_pairs={{0,2},{1,3},{2,0},{3,1},{4,6},{5,7},{6,4},{7,5},{8,10},{9,11},{10,... | collective-permute-start | bytes 245768 | tf_op jit(solution)/shard_map/ppermute | solution.py:469
  30.8 5.7 %collective-permute-start.7 = (bf16[64,640]{1,0:T(8,128)(2,1)S(1)}, bf16[64,640]{1,0:T(8,128)(2,1)S(1)}, u32[]{:S(2)}, u32[]{:S(2)}) collective-permute-start(bf16[64,640]{1,0:T(8,128)(2,1)S(1)} %get-tuple-element.603.refs_3_.refs_7_), channel_id=1, source_target_pairs={{0,3},{1,0},{2,1},{3,2},{4,7},{5,4},{6,5},{7,6},{8,11},{9,8},{10,9... | collective-permute-start | bytes 245768 | tf_op jit(solution)/shard_map/ppermute | solution.py:469
  32.1 55.6 %collective-permute-start.15 = (bf16[448,640]{1,0:T(8,128)(2,1)}, bf16[448,640]{1,0:T(8,128)(2,1)}, u32[]{:S(2)}, u32[]{:S(2)}) collective-permute-start(bf16[448,640]{1,0:T(8,128)(2,1)} %get-tuple-element.862.refs_7_), channel_id=1, source_target_pairs={{0,1},{1,2},{2,3},{3,0},{4,5},{5,6},{6,7},{7,4},{8,9},{9,10},{10,1... | collective-permute-start | bytes 1720328 | tf_op jit(solution)/shard_map/ppermute | solution.py:469
  35.6 55.8 %collective-permute-start.16 = (bf16[448,640]{1,0:T(8,128)(2,1)}, bf16[448,640]{1,0:T(8,128)(2,1)}, u32[]{:S(2)}, u32[]{:S(2)}) collective-permute-start(bf16[448,640]{1,0:T(8,128)(2,1)} %get-tuple-element.862.refs_7_), channel_id=1, source_target_pairs={{0,2},{1,3},{2,0},{3,1},{4,6},{5,7},{6,4},{7,5},{8,10},{9,11},{10,... | collective-permute-start | bytes 1720328 | tf_op jit(solution)/shard_map/ppermute | solution.py:469
  36.4 57.6 %collective-permute-start.17 = (bf16[448,640]{1,0:T(8,128)(2,1)}, bf16[448,640]{1,0:T(8,128)(2,1)}, u32[]{:S(2)}, u32[]{:S(2)}) collective-permute-start(bf16[448,640]{1,0:T(8,128)(2,1)} %get-tuple-element.862.refs_7_), channel_id=1, source_target_pairs={{0,3},{1,0},{2,1},{3,2},{4,7},{5,4},{6,5},{7,6},{8,11},{9,8},{10,9... | collective-permute-start | bytes 1720328 | tf_op jit(solution)/shard_map/ppermute | solution.py:469
  85.6 14.5 %collective-permute-start.10 = (bf16[64,4096]{1,0:T(8,128)(2,1)S(1)}, bf16[64,4096]{1,0:T(8,128)(2,1)}, u32[]{:S(2)}, u32[]{:S(2)}) collective-permute-start(bf16[64,4096]{1,0:T(8,128)(2,1)S(1)} %get-tuple-element.607), channel_id=1, source_target_pairs={{0,4},{4,8},{8,12},{12,16},{16,20},{20,24},{24,28},{1,5},{5,9},{9,... | collective-permute-start | bytes 1572872 | tf_op jit(solution)/shard_map/ppermute | solution.py:542
  89.8 6.7 %collective-permute-start.12 = (bf16[64,640]{1,0:T(8,128)(2,1)S(1)}, bf16[64,640]{1,0:T(8,128)(2,1)S(1)}, u32[]{:S(2)}, u32[]{:S(2)}) collective-permute-start(bf16[64,640]{1,0:T(8,128)(2,1)S(1)} %collective-permute-done.11), channel_id=1, source_target_pairs={{0,1},{1,2},{2,3},{3,0},{4,5},{5,6},{6,7},{7,4},{8,9},{9,10},{10,1... | collective-permute-start | bytes 245768 | tf_op jit(solution)/shard_map/ppermute | solution.py:469
  91.4 8.7 %collective-permute-start.13 = (bf16[64,640]{1,0:T(8,128)(2,1)S(1)}, bf16[64,640]{1,0:T(8,128)(2,1)S(1)}, u32[]{:S(2)}, u32[]{:S(2)}) collective-permute-start(bf16[64,640]{1,0:T(8,128)(2,1)S(1)} %collective-permute-done.11), channel_id=1, source_target_pairs={{0,2},{1,3},{2,0},{3,1},{4,6},{5,7},{6,4},{7,5},{8,10},{9,11},{10,... | collective-permute-start | bytes 245768 | tf_op jit(solution)/shard_map/ppermute | solution.py:469
  94.0 6.1 %collective-permute-start.14 = (bf16[64,640]{1,0:T(8,128)(2,1)S(1)}, bf16[64,640]{1,0:T(8,128)(2,1)S(1)}, u32[]{:S(2)}, u32[]{:S(2)}) collective-permute-start(bf16[64,640]{1,0:T(8,128)(2,1)S(1)} %collective-permute-done.11), channel_id=1, source_target_pairs={{0,3},{1,0},{2,1},{3,2},{4,7},{5,4},{6,5},{7,6},{8,11},{9,8},{10,9... | collective-permute-start | bytes 245768 | tf_op jit(solution)/shard_map/ppermute | solution.py:469
  112.5 29.9 %collective-permute-start = (bf16[64,4096]{1,0:T(8,128)(2,1)S(1)}, bf16[64,4096]{1,0:T(8,128)(2,1)}, u32[]{:S(2)}, u32[]{:S(2)}) collective-permute-start(bf16[64,4096]{1,0:T(8,128)(2,1)S(1)} %get-tuple-element.846), channel_id=1, source_target_pairs={{0,4},{4,8},{8,12},{12,16},{16,20},{20,24},{24,28},{1,5},{5,9},{9,... | collective-permute-start | bytes 1572872 | tf_op jit(solution)/shard_map/while/body/eval_jaxpr/ppermute | solution.py:542
  120.0 13.5 %collective-permute-start.1 = (bf16[64,640]{1,0:T(8,128)(2,1)S(1)}, bf16[64,640]{1,0:T(8,128)(2,1)S(1)}, u32[]{:S(2)}, u32[]{:S(2)}) collective-permute-start(bf16[64,640]{1,0:T(8,128)(2,1)S(1)} %get-tuple-element.847), channel_id=1, source_target_pairs={{0,4},{4,8},{8,12},{12,16},{16,20},{20,24},{24,28},{1,5},{5,9},{9,... | collective-permute-start | bytes 245768 | tf_op jit(solution)/shard_map/while/body/eval_jaxpr/ppermute | solution.py:541
  133.5 6.2 %collective-permute-start.2 = (bf16[64,640]{1,0:T(8,128)(2,1)S(1)}, bf16[64,640]{1,0:T(8,128)(2,1)S(1)}, u32[]{:S(2)}, u32[]{:S(2)}) collective-permute-start(bf16[64,640]{1,0:T(8,128)(2,1)S(1)} %collective-permute-done.1), channel_id=1, source_target_pairs={{0,1},{1,2},{2,3},{3,0},{4,5},{5,6},{6,7},{7,4},{8,9},{9,10},{10,1... | collective-permute-start | bytes 245768 | tf_op jit(solution)/shard_map/while/body/eval_jaxpr/ppermute | solution.py:469
  136.2 5.8 %collective-permute-start.3 = (bf16[64,640]{1,0:T(8,128)(2,1)S(1)}, bf16[64,640]{1,0:T(8,128)(2,1)S(1)}, u32[]{:S(2)}, u32[]{:S(2)}) collective-permute-start(bf16[64,640]{1,0:T(8,128)(2,1)S(1)} %collective-permute-done.1), channel_id=1, source_target_pairs={{0,2},{1,3},{2,0},{3,1},{4,6},{5,7},{6,4},{7,5},{8,10},{9,11},{10,... | collective-permute-start | bytes 245768 | tf_op jit(solution)/shard_map/while/body/eval_jaxpr/ppermute | solution.py:469
  155.1 21.6 %collective-permute-start = (bf16[64,4096]{1,0:T(8,128)(2,1)S(1)}, bf16[64,4096]{1,0:T(8,128)(2,1)}, u32[]{:S(2)}, u32[]{:S(2)}) collective-permute-start(bf16[64,4096]{1,0:T(8,128)(2,1)S(1)} %get-tuple-element.846), channel_id=1, source_target_pairs={{0,4},{4,8},{8,12},{12,16},{16,20},{20,24},{24,28},{1,5},{5,9},{9,... | collective-permute-start | bytes 1572872 | tf_op jit(solution)/shard_map/while/body/eval_jaxpr/ppermute | solution.py:542
  160.6 7.6 %collective-permute-start.1 = (bf16[64,640]{1,0:T(8,128)(2,1)S(1)}, bf16[64,640]{1,0:T(8,128)(2,1)S(1)}, u32[]{:S(2)}, u32[]{:S(2)}) collective-permute-start(bf16[64,640]{1,0:T(8,128)(2,1)S(1)} %get-tuple-element.847), channel_id=1, source_target_pairs={{0,4},{4,8},{8,12},{12,16},{16,20},{20,24},{24,28},{1,5},{5,9},{9,... | collective-permute-start | bytes 245768 | tf_op jit(solution)/shard_map/while/body/eval_jaxpr/ppermute | solution.py:541
  168.2 6.2 %collective-permute-start.2 = (bf16[64,640]{1,0:T(8,128)(2,1)S(1)}, bf16[64,640]{1,0:T(8,128)(2,1)S(1)}, u32[]{:S(2)}, u32[]{:S(2)}) collective-permute-start(bf16[64,640]{1,0:T(8,128)(2,1)S(1)} %collective-permute-done.1), channel_id=1, source_target_pairs={{0,1},{1,2},{2,3},{3,0},{4,5},{5,6},{6,7},{7,4},{8,9},{9,10},{10,1... | collective-permute-start | bytes 245768 | tf_op jit(solution)/shard_map/while/body/eval_jaxpr/ppermute | solution.py:469
  170.4 5.9 %collective-permute-start.3 = (bf16[64,640]{1,0:T(8,128)(2,1)S(1)}, bf16[64,640]{1,0:T(8,128)(2,1)S(1)}, u32[]{:S(2)}, u32[]{:S(2)}) collective-permute-start(bf16[64,640]{1,0:T(8,128)(2,1)S(1)} %collective-permute-done.1), channel_id=1, source_target_pairs={{0,2},{1,3},{2,0},{3,1},{4,6},{5,7},{6,4},{7,5},{8,10},{9,11},{10,... | collective-permute-start | bytes 245768 | tf_op jit(solution)/shard_map/while/body/eval_jaxpr/ppermute | solution.py:469
  189.1 19.8 %collective-permute-start = (bf16[64,4096]{1,0:T(8,128)(2,1)S(1)}, bf16[64,4096]{1,0:T(8,128)(2,1)}, u32[]{:S(2)}, u32[]{:S(2)}) collective-permute-start(bf16[64,4096]{1,0:T(8,128)(2,1)S(1)} %get-tuple-element.846), channel_id=1, source_target_pairs={{0,4},{4,8},{8,12},{12,16},{16,20},{20,24},{24,28},{1,5},{5,9},{9,... | collective-permute-start | bytes 1572872 | tf_op jit(solution)/shard_map/while/body/eval_jaxpr/ppermute | solution.py:542
  195.0 5.7 %collective-permute-start.1 = (bf16[64,640]{1,0:T(8,128)(2,1)S(1)}, bf16[64,640]{1,0:T(8,128)(2,1)S(1)}, u32[]{:S(2)}, u32[]{:S(2)}) collective-permute-start(bf16[64,640]{1,0:T(8,128)(2,1)S(1)} %get-tuple-element.847), channel_id=1, source_target_pairs={{0,4},{4,8},{8,12},{12,16},{16,20},{20,24},{24,28},{1,5},{5,9},{9,... | collective-permute-start | bytes 245768 | tf_op jit(solution)/shard_map/while/body/eval_jaxpr/ppermute | solution.py:541
  200.7 6.3 %collective-permute-start.2 = (bf16[64,640]{1,0:T(8,128)(2,1)S(1)}, bf16[64,640]{1,0:T(8,128)(2,1)S(1)}, u32[]{:S(2)}, u32[]{:S(2)}) collective-permute-start(bf16[64,640]{1,0:T(8,128)(2,1)S(1)} %collective-permute-done.1), channel_id=1, source_target_pairs={{0,1},{1,2},{2,3},{3,0},{4,5},{5,6},{6,7},{7,4},{8,9},{9,10},{10,1... | collective-permute-start | bytes 245768 | tf_op jit(solution)/shard_map/while/body/eval_jaxpr/ppermute | solution.py:469
  201.6 7.1 %collective-permute-start.3 = (bf16[64,640]{1,0:T(8,128)(2,1)S(1)}, bf16[64,640]{1,0:T(8,128)(2,1)S(1)}, u32[]{:S(2)}, u32[]{:S(2)}) collective-permute-start(bf16[64,640]{1,0:T(8,128)(2,1)S(1)} %collective-permute-done.1), channel_id=1, source_target_pairs={{0,2},{1,3},{2,0},{3,1},{4,6},{5,7},{6,4},{7,5},{8,10},{9,11},{10,... | collective-permute-start | bytes 245768 | tf_op jit(solution)/shard_map/while/body/eval_jaxpr/ppermute | solution.py:469
  221.4 20.1 %collective-permute-start = (bf16[64,4096]{1,0:T(8,128)(2,1)S(1)}, bf16[64,4096]{1,0:T(8,128)(2,1)}, u32[]{:S(2)}, u32[]{:S(2)}) collective-permute-start(bf16[64,4096]{1,0:T(8,128)(2,1)S(1)} %get-tuple-element.846), channel_id=1, source_target_pairs={{0,4},{4,8},{8,12},{12,16},{16,20},{20,24},{24,28},{1,5},{5,9},{9,... | collective-permute-start | bytes 1572872 | tf_op jit(solution)/shard_map/while/body/eval_jaxpr/ppermute | solution.py:542
  232.9 6.3 %collective-permute-start.2 = (bf16[64,640]{1,0:T(8,128)(2,1)S(1)}, bf16[64,640]{1,0:T(8,128)(2,1)S(1)}, u32[]{:S(2)}, u32[]{:S(2)}) collective-permute-start(bf16[64,640]{1,0:T(8,128)(2,1)S(1)} %collective-permute-done.1), channel_id=1, source_target_pairs={{0,1},{1,2},{2,3},{3,0},{4,5},{5,6},{6,7},{7,4},{8,9},{9,10},{10,1... | collective-permute-start | bytes 245768 | tf_op jit(solution)/shard_map/while/body/eval_jaxpr/ppermute | solution.py:469
  234.1 6.9 %collective-permute-start.3 = (bf16[64,640]{1,0:T(8,128)(2,1)S(1)}, bf16[64,640]{1,0:T(8,128)(2,1)S(1)}, u32[]{:S(2)}, u32[]{:S(2)}) collective-permute-start(bf16[64,640]{1,0:T(8,128)(2,1)S(1)} %collective-permute-done.1), channel_id=1, source_target_pairs={{0,2},{1,3},{2,0},{3,1},{4,6},{5,7},{6,4},{7,5},{8,10},{9,11},{10,... | collective-permute-start | bytes 245768 | tf_op jit(solution)/shard_map/while/body/eval_jaxpr/ppermute | solution.py:469
  253.9 19.8 %collective-permute-start = (bf16[64,4096]{1,0:T(8,128)(2,1)S(1)}, bf16[64,4096]{1,0:T(8,128)(2,1)}, u32[]{:S(2)}, u32[]{:S(2)}) collective-permute-start(bf16[64,4096]{1,0:T(8,128)(2,1)S(1)} %get-tuple-element.846), channel_id=1, source_target_pairs={{0,4},{4,8},{8,12},{12,16},{16,20},{20,24},{24,28},{1,5},{5,9},{9,... | collective-permute-start | bytes 1572872 | tf_op jit(solution)/shard_map/while/body/eval_jaxpr/ppermute | solution.py:542
  259.7 5.8 %collective-permute-start.1 = (bf16[64,640]{1,0:T(8,128)(2,1)S(1)}, bf16[64,640]{1,0:T(8,128)(2,1)S(1)}, u32[]{:S(2)}, u32[]{:S(2)}) collective-permute-start(bf16[64,640]{1,0:T(8,128)(2,1)S(1)} %get-tuple-element.847), channel_id=1, source_target_pairs={{0,4},{4,8},{8,12},{12,16},{16,20},{20,24},{24,28},{1,5},{5,9},{9,... | collective-permute-start | bytes 245768 | tf_op jit(solution)/shard_map/while/body/eval_jaxpr/ppermute | solution.py:541
  265.4 6.3 %collective-permute-start.2 = (bf16[64,640]{1,0:T(8,128)(2,1)S(1)}, bf16[64,640]{1,0:T(8,128)(2,1)S(1)}, u32[]{:S(2)}, u32[]{:S(2)}) collective-permute-start(bf16[64,640]{1,0:T(8,128)(2,1)S(1)} %collective-permute-done.1), channel_id=1, source_target_pairs={{0,1},{1,2},{2,3},{3,0},{4,5},{5,6},{6,7},{7,4},{8,9},{9,10},{10,1... | collective-permute-start | bytes 245768 | tf_op jit(solution)/shard_map/while/body/eval_jaxpr/ppermute | solution.py:469
  266.4 7.2 %collective-permute-start.3 = (bf16[64,640]{1,0:T(8,128)(2,1)S(1)}, bf16[64,640]{1,0:T(8,128)(2,1)S(1)}, u32[]{:S(2)}, u32[]{:S(2)}) collective-permute-start(bf16[64,640]{1,0:T(8,128)(2,1)S(1)} %collective-permute-done.1), channel_id=1, source_target_pairs={{0,2},{1,3},{2,0},{3,1},{4,6},{5,7},{6,4},{7,5},{8,10},{9,11},{10,... | collective-permute-start | bytes 245768 | tf_op jit(solution)/shard_map/while/body/eval_jaxpr/ppermute | solution.py:469
  286.3 20.1 %collective-permute-start = (bf16[64,4096]{1,0:T(8,128)(2,1)S(1)}, bf16[64,4096]{1,0:T(8,128)(2,1)}, u32[]{:S(2)}, u32[]{:S(2)}) collective-permute-start(bf16[64,4096]{1,0:T(8,128)(2,1)S(1)} %get-tuple-element.846), channel_id=1, source_target_pairs={{0,4},{4,8},{8,12},{12,16},{16,20},{20,24},{24,28},{1,5},{5,9},{9,... | collective-permute-start | bytes 1572872 | tf_op jit(solution)/shard_map/while/body/eval_jaxpr/ppermute | solution.py:542
  292.1 5.8 %collective-permute-start.1 = (bf16[64,640]{1,0:T(8,128)(2,1)S(1)}, bf16[64,640]{1,0:T(8,128)(2,1)S(1)}, u32[]{:S(2)}, u32[]{:S(2)}) collective-permute-start(bf16[64,640]{1,0:T(8,128)(2,1)S(1)} %get-tuple-element.847), channel_id=1, source_target_pairs={{0,4},{4,8},{8,12},{12,16},{16,20},{20,24},{24,28},{1,5},{5,9},{9,... | collective-permute-start | bytes 245768 | tf_op jit(solution)/shard_map/while/body/eval_jaxpr/ppermute | solution.py:541
  297.9 6.3 %collective-permute-start.2 = (bf16[64,640]{1,0:T(8,128)(2,1)S(1)}, bf16[64,640]{1,0:T(8,128)(2,1)S(1)}, u32[]{:S(2)}, u32[]{:S(2)}) collective-permute-start(bf16[64,640]{1,0:T(8,128)(2,1)S(1)} %collective-permute-done.1), channel_id=1, source_target_pairs={{0,1},{1,2},{2,3},{3,0},{4,5},{5,6},{6,7},{7,4},{8,9},{9,10},{10,1... | collective-permute-start | bytes 245768 | tf_op jit(solution)/shard_map/while/body/eval_jaxpr/ppermute | solution.py:469
  299.1 6.9 %collective-permute-start.3 = (bf16[64,640]{1,0:T(8,128)(2,1)S(1)}, bf16[64,640]{1,0:T(8,128)(2,1)S(1)}, u32[]{:S(2)}, u32[]{:S(2)}) collective-permute-start(bf16[64,640]{1,0:T(8,128)(2,1)S(1)} %collective-permute-done.1), channel_id=1, source_target_pairs={{0,2},{1,3},{2,0},{3,1},{4,6},{5,7},{6,4},{7,5},{8,10},{9,11},{10,... | collective-permute-start | bytes 245768 | tf_op jit(solution)/shard_map/while/body/eval_jaxpr/ppermute | solution.py:469
  319.0 19.8 %collective-permute-start = (bf16[64,4096]{1,0:T(8,128)(2,1)S(1)}, bf16[64,4096]{1,0:T(8,128)(2,1)}, u32[]{:S(2)}, u32[]{:S(2)}) collective-permute-start(bf16[64,4096]{1,0:T(8,128)(2,1)S(1)} %get-tuple-element.846), channel_id=1, source_target_pairs={{0,4},{4,8},{8,12},{12,16},{16,20},{20,24},{24,28},{1,5},{5,9},{9,... | collective-permute-start | bytes 1572872 | tf_op jit(solution)/shard_map/while/body/eval_jaxpr/ppermute | solution.py:542
  324.6 6.0 %collective-permute-start.1 = (bf16[64,640]{1,0:T(8,128)(2,1)S(1)}, bf16[64,640]{1,0:T(8,128)(2,1)S(1)}, u32[]{:S(2)}, u32[]{:S(2)}) collective-permute-start(bf16[64,640]{1,0:T(8,128)(2,1)S(1)} %get-tuple-element.847), channel_id=1, source_target_pairs={{0,4},{4,8},{8,12},{12,16},{16,20},{20,24},{24,28},{1,5},{5,9},{9,... | collective-permute-start | bytes 245768 | tf_op jit(solution)/shard_map/while/body/eval_jaxpr/ppermute | solution.py:541
  330.6 6.3 %collective-permute-start.2 = (bf16[64,640]{1,0:T(8,128)(2,1)S(1)}, bf16[64,640]{1,0:T(8,128)(2,1)S(1)}, u32[]{:S(2)}, u32[]{:S(2)}) collective-permute-start(bf16[64,640]{1,0:T(8,128)(2,1)S(1)} %collective-permute-done.1), channel_id=1, source_target_pairs={{0,1},{1,2},{2,3},{3,0},{4,5},{5,6},{6,7},{7,4},{8,9},{9,10},{10,1... | collective-permute-start | bytes 245768 | tf_op jit(solution)/shard_map/while/body/eval_jaxpr/ppermute | solution.py:469
  331.5 7.2 %collective-permute-start.3 = (bf16[64,640]{1,0:T(8,128)(2,1)S(1)}, bf16[64,640]{1,0:T(8,128)(2,1)S(1)}, u32[]{:S(2)}, u32[]{:S(2)}) collective-permute-start(bf16[64,640]{1,0:T(8,128)(2,1)S(1)} %collective-permute-done.1), channel_id=1, source_target_pairs={{0,2},{1,3},{2,0},{3,1},{4,6},{5,7},{6,4},{7,5},{8,10},{9,11},{10,... | collective-permute-start | bytes 245768 | tf_op jit(solution)/shard_map/while/body/eval_jaxpr/ppermute | solution.py:469
  339.9 31.5 %collective-permute-start = (bf16[64,4096]{1,0:T(8,128)(2,1)S(1)}, bf16[64,4096]{1,0:T(8,128)(2,1)}, u32[]{:S(2)}, u32[]{:S(2)}) collective-permute-start(bf16[64,4096]{1,0:T(8,128)(2,1)S(1)} %get-tuple-element.846), channel_id=1, source_target_pairs={{0,4},{4,8},{8,12},{12,16},{16,20},{20,24},{24,28},{1,5},{5,9},{9,... | collective-permute-start | bytes 1572872 | tf_op jit(solution)/shard_map/while/body/eval_jaxpr/ppermute | solution.py:542
  362.9 6.3 %collective-permute-start.2 = (bf16[64,640]{1,0:T(8,128)(2,1)S(1)}, bf16[64,640]{1,0:T(8,128)(2,1)S(1)}, u32[]{:S(2)}, u32[]{:S(2)}) collective-permute-start(bf16[64,640]{1,0:T(8,128)(2,1)S(1)} %collective-permute-done.1), channel_id=1, source_target_pairs={{0,1},{1,2},{2,3},{3,0},{4,5},{5,6},{6,7},{7,4},{8,9},{9,10},{10,1... | collective-permute-start | bytes 245768 | tf_op jit(solution)/shard_map/while/body/eval_jaxpr/ppermute | solution.py:469
  364.1 6.9 %collective-permute-start.3 = (bf16[64,640]{1,0:T(8,128)(2,1)S(1)}, bf16[64,640]{1,0:T(8,128)(2,1)S(1)}, u32[]{:S(2)}, u32[]{:S(2)}) collective-permute-start(bf16[64,640]{1,0:T(8,128)(2,1)S(1)} %collective-permute-done.1), channel_id=1, source_target_pairs={{0,2},{1,3},{2,0},{3,1},{4,6},{5,7},{6,4},{7,5},{8,10},{9,11},{10,... | collective-permute-start | bytes 245768 | tf_op jit(solution)/shard_map/while/body/eval_jaxpr/ppermute | solution.py:469
  372.5 31.4 %collective-permute-start = (bf16[64,4096]{1,0:T(8,128)(2,1)S(1)}, bf16[64,4096]{1,0:T(8,128)(2,1)}, u32[]{:S(2)}, u32[]{:S(2)}) collective-permute-start(bf16[64,4096]{1,0:T(8,128)(2,1)S(1)} %get-tuple-element.846), channel_id=1, source_target_pairs={{0,4},{4,8},{8,12},{12,16},{16,20},{20,24},{24,28},{1,5},{5,9},{9,... | collective-permute-start | bytes 1572872 | tf_op jit(solution)/shard_map/while/body/eval_jaxpr/ppermute | solution.py:542
  378.0 17.6 %collective-permute-start.1 = (bf16[64,640]{1,0:T(8,128)(2,1)S(1)}, bf16[64,640]{1,0:T(8,128)(2,1)S(1)}, u32[]{:S(2)}, u32[]{:S(2)}) collective-permute-start(bf16[64,640]{1,0:T(8,128)(2,1)S(1)} %get-tuple-element.847), channel_id=1, source_target_pairs={{0,4},{4,8},{8,12},{12,16},{16,20},{20,24},{24,28},{1,5},{5,9},{9,... | collective-permute-start | bytes 245768 | tf_op jit(solution)/shard_map/while/body/eval_jaxpr/ppermute | solution.py:541
  395.6 6.3 %collective-permute-start.2 = (bf16[64,640]{1,0:T(8,128)(2,1)S(1)}, bf16[64,640]{1,0:T(8,128)(2,1)S(1)}, u32[]{:S(2)}, u32[]{:S(2)}) collective-permute-start(bf16[64,640]{1,0:T(8,128)(2,1)S(1)} %collective-permute-done.1), channel_id=1, source_target_pairs={{0,1},{1,2},{2,3},{3,0},{4,5},{5,6},{6,7},{7,4},{8,9},{9,10},{10,1... | collective-permute-start | bytes 245768 | tf_op jit(solution)/shard_map/while/body/eval_jaxpr/ppermute | solution.py:469
  396.6 7.2 %collective-permute-start.3 = (bf16[64,640]{1,0:T(8,128)(2,1)S(1)}, bf16[64,640]{1,0:T(8,128)(2,1)S(1)}, u32[]{:S(2)}, u32[]{:S(2)}) collective-permute-start(bf16[64,640]{1,0:T(8,128)(2,1)S(1)} %collective-permute-done.1), channel_id=1, source_target_pairs={{0,2},{1,3},{2,0},{3,1},{4,6},{5,7},{6,4},{7,5},{8,10},{9,11},{10,... | collective-permute-start | bytes 245768 | tf_op jit(solution)/shard_map/while/body/eval_jaxpr/ppermute | solution.py:469
  404.9 19.9 %collective-permute-start = (bf16[64,4096]{1,0:T(8,128)(2,1)S(1)}, bf16[64,4096]{1,0:T(8,128)(2,1)}, u32[]{:S(2)}, u32[]{:S(2)}) collective-permute-start(bf16[64,4096]{1,0:T(8,128)(2,1)S(1)} %get-tuple-element.846), channel_id=1, source_target_pairs={{0,4},{4,8},{8,12},{12,16},{16,20},{20,24},{24,28},{1,5},{5,9},{9,... | collective-permute-start | bytes 1572872 | tf_op jit(solution)/shard_map/while/body/eval_jaxpr/ppermute | solution.py:542
  416.3 6.3 %collective-permute-start.2 = (bf16[64,640]{1,0:T(8,128)(2,1)S(1)}, bf16[64,640]{1,0:T(8,128)(2,1)S(1)}, u32[]{:S(2)}, u32[]{:S(2)}) collective-permute-start(bf16[64,640]{1,0:T(8,128)(2,1)S(1)} %collective-permute-done.1), channel_id=1, source_target_pairs={{0,1},{1,2},{2,3},{3,0},{4,5},{5,6},{6,7},{7,4},{8,9},{9,10},{10,1... | collective-permute-start | bytes 245768 | tf_op jit(solution)/shard_map/while/body/eval_jaxpr/ppermute | solution.py:469
  417.5 6.9 %collective-permute-start.3 = (bf16[64,640]{1,0:T(8,128)(2,1)S(1)}, bf16[64,640]{1,0:T(8,128)(2,1)S(1)}, u32[]{:S(2)}, u32[]{:S(2)}) collective-permute-start(bf16[64,640]{1,0:T(8,128)(2,1)S(1)} %collective-permute-done.1), channel_id=1, source_target_pairs={{0,2},{1,3},{2,0},{3,1},{4,6},{5,7},{6,4},{7,5},{8,10},{9,11},{10,... | collective-permute-start | bytes 245768 | tf_op jit(solution)/shard_map/while/body/eval_jaxpr/ppermute | solution.py:469
  425.9 25.0 %collective-permute-start = (bf16[64,4096]{1,0:T(8,128)(2,1)S(1)}, bf16[64,4096]{1,0:T(8,128)(2,1)}, u32[]{:S(2)}, u32[]{:S(2)}) collective-permute-start(bf16[64,4096]{1,0:T(8,128)(2,1)S(1)} %get-tuple-element.846), channel_id=1, source_target_pairs={{0,4},{4,8},{8,12},{12,16},{16,20},{20,24},{24,28},{1,5},{5,9},{9,... | collective-permute-start | bytes 1572872 | tf_op jit(solution)/shard_map/while/body/eval_jaxpr/ppermute | solution.py:542
  432.9 7.6 %collective-permute-start.1 = (bf16[64,640]{1,0:T(8,128)(2,1)S(1)}, bf16[64,640]{1,0:T(8,128)(2,1)S(1)}, u32[]{:S(2)}, u32[]{:S(2)}) collective-permute-start(bf16[64,640]{1,0:T(8,128)(2,1)S(1)} %get-tuple-element.847), channel_id=1, source_target_pairs={{0,4},{4,8},{8,12},{12,16},{16,20},{20,24},{24,28},{1,5},{5,9},{9,... | collective-permute-start | bytes 245768 | tf_op jit(solution)/shard_map/while/body/eval_jaxpr/ppermute | solution.py:541
  440.5 7.7 %collective-permute-start.2 = (bf16[64,640]{1,0:T(8,128)(2,1)S(1)}, bf16[64,640]{1,0:T(8,128)(2,1)S(1)}, u32[]{:S(2)}, u32[]{:S(2)}) collective-permute-start(bf16[64,640]{1,0:T(8,128)(2,1)S(1)} %collective-permute-done.1), channel_id=1, source_target_pairs={{0,1},{1,2},{2,3},{3,0},{4,5},{5,6},{6,7},{7,4},{8,9},{9,10},{10,1... | collective-permute-start | bytes 245768 | tf_op jit(solution)/shard_map/while/body/eval_jaxpr/ppermute | solution.py:469
  444.0 6.0 %collective-permute-start.3 = (bf16[64,640]{1,0:T(8,128)(2,1)S(1)}, bf16[64,640]{1,0:T(8,128)(2,1)S(1)}, u32[]{:S(2)}, u32[]{:S(2)}) collective-permute-start(bf16[64,640]{1,0:T(8,128)(2,1)S(1)} %collective-permute-done.1), channel_id=1, source_target_pairs={{0,2},{1,3},{2,0},{3,1},{4,6},{5,7},{6,4},{7,5},{8,10},{9,11},{10,... | collective-permute-start | bytes 245768 | tf_op jit(solution)/shard_map/while/body/eval_jaxpr/ppermute | solution.py:469
  452.0 31.7 %collective-permute-start = (bf16[64,4096]{1,0:T(8,128)(2,1)S(1)}, bf16[64,4096]{1,0:T(8,128)(2,1)}, u32[]{:S(2)}, u32[]{:S(2)}) collective-permute-start(bf16[64,4096]{1,0:T(8,128)(2,1)S(1)} %get-tuple-element.846), channel_id=1, source_target_pairs={{0,4},{4,8},{8,12},{12,16},{16,20},{20,24},{24,28},{1,5},{5,9},{9,... | collective-permute-start | bytes 1572872 | tf_op jit(solution)/shard_map/while/body/eval_jaxpr/ppermute | solution.py:542
  457.9 16.3 %collective-permute-start.1 = (bf16[64,640]{1,0:T(8,128)(2,1)S(1)}, bf16[64,640]{1,0:T(8,128)(2,1)S(1)}, u32[]{:S(2)}, u32[]{:S(2)}) collective-permute-start(bf16[64,640]{1,0:T(8,128)(2,1)S(1)} %get-tuple-element.847), channel_id=1, source_target_pairs={{0,4},{4,8},{8,12},{12,16},{16,20},{20,24},{24,28},{1,5},{5,9},{9,... | collective-permute-start | bytes 245768 | tf_op jit(solution)/shard_map/while/body/eval_jaxpr/ppermute | solution.py:541
  474.2 6.2 %collective-permute-start.2 = (bf16[64,640]{1,0:T(8,128)(2,1)S(1)}, bf16[64,640]{1,0:T(8,128)(2,1)S(1)}, u32[]{:S(2)}, u32[]{:S(2)}) collective-permute-start(bf16[64,640]{1,0:T(8,128)(2,1)S(1)} %collective-permute-done.1), channel_id=1, source_target_pairs={{0,1},{1,2},{2,3},{3,0},{4,5},{5,6},{6,7},{7,4},{8,9},{9,10},{10,1... | collective-permute-start | bytes 245768 | tf_op jit(solution)/shard_map/while/body/eval_jaxpr/ppermute | solution.py:469
  477.1 5.8 %collective-permute-start.3 = (bf16[64,640]{1,0:T(8,128)(2,1)S(1)}, bf16[64,640]{1,0:T(8,128)(2,1)S(1)}, u32[]{:S(2)}, u32[]{:S(2)}) collective-permute-start(bf16[64,640]{1,0:T(8,128)(2,1)S(1)} %collective-permute-done.1), channel_id=1, source_target_pairs={{0,2},{1,3},{2,0},{3,1},{4,6},{5,7},{6,4},{7,5},{8,10},{9,11},{10,... | collective-permute-start | bytes 245768 | tf_op jit(solution)/shard_map/while/body/eval_jaxpr/ppermute | solution.py:469
  477.8 6.0 %collective-permute-start.4 = (bf16[64,640]{1,0:T(8,128)(2,1)S(1)}, bf16[64,640]{1,0:T(8,128)(2,1)S(1)}, u32[]{:S(2)}, u32[]{:S(2)}) collective-permute-start(bf16[64,640]{1,0:T(8,128)(2,1)S(1)} %collective-permute-done.1), channel_id=1, source_target_pairs={{0,3},{1,0},{2,1},{3,2},{4,7},{5,4},{6,5},{7,6},{8,11},{9,8},{10,9... | collective-permute-start | bytes 245768 | tf_op jit(solution)/shard_map/while/body/eval_jaxpr/ppermute | solution.py:469
  484.8 21.2 %collective-permute-start = (bf16[64,4096]{1,0:T(8,128)(2,1)S(1)}, bf16[64,4096]{1,0:T(8,128)(2,1)}, u32[]{:S(2)}, u32[]{:S(2)}) collective-permute-start(bf16[64,4096]{1,0:T(8,128)(2,1)S(1)} %get-tuple-element.846), channel_id=1, source_target_pairs={{0,4},{4,8},{8,12},{12,16},{16,20},{20,24},{24,28},{1,5},{5,9},{9,... | collective-permute-start | bytes 1572872 | tf_op jit(solution)/shard_map/while/body/eval_jaxpr/ppermute | solution.py:542
  489.9 6.0 %collective-permute-start.1 = (bf16[64,640]{1,0:T(8,128)(2,1)S(1)}, bf16[64,640]{1,0:T(8,128)(2,1)S(1)}, u32[]{:S(2)}, u32[]{:S(2)}) collective-permute-start(bf16[64,640]{1,0:T(8,128)(2,1)S(1)} %get-tuple-element.847), channel_id=1, source_target_pairs={{0,4},{4,8},{8,12},{12,16},{16,20},{20,24},{24,28},{1,5},{5,9},{9,... | collective-permute-start | bytes 245768 | tf_op jit(solution)/shard_map/while/body/eval_jaxpr/ppermute | solution.py:541
  495.9 7.5 %collective-permute-start.2 = (bf16[64,640]{1,0:T(8,128)(2,1)S(1)}, bf16[64,640]{1,0:T(8,128)(2,1)S(1)}, u32[]{:S(2)}, u32[]{:S(2)}) collective-permute-start(bf16[64,640]{1,0:T(8,128)(2,1)S(1)} %collective-permute-done.1), channel_id=1, source_target_pairs={{0,1},{1,2},{2,3},{3,0},{4,5},{5,6},{6,7},{7,4},{8,9},{9,10},{10,1... | collective-permute-start | bytes 245768 | tf_op jit(solution)/shard_map/while/body/eval_jaxpr/ppermute | solution.py:469
  499.0 6.1 %collective-permute-start.3 = (bf16[64,640]{1,0:T(8,128)(2,1)S(1)}, bf16[64,640]{1,0:T(8,128)(2,1)S(1)}, u32[]{:S(2)}, u32[]{:S(2)}) collective-permute-start(bf16[64,640]{1,0:T(8,128)(2,1)S(1)} %collective-permute-done.1), channel_id=1, source_target_pairs={{0,2},{1,3},{2,0},{3,1},{4,6},{5,7},{6,4},{7,5},{8,10},{9,11},{10,... | collective-permute-start | bytes 245768 | tf_op jit(solution)/shard_map/while/body/eval_jaxpr/ppermute | solution.py:469
  (24 other events, 334.2 us)

commit v3 on v2

v3 whole, which is shorter than its diff:
```python
import functools

import jax
import jax.numpy as jnp
from jax import lax
from jax.experimental import pallas as pl
from jax.experimental.pallas import tpu as pltpu
from jax.sharding import PartitionSpec as P

ROWS = 16
LANES = 128
COLS = 512
DEPTH = 1024
ANY = pl.BlockSpec(memory_space=pl.ANY)
HBM = pl.BlockSpec(memory_space=pltpu.HBM)
VMEM = pl.BlockSpec(memory_space=pltpu.VMEM)
SMEM = pl.BlockSpec(memory_space=pltpu.SMEM)
LOG2E = 1.4426950408889634


def softplus(value):
    small = jnp.exp(-jnp.abs(value))
    return jnp.maximum(value, 0.0) + jnp.where(
        small < 1e-3, small - 0.5 * small * small, jnp.log(1.0 + small)
    )


def finish(total, squares, rank):
    rows, width = total.shape
    extra = width - rank
    lane = lax.broadcasted_iota(jnp.int32, (rows, LANES), 1)
    high = squares.astype(jnp.bfloat16).astype(jnp.float32)
    tail = jnp.concatenate(
        [total[:, rank:], jnp.zeros((rows, LANES - extra), jnp.float32)], axis=1
    )
    tail = jnp.where(lane == extra, high, jnp.where(lane == extra + 1, squares - high, tail))
    return total[:, :rank].astype(jnp.bfloat16), tail.astype(jnp.bfloat16)


def merge(even, odd, sublane, distance):
    clear = (sublane & distance) == 0
    size = sublane.shape[0]
    near = jnp.where(clear, even, pltpu.roll(odd, distance, 0))
    far = jnp.where(clear, pltpu.roll(even, size - distance, 0), odd)
    return near + far


def step_kernel(width, layers, peers, *refs):
    meta, plan, arrived = refs[:3]
    others = refs[3 : 2 + peers]
    (
        inputs,
        state,
        landed,
        dt_weight,
        dt_bias,
        rates,
        skip,
        gain,
        next_gain,
        gate,
        next_weight,
        final_in,
        mixed_in,
        leaving_in,
        onward,
        partial,
        final,
        mixed,
        leaving,
        gates,
        result,
        hold,
        held,
        weight,
        coming,
        going,
        size_rows,
        drive_rows,
        base_rows,
        totals,
        spread_in,
        spread_out,
        input_sem,
        gate_sem,
        state_sem,
        held_sem,
        weight_sem,
        final_sem,
        mixed_sem,
        coming_sem,
        going_sem,
    ) = refs[2 + peers :]
    steps, rows, channels = gates.shape
    units = steps * rows
    rank = dt_weight.shape[1]
    states = rates.shape[0]
    swaps = going.shape[0]
    cols = min(COLS, channels)
    parts = channels // cols
    depth = min(DEPTH, channels)
    wide_lanes = min(2 * LANES, cols)
    layer = meta[2]
    ahead = (meta[3] == 1) & (layer == layers - 1)
    first = pl.multiple_of(meta[1], ROWS)

    def at(j):
        return pl.ds(pl.multiple_of(j * cols, cols), cols)

    def input_copy(t):
        return pltpu.make_async_copy(
            inputs.at[t, pl.ds(pl.multiple_of(meta[4], ROWS), rows)],
            onward.at[pl.ds(t * rows, rows), pl.ds(0, channels)],
            input_sem.at[t],
        )

    def weight_copy(k):
        span = pl.ds(k * depth, depth)
        return pltpu.make_async_copy(next_weight.at[:, span], weight.at[:, span], weight_sem.at[k])

    def final_copy(j):
        return pltpu.make_async_copy(
            hold.at[:, :, at(j)], final.at[0, pl.ds(first, rows), :, at(j)], final_sem.at[j]
        )

    def mixed_copy(j):
        return pltpu.make_async_copy(
            result.at[:, :, at(j)], mixed.at[0, :, pl.ds(first, rows), at(j)], mixed_sem.at[j]
        )

    @pl.when(ahead)
    def _():
        for t in range(steps):
            input_copy(t).start()

    @pl.when((meta[3] == 1) & (meta[0] == 0))
    def _():
        for k in range(channels // depth):
            weight_copy(k).start()

    @pl.when(meta[0] == 1)
    def _():
        def planned(which, row, k):
            return plan[((which * 3 + row) * layers + layer) * swaps + k]

        gate_copy = pltpu.make_async_copy(gate.at[0, :, pl.ds(first, rows)], gates, gate_sem)

        def held_copy(j):
            return pltpu.make_async_copy(
                dt_weight.at[0, :, at(j)], held.at[:, at(j)], held_sem.at[j]
            )

        def state_copy(j):
            return pltpu.make_async_copy(
                state.at[0, pl.ds(first, rows), :, at(j)], hold.at[:, :, at(j)], state_sem.at[j]
            )

        def coming_copy(k):
            return pltpu.make_async_copy(
                landed.at[planned(0, 1, k)], coming.at[k], coming_sem.at[k]
            )

        def going_copy(k):
            return pltpu.make_async_copy(
                going.at[k], leaving.at[planned(1, 1, k)], going_sem.at[k]
            )

        def inside(which, k):
            place = planned(which, 0, k) - first
            return (place >= 0) & (place < rows)

        gate_copy.start()
        for k in range(swaps):

            @pl.when(inside(0, k))
            def _():
                coming_copy(k).start()

        for j in range(parts):
            held_copy(j).start()
            state_copy(j).start()

        @pl.when(meta[3] == 1)
        def _():
            for k in range(channels // depth):
                weight_copy(k).start()

        total = arrived[:, channels:].astype(jnp.float32)
        for other in others:
            total += other[...].astype(jnp.float32)
        tail = total[:, rank:]
        squares = tail[:, 2 * states : 2 * states + 1] + tail[:, 2 * states + 1 : 2 * states + 2]
        inverse = 1.0 / jnp.sqrt(squares / width + 1e-05)
        low = (total[:, :rank] * inverse).astype(jnp.bfloat16)
        turned = (tail * inverse).T
        for row in range(units):
            column = turned[: 2 * states, row : row + 1]
            wide = jnp.broadcast_to(column, (2 * states, LANES)).astype(jnp.bfloat16)
            spread_in[row] = wide[:states]
            spread_out[row] = wide[states:]
        sublane = lax.broadcasted_iota(jnp.int32, (states // 2, wide_lanes), 0)
        for k in range(swaps):

            @pl.when(inside(0, k))
            def _():
                coming_copy(k).wait()

        gate_copy.wait()

        def prepare(j, slot):
            here = at(j)
            size = softplus(
                jnp.dot(low, held[:, here], preferred_element_type=jnp.float32) + dt_bias[:, here]
            )
            normed = arrived[:, here].astype(jnp.float32) * gain[:, here] * inverse
            size_rows[slot] = size
            drive_rows[slot] = size * normed
            base_rows[slot] = skip[:, here] * normed

        held_copy(0).wait()
        prepare(0, 0)

        def part(j, carry):
            here = at(j)
            slot = lax.rem(j, 2)
            later = jnp.minimum(j + 1, parts - 1)
            state_copy(j).wait()

            @pl.when(j + 1 < parts)
            def _():
                held_copy(j + 1).wait()

            for k in range(swaps):
                place = planned(0, 0, k) - first

                @pl.when((place >= 0) & (place < rows))
                def _():
                    hold[place, :, here] = coming[k, :, here].astype(jnp.float32)

            for strip in range(cols // wide_lanes):
                lanes = pl.ds(strip * wide_lanes, wide_lanes)
                full = pl.ds(pl.multiple_of(j * cols + strip * wide_lanes, LANES), wide_lanes)
                rate = rates[:, full]
                pending = {}
                for r in range(rows):
                    h = hold[r, :, full].astype(jnp.bfloat16)
                    for t in range(steps):
                        row = t * rows + r
                        size_row = jnp.broadcast_to(
                            size_rows[slot, row : row + 1, lanes], (states, wide_lanes)
                        ).astype(jnp.bfloat16)
                        drive_row = jnp.broadcast_to(
                            drive_rows[slot, row : row + 1, lanes], (states, wide_lanes)
                        ).astype(jnp.bfloat16)
                        b = jnp.concatenate([spread_in[row]] * (wide_lanes // LANES), axis=1)
                        c = jnp.concatenate([spread_out[row]] * (wide_lanes // LANES), axis=1)
                        h = jnp.exp2(size_row * rate) * h + drive_row * b
                        term = (h * c).astype(jnp.float32)
                        term = term[: states // 2] + term[states // 2 :]
                        distance = 1
                        while (t, distance) in pending:
                            term = merge(pending.pop((t, distance)), term, sublane, distance)
                            distance *= 2
                        if distance == states // 2:
                            start = row - row % (states // 2)
                            totals[start : start + states // 2, lanes] = term
                        else:
                            pending[t, distance] = term
                    hold[r, :, full] = h.astype(jnp.float32)

            opened = gates[:, :, here].astype(jnp.float32).reshape(units, cols)
            value = (totals[...] + base_rows[slot]) * (opened * jax.nn.sigmoid(opened))
            value = value.astype(jnp.bfloat16)
            result[:, :, here] = value.reshape(steps, rows, cols)
            passed = arrived[:, here].astype(jnp.float32) + value.astype(jnp.float32)
            passed = passed.astype(jnp.bfloat16)
            prepare(later, 1 - slot)

            @pl.when(layer < layers - 1)
            def _():
                onward[:, here] = passed

            final_copy(j).start()
            mixed_copy(j).start()
            return carry

        lax.fori_loop(0, parts, part, 0)
        for k in range(swaps):
            place = planned(1, 0, k) - first

            @pl.when((place >= 0) & (place < rows))
            def _():
                going[k] = hold[place].astype(jnp.bfloat16)
                going_copy(k).start()
                going_copy(k).wait()

    @pl.when(ahead)
    def _():
        for t in range(steps):
            input_copy(t).wait()

    @pl.when(meta[3] == 1)
    def _():
        total = jnp.zeros((units, weight.shape[0]), jnp.float32)
        squares = jnp.zeros((units, 1), jnp.float32)
        for k in range(channels // depth):
            span = pl.ds(k * depth, depth)
            wide = onward[:, span].astype(jnp.float32)
            squares += jnp.sum(wide * wide, axis=1, keepdims=True)
            scaled = (wide * next_gain[:, span]).astype(jnp.bfloat16)
            weight_copy(k).wait()
            total += lax.dot_general(
                scaled,
                weight[:, span],
                (((1,), (1,)), ((), ())),
                preferred_element_type=jnp.float32,
            )
        low, tail = finish(total, squares, rank)
        onward[:, channels : channels + rank] = low
        onward[:, channels + rank :] = tail
        partial[:, :rank] = low
        partial[:, rank:] = tail

    @pl.when(meta[0] == 1)
    def _():
        for j in range(parts):
            mixed_copy(j).wait()
            final_copy(j).wait()


def pick_kernel(meta, plan, store, out):
    layers = out.shape[0]
    swaps = plan.shape[0] // (6 * layers)
    for layer in range(layers):
        slot = 0
        for k in range(swaps):
            asked = plan[(layers + layer) * swaps + k] == meta[0]
            slot = jnp.where(asked, plan[(2 * layers + layer) * swaps + k], slot)
        out[layer] = store[0, slot].astype(out.dtype)


def keep_kernel(meta, plan, store, returned, out):
    layers = returned.shape[0]
    swaps = plan.shape[0] // (6 * layers)
    for slot in range(store.shape[1]):
        source = -1
        for layer in range(layers):
            for k in range(swaps):
                named = (plan[(4 * layers + layer) * swaps + k] == meta[0]) & (
                    plan[(5 * layers + layer) * swaps + k] == slot
                )
                source = jnp.where(named, layer, source)

        @pl.when(source >= 0)
        def _():
            out[0, slot] = returned[source].astype(out.dtype)

        @pl.when(source < 0)
        def _():
            out[0, slot] = store[0, slot]


def leave(*refs):
    pass


def empty(shapes):
    return pl.pallas_call(leave, out_shape=shapes, out_specs=[HBM] * len(shapes))()


def shards(
    inputs,
    state,
    pool,
    x_weight,
    dt_weight,
    dt_bias,
    a_log,
    skip,
    gain,
    gate_input,
    swap_plan,
    evict_plan,
):
    section = lax.axis_index("section")
    holders = lax.axis_size("section")
    peers = lax.axis_size("tensor")
    channels = x_weight.shape[1]
    width = channels * peers
    rank = dt_weight.shape[1]
    states = a_log.shape[1]
    requests = state.shape[1]
    steps = inputs.shape[0]
    swaps = swap_plan.shape[2]
    pairs = requests // (2 * ROWS)
    rows = steps * ROWS
    cols = min(COLS, channels)
    parts = channels // cols
    depth = min(DEPTH, channels)
    turns = pairs + holders - 1
    plan = jnp.concatenate([swap_plan.reshape(-1), evict_plan.reshape(-1)])
    down = [((i + 1) % holders, i) for i in range(holders)]
    weight = lax.ppermute(jnp.swapaxes(x_weight[0], 0, 1), "section", down)
    next_gain = lax.ppermute(gain, "section", down)
    rates = (-LOG2E * jnp.exp(a_log[0])).astype(jnp.bfloat16)
    place = section.astype(jnp.int32)[None]

    block_shape = jax.ShapeDtypeStruct((rows, channels + rank + LANES), jnp.bfloat16)
    partial_shape = jax.ShapeDtypeStruct((rows, rank + LANES), jnp.bfloat16)
    stream_shape = (steps, ROWS, channels)
    state_shape = jax.ShapeDtypeStruct(state.shape, state.dtype)
    mixed_shape = jax.ShapeDtypeStruct(gate_input.shape, gate_input.dtype)
    moved_shape = jax.ShapeDtypeStruct((holders, states, channels), jnp.bfloat16)

    def meta_of(turn, half):
        pair = turn - section
        valid = (pair >= 0) & (pair < pairs)
        last = section == holders - 1
        following = turn + 1
        ahead = jnp.where(last, (following >= 0) & (following < pairs), valid)
        first = (jnp.clip(pair, 0, pairs - 1) * 2 + half) * ROWS
        then = (jnp.clip(following, 0, pairs - 1) * 2 + half) * ROWS
        return jnp.stack([valid, first, section, ahead, then]).astype(jnp.int32)

    def step(meta, blocks, final, mixed, leaving):
        given = 2 + peers
        return pl.pallas_call(
            functools.partial(step_kernel, width, holders, peers),
            out_shape=[block_shape, partial_shape, state_shape, mixed_shape, moved_shape],
            in_specs=[SMEM, SMEM]
            + [VMEM] * peers
            + [HBM, HBM, ANY, ANY]
            + [VMEM] * 5
            + [HBM, ANY]
            + [HBM] * 3,
            out_specs=[VMEM, VMEM, HBM, HBM, HBM],
            scratch_shapes=[
                pltpu.VMEM(stream_shape, jnp.bfloat16),
                pltpu.VMEM(stream_shape, jnp.bfloat16),
                pltpu.VMEM((ROWS, states, channels), jnp.float32),
                pltpu.VMEM((rank, channels), jnp.bfloat16),
                pltpu.VMEM(weight.shape, jnp.bfloat16),
                pltpu.VMEM((swaps, states, channels), jnp.bfloat16),
                pltpu.VMEM((swaps, states, channels), jnp.bfloat16),
                pltpu.VMEM((2, rows, cols), jnp.float32),
                pltpu.VMEM((2, rows, cols), jnp.float32),
                pltpu.VMEM((2, rows, cols), jnp.float32),
                pltpu.VMEM((rows, cols), jnp.float32),
                pltpu.VMEM((rows, states, LANES), jnp.bfloat16),
                pltpu.VMEM((rows, states, LANES), jnp.bfloat16),
                pltpu.SemaphoreType.DMA((steps,)),
                pltpu.SemaphoreType.DMA,
                pltpu.SemaphoreType.DMA((parts,)),
                pltpu.SemaphoreType.DMA((parts,)),
                pltpu.SemaphoreType.DMA((channels // depth,)),
                pltpu.SemaphoreType.DMA((parts,)),
                pltpu.SemaphoreType.DMA((parts,)),
                pltpu.SemaphoreType.DMA((swaps,)),
                pltpu.SemaphoreType.DMA((swaps,)),
            ],
            input_output_aliases={given + 11 + k: 2 + k for k in range(3)},
            compiler_params=pltpu.CompilerParams(vmem_limit_bytes=28 * 2**20),
            cost_estimate=pl.CostEstimate(
                flops=4 * rows * channels * (rank + LANES) + 8 * rows * states * channels,
                bytes_accessed=4 * channels * rank + 8 * ROWS * states * channels,
                transcendentals=rows * states * channels,
            ),
            name="step",
        )(
            meta,
            plan,
            *blocks,
            inputs,
            state,
            landed,
            dt_weight,
            dt_bias,
            rates,
            skip,
            gain,
            next_gain,
            gate_input,
            weight,
            final,
            mixed,
            leaving,
        )

    def send(block, partial):
        axes = ("section", "tensor")
        blocks = []
        for shift in range(peers):
            route = [
                (l * peers + i, (l + 1) % holders * peers + (i + shift) % peers)
                for l in range(holders)
                for i in range(peers)
            ]
            blocks.append(lax.ppermute(partial if shift else block, axes, route))
        return blocks

    def swap(block):
        return lax.all_to_all(block, "section", split_axis=0, concat_axis=0, tiled=True)

    def turn(index, carry):
        out, late, kept = carry
        early = send(*out)
        *out, final, mixed, leaving = step(meta_of(index - 1, 1), late, *kept)
        late = send(*out)
        *out, final, mixed, leaving = step(meta_of(index, 0), early, final, mixed, leaving)
        return tuple(out), tuple(late), (final, mixed, leaving)

    picked = pl.pallas_call(
        pick_kernel, out_shape=moved_shape, in_specs=[SMEM, SMEM, VMEM], out_specs=VMEM, name="pick"
    )(place, plan, pool)
    landed = swap(picked)
    *kept, block, partial = empty(
        [state_shape, mixed_shape, moved_shape, block_shape, partial_shape]
    )
    late = (block,) + (partial,) * (peers - 1)
    *out, final, mixed, leaving = step(meta_of(-1, 0), late, *kept)
    out, late, kept = lax.fori_loop(
        0, turns, turn, (tuple(out), late, (final, mixed, leaving))
    )
    _, _, final, mixed, leaving = step(meta_of(turns - 1, 1), late, *kept)
    stored = pl.pallas_call(
        keep_kernel,
        out_shape=jax.ShapeDtypeStruct(pool.shape, pool.dtype),
        in_specs=[SMEM, SMEM, VMEM, VMEM],
        out_specs=VMEM,
        name="keep",
    )(place, plan, pool, swap(leaving))
    return (mixed, final, stored)


def solution(mesh):
    placed = (
        P(None, None, "tensor"),
        P("section", None, None, "tensor"),
        P("section", None, None, "tensor"),
        P("section", "tensor", None),
        P("section", None, "tensor"),
        P("section", "tensor"),
        P("section", None, "tensor"),
        P("section", "tensor"),
        P("section", "tensor"),
        P("section", None, None, "tensor"),
        P(),
        P(),
    )
    return jax.shard_map(
        shards,
        mesh=mesh,
        in_specs=placed,
        out_specs=(
            P("section", None, None, "tensor"),
            P("section", None, None, "tensor"),
            P("section", None, None, "tensor"),
        ),
        check_vma=False,
    )
```

time: 556 us -> 528 us (0.950)
  starting transfers between devices: 271 us -> 215 us
  waiting for transfers between devices: 110 us -> 129 us
  Pallas kernels: 123 us -> 137 us
  blocking collectives: 44.6 us -> 37.6 us
    ppermute x79 -> x90, starting transfers between devices: 268 us -> 212 us  [the longest x88 206 us: send(): blocks.append(lax.ppermute(partial if shift else block, axes, route))]
    ppermute x79 -> x90, waiting for transfers between devices: 77 us -> 128 us  [the longest x88 79.6 us: send(): blocks.append(lax.ppermute(partial if shift else block, axes, route))]
    all_to_all x1, waiting for transfers between devices: 33.3 us -> 0.76 us  [swap(): lax.all_to_all(block, 'section', split_axis=0, concat_axis=0, tiled=True)]
    pallas_call x15 -> x24, Pallas kernels: 108 us -> 132 us  [step(): pl.pallas_call(functools.partial(step_kernel, width, holders, peers), out...]
    pallas_call x1 -> x0, Pallas kernels: 10.5 us -> none  [shards(): pl.pallas_call(open_kernel, out_shape=[partial_shape, rest_shape], in_spe...]
    all_to_all x1, blocking collectives: 44.6 us -> 37.6 us  [swap(): lax.all_to_all(block, 'section', split_axis=0, concat_axis=0, tiled=True)]
  transfers between devices with their start and end apart: 80 -> 91, of which waited for: 57 -> 29; matrix products, arithmetic and copies ran while one was open for 0% -> 1% of each run, Pallas kernels for 5% -> 25%
where the time goes in v3:
time: 528 us; the launch traced here: 526 us
  starting transfers between devices  215 us (41%)
  Pallas kernels  137 us (26%)
  waiting for transfers between devices  129 us (24%)
  blocking collectives  37.6 us (7%)
    ppermute x88, starting transfers between devices, send(): blocks.append(lax.ppermute(partial if shift else block, axes, route))  206 us
    pallas_call x24, Pallas kernels, step(): pl.pallas_call(functools.partial(step_kernel, width, holders, peers), out...  132 us
    ppermute x88, waiting for transfers between devices, send(): blocks.append(lax.ppermute(partial if shift else block, axes, route))  79.6 us
    ppermute x1, waiting for transfers between devices, shards(): next_gain = lax.ppermute(gain, 'section', down)  48.5 us
    all_to_all x1, blocking collectives, swap(): lax.all_to_all(block, 'section', split_axis=0, concat_axis=0, tiled=True)  37.6 us
  transfers between devices with their start and end apart: 91, of which 29 were waited for; matrix products, arithmetic and copies ran while one was open for 1% of the time, Pallas kernels for 25%

profile of v3, /device:TPU:0, one launch (start us, length us, event | category | flops | bytes accessed | tf_op | source)
XLA Modules:
  0.0 525.8 jit_solution(2314943686621109435)
XLA Ops:
  0.7 3.4 collective-permute-start.9
  5.9 2.3 pick.1
  8.1 3.6 all-to-all-start
  11.7 2.6 collective-permute-start.8
  16.1 48.5 %collective-permute-done.8.refs_14_ = f32[1,4096]{1,0:T(1,128)} collective-permute-done((f32[1,4096]{1,0:T(1,128)}, f32[1,4096]{1,0:T(1,128)}, u32[]{:S(2)}, u32[]{:S(2)}) %collective-permute-start.8) | collective-permute-done | bytes 16416 | tf_op jit(solution)/shard_map/ppermute | solution.py:404
  65.4 2.1 step.26
  67.4 416.0 %while.34 = (s32[]{:T(128)}, bf16[64,4736]{1,0:T(8,128)(2,1)}, bf16[64,640]{1,0:T(8,128)(2,1)}, bf16[64,4736]{1,0:T(8,128)(2,1)S(1)}, bf16[64,640]{1,0:T(8,128)(...) while((s32[]{:T(128)}, bf16[64,4736]{1,0:T(8,128)(2,1)}, ...), condition=%wide.region_1.2_spmd, body=%wide.region_0.1_spmd.sunk | while | flops 1409286144 | bytes 40371192 | solution.py:521
  71.9 2.5 collective-permute-start.2
  75.6 9.6 %collective-permute-done.1.refs_3_ = bf16[64,640]{1,0:T(8,128)(2,1)S(1)} collective-permute-done((bf16[64,640]{1,0:T(8,128)(2,1)}, bf16[64,640]{1,0:T(8,128)(2,1)S(1)}, u32[]{:S(2)}, u32[]{:S(2)}) %collective-permute-start.1) | collective-permute-done | bytes 81952 | tf_op jit(solution)/shard_map/while/body/eval_jaxpr/ppermute | solution.py:498
  85.2 2.8 collective-permute-start.7
  88.0 13.0 %step.29 = (bf16[64,4736]{1,0:T(8,128)(2,1)}, bf16[64,640]{1,0:T(8,128)(2,1)}, f32[1,128,16,4096]{3,2,1,0:T(8,128)}, bf16[1,4,128,4096]{3,2,1,0:T(8,128)(2,1)}, bf16[8,16,4096]{2,1,0:T(8,128)(2,1)}) custom-call(s32[5]{0:T(128)S(1)} %stack.216.refs_0_, ...), custom_call_target="tpu_custom_call", output_to_operand_aliasing={{2}: (17, {}), {3}: (18, {}), {4}: (19, {})} | custom-call | flops 704643072 | bytes 16777216 | tf_op jit(solution)/shard_map/while/body/eval_jaxpr/step/pallas_call | solution.py:427
  101.3 12.3 %step.28 = (bf16[64,4736]{1,0:T(8,128)(2,1)S(1)}, bf16[64,640]{1,0:T(8,128)(2,1)S(1)}, f32[1,128,16,4096]{3,2,1,0:T(8,128)}, bf16[1,4,128,4096]{3,2,1,0:T(8,128)(2,1)}, bf16[8,16,4096]{2,1,0:T(8,128)(2,1)}) custom-call(s32[5]{0:T(128)S(1)} %stack.219.refs_0_, ...), custom_call_target="tpu_custom_call", output_to_operand_aliasing={{2}: (17, {}), {3}: (18, {}), {4}: (19, {})} | custom-call | flops 704643072 | bytes 16777216 | tf_op jit(solution)/shard_map/while/body/eval_jaxpr/step/pallas_call | solution.py:427
  113.9 7.9 %collective-permute-done.1.refs_3_ = bf16[64,640]{1,0:T(8,128)(2,1)S(1)} collective-permute-done((bf16[64,640]{1,0:T(8,128)(2,1)}, bf16[64,640]{1,0:T(8,128)(2,1)S(1)}, u32[]{:S(2)}, u32[]{:S(2)}) %collective-permute-start.1) | collective-permute-done | bytes 81952 | tf_op jit(solution)/shard_map/while/body/eval_jaxpr/ppermute | solution.py:498
  124.5 13.0 %step.29 = (bf16[64,4736]{1,0:T(8,128)(2,1)}, bf16[64,640]{1,0:T(8,128)(2,1)}, f32[1,128,16,4096]{3,2,1,0:T(8,128)}, bf16[1,4,128,4096]{3,2,1,0:T(8,128)(2,1)}, bf16[8,16,4096]{2,1,0:T(8,128)(2,1)}) custom-call(s32[5]{0:T(128)S(1)} %stack.216.refs_0_, ...), custom_call_target="tpu_custom_call", output_to_operand_aliasing={{2}: (17, {}), {3}: (18, {}), {4}: (19, {})} | custom-call | flops 704643072 | bytes 16777216 | tf_op jit(solution)/shard_map/while/body/eval_jaxpr/step/pallas_call | solution.py:427
  139.1 12.3 %step.28 = (bf16[64,4736]{1,0:T(8,128)(2,1)S(1)}, bf16[64,640]{1,0:T(8,128)(2,1)S(1)}, f32[1,128,16,4096]{3,2,1,0:T(8,128)}, bf16[1,4,128,4096]{3,2,1,0:T(8,128)(2,1)}, bf16[8,16,4096]{2,1,0:T(8,128)(2,1)}) custom-call(s32[5]{0:T(128)S(1)} %stack.219.refs_0_, ...), custom_call_target="tpu_custom_call", output_to_operand_aliasing={{2}: (17, {}), {3}: (18, {}), {4}: (19, {})} | custom-call | flops 704643072 | bytes 16777216 | tf_op jit(solution)/shard_map/while/body/eval_jaxpr/step/pallas_call | solution.py:427
  151.6 2.3 collective-permute-start.2
  153.9 5.7 %collective-permute-done.1.refs_3_ = bf16[64,640]{1,0:T(8,128)(2,1)S(1)} collective-permute-done((bf16[64,640]{1,0:T(8,128)(2,1)}, bf16[64,640]{1,0:T(8,128)(2,1)S(1)}, u32[]{:S(2)}, u32[]{:S(2)}) %collective-permute-start.1) | collective-permute-done | bytes 81952 | tf_op jit(solution)/shard_map/while/body/eval_jaxpr/ppermute | solution.py:498
  159.6 3.3 collective-permute-done.2.refs_4_
  162.8 2.6 collective-permute-start.7
  165.5 13.0 %step.29 = (bf16[64,4736]{1,0:T(8,128)(2,1)}, bf16[64,640]{1,0:T(8,128)(2,1)}, f32[1,128,16,4096]{3,2,1,0:T(8,128)}, bf16[1,4,128,4096]{3,2,1,0:T(8,128)(2,1)}, bf16[8,16,4096]{2,1,0:T(8,128)(2,1)}) custom-call(s32[5]{0:T(128)S(1)} %stack.216.refs_0_, ...), custom_call_target="tpu_custom_call", output_to_operand_aliasing={{2}: (17, {}), {3}: (18, {}), {4}: (19, {})} | custom-call | flops 704643072 | bytes 16777216 | tf_op jit(solution)/shard_map/while/body/eval_jaxpr/step/pallas_call | solution.py:427
  178.7 13.2 %step.28 = (bf16[64,4736]{1,0:T(8,128)(2,1)S(1)}, bf16[64,640]{1,0:T(8,128)(2,1)S(1)}, f32[1,128,16,4096]{3,2,1,0:T(8,128)}, bf16[1,4,128,4096]{3,2,1,0:T(8,128)(2,1)}, bf16[8,16,4096]{2,1,0:T(8,128)(2,1)}) custom-call(s32[5]{0:T(128)S(1)} %stack.219.refs_0_, ...), custom_call_target="tpu_custom_call", output_to_operand_aliasing={{2}: (17, {}), {3}: (18, {}), {4}: (19, {})} | custom-call | flops 704643072 | bytes 16777216 | tf_op jit(solution)/shard_map/while/body/eval_jaxpr/step/pallas_call | solution.py:427
  192.8 7.2 %collective-permute-done.1.refs_3_ = bf16[64,640]{1,0:T(8,128)(2,1)S(1)} collective-permute-done((bf16[64,640]{1,0:T(8,128)(2,1)}, bf16[64,640]{1,0:T(8,128)(2,1)S(1)}, u32[]{:S(2)}, u32[]{:S(2)}) %collective-permute-start.1) | collective-permute-done | bytes 81952 | tf_op jit(solution)/shard_map/while/body/eval_jaxpr/ppermute | solution.py:498
  202.5 13.3 %step.29 = (bf16[64,4736]{1,0:T(8,128)(2,1)}, bf16[64,640]{1,0:T(8,128)(2,1)}, f32[1,128,16,4096]{3,2,1,0:T(8,128)}, bf16[1,4,128,4096]{3,2,1,0:T(8,128)(2,1)}, bf16[8,16,4096]{2,1,0:T(8,128)(2,1)}) custom-call(s32[5]{0:T(128)S(1)} %stack.216.refs_0_, ...), custom_call_target="tpu_custom_call", output_to_operand_aliasing={{2}: (17, {}), {3}: (18, {}), {4}: (19, {})} | custom-call | flops 704643072 | bytes 16777216 | tf_op jit(solution)/shard_map/while/body/eval_jaxpr/step/pallas_call | solution.py:427
  216.7 14.0 %step.28 = (bf16[64,4736]{1,0:T(8,128)(2,1)S(1)}, bf16[64,640]{1,0:T(8,128)(2,1)S(1)}, f32[1,128,16,4096]{3,2,1,0:T(8,128)}, bf16[1,4,128,4096]{3,2,1,0:T(8,128)(2,1)}, bf16[8,16,4096]{2,1,0:T(8,128)(2,1)}) custom-call(s32[5]{0:T(128)S(1)} %stack.219.refs_0_, ...), custom_call_target="tpu_custom_call", output_to_operand_aliasing={{2}: (17, {}), {3}: (18, {}), {4}: (19, {})} | custom-call | flops 704643072 | bytes 16777216 | tf_op jit(solution)/shard_map/while/body/eval_jaxpr/step/pallas_call | solution.py:427
  230.9 3.8 collective-permute-start.3
  234.7 4.0 collective-permute-done.1.refs_3_
  238.8 2.8 collective-permute-done.3.refs_5_
  247.1 3.9 collective-permute-done.7
  251.0 6.7 %collective-permute-start = (bf16[64,4736]{1,0:T(8,128)(2,1)}, bf16[64,4736]{1,0:T(8,128)(2,1)S(1)}, u32[]{:S(2)}, u32[]{:S(2)}) collective-permute-start(bf16[64,4736]{1,0:T(8,128)(2,1)} %get-tuple-element.1060), channel_id=1, source_target_pairs={{0,4},{1,5},{2,6},{3,7},{4,8},{5,9},{6,10},{7,11},{8,12},{9,13},{1... | collective-permute-start | bytes 1818632 | tf_op jit(solution)/shard_map/while/body/eval_jaxpr/ppermute | solution.py:498
  259.2 12.0 %collective-permute-start.4 = (bf16[64,4736]{1,0:T(8,128)(2,1)S(1)}, bf16[64,4736]{1,0:T(8,128)(2,1)S(1)}, u32[]{:S(2)}, u32[]{:S(2)}) collective-permute-start(bf16[64,4736]{1,0:T(8,128)(2,1)S(1)} %get-tuple-element.1022), channel_id=1, source_target_pairs={{0,4},{1,5},{2,6},{3,7},{4,8},{5,9},{6,10},{7,11},{8,12},{9,13},{1... | collective-permute-start | bytes 1818632 | tf_op jit(solution)/shard_map/while/body/eval_jaxpr/ppermute | solution.py:498
  271.4 4.0 collective-permute-start.2
  275.4 3.3 collective-permute-start.3
  282.1 4.9 collective-permute-start.7
  292.2 10.2 %collective-permute-start.4 = (bf16[64,4736]{1,0:T(8,128)(2,1)S(1)}, bf16[64,4736]{1,0:T(8,128)(2,1)S(1)}, u32[]{:S(2)}, u32[]{:S(2)}) collective-permute-start(bf16[64,4736]{1,0:T(8,128)(2,1)S(1)} %get-tuple-element.1022), channel_id=1, source_target_pairs={{0,4},{1,5},{2,6},{3,7},{4,8},{5,9},{6,10},{7,11},{8,12},{9,13},{1... | collective-permute-start | bytes 1818632 | tf_op jit(solution)/shard_map/while/body/eval_jaxpr/ppermute | solution.py:498
  302.5 13.4 %collective-permute-start.1 = (bf16[64,640]{1,0:T(8,128)(2,1)}, bf16[64,640]{1,0:T(8,128)(2,1)S(1)}, u32[]{:S(2)}, u32[]{:S(2)}) collective-permute-start(bf16[64,640]{1,0:T(8,128)(2,1)} %get-tuple-element.1061), channel_id=1, source_target_pairs={{0,5},{1,6},{2,7},{3,4},{4,9},{5,10},{6,11},{7,8},{8,13},{9,14},{1... | collective-permute-start | bytes 245768 | tf_op jit(solution)/shard_map/while/body/eval_jaxpr/ppermute | solution.py:498
  319.0 2.1 collective-permute-start.5
  323.8 3.2 collective-permute-start.7
  333.3 8.3 %collective-permute-start.1 = (bf16[64,640]{1,0:T(8,128)(2,1)}, bf16[64,640]{1,0:T(8,128)(2,1)S(1)}, u32[]{:S(2)}, u32[]{:S(2)}) collective-permute-start(bf16[64,640]{1,0:T(8,128)(2,1)} %get-tuple-element.1061), channel_id=1, source_target_pairs={{0,5},{1,6},{2,7},{3,4},{4,9},{5,10},{6,11},{7,8},{8,13},{9,14},{1... | collective-permute-start | bytes 245768 | tf_op jit(solution)/shard_map/while/body/eval_jaxpr/ppermute | solution.py:498
  341.6 12.0 %collective-permute-start.2 = (bf16[64,640]{1,0:T(8,128)(2,1)}, bf16[64,640]{1,0:T(8,128)(2,1)S(1)}, u32[]{:S(2)}, u32[]{:S(2)}) collective-permute-start(bf16[64,640]{1,0:T(8,128)(2,1)} %get-tuple-element.1061), channel_id=1, source_target_pairs={{0,6},{1,7},{2,4},{3,5},{4,10},{5,11},{6,8},{7,9},{8,14},{9,15},{1... | collective-permute-start | bytes 245768 | tf_op jit(solution)/shard_map/while/body/eval_jaxpr/ppermute | solution.py:498
  353.6 2.7 collective-permute-start.3
  356.3 2.5 collective-permute-start.5
  358.8 3.1 collective-permute-start.6
  361.9 5.7 %collective-permute-start.7 = (bf16[64,640]{1,0:T(8,128)(2,1)S(1)}, bf16[64,640]{1,0:T(8,128)(2,1)}, u32[]{:S(2)}, u32[]{:S(2)}) collective-permute-start(bf16[64,640]{1,0:T(8,128)(2,1)S(1)} %get-tuple-element.1023), channel_id=1, source_target_pairs={{0,7},{1,4},{2,5},{3,6},{4,11},{5,8},{6,9},{7,10},{8,15},{9,12},{1... | collective-permute-start | bytes 245768 | tf_op jit(solution)/shard_map/while/body/eval_jaxpr/ppermute | solution.py:498
  371.3 2.3 collective-permute-start.4
  373.6 2.5 collective-permute-start.1
  376.1 8.3 %collective-permute-start.2 = (bf16[64,640]{1,0:T(8,128)(2,1)}, bf16[64,640]{1,0:T(8,128)(2,1)S(1)}, u32[]{:S(2)}, u32[]{:S(2)}) collective-permute-start(bf16[64,640]{1,0:T(8,128)(2,1)} %get-tuple-element.1061), channel_id=1, source_target_pairs={{0,6},{1,7},{2,4},{3,5},{4,10},{5,11},{6,8},{7,9},{8,14},{9,15},{1... | collective-permute-start | bytes 245768 | tf_op jit(solution)/shard_map/while/body/eval_jaxpr/ppermute | solution.py:498
  384.4 13.9 %collective-permute-start.3 = (bf16[64,640]{1,0:T(8,128)(2,1)}, bf16[64,640]{1,0:T(8,128)(2,1)S(1)}, u32[]{:S(2)}, u32[]{:S(2)}) collective-permute-start(bf16[64,640]{1,0:T(8,128)(2,1)} %get-tuple-element.1061), channel_id=1, source_target_pairs={{0,7},{1,4},{2,5},{3,6},{4,11},{5,8},{6,9},{7,10},{8,15},{9,12},{1... | collective-permute-start | bytes 245768 | tf_op jit(solution)/shard_map/while/body/eval_jaxpr/ppermute | solution.py:498
  399.1 2.8 collective-permute-start.6
  402.0 5.3 %collective-permute-start.7 = (bf16[64,640]{1,0:T(8,128)(2,1)S(1)}, bf16[64,640]{1,0:T(8,128)(2,1)}, u32[]{:S(2)}, u32[]{:S(2)}) collective-permute-start(bf16[64,640]{1,0:T(8,128)(2,1)S(1)} %get-tuple-element.1023), channel_id=1, source_target_pairs={{0,7},{1,4},{2,5},{3,6},{4,11},{5,8},{6,9},{7,10},{8,15},{9,12},{1... | collective-permute-start | bytes 245768 | tf_op jit(solution)/shard_map/while/body/eval_jaxpr/ppermute | solution.py:498
  413.5 2.4 collective-permute-start.1
  415.9 4.1 collective-permute-start.2
  419.9 6.8 %collective-permute-start.3 = (bf16[64,640]{1,0:T(8,128)(2,1)}, bf16[64,640]{1,0:T(8,128)(2,1)S(1)}, u32[]{:S(2)}, u32[]{:S(2)}) collective-permute-start(bf16[64,640]{1,0:T(8,128)(2,1)} %get-tuple-element.1061), channel_id=1, source_target_pairs={{0,7},{1,4},{2,5},{3,6},{4,11},{5,8},{6,9},{7,10},{8,15},{9,12},{1... | collective-permute-start | bytes 245768 | tf_op jit(solution)/shard_map/while/body/eval_jaxpr/ppermute | solution.py:498
  426.8 5.5 %collective-permute-done.1.refs_3_ = bf16[64,640]{1,0:T(8,128)(2,1)S(1)} collective-permute-done((bf16[64,640]{1,0:T(8,128)(2,1)}, bf16[64,640]{1,0:T(8,128)(2,1)S(1)}, u32[]{:S(2)}, u32[]{:S(2)}) %collective-permute-start.1) | collective-permute-done | bytes 81952 | tf_op jit(solution)/shard_map/while/body/eval_jaxpr/ppermute | solution.py:498
  432.3 4.8 collective-permute-start.5
  438.8 6.7 %collective-permute-start.7 = (bf16[64,640]{1,0:T(8,128)(2,1)S(1)}, bf16[64,640]{1,0:T(8,128)(2,1)}, u32[]{:S(2)}, u32[]{:S(2)}) collective-permute-start(bf16[64,640]{1,0:T(8,128)(2,1)S(1)} %get-tuple-element.1023), channel_id=1, source_target_pairs={{0,7},{1,4},{2,5},{3,6},{4,11},{5,8},{6,9},{7,10},{8,15},{9,12},{1... | collective-permute-start | bytes 245768 | tf_op jit(solution)/shard_map/while/body/eval_jaxpr/ppermute | solution.py:498
  445.6 2.0 step.29
  450.3 4.2 collective-permute-start.1
  454.5 3.6 collective-permute-start.2
  459.0 11.3 %collective-permute-done.1.refs_3_ = bf16[64,640]{1,0:T(8,128)(2,1)S(1)} collective-permute-done((bf16[64,640]{1,0:T(8,128)(2,1)}, bf16[64,640]{1,0:T(8,128)(2,1)S(1)}, u32[]{:S(2)}, u32[]{:S(2)}) %collective-permute-start.1) | collective-permute-done | bytes 81952 | tf_op jit(solution)/shard_map/while/body/eval_jaxpr/ppermute | solution.py:498
  472.0 5.0 collective-permute-start.6
  477.0 2.8 collective-permute-start.7
  483.5 2.2 step.27
  485.7 37.6 %all_to_all.10.returned = bf16[8,16,4096]{2,1,0:T(8,128)(2,1)} all-to-all(bf16[8,16,4096]{2,1,0:T(8,128)(2,1)} %get-tuple-element.813), channel_id=1, replica_groups=mesh['section'=8,'tensor'=4] {'section'}, dimensions={0} | all-to-all | bytes 2097152 | tf_op jit(solution)/shard_map/all_to_all | solution.py:502
  523.2 2.6 keep.1
  (185 shorter events, 68.5 us)
Async XLA Ops:
  0.7 64.7 %collective-permute-start.9 = (bf16[544,4096]{1,0:T(8,128)(2,1)}, bf16[544,4096]{1,0:T(8,128)(2,1)}, u32[]{:S(2)}, u32[]{:S(2)}) collective-permute-start(bf16[544,4096]{1,0:T(8,128)(2,1)} %bitcast.39), channel_id=1, source_target_pairs={{4,0},{8,4},{12,8},{16,12},{20,16},{24,20},{28,24},{0,28},{5,1},{9... | collective-permute-start | bytes 13369352 | tf_op jit(solution)/shard_map/ppermute | solution.py:403
  8.1 57.2 %all-to-all-start = ((bf16[8,16,4096]{2,1,0:T(8,128)(2,1)}), bf16[8,16,4096]{2,1,0:T(8,128)(2,1)S(1)}, u32[]{:S(2)}, u32[]{:S(2)}) async-start(bf16[8,16,4096]{2,1,0:T(8,128)(2,1)} %pick.1), calls=%async_computation | async-start | bytes 2097152 | tf_op jit(solution)/shard_map/all_to_all | solution.py:502
  11.7 52.9 %collective-permute-start.8 = (f32[1,4096]{1,0:T(1,128)}, f32[1,4096]{1,0:T(1,128)}, u32[]{:S(2)}, u32[]{:S(2)}) collective-permute-start(f32[1,4096]{1,0:T(1,128)} %refs_13_.3), channel_id=1, source_target_pairs={{4,0},{8,4},{12,8},{16,12},{20,16},{24,20},{28,24},{0,28},{5,1},{9... | collective-permute-start | bytes 49160 | tf_op jit(solution)/shard_map/ppermute | solution.py:404
  67.4 20.6 %collective-permute-start = (bf16[64,4736]{1,0:T(8,128)(2,1)}, bf16[64,4736]{1,0:T(8,128)(2,1)S(1)}, u32[]{:S(2)}, u32[]{:S(2)}) collective-permute-start(bf16[64,4736]{1,0:T(8,128)(2,1)} %get-tuple-element.1060), channel_id=1, source_target_pairs={{0,4},{1,5},{2,6},{3,7},{4,8},{5,9},{6,10},{7,11},{8,12},{9,13},{1... | collective-permute-start | bytes 1818632 | tf_op jit(solution)/shard_map/while/body/eval_jaxpr/ppermute | solution.py:498
  69.0 32.0 %collective-permute-start.4 = (bf16[64,4736]{1,0:T(8,128)(2,1)S(1)}, bf16[64,4736]{1,0:T(8,128)(2,1)S(1)}, u32[]{:S(2)}, u32[]{:S(2)}) collective-permute-start(bf16[64,4736]{1,0:T(8,128)(2,1)S(1)} %get-tuple-element.1022), channel_id=1, source_target_pairs={{0,4},{1,5},{2,6},{3,7},{4,8},{5,9},{6,10},{7,11},{8,12},{9,13},{1... | collective-permute-start | bytes 1818632 | tf_op jit(solution)/shard_map/while/body/eval_jaxpr/ppermute | solution.py:498
  70.7 14.5 %collective-permute-start.1 = (bf16[64,640]{1,0:T(8,128)(2,1)}, bf16[64,640]{1,0:T(8,128)(2,1)S(1)}, u32[]{:S(2)}, u32[]{:S(2)}) collective-permute-start(bf16[64,640]{1,0:T(8,128)(2,1)} %get-tuple-element.1061), channel_id=1, source_target_pairs={{0,5},{1,6},{2,7},{3,4},{4,9},{5,10},{6,11},{7,8},{8,13},{9,14},{1... | collective-permute-start | bytes 245768 | tf_op jit(solution)/shard_map/while/body/eval_jaxpr/ppermute | solution.py:498
  71.9 13.2 %collective-permute-start.2 = (bf16[64,640]{1,0:T(8,128)(2,1)}, bf16[64,640]{1,0:T(8,128)(2,1)S(1)}, u32[]{:S(2)}, u32[]{:S(2)}) collective-permute-start(bf16[64,640]{1,0:T(8,128)(2,1)} %get-tuple-element.1061), channel_id=1, source_target_pairs={{0,6},{1,7},{2,4},{3,5},{4,10},{5,11},{6,8},{7,9},{8,14},{9,15},{1... | collective-permute-start | bytes 245768 | tf_op jit(solution)/shard_map/while/body/eval_jaxpr/ppermute | solution.py:498
  74.4 10.7 %collective-permute-start.3 = (bf16[64,640]{1,0:T(8,128)(2,1)}, bf16[64,640]{1,0:T(8,128)(2,1)S(1)}, u32[]{:S(2)}, u32[]{:S(2)}) collective-permute-start(bf16[64,640]{1,0:T(8,128)(2,1)} %get-tuple-element.1061), channel_id=1, source_target_pairs={{0,7},{1,4},{2,5},{3,6},{4,11},{5,8},{6,9},{7,10},{8,15},{9,12},{1... | collective-permute-start | bytes 245768 | tf_op jit(solution)/shard_map/while/body/eval_jaxpr/ppermute | solution.py:498
  85.2 15.9 %collective-permute-start.5 = (bf16[64,640]{1,0:T(8,128)(2,1)S(1)}, bf16[64,640]{1,0:T(8,128)(2,1)S(1)}, u32[]{:S(2)}, u32[]{:S(2)}) collective-permute-start(bf16[64,640]{1,0:T(8,128)(2,1)S(1)} %get-tuple-element.1023), channel_id=1, source_target_pairs={{0,5},{1,6},{2,7},{3,4},{4,9},{5,10},{6,11},{7,8},{8,13},{9,14},{1... | collective-permute-start | bytes 245768 | tf_op jit(solution)/shard_map/while/body/eval_jaxpr/ppermute | solution.py:498
  85.2 15.9 %collective-permute-start.6 = (bf16[64,640]{1,0:T(8,128)(2,1)S(1)}, bf16[64,640]{1,0:T(8,128)(2,1)S(1)}, u32[]{:S(2)}, u32[]{:S(2)}) collective-permute-start(bf16[64,640]{1,0:T(8,128)(2,1)S(1)} %get-tuple-element.1023), channel_id=1, source_target_pairs={{0,6},{1,7},{2,4},{3,5},{4,10},{5,11},{6,8},{7,9},{8,14},{9,15},{1... | collective-permute-start | bytes 245768 | tf_op jit(solution)/shard_map/while/body/eval_jaxpr/ppermute | solution.py:498
  85.2 15.9 %collective-permute-start.7 = (bf16[64,640]{1,0:T(8,128)(2,1)S(1)}, bf16[64,640]{1,0:T(8,128)(2,1)}, u32[]{:S(2)}, u32[]{:S(2)}) collective-permute-start(bf16[64,640]{1,0:T(8,128)(2,1)S(1)} %get-tuple-element.1023), channel_id=1, source_target_pairs={{0,7},{1,4},{2,5},{3,6},{4,11},{5,8},{6,9},{7,10},{8,15},{9,12},{1... | collective-permute-start | bytes 245768 | tf_op jit(solution)/shard_map/while/body/eval_jaxpr/ppermute | solution.py:498
  101.1 23.4 %collective-permute-start = (bf16[64,4736]{1,0:T(8,128)(2,1)}, bf16[64,4736]{1,0:T(8,128)(2,1)S(1)}, u32[]{:S(2)}, u32[]{:S(2)}) collective-permute-start(bf16[64,4736]{1,0:T(8,128)(2,1)} %get-tuple-element.1060), channel_id=1, source_target_pairs={{0,4},{1,5},{2,6},{3,7},{4,8},{5,9},{6,10},{7,11},{8,12},{9,13},{1... | collective-permute-start | bytes 1818632 | tf_op jit(solution)/shard_map/while/body/eval_jaxpr/ppermute | solution.py:498
  113.6 23.9 %collective-permute-start.4 = (bf16[64,4736]{1,0:T(8,128)(2,1)S(1)}, bf16[64,4736]{1,0:T(8,128)(2,1)S(1)}, u32[]{:S(2)}, u32[]{:S(2)}) collective-permute-start(bf16[64,4736]{1,0:T(8,128)(2,1)S(1)} %get-tuple-element.1022), channel_id=1, source_target_pairs={{0,4},{1,5},{2,6},{3,7},{4,8},{5,9},{6,10},{7,11},{8,12},{9,13},{1... | collective-permute-start | bytes 1818632 | tf_op jit(solution)/shard_map/while/body/eval_jaxpr/ppermute | solution.py:498
  113.8 10.6 %collective-permute-start.3 = (bf16[64,640]{1,0:T(8,128)(2,1)}, bf16[64,640]{1,0:T(8,128)(2,1)S(1)}, u32[]{:S(2)}, u32[]{:S(2)}) collective-permute-start(bf16[64,640]{1,0:T(8,128)(2,1)} %get-tuple-element.1061), channel_id=1, source_target_pairs={{0,7},{1,4},{2,5},{3,6},{4,11},{5,8},{6,9},{7,10},{8,15},{9,12},{1... | collective-permute-start | bytes 245768 | tf_op jit(solution)/shard_map/while/body/eval_jaxpr/ppermute | solution.py:498
  121.8 15.7 %collective-permute-start.5 = (bf16[64,640]{1,0:T(8,128)(2,1)S(1)}, bf16[64,640]{1,0:T(8,128)(2,1)S(1)}, u32[]{:S(2)}, u32[]{:S(2)}) collective-permute-start(bf16[64,640]{1,0:T(8,128)(2,1)S(1)} %get-tuple-element.1023), channel_id=1, source_target_pairs={{0,5},{1,6},{2,7},{3,4},{4,9},{5,10},{6,11},{7,8},{8,13},{9,14},{1... | collective-permute-start | bytes 245768 | tf_op jit(solution)/shard_map/while/body/eval_jaxpr/ppermute | solution.py:498
  123.7 13.8 %collective-permute-start.6 = (bf16[64,640]{1,0:T(8,128)(2,1)S(1)}, bf16[64,640]{1,0:T(8,128)(2,1)S(1)}, u32[]{:S(2)}, u32[]{:S(2)}) collective-permute-start(bf16[64,640]{1,0:T(8,128)(2,1)S(1)} %get-tuple-element.1023), channel_id=1, source_target_pairs={{0,6},{1,7},{2,4},{3,5},{4,10},{5,11},{6,8},{7,9},{8,14},{9,15},{1... | collective-permute-start | bytes 245768 | tf_op jit(solution)/shard_map/while/body/eval_jaxpr/ppermute | solution.py:498
  124.4 13.1 %collective-permute-start.7 = (bf16[64,640]{1,0:T(8,128)(2,1)S(1)}, bf16[64,640]{1,0:T(8,128)(2,1)}, u32[]{:S(2)}, u32[]{:S(2)}) collective-permute-start(bf16[64,640]{1,0:T(8,128)(2,1)S(1)} %get-tuple-element.1023), channel_id=1, source_target_pairs={{0,7},{1,4},{2,5},{3,6},{4,11},{5,8},{6,9},{7,10},{8,15},{9,12},{1... | collective-permute-start | bytes 245768 | tf_op jit(solution)/shard_map/while/body/eval_jaxpr/ppermute | solution.py:498
  137.5 28.0 %collective-permute-start = (bf16[64,4736]{1,0:T(8,128)(2,1)}, bf16[64,4736]{1,0:T(8,128)(2,1)S(1)}, u32[]{:S(2)}, u32[]{:S(2)}) collective-permute-start(bf16[64,4736]{1,0:T(8,128)(2,1)} %get-tuple-element.1060), channel_id=1, source_target_pairs={{0,4},{1,5},{2,6},{3,7},{4,8},{5,9},{6,10},{7,11},{8,12},{9,13},{1... | collective-permute-start | bytes 1818632 | tf_op jit(solution)/shard_map/while/body/eval_jaxpr/ppermute | solution.py:498
  151.4 27.1 %collective-permute-start.4 = (bf16[64,4736]{1,0:T(8,128)(2,1)S(1)}, bf16[64,4736]{1,0:T(8,128)(2,1)S(1)}, u32[]{:S(2)}, u32[]{:S(2)}) collective-permute-start(bf16[64,4736]{1,0:T(8,128)(2,1)S(1)} %get-tuple-element.1022), channel_id=1, source_target_pairs={{0,4},{1,5},{2,6},{3,7},{4,8},{5,9},{6,10},{7,11},{8,12},{9,13},{1... | collective-permute-start | bytes 1818632 | tf_op jit(solution)/shard_map/while/body/eval_jaxpr/ppermute | solution.py:498
  151.6 11.3 %collective-permute-start.2 = (bf16[64,640]{1,0:T(8,128)(2,1)}, bf16[64,640]{1,0:T(8,128)(2,1)S(1)}, u32[]{:S(2)}, u32[]{:S(2)}) collective-permute-start(bf16[64,640]{1,0:T(8,128)(2,1)} %get-tuple-element.1061), channel_id=1, source_target_pairs={{0,6},{1,7},{2,4},{3,5},{4,10},{5,11},{6,8},{7,9},{8,14},{9,15},{1... | collective-permute-start | bytes 245768 | tf_op jit(solution)/shard_map/while/body/eval_jaxpr/ppermute | solution.py:498
  159.5 18.9 %collective-permute-start.5 = (bf16[64,640]{1,0:T(8,128)(2,1)S(1)}, bf16[64,640]{1,0:T(8,128)(2,1)S(1)}, u32[]{:S(2)}, u32[]{:S(2)}) collective-permute-start(bf16[64,640]{1,0:T(8,128)(2,1)S(1)} %get-tuple-element.1023), channel_id=1, source_target_pairs={{0,5},{1,6},{2,7},{3,4},{4,9},{5,10},{6,11},{7,8},{8,13},{9,14},{1... | collective-permute-start | bytes 245768 | tf_op jit(solution)/shard_map/while/body/eval_jaxpr/ppermute | solution.py:498
  162.8 15.7 %collective-permute-start.6 = (bf16[64,640]{1,0:T(8,128)(2,1)S(1)}, bf16[64,640]{1,0:T(8,128)(2,1)S(1)}, u32[]{:S(2)}, u32[]{:S(2)}) collective-permute-start(bf16[64,640]{1,0:T(8,128)(2,1)S(1)} %get-tuple-element.1023), channel_id=1, source_target_pairs={{0,6},{1,7},{2,4},{3,5},{4,10},{5,11},{6,8},{7,9},{8,14},{9,15},{1... | collective-permute-start | bytes 245768 | tf_op jit(solution)/shard_map/while/body/eval_jaxpr/ppermute | solution.py:498
  162.8 15.7 %collective-permute-start.7 = (bf16[64,640]{1,0:T(8,128)(2,1)S(1)}, bf16[64,640]{1,0:T(8,128)(2,1)}, u32[]{:S(2)}, u32[]{:S(2)}) collective-permute-start(bf16[64,640]{1,0:T(8,128)(2,1)S(1)} %get-tuple-element.1023), channel_id=1, source_target_pairs={{0,7},{1,4},{2,5},{3,6},{4,11},{5,8},{6,9},{7,10},{8,15},{9,12},{1... | collective-permute-start | bytes 245768 | tf_op jit(solution)/shard_map/while/body/eval_jaxpr/ppermute | solution.py:498
  178.5 24.0 %collective-permute-start = (bf16[64,4736]{1,0:T(8,128)(2,1)}, bf16[64,4736]{1,0:T(8,128)(2,1)S(1)}, u32[]{:S(2)}, u32[]{:S(2)}) collective-permute-start(bf16[64,4736]{1,0:T(8,128)(2,1)} %get-tuple-element.1060), channel_id=1, source_target_pairs={{0,4},{1,5},{2,6},{3,7},{4,8},{5,9},{6,10},{7,11},{8,12},{9,13},{1... | collective-permute-start | bytes 1818632 | tf_op jit(solution)/shard_map/while/body/eval_jaxpr/ppermute | solution.py:498
  191.9 24.0 %collective-permute-start.4 = (bf16[64,4736]{1,0:T(8,128)(2,1)S(1)}, bf16[64,4736]{1,0:T(8,128)(2,1)S(1)}, u32[]{:S(2)}, u32[]{:S(2)}) collective-permute-start(bf16[64,4736]{1,0:T(8,128)(2,1)S(1)} %get-tuple-element.1022), channel_id=1, source_target_pairs={{0,4},{1,5},{2,6},{3,7},{4,8},{5,9},{6,10},{7,11},{8,12},{9,13},{1... | collective-permute-start | bytes 1818632 | tf_op jit(solution)/shard_map/while/body/eval_jaxpr/ppermute | solution.py:498
  192.1 10.3 %collective-permute-start.3 = (bf16[64,640]{1,0:T(8,128)(2,1)}, bf16[64,640]{1,0:T(8,128)(2,1)S(1)}, u32[]{:S(2)}, u32[]{:S(2)}) collective-permute-start(bf16[64,640]{1,0:T(8,128)(2,1)} %get-tuple-element.1061), channel_id=1, source_target_pairs={{0,7},{1,4},{2,5},{3,6},{4,11},{5,8},{6,9},{7,10},{8,15},{9,12},{1... | collective-permute-start | bytes 245768 | tf_op jit(solution)/shard_map/while/body/eval_jaxpr/ppermute | solution.py:498
  200.0 15.8 %collective-permute-start.5 = (bf16[64,640]{1,0:T(8,128)(2,1)S(1)}, bf16[64,640]{1,0:T(8,128)(2,1)S(1)}, u32[]{:S(2)}, u32[]{:S(2)}) collective-permute-start(bf16[64,640]{1,0:T(8,128)(2,1)S(1)} %get-tuple-element.1023), channel_id=1, source_target_pairs={{0,5},{1,6},{2,7},{3,4},{4,9},{5,10},{6,11},{7,8},{8,13},{9,14},{1... | collective-permute-start | bytes 245768 | tf_op jit(solution)/shard_map/while/body/eval_jaxpr/ppermute | solution.py:498
  201.9 14.0 %collective-permute-start.6 = (bf16[64,640]{1,0:T(8,128)(2,1)S(1)}, bf16[64,640]{1,0:T(8,128)(2,1)S(1)}, u32[]{:S(2)}, u32[]{:S(2)}) collective-permute-start(bf16[64,640]{1,0:T(8,128)(2,1)S(1)} %get-tuple-element.1023), channel_id=1, source_target_pairs={{0,6},{1,7},{2,4},{3,5},{4,10},{5,11},{6,8},{7,9},{8,14},{9,15},{1... | collective-permute-start | bytes 245768 | tf_op jit(solution)/shard_map/while/body/eval_jaxpr/ppermute | solution.py:498
  202.4 13.5 %collective-permute-start.7 = (bf16[64,640]{1,0:T(8,128)(2,1)S(1)}, bf16[64,640]{1,0:T(8,128)(2,1)}, u32[]{:S(2)}, u32[]{:S(2)}) collective-permute-start(bf16[64,640]{1,0:T(8,128)(2,1)S(1)} %get-tuple-element.1023), channel_id=1, source_target_pairs={{0,7},{1,4},{2,5},{3,6},{4,11},{5,8},{6,9},{7,10},{8,15},{9,12},{1... | collective-permute-start | bytes 245768 | tf_op jit(solution)/shard_map/while/body/eval_jaxpr/ppermute | solution.py:498
  215.9 27.4 %collective-permute-start = (bf16[64,4736]{1,0:T(8,128)(2,1)}, bf16[64,4736]{1,0:T(8,128)(2,1)S(1)}, u32[]{:S(2)}, u32[]{:S(2)}) collective-permute-start(bf16[64,4736]{1,0:T(8,128)(2,1)} %get-tuple-element.1060), channel_id=1, source_target_pairs={{0,4},{1,5},{2,6},{3,7},{4,8},{5,9},{6,10},{7,11},{8,12},{9,13},{1... | collective-permute-start | bytes 1818632 | tf_op jit(solution)/shard_map/while/body/eval_jaxpr/ppermute | solution.py:498
  230.7 20.3 %collective-permute-start.4 = (bf16[64,4736]{1,0:T(8,128)(2,1)S(1)}, bf16[64,4736]{1,0:T(8,128)(2,1)S(1)}, u32[]{:S(2)}, u32[]{:S(2)}) collective-permute-start(bf16[64,4736]{1,0:T(8,128)(2,1)S(1)} %get-tuple-element.1022), channel_id=1, source_target_pairs={{0,4},{1,5},{2,6},{3,7},{4,8},{5,9},{6,10},{7,11},{8,12},{9,13},{1... | collective-permute-start | bytes 1818632 | tf_op jit(solution)/shard_map/while/body/eval_jaxpr/ppermute | solution.py:498
  230.9 10.6 %collective-permute-start.3 = (bf16[64,640]{1,0:T(8,128)(2,1)}, bf16[64,640]{1,0:T(8,128)(2,1)S(1)}, u32[]{:S(2)}, u32[]{:S(2)}) collective-permute-start(bf16[64,640]{1,0:T(8,128)(2,1)} %get-tuple-element.1061), channel_id=1, source_target_pairs={{0,7},{1,4},{2,5},{3,6},{4,11},{5,8},{6,9},{7,10},{8,15},{9,12},{1... | collective-permute-start | bytes 245768 | tf_op jit(solution)/shard_map/while/body/eval_jaxpr/ppermute | solution.py:498
  251.0 36.1 %collective-permute-start = (bf16[64,4736]{1,0:T(8,128)(2,1)}, bf16[64,4736]{1,0:T(8,128)(2,1)S(1)}, u32[]{:S(2)}, u32[]{:S(2)}) collective-permute-start(bf16[64,4736]{1,0:T(8,128)(2,1)} %get-tuple-element.1060), channel_id=1, source_target_pairs={{0,4},{1,5},{2,6},{3,7},{4,8},{5,9},{6,10},{7,11},{8,12},{9,13},{1... | collective-permute-start | bytes 1818632 | tf_op jit(solution)/shard_map/while/body/eval_jaxpr/ppermute | solution.py:498
  259.2 31.4 %collective-permute-start.4 = (bf16[64,4736]{1,0:T(8,128)(2,1)S(1)}, bf16[64,4736]{1,0:T(8,128)(2,1)S(1)}, u32[]{:S(2)}, u32[]{:S(2)}) collective-permute-start(bf16[64,4736]{1,0:T(8,128)(2,1)S(1)} %get-tuple-element.1022), channel_id=1, source_target_pairs={{0,4},{1,5},{2,6},{3,7},{4,8},{5,9},{6,10},{7,11},{8,12},{9,13},{1... | collective-permute-start | bytes 1818632 | tf_op jit(solution)/shard_map/while/body/eval_jaxpr/ppermute | solution.py:498
  290.6 36.5 %collective-permute-start = (bf16[64,4736]{1,0:T(8,128)(2,1)}, bf16[64,4736]{1,0:T(8,128)(2,1)S(1)}, u32[]{:S(2)}, u32[]{:S(2)}) collective-permute-start(bf16[64,4736]{1,0:T(8,128)(2,1)} %get-tuple-element.1060), channel_id=1, source_target_pairs={{0,4},{1,5},{2,6},{3,7},{4,8},{5,9},{6,10},{7,11},{8,12},{9,13},{1... | collective-permute-start | bytes 1818632 | tf_op jit(solution)/shard_map/while/body/eval_jaxpr/ppermute | solution.py:498
  292.2 38.9 %collective-permute-start.4 = (bf16[64,4736]{1,0:T(8,128)(2,1)S(1)}, bf16[64,4736]{1,0:T(8,128)(2,1)S(1)}, u32[]{:S(2)}, u32[]{:S(2)}) collective-permute-start(bf16[64,4736]{1,0:T(8,128)(2,1)S(1)} %get-tuple-element.1022), channel_id=1, source_target_pairs={{0,4},{1,5},{2,6},{3,7},{4,8},{5,9},{6,10},{7,11},{8,12},{9,13},{1... | collective-permute-start | bytes 1818632 | tf_op jit(solution)/shard_map/while/body/eval_jaxpr/ppermute | solution.py:498
  302.5 16.5 %collective-permute-start.1 = (bf16[64,640]{1,0:T(8,128)(2,1)}, bf16[64,640]{1,0:T(8,128)(2,1)S(1)}, u32[]{:S(2)}, u32[]{:S(2)}) collective-permute-start(bf16[64,640]{1,0:T(8,128)(2,1)} %get-tuple-element.1061), channel_id=1, source_target_pairs={{0,5},{1,6},{2,7},{3,4},{4,9},{5,10},{6,11},{7,8},{8,13},{9,14},{1... | collective-permute-start | bytes 245768 | tf_op jit(solution)/shard_map/while/body/eval_jaxpr/ppermute | solution.py:498
  319.0 10.2 %collective-permute-start.5 = (bf16[64,640]{1,0:T(8,128)(2,1)S(1)}, bf16[64,640]{1,0:T(8,128)(2,1)S(1)}, u32[]{:S(2)}, u32[]{:S(2)}) collective-permute-start(bf16[64,640]{1,0:T(8,128)(2,1)S(1)} %get-tuple-element.1023), channel_id=1, source_target_pairs={{0,5},{1,6},{2,7},{3,4},{4,9},{5,10},{6,11},{7,8},{8,13},{9,14},{1... | collective-permute-start | bytes 245768 | tf_op jit(solution)/shard_map/while/body/eval_jaxpr/ppermute | solution.py:498
  331.1 36.5 %collective-permute-start = (bf16[64,4736]{1,0:T(8,128)(2,1)}, bf16[64,4736]{1,0:T(8,128)(2,1)S(1)}, u32[]{:S(2)}, u32[]{:S(2)}) collective-permute-start(bf16[64,4736]{1,0:T(8,128)(2,1)} %get-tuple-element.1060), channel_id=1, source_target_pairs={{0,4},{1,5},{2,6},{3,7},{4,8},{5,9},{6,10},{7,11},{8,12},{9,13},{1... | collective-permute-start | bytes 1818632 | tf_op jit(solution)/shard_map/while/body/eval_jaxpr/ppermute | solution.py:498
  332.7 37.0 %collective-permute-start.4 = (bf16[64,4736]{1,0:T(8,128)(2,1)S(1)}, bf16[64,4736]{1,0:T(8,128)(2,1)S(1)}, u32[]{:S(2)}, u32[]{:S(2)}) collective-permute-start(bf16[64,4736]{1,0:T(8,128)(2,1)S(1)} %get-tuple-element.1022), channel_id=1, source_target_pairs={{0,4},{1,5},{2,6},{3,7},{4,8},{5,9},{6,10},{7,11},{8,12},{9,13},{1... | collective-permute-start | bytes 1818632 | tf_op jit(solution)/shard_map/while/body/eval_jaxpr/ppermute | solution.py:498
  333.3 23.0 %collective-permute-start.1 = (bf16[64,640]{1,0:T(8,128)(2,1)}, bf16[64,640]{1,0:T(8,128)(2,1)S(1)}, u32[]{:S(2)}, u32[]{:S(2)}) collective-permute-start(bf16[64,640]{1,0:T(8,128)(2,1)} %get-tuple-element.1061), channel_id=1, source_target_pairs={{0,5},{1,6},{2,7},{3,4},{4,9},{5,10},{6,11},{7,8},{8,13},{9,14},{1... | collective-permute-start | bytes 245768 | tf_op jit(solution)/shard_map/while/body/eval_jaxpr/ppermute | solution.py:498
  341.6 17.2 %collective-permute-start.2 = (bf16[64,640]{1,0:T(8,128)(2,1)}, bf16[64,640]{1,0:T(8,128)(2,1)S(1)}, u32[]{:S(2)}, u32[]{:S(2)}) collective-permute-start(bf16[64,640]{1,0:T(8,128)(2,1)} %get-tuple-element.1061), channel_id=1, source_target_pairs={{0,6},{1,7},{2,4},{3,5},{4,10},{5,11},{6,8},{7,9},{8,14},{9,15},{1... | collective-permute-start | bytes 245768 | tf_op jit(solution)/shard_map/while/body/eval_jaxpr/ppermute | solution.py:498
  356.3 13.4 %collective-permute-start.5 = (bf16[64,640]{1,0:T(8,128)(2,1)S(1)}, bf16[64,640]{1,0:T(8,128)(2,1)S(1)}, u32[]{:S(2)}, u32[]{:S(2)}) collective-permute-start(bf16[64,640]{1,0:T(8,128)(2,1)S(1)} %get-tuple-element.1023), channel_id=1, source_target_pairs={{0,5},{1,6},{2,7},{3,4},{4,9},{5,10},{6,11},{7,8},{8,13},{9,14},{1... | collective-permute-start | bytes 245768 | tf_op jit(solution)/shard_map/while/body/eval_jaxpr/ppermute | solution.py:498
  358.8 10.9 %collective-permute-start.6 = (bf16[64,640]{1,0:T(8,128)(2,1)S(1)}, bf16[64,640]{1,0:T(8,128)(2,1)S(1)}, u32[]{:S(2)}, u32[]{:S(2)}) collective-permute-start(bf16[64,640]{1,0:T(8,128)(2,1)S(1)} %get-tuple-element.1023), channel_id=1, source_target_pairs={{0,6},{1,7},{2,4},{3,5},{4,10},{5,11},{6,8},{7,9},{8,14},{9,15},{1... | collective-permute-start | bytes 245768 | tf_op jit(solution)/shard_map/while/body/eval_jaxpr/ppermute | solution.py:498
  369.7 37.6 %collective-permute-start = (bf16[64,4736]{1,0:T(8,128)(2,1)}, bf16[64,4736]{1,0:T(8,128)(2,1)S(1)}, u32[]{:S(2)}, u32[]{:S(2)}) collective-permute-start(bf16[64,4736]{1,0:T(8,128)(2,1)} %get-tuple-element.1060), channel_id=1, source_target_pairs={{0,4},{1,5},{2,6},{3,7},{4,8},{5,9},{6,10},{7,11},{8,12},{9,13},{1... | collective-permute-start | bytes 1818632 | tf_op jit(solution)/shard_map/while/body/eval_jaxpr/ppermute | solution.py:498
  371.3 38.3 %collective-permute-start.4 = (bf16[64,4736]{1,0:T(8,128)(2,1)S(1)}, bf16[64,4736]{1,0:T(8,128)(2,1)S(1)}, u32[]{:S(2)}, u32[]{:S(2)}) collective-permute-start(bf16[64,4736]{1,0:T(8,128)(2,1)S(1)} %get-tuple-element.1022), channel_id=1, source_target_pairs={{0,4},{1,5},{2,6},{3,7},{4,8},{5,9},{6,10},{7,11},{8,12},{9,13},{1... | collective-permute-start | bytes 1818632 | tf_op jit(solution)/shard_map/while/body/eval_jaxpr/ppermute | solution.py:498
  373.6 24.7 %collective-permute-start.1 = (bf16[64,640]{1,0:T(8,128)(2,1)}, bf16[64,640]{1,0:T(8,128)(2,1)S(1)}, u32[]{:S(2)}, u32[]{:S(2)}) collective-permute-start(bf16[64,640]{1,0:T(8,128)(2,1)} %get-tuple-element.1061), channel_id=1, source_target_pairs={{0,5},{1,6},{2,7},{3,4},{4,9},{5,10},{6,11},{7,8},{8,13},{9,14},{1... | collective-permute-start | bytes 245768 | tf_op jit(solution)/shard_map/while/body/eval_jaxpr/ppermute | solution.py:498
  376.1 23.0 %collective-permute-start.2 = (bf16[64,640]{1,0:T(8,128)(2,1)}, bf16[64,640]{1,0:T(8,128)(2,1)S(1)}, u32[]{:S(2)}, u32[]{:S(2)}) collective-permute-start(bf16[64,640]{1,0:T(8,128)(2,1)} %get-tuple-element.1061), channel_id=1, source_target_pairs={{0,6},{1,7},{2,4},{3,5},{4,10},{5,11},{6,8},{7,9},{8,14},{9,15},{1... | collective-permute-start | bytes 245768 | tf_op jit(solution)/shard_map/while/body/eval_jaxpr/ppermute | solution.py:498
  384.4 17.6 %collective-permute-start.3 = (bf16[64,640]{1,0:T(8,128)(2,1)}, bf16[64,640]{1,0:T(8,128)(2,1)S(1)}, u32[]{:S(2)}, u32[]{:S(2)}) collective-permute-start(bf16[64,640]{1,0:T(8,128)(2,1)} %get-tuple-element.1061), channel_id=1, source_target_pairs={{0,7},{1,4},{2,5},{3,6},{4,11},{5,8},{6,9},{7,10},{8,15},{9,12},{1... | collective-permute-start | bytes 245768 | tf_op jit(solution)/shard_map/while/body/eval_jaxpr/ppermute | solution.py:498
  398.3 11.1 %collective-permute-start.5 = (bf16[64,640]{1,0:T(8,128)(2,1)S(1)}, bf16[64,640]{1,0:T(8,128)(2,1)S(1)}, u32[]{:S(2)}, u32[]{:S(2)}) collective-permute-start(bf16[64,640]{1,0:T(8,128)(2,1)S(1)} %get-tuple-element.1023), channel_id=1, source_target_pairs={{0,5},{1,6},{2,7},{3,4},{4,9},{5,10},{6,11},{7,8},{8,13},{9,14},{1... | collective-permute-start | bytes 245768 | tf_op jit(solution)/shard_map/while/body/eval_jaxpr/ppermute | solution.py:498
  399.1 10.3 %collective-permute-start.6 = (bf16[64,640]{1,0:T(8,128)(2,1)S(1)}, bf16[64,640]{1,0:T(8,128)(2,1)S(1)}, u32[]{:S(2)}, u32[]{:S(2)}) collective-permute-start(bf16[64,640]{1,0:T(8,128)(2,1)S(1)} %get-tuple-element.1023), channel_id=1, source_target_pairs={{0,6},{1,7},{2,4},{3,5},{4,10},{5,11},{6,8},{7,9},{8,14},{9,15},{1... | collective-permute-start | bytes 245768 | tf_op jit(solution)/shard_map/while/body/eval_jaxpr/ppermute | solution.py:498
  409.6 36.0 %collective-permute-start = (bf16[64,4736]{1,0:T(8,128)(2,1)}, bf16[64,4736]{1,0:T(8,128)(2,1)S(1)}, u32[]{:S(2)}, u32[]{:S(2)}) collective-permute-start(bf16[64,4736]{1,0:T(8,128)(2,1)} %get-tuple-element.1060), channel_id=1, source_target_pairs={{0,4},{1,5},{2,6},{3,7},{4,8},{5,9},{6,10},{7,11},{8,12},{9,13},{1... | collective-permute-start | bytes 1818632 | tf_op jit(solution)/shard_map/while/body/eval_jaxpr/ppermute | solution.py:498
  411.6 36.1 %collective-permute-start.4 = (bf16[64,4736]{1,0:T(8,128)(2,1)S(1)}, bf16[64,4736]{1,0:T(8,128)(2,1)S(1)}, u32[]{:S(2)}, u32[]{:S(2)}) collective-permute-start(bf16[64,4736]{1,0:T(8,128)(2,1)S(1)} %get-tuple-element.1022), channel_id=1, source_target_pairs={{0,4},{1,5},{2,6},{3,7},{4,8},{5,9},{6,10},{7,11},{8,12},{9,13},{1... | collective-permute-start | bytes 1818632 | tf_op jit(solution)/shard_map/while/body/eval_jaxpr/ppermute | solution.py:498
  413.5 18.8 %collective-permute-start.1 = (bf16[64,640]{1,0:T(8,128)(2,1)}, bf16[64,640]{1,0:T(8,128)(2,1)S(1)}, u32[]{:S(2)}, u32[]{:S(2)}) collective-permute-start(bf16[64,640]{1,0:T(8,128)(2,1)} %get-tuple-element.1061), channel_id=1, source_target_pairs={{0,5},{1,6},{2,7},{3,4},{4,9},{5,10},{6,11},{7,8},{8,13},{9,14},{1... | collective-permute-start | bytes 245768 | tf_op jit(solution)/shard_map/while/body/eval_jaxpr/ppermute | solution.py:498
  415.9 21.2 %collective-permute-start.2 = (bf16[64,640]{1,0:T(8,128)(2,1)}, bf16[64,640]{1,0:T(8,128)(2,1)S(1)}, u32[]{:S(2)}, u32[]{:S(2)}) collective-permute-start(bf16[64,640]{1,0:T(8,128)(2,1)} %get-tuple-element.1061), channel_id=1, source_target_pairs={{0,6},{1,7},{2,4},{3,5},{4,10},{5,11},{6,8},{7,9},{8,14},{9,15},{1... | collective-permute-start | bytes 245768 | tf_op jit(solution)/shard_map/while/body/eval_jaxpr/ppermute | solution.py:498
  419.9 18.9 %collective-permute-start.3 = (bf16[64,640]{1,0:T(8,128)(2,1)}, bf16[64,640]{1,0:T(8,128)(2,1)S(1)}, u32[]{:S(2)}, u32[]{:S(2)}) collective-permute-start(bf16[64,640]{1,0:T(8,128)(2,1)} %get-tuple-element.1061), channel_id=1, source_target_pairs={{0,7},{1,4},{2,5},{3,6},{4,11},{5,8},{6,9},{7,10},{8,15},{9,12},{1... | collective-permute-start | bytes 245768 | tf_op jit(solution)/shard_map/while/body/eval_jaxpr/ppermute | solution.py:498
  432.3 15.4 %collective-permute-start.5 = (bf16[64,640]{1,0:T(8,128)(2,1)S(1)}, bf16[64,640]{1,0:T(8,128)(2,1)S(1)}, u32[]{:S(2)}, u32[]{:S(2)}) collective-permute-start(bf16[64,640]{1,0:T(8,128)(2,1)S(1)} %get-tuple-element.1023), channel_id=1, source_target_pairs={{0,5},{1,6},{2,7},{3,4},{4,9},{5,10},{6,11},{7,8},{8,13},{9,14},{1... | collective-permute-start | bytes 245768 | tf_op jit(solution)/shard_map/while/body/eval_jaxpr/ppermute | solution.py:498
  437.1 10.6 %collective-permute-start.6 = (bf16[64,640]{1,0:T(8,128)(2,1)S(1)}, bf16[64,640]{1,0:T(8,128)(2,1)S(1)}, u32[]{:S(2)}, u32[]{:S(2)}) collective-permute-start(bf16[64,640]{1,0:T(8,128)(2,1)S(1)} %get-tuple-element.1023), channel_id=1, source_target_pairs={{0,6},{1,7},{2,4},{3,5},{4,10},{5,11},{6,8},{7,9},{8,14},{9,15},{1... | collective-permute-start | bytes 245768 | tf_op jit(solution)/shard_map/while/body/eval_jaxpr/ppermute | solution.py:498
  447.8 32.2 %collective-permute-start = (bf16[64,4736]{1,0:T(8,128)(2,1)}, bf16[64,4736]{1,0:T(8,128)(2,1)S(1)}, u32[]{:S(2)}, u32[]{:S(2)}) collective-permute-start(bf16[64,4736]{1,0:T(8,128)(2,1)} %get-tuple-element.1060), channel_id=1, source_target_pairs={{0,4},{1,5},{2,6},{3,7},{4,8},{5,9},{6,10},{7,11},{8,12},{9,13},{1... | collective-permute-start | bytes 1818632 | tf_op jit(solution)/shard_map/while/body/eval_jaxpr/ppermute | solution.py:498
  449.3 34.1 %collective-permute-start.4 = (bf16[64,4736]{1,0:T(8,128)(2,1)S(1)}, bf16[64,4736]{1,0:T(8,128)(2,1)S(1)}, u32[]{:S(2)}, u32[]{:S(2)}) collective-permute-start(bf16[64,4736]{1,0:T(8,128)(2,1)S(1)} %get-tuple-element.1022), channel_id=1, source_target_pairs={{0,4},{1,5},{2,6},{3,7},{4,8},{5,9},{6,10},{7,11},{8,12},{9,13},{1... | collective-permute-start | bytes 1818632 | tf_op jit(solution)/shard_map/while/body/eval_jaxpr/ppermute | solution.py:498
  450.3 20.1 %collective-permute-start.1 = (bf16[64,640]{1,0:T(8,128)(2,1)}, bf16[64,640]{1,0:T(8,128)(2,1)S(1)}, u32[]{:S(2)}, u32[]{:S(2)}) collective-permute-start(bf16[64,640]{1,0:T(8,128)(2,1)} %get-tuple-element.1061), channel_id=1, source_target_pairs={{0,5},{1,6},{2,7},{3,4},{4,9},{5,10},{6,11},{7,8},{8,13},{9,14},{1... | collective-permute-start | bytes 245768 | tf_op jit(solution)/shard_map/while/body/eval_jaxpr/ppermute | solution.py:498
  454.5 17.4 %collective-permute-start.2 = (bf16[64,640]{1,0:T(8,128)(2,1)}, bf16[64,640]{1,0:T(8,128)(2,1)S(1)}, u32[]{:S(2)}, u32[]{:S(2)}) collective-permute-start(bf16[64,640]{1,0:T(8,128)(2,1)} %get-tuple-element.1061), channel_id=1, source_target_pairs={{0,6},{1,7},{2,4},{3,5},{4,10},{5,11},{6,8},{7,9},{8,14},{9,15},{1... | collective-permute-start | bytes 245768 | tf_op jit(solution)/shard_map/while/body/eval_jaxpr/ppermute | solution.py:498
  458.2 18.9 %collective-permute-start.3 = (bf16[64,640]{1,0:T(8,128)(2,1)}, bf16[64,640]{1,0:T(8,128)(2,1)S(1)}, u32[]{:S(2)}, u32[]{:S(2)}) collective-permute-start(bf16[64,640]{1,0:T(8,128)(2,1)} %get-tuple-element.1061), channel_id=1, source_target_pairs={{0,7},{1,4},{2,5},{3,6},{4,11},{5,8},{6,9},{7,10},{8,15},{9,12},{1... | collective-permute-start | bytes 245768 | tf_op jit(solution)/shard_map/while/body/eval_jaxpr/ppermute | solution.py:498
  470.4 11.6 %collective-permute-start.5 = (bf16[64,640]{1,0:T(8,128)(2,1)S(1)}, bf16[64,640]{1,0:T(8,128)(2,1)S(1)}, u32[]{:S(2)}, u32[]{:S(2)}) collective-permute-start(bf16[64,640]{1,0:T(8,128)(2,1)S(1)} %get-tuple-element.1023), channel_id=1, source_target_pairs={{0,5},{1,6},{2,7},{3,4},{4,9},{5,10},{6,11},{7,8},{8,13},{9,14},{1... | collective-permute-start | bytes 245768 | tf_op jit(solution)/shard_map/while/body/eval_jaxpr/ppermute | solution.py:498
  (30 other events, 418.3 us)

commit v4 on v3

--- a/solution.py
+++ b/solution.py
@@ -59,7 +59,7 @@
         gain,
         next_gain,
         gate,
-        next_weight,
+        weight,
         final_in,
         mixed_in,
         leaving_in,
@@ -71,8 +71,6 @@
         gates,
         result,
         hold,
-        held,
-        weight,
         coming,
         going,
         size_rows,
@@ -84,8 +82,6 @@
         input_sem,
         gate_sem,
         state_sem,
-        held_sem,
-        weight_sem,
         final_sem,
         mixed_sem,
         coming_sem,
@@ -114,10 +110,6 @@
             input_sem.at[t],
         )
 
-    def weight_copy(k):
-        span = pl.ds(k * depth, depth)
-        return pltpu.make_async_copy(next_weight.at[:, span], weight.at[:, span], weight_sem.at[k])
-
     def final_copy(j):
         return pltpu.make_async_copy(
             hold.at[:, :, at(j)], final.at[0, pl.ds(first, rows), :, at(j)], final_sem.at[j]
@@ -133,11 +125,6 @@
         for t in range(steps):
             input_copy(t).start()
 
-    @pl.when((meta[3] == 1) & (meta[0] == 0))
-    def _():
-        for k in range(channels // depth):
-            weight_copy(k).start()
-
     @pl.when(meta[0] == 1)
     def _():
         def planned(which, row, k):
@@ -145,11 +132,6 @@
 
         gate_copy = pltpu.make_async_copy(gate.at[0, :, pl.ds(first, rows)], gates, gate_sem)
 
-        def held_copy(j):
-            return pltpu.make_async_copy(
-                dt_weight.at[0, :, at(j)], held.at[:, at(j)], held_sem.at[j]
-            )
-
         def state_copy(j):
             return pltpu.make_async_copy(
                 state.at[0, pl.ds(first, rows), :, at(j)], hold.at[:, :, at(j)], state_sem.at[j]
@@ -177,13 +159,7 @@
                 coming_copy(k).start()
 
         for j in range(parts):
-            held_copy(j).start()
             state_copy(j).start()
-
-        @pl.when(meta[3] == 1)
-        def _():
-            for k in range(channels // depth):
-                weight_copy(k).start()
 
         total = arrived[:, channels:].astype(jnp.float32)
         for other in others:
@@ -195,7 +171,7 @@
         turned = (tail * inverse).T
         for row in range(units):
             column = turned[: 2 * states, row : row + 1]
-            wide = jnp.broadcast_to(column, (2 * states, LANES)).astype(jnp.bfloat16)
+            wide = jnp.broadcast_to(column, (2 * states, LANES))
             spread_in[row] = wide[:states]
             spread_out[row] = wide[states:]
         sublane = lax.broadcasted_iota(jnp.int32, (states // 2, wide_lanes), 0)
@@ -210,14 +186,13 @@
         def prepare(j, slot):
             here = at(j)
             size = softplus(
-                jnp.dot(low, held[:, here], preferred_element_type=jnp.float32) + dt_bias[:, here]
+                jnp.dot(low, dt_weight[0, :, here], preferred_element_type=jnp.float32) + dt_bias[:, here]
             )
             normed = arrived[:, here].astype(jnp.float32) * gain[:, here] * inverse
             size_rows[slot] = size
             drive_rows[slot] = size * normed
             base_rows[slot] = skip[:, here] * normed
 
-        held_copy(0).wait()
         prepare(0, 0)
 
         def part(j, carry):
@@ -225,10 +200,6 @@
             slot = lax.rem(j, 2)
             later = jnp.minimum(j + 1, parts - 1)
             state_copy(j).wait()
-
-            @pl.when(j + 1 < parts)
-            def _():
-                held_copy(j + 1).wait()
 
             for k in range(swaps):
                 place = planned(0, 0, k) - first
@@ -243,19 +214,19 @@
                 rate = rates[:, full]
                 pending = {}
                 for r in range(rows):
-                    h = hold[r, :, full].astype(jnp.bfloat16)
+                    h = hold[r, :, full]
                     for t in range(steps):
                         row = t * rows + r
                         size_row = jnp.broadcast_to(
                             size_rows[slot, row : row + 1, lanes], (states, wide_lanes)
-                        ).astype(jnp.bfloat16)
+                        )
                         drive_row = jnp.broadcast_to(
                             drive_rows[slot, row : row + 1, lanes], (states, wide_lanes)
-                        ).astype(jnp.bfloat16)
+                        )
                         b = jnp.concatenate([spread_in[row]] * (wide_lanes // LANES), axis=1)
                         c = jnp.concatenate([spread_out[row]] * (wide_lanes // LANES), axis=1)
                         h = jnp.exp2(size_row * rate) * h + drive_row * b
-                        term = (h * c).astype(jnp.float32)
+                        term = h * c
                         term = term[: states // 2] + term[states // 2 :]
                         distance = 1
                         while (t, distance) in pending:
@@ -266,7 +237,7 @@
                             totals[start : start + states // 2, lanes] = term
                         else:
                             pending[t, distance] = term
-                    hold[r, :, full] = h.astype(jnp.float32)
+                    hold[r, :, full] = h
 
             opened = gates[:, :, here].astype(jnp.float32).reshape(units, cols)
             value = (totals[...] + base_rows[slot]) * (opened * jax.nn.sigmoid(opened))
@@ -308,7 +279,6 @@
             wide = onward[:, span].astype(jnp.float32)
             squares += jnp.sum(wide * wide, axis=1, keepdims=True)
             scaled = (wide * next_gain[:, span]).astype(jnp.bfloat16)
-            weight_copy(k).wait()
             total += lax.dot_general(
                 scaled,
                 weight[:, span],
@@ -392,17 +362,17 @@
     requests = state.shape[1]
     steps = inputs.shape[0]
     swaps = swap_plan.shape[2]
-    pairs = requests // (2 * ROWS)
+    units = requests // ROWS
     rows = steps * ROWS
     cols = min(COLS, channels)
     parts = channels // cols
     depth = min(DEPTH, channels)
-    turns = pairs + holders - 1
+    turns = units + holders - 1
     plan = jnp.concatenate([swap_plan.reshape(-1), evict_plan.reshape(-1)])
     down = [((i + 1) % holders, i) for i in range(holders)]
     weight = lax.ppermute(jnp.swapaxes(x_weight[0], 0, 1), "section", down)
     next_gain = lax.ppermute(gain, "section", down)
-    rates = (-LOG2E * jnp.exp(a_log[0])).astype(jnp.bfloat16)
+    rates = -LOG2E * jnp.exp(a_log[0])
     place = section.astype(jnp.int32)[None]
 
     block_shape = jax.ShapeDtypeStruct((rows, channels + rank + LANES), jnp.bfloat16)
@@ -412,14 +382,14 @@
     mixed_shape = jax.ShapeDtypeStruct(gate_input.shape, gate_input.dtype)
     moved_shape = jax.ShapeDtypeStruct((holders, states, channels), jnp.bfloat16)
 
-    def meta_of(turn, half):
-        pair = turn - section
-        valid = (pair >= 0) & (pair < pairs)
+    def meta_of(turn):
+        unit = turn - section
+        valid = (unit >= 0) & (unit < units)
         last = section == holders - 1
         following = turn + 1
-        ahead = jnp.where(last, (following >= 0) & (following < pairs), valid)
-        first = (jnp.clip(pair, 0, pairs - 1) * 2 + half) * ROWS
-        then = (jnp.clip(following, 0, pairs - 1) * 2 + half) * ROWS
+        ahead = jnp.where(last, following < units, valid)
+        first = jnp.clip(unit, 0, units - 1) * ROWS
+        then = jnp.clip(following, 0, units - 1) * ROWS
         return jnp.stack([valid, first, section, ahead, then]).astype(jnp.int32)
 
     def step(meta, blocks, final, mixed, leaving):
@@ -429,30 +399,26 @@
             out_shape=[block_shape, partial_shape, state_shape, mixed_shape, moved_shape],
             in_specs=[SMEM, SMEM]
             + [VMEM] * peers
-            + [HBM, HBM, ANY, ANY]
-            + [VMEM] * 5
-            + [HBM, ANY]
+            + [HBM, HBM, ANY]
+            + [VMEM] * 6
+            + [HBM, VMEM]
             + [HBM] * 3,
             out_specs=[VMEM, VMEM, HBM, HBM, HBM],
             scratch_shapes=[
                 pltpu.VMEM(stream_shape, jnp.bfloat16),
                 pltpu.VMEM(stream_shape, jnp.bfloat16),
                 pltpu.VMEM((ROWS, states, channels), jnp.float32),
-                pltpu.VMEM((rank, channels), jnp.bfloat16),
-                pltpu.VMEM(weight.shape, jnp.bfloat16),
                 pltpu.VMEM((swaps, states, channels), jnp.bfloat16),
                 pltpu.VMEM((swaps, states, channels), jnp.bfloat16),
                 pltpu.VMEM((2, rows, cols), jnp.float32),
                 pltpu.VMEM((2, rows, cols), jnp.float32),
                 pltpu.VMEM((2, rows, cols), jnp.float32),
                 pltpu.VMEM((rows, cols), jnp.float32),
-                pltpu.VMEM((rows, states, LANES), jnp.bfloat16),
-                pltpu.VMEM((rows, states, LANES), jnp.bfloat16),
+                pltpu.VMEM((rows, states, LANES), jnp.float32),
+                pltpu.VMEM((rows, states, LANES), jnp.float32),
                 pltpu.SemaphoreType.DMA((steps,)),
                 pltpu.SemaphoreType.DMA,
                 pltpu.SemaphoreType.DMA((parts,)),
-                pltpu.SemaphoreType.DMA((parts,)),
-                pltpu.SemaphoreType.DMA((channels // depth,)),
                 pltpu.SemaphoreType.DMA((parts,)),
                 pltpu.SemaphoreType.DMA((parts,)),
                 pltpu.SemaphoreType.DMA((swaps,)),
@@ -473,14 +439,14 @@
             inputs,
             state,
             landed,
-            dt_weight,
+            pltpu.with_memory_space_constraint(dt_weight, pltpu.VMEM),
             dt_bias,
             rates,
             skip,
             gain,
             next_gain,
             gate_input,
-            weight,
+            pltpu.with_memory_space_constraint(weight, pltpu.VMEM),
             final,
             mixed,
             leaving,
@@ -502,12 +468,9 @@
         return lax.all_to_all(block, "section", split_axis=0, concat_axis=0, tiled=True)
 
     def turn(index, carry):
-        out, late, kept = carry
-        early = send(*out)
-        *out, final, mixed, leaving = step(meta_of(index - 1, 1), late, *kept)
-        late = send(*out)
-        *out, final, mixed, leaving = step(meta_of(index, 0), early, final, mixed, leaving)
-        return tuple(out), tuple(late), (final, mixed, leaving)
+        blocks, kept = carry
+        block, partial, *kept = step(meta_of(index), blocks, *kept)
+        return send(block, partial), kept
 
     picked = pl.pallas_call(
         pick_kernel, out_shape=moved_shape, in_specs=[SMEM, SMEM, VMEM], out_specs=VMEM, name="pick"
@@ -516,12 +479,9 @@
     *kept, block, partial = empty(
         [state_shape, mixed_shape, moved_shape, block_shape, partial_shape]
     )
-    late = (block,) + (partial,) * (peers - 1)
-    *out, final, mixed, leaving = step(meta_of(-1, 0), late, *kept)
-    out, late, kept = lax.fori_loop(
-        0, turns, turn, (tuple(out), late, (final, mixed, leaving))
-    )
-    _, _, final, mixed, leaving = step(meta_of(turns - 1, 1), late, *kept)
+    blocks = [block] + [partial] * (peers - 1)
+    blocks, kept = lax.fori_loop(-1, turns - 1, turn, (blocks, kept))
+    _, _, final, mixed, leaving = step(meta_of(turns - 1), blocks, *kept)
     stored = pl.pallas_call(
         keep_kernel,
         out_shape=jax.ShapeDtypeStruct(pool.shape, pool.dtype),

time: 528 us -> 511 us (0.968)
  starting transfers between devices: 215 us -> 112 us
  waiting for transfers between devices: 129 us -> 192 us
  local copies, waits for them, and re-layouts: 4.41 us -> 39.4 us
  blocking collectives: 37.6 us -> 28.9 us
    ppermute x88 -> x60, starting transfers between devices: 206 us -> 102 us  [send(): blocks.append(lax.ppermute(partial if shift else block, axes, route))]
    ppermute x88 -> x60, waiting for transfers between devices: 79.6 us -> 144 us  [send(): blocks.append(lax.ppermute(partial if shift else block, axes, route))]
    while x0 -> x30, local copies, waits for them, and re-layouts: none -> 32.8 us
    all_to_all x1, blocking collectives: 37.6 us -> 28.9 us  [swap(): lax.all_to_all(block, 'section', split_axis=0, concat_axis=0, tiled=True)]
    pallas_call x24 -> x16, Pallas kernels: 132 us -> 130 us  [step(): pl.pallas_call(functools.partial(step_kernel, width, holders, peers), out...]
  transfers between devices with their start and end apart: 91 -> 63, of which waited for: 29 -> 42; matrix products, arithmetic and copies ran while one was open for 1% -> 1% of each run, Pallas kernels for 25% -> 0%
where the time goes in v4:
time: 511 us; the launch traced here: 509 us
  waiting for transfers between devices  192 us (38%)
  Pallas kernels  135 us (26%)
  starting transfers between devices  112 us (22%)
  local copies, waits for them, and re-layouts  39.4 us (8%)
  blocking collectives  28.9 us (6%)
    ppermute x60, waiting for transfers between devices, send(): blocks.append(lax.ppermute(partial if shift else block, axes, route))  144 us
    pallas_call x16, Pallas kernels, step(): pl.pallas_call(functools.partial(step_kernel, width, holders, peers), out...  130 us
    ppermute x60, starting transfers between devices, send(): blocks.append(lax.ppermute(partial if shift else block, axes, route))  102 us
    ppermute x1, waiting for transfers between devices, shards(): next_gain = lax.ppermute(gain, 'section', down)  47.2 us
    while x30, local copies, waits for them, and re-layouts  32.8 us
    all_to_all x1, blocking collectives, swap(): lax.all_to_all(block, 'section', split_axis=0, concat_axis=0, tiled=True)  28.9 us
  transfers between devices with their start and end apart: 63, of which 42 were waited for; matrix products, arithmetic and copies ran while one was open for 1% of the time, Pallas kernels for 0%

profile of v4, /device:TPU:0, one launch (start us, length us, event | category | flops | bytes accessed | tf_op | source)
XLA Modules:
  0.0 509.2 jit_solution(5434977141369557357)
XLA Ops:
  0.7 3.4 collective-permute-start.5
  8.1 3.6 all-to-all-start
  11.7 2.6 collective-permute-start.4
  17.4 47.2 %collective-permute-done.4.refs_14_ = f32[1,4096]{1,0:T(1,128)S(1)} collective-permute-done((f32[1,4096]{1,0:T(1,128)}, f32[1,4096]{1,0:T(1,128)S(1)}, u32[]{:S(2)}, u32[]{:S(2)}) %collective-permute-start.4) | collective-permute-done | bytes 16416 | tf_op jit(solution)/shard_map/ppermute | solution.py:374
  65.4 406.5 %while.28 = (s32[]{:T(128)}, bf16[64,4736]{1,0:T(8,128)(2,1)S(1)}, bf16[64,640]{1,0:T(8,128)(2,1)S(1)}, bf16[64,640]{1,0:T(8,128)(2,1)}, bf16[64,640]{1,0:T(8,12...) while((s32[]{:T(128)}, bf16[64,4736]{1,0:T(8,128)(2,1)S(1)}, ...), condition=%wide.region_1.2_spmd, body=%wide.region_0.1_spmd.sunk | while | flops 704643072 | bytes 36962916 | solution.py:483
  67.7 2.8 step.11
  70.6 2.8 collective-permute-start.1
  76.9 4.0 collective-permute-done.1
  80.9 3.0 collective-permute-done.2
  87.8 13.2 %step.11 = (bf16[64,4736]{1,0:T(8,128)(2,1)S(1)}, bf16[64,640]{1,0:T(8,128)(2,1)S(1)}, f32[1,128,16,4096]{3,2,1,0:T(8,128)}, bf16[1,4,128,4096]{3,2,1,0:T(8,128)(2,1)}, bf16[8,16,4096]{2,1,0:T(8,128)(2,1)S(1)}) custom-call(s32[5]{0:T(128)S(1)} %stack.102.refs_0_, ...), custom_call_target="tpu_custom_call", output_to_operand_aliasing={{2}: (17, {}), {3}: (18, {}), {4}: (19, {})} | custom-call | flops 704643072 | bytes 16777216 | tf_op jit(solution)/shard_map/while/body/eval_jaxpr/step/pallas_call | solution.py:397
  101.4 8.1 %collective-permute-done.1 = bf16[64,640]{1,0:T(8,128)(2,1)S(1)} collective-permute-done((bf16[64,640]{1,0:T(8,128)(2,1)S(1)}, bf16[64,640]{1,0:T(8,128)(2,1)S(1)}, u32[]{:S(2)}, u32[]{:S(2)}) %collective-permute-start.1) | collective-permute-done | bytes 81952 | tf_op jit(solution)/shard_map/while/body/eval_jaxpr/ppermute | solution.py:464
  109.5 3.8 collective-permute-done.2
  116.4 13.2 %step.11 = (bf16[64,4736]{1,0:T(8,128)(2,1)S(1)}, bf16[64,640]{1,0:T(8,128)(2,1)S(1)}, f32[1,128,16,4096]{3,2,1,0:T(8,128)}, bf16[1,4,128,4096]{3,2,1,0:T(8,128)(2,1)}, bf16[8,16,4096]{2,1,0:T(8,128)(2,1)S(1)}) custom-call(s32[5]{0:T(128)S(1)} %stack.102.refs_0_, ...), custom_call_target="tpu_custom_call", output_to_operand_aliasing={{2}: (17, {}), {3}: (18, {}), {4}: (19, {})} | custom-call | flops 704643072 | bytes 16777216 | tf_op jit(solution)/shard_map/while/body/eval_jaxpr/step/pallas_call | solution.py:397
  130.0 8.1 %collective-permute-done.1 = bf16[64,640]{1,0:T(8,128)(2,1)S(1)} collective-permute-done((bf16[64,640]{1,0:T(8,128)(2,1)S(1)}, bf16[64,640]{1,0:T(8,128)(2,1)S(1)}, u32[]{:S(2)}, u32[]{:S(2)}) %collective-permute-start.1) | collective-permute-done | bytes 81952 | tf_op jit(solution)/shard_map/while/body/eval_jaxpr/ppermute | solution.py:464
  138.1 3.8 collective-permute-done.2
  145.0 13.4 %step.11 = (bf16[64,4736]{1,0:T(8,128)(2,1)S(1)}, bf16[64,640]{1,0:T(8,128)(2,1)S(1)}, f32[1,128,16,4096]{3,2,1,0:T(8,128)}, bf16[1,4,128,4096]{3,2,1,0:T(8,128)(2,1)}, bf16[8,16,4096]{2,1,0:T(8,128)(2,1)S(1)}) custom-call(s32[5]{0:T(128)S(1)} %stack.102.refs_0_, ...), custom_call_target="tpu_custom_call", output_to_operand_aliasing={{2}: (17, {}), {3}: (18, {}), {4}: (19, {})} | custom-call | flops 704643072 | bytes 16777216 | tf_op jit(solution)/shard_map/while/body/eval_jaxpr/step/pallas_call | solution.py:397
  158.7 8.1 %collective-permute-done.1 = bf16[64,640]{1,0:T(8,128)(2,1)S(1)} collective-permute-done((bf16[64,640]{1,0:T(8,128)(2,1)S(1)}, bf16[64,640]{1,0:T(8,128)(2,1)S(1)}, u32[]{:S(2)}, u32[]{:S(2)}) %collective-permute-start.1) | collective-permute-done | bytes 81952 | tf_op jit(solution)/shard_map/while/body/eval_jaxpr/ppermute | solution.py:464
  166.9 3.8 collective-permute-done.2
  173.8 13.3 %step.11 = (bf16[64,4736]{1,0:T(8,128)(2,1)S(1)}, bf16[64,640]{1,0:T(8,128)(2,1)S(1)}, f32[1,128,16,4096]{3,2,1,0:T(8,128)}, bf16[1,4,128,4096]{3,2,1,0:T(8,128)(2,1)}, bf16[8,16,4096]{2,1,0:T(8,128)(2,1)S(1)}) custom-call(s32[5]{0:T(128)S(1)} %stack.102.refs_0_, ...), custom_call_target="tpu_custom_call", output_to_operand_aliasing={{2}: (17, {}), {3}: (18, {}), {4}: (19, {})} | custom-call | flops 704643072 | bytes 16777216 | tf_op jit(solution)/shard_map/while/body/eval_jaxpr/step/pallas_call | solution.py:397
  187.3 8.1 %collective-permute-done.1 = bf16[64,640]{1,0:T(8,128)(2,1)S(1)} collective-permute-done((bf16[64,640]{1,0:T(8,128)(2,1)S(1)}, bf16[64,640]{1,0:T(8,128)(2,1)S(1)}, u32[]{:S(2)}, u32[]{:S(2)}) %collective-permute-start.1) | collective-permute-done | bytes 81952 | tf_op jit(solution)/shard_map/while/body/eval_jaxpr/ppermute | solution.py:464
  195.5 3.8 collective-permute-done.2
  202.4 13.3 %step.11 = (bf16[64,4736]{1,0:T(8,128)(2,1)S(1)}, bf16[64,640]{1,0:T(8,128)(2,1)S(1)}, f32[1,128,16,4096]{3,2,1,0:T(8,128)}, bf16[1,4,128,4096]{3,2,1,0:T(8,128)(2,1)}, bf16[8,16,4096]{2,1,0:T(8,128)(2,1)S(1)}) custom-call(s32[5]{0:T(128)S(1)} %stack.102.refs_0_, ...), custom_call_target="tpu_custom_call", output_to_operand_aliasing={{2}: (17, {}), {3}: (18, {}), {4}: (19, {})} | custom-call | flops 704643072 | bytes 16777216 | tf_op jit(solution)/shard_map/while/body/eval_jaxpr/step/pallas_call | solution.py:397
  217.3 6.8 %collective-permute-done.1 = bf16[64,640]{1,0:T(8,128)(2,1)S(1)} collective-permute-done((bf16[64,640]{1,0:T(8,128)(2,1)S(1)}, bf16[64,640]{1,0:T(8,128)(2,1)S(1)}, u32[]{:S(2)}, u32[]{:S(2)}) %collective-permute-start.1) | collective-permute-done | bytes 81952 | tf_op jit(solution)/shard_map/while/body/eval_jaxpr/ppermute | solution.py:464
  224.1 3.8 collective-permute-done.2
  231.0 13.2 %step.11 = (bf16[64,4736]{1,0:T(8,128)(2,1)S(1)}, bf16[64,640]{1,0:T(8,128)(2,1)S(1)}, f32[1,128,16,4096]{3,2,1,0:T(8,128)}, bf16[1,4,128,4096]{3,2,1,0:T(8,128)(2,1)}, bf16[8,16,4096]{2,1,0:T(8,128)(2,1)S(1)}) custom-call(s32[5]{0:T(128)S(1)} %stack.102.refs_0_, ...), custom_call_target="tpu_custom_call", output_to_operand_aliasing={{2}: (17, {}), {3}: (18, {}), {4}: (19, {})} | custom-call | flops 704643072 | bytes 16777216 | tf_op jit(solution)/shard_map/while/body/eval_jaxpr/step/pallas_call | solution.py:397
  245.9 6.8 %collective-permute-done.1 = bf16[64,640]{1,0:T(8,128)(2,1)S(1)} collective-permute-done((bf16[64,640]{1,0:T(8,128)(2,1)S(1)}, bf16[64,640]{1,0:T(8,128)(2,1)S(1)}, u32[]{:S(2)}, u32[]{:S(2)}) %collective-permute-start.1) | collective-permute-done | bytes 81952 | tf_op jit(solution)/shard_map/while/body/eval_jaxpr/ppermute | solution.py:464
  252.7 3.8 collective-permute-done.2
  259.6 13.4 %step.11 = (bf16[64,4736]{1,0:T(8,128)(2,1)S(1)}, bf16[64,640]{1,0:T(8,128)(2,1)S(1)}, f32[1,128,16,4096]{3,2,1,0:T(8,128)}, bf16[1,4,128,4096]{3,2,1,0:T(8,128)(2,1)}, bf16[8,16,4096]{2,1,0:T(8,128)(2,1)S(1)}) custom-call(s32[5]{0:T(128)S(1)} %stack.102.refs_0_, ...), custom_call_target="tpu_custom_call", output_to_operand_aliasing={{2}: (17, {}), {3}: (18, {}), {4}: (19, {})} | custom-call | flops 704643072 | bytes 16777216 | tf_op jit(solution)/shard_map/while/body/eval_jaxpr/step/pallas_call | solution.py:397
  274.5 7.0 %collective-permute-done.1 = bf16[64,640]{1,0:T(8,128)(2,1)S(1)} collective-permute-done((bf16[64,640]{1,0:T(8,128)(2,1)S(1)}, bf16[64,640]{1,0:T(8,128)(2,1)S(1)}, u32[]{:S(2)}, u32[]{:S(2)}) %collective-permute-start.1) | collective-permute-done | bytes 81952 | tf_op jit(solution)/shard_map/while/body/eval_jaxpr/ppermute | solution.py:464
  281.5 3.8 collective-permute-done.2
  288.4 13.4 %step.11 = (bf16[64,4736]{1,0:T(8,128)(2,1)S(1)}, bf16[64,640]{1,0:T(8,128)(2,1)S(1)}, f32[1,128,16,4096]{3,2,1,0:T(8,128)}, bf16[1,4,128,4096]{3,2,1,0:T(8,128)(2,1)}, bf16[8,16,4096]{2,1,0:T(8,128)(2,1)S(1)}) custom-call(s32[5]{0:T(128)S(1)} %stack.102.refs_0_, ...), custom_call_target="tpu_custom_call", output_to_operand_aliasing={{2}: (17, {}), {3}: (18, {}), {4}: (19, {})} | custom-call | flops 704643072 | bytes 16777216 | tf_op jit(solution)/shard_map/while/body/eval_jaxpr/step/pallas_call | solution.py:397
  303.4 6.9 %collective-permute-done.1 = bf16[64,640]{1,0:T(8,128)(2,1)S(1)} collective-permute-done((bf16[64,640]{1,0:T(8,128)(2,1)S(1)}, bf16[64,640]{1,0:T(8,128)(2,1)S(1)}, u32[]{:S(2)}, u32[]{:S(2)}) %collective-permute-start.1) | collective-permute-done | bytes 81952 | tf_op jit(solution)/shard_map/while/body/eval_jaxpr/ppermute | solution.py:464
  310.3 3.8 collective-permute-done.2
  317.2 2.8 step.11
  320.0 5.9 %collective-permute-start = (bf16[64,4736]{1,0:T(8,128)(2,1)S(1)}, bf16[64,4736]{1,0:T(8,128)(2,1)S(1)}, u32[]{:S(2)}, u32[]{:S(2)}) collective-permute-start(bf16[64,4736]{1,0:T(8,128)(2,1)S(1)} %get-tuple-element.771), channel_id=1, source_target_pairs={{0,4},{1,5},{2,6},{3,7},{4,8},{5,9},{6,10},{7,11},{8,12},{9,13},{1... | collective-permute-start | bytes 1818632 | tf_op jit(solution)/shard_map/while/body/eval_jaxpr/ppermute | solution.py:464
  329.1 2.9 collective-permute-start.3
  332.0 2.6 collective-permute-done.1
  334.6 3.9 collective-permute-done.2
  341.7 2.8 step.11
  344.6 11.7 %collective-permute-start.1 = (bf16[64,640]{1,0:T(8,128)(2,1)S(1)}, bf16[64,640]{1,0:T(8,128)(2,1)S(1)}, u32[]{:S(2)}, u32[]{:S(2)}) collective-permute-start(bf16[64,640]{1,0:T(8,128)(2,1)S(1)} %get-tuple-element.772), channel_id=1, source_target_pairs={{0,5},{1,6},{2,7},{3,4},{4,9},{5,10},{6,11},{7,8},{8,13},{9,14},{1... | collective-permute-start | bytes 245768 | tf_op jit(solution)/shard_map/while/body/eval_jaxpr/ppermute | solution.py:464
  357.7 2.9 collective-permute-start.3
  360.6 4.9 collective-permute-done.2
  368.0 2.8 step.11
  371.3 2.8 collective-permute-start.1
  374.1 12.1 %collective-permute-start.2 = (bf16[64,640]{1,0:T(8,128)(2,1)S(1)}, bf16[64,640]{1,0:T(8,128)(2,1)}, u32[]{:S(2)}, u32[]{:S(2)}) collective-permute-start(bf16[64,640]{1,0:T(8,128)(2,1)S(1)} %get-tuple-element.772), channel_id=1, source_target_pairs={{0,6},{1,7},{2,4},{3,5},{4,10},{5,11},{6,8},{7,9},{8,14},{9,15},{1... | collective-permute-start | bytes 245768 | tf_op jit(solution)/shard_map/while/body/eval_jaxpr/ppermute | solution.py:464
  386.2 3.0 collective-permute-start.3
  389.2 2.8 collective-permute-done.3
  394.3 2.8 step.11
  400.7 3.2 collective-permute-start.2
  403.9 14.3 %collective-permute-start.3 = (bf16[64,640]{1,0:T(8,128)(2,1)S(1)}, bf16[64,640]{1,0:T(8,128)(2,1)}, u32[]{:S(2)}, u32[]{:S(2)}) collective-permute-start(bf16[64,640]{1,0:T(8,128)(2,1)S(1)} %get-tuple-element.772), channel_id=1, source_target_pairs={{0,7},{1,4},{2,5},{3,6},{4,11},{5,8},{6,9},{7,10},{8,15},{9,12},{1... | collective-permute-start | bytes 245768 | tf_op jit(solution)/shard_map/while/body/eval_jaxpr/ppermute | solution.py:464
  418.2 2.8 collective-permute-done.3
  423.3 2.8 step.11
  429.7 3.2 collective-permute-start.2
  432.8 3.5 collective-permute-start.3
  438.7 5.5 %collective-permute-done = bf16[64,4736]{1,0:T(8,128)(2,1)S(1)} collective-permute-done((bf16[64,4736]{1,0:T(8,128)(2,1)S(1)}, bf16[64,4736]{1,0:T(8,128)(2,1)S(1)}, u32[]{:S(2)}, u32[]{:S(2)}) %collective-permute-start) | collective-permute-done | bytes 606240 | tf_op jit(solution)/shard_map/while/body/eval_jaxpr/ppermute | solution.py:464
  446.4 2.8 step.11
  450.6 3.7 collective-permute-start.1
  454.3 3.2 collective-permute-start.2
  457.5 2.6 collective-permute-start.3
  460.1 5.5 %collective-permute-done.1 = bf16[64,640]{1,0:T(8,128)(2,1)S(1)} collective-permute-done((bf16[64,640]{1,0:T(8,128)(2,1)S(1)}, bf16[64,640]{1,0:T(8,128)(2,1)S(1)}, u32[]{:S(2)}, u32[]{:S(2)}) %collective-permute-start.1) | collective-permute-done | bytes 81952 | tf_op jit(solution)/shard_map/while/body/eval_jaxpr/ppermute | solution.py:464
  466.0 5.8 %collective-permute-done = bf16[64,4736]{1,0:T(8,128)(2,1)S(1)} collective-permute-done((bf16[64,4736]{1,0:T(8,128)(2,1)S(1)}, bf16[64,4736]{1,0:T(8,128)(2,1)S(1)}, u32[]{:S(2)}, u32[]{:S(2)}) %collective-permute-start) | collective-permute-done | bytes 606240 | tf_op jit(solution)/shard_map/while/body/eval_jaxpr/ppermute | solution.py:464
  474.0 3.6 step.10
  477.7 28.9 %all_to_all.10.returned = bf16[8,16,4096]{2,1,0:T(8,128)(2,1)} all-to-all(bf16[8,16,4096]{2,1,0:T(8,128)(2,1)S(1)} %get-tuple-element.588), channel_id=1, replica_groups=mesh['section'=8,'tensor'=4] {'section'}, dimensions={0} | all-to-all | bytes 2097152 | tf_op jit(solution)/shard_map/all_to_all | solution.py:468
  506.6 2.6 keep.1
  (145 shorter events, 80.7 us)
Async XLA Ops:
  0.6 64.7 %copy-start.4 = (f32[1,4096]{1,0:T(1,128)S(1)}, f32[1,4096]{1,0:T(1,128)}, u32[]{:S(2)}) copy-start(f32[1,4096]{1,0:T(1,128)} %refs_13_.1) | copy-start | bytes 49156
  0.7 64.7 %collective-permute-start.5 = (bf16[544,4096]{1,0:T(8,128)(2,1)}, bf16[544,4096]{1,0:T(8,128)(2,1)}, u32[]{:S(2)}, u32[]{:S(2)}) collective-permute-start(bf16[544,4096]{1,0:T(8,128)(2,1)} %bitcast.24), channel_id=1, source_target_pairs={{4,0},{8,4},{12,8},{16,12},{20,16},{24,20},{28,24},{0,28},{5,1},{9... | collective-permute-start | bytes 13369352 | tf_op jit(solution)/shard_map/ppermute | solution.py:373
  8.1 57.2 %all-to-all-start = ((bf16[8,16,4096]{2,1,0:T(8,128)(2,1)}), bf16[8,16,4096]{2,1,0:T(8,128)(2,1)S(1)}, u32[]{:S(2)}, u32[]{:S(2)}) async-start(bf16[8,16,4096]{2,1,0:T(8,128)(2,1)} %pick.1), calls=%async_computation | async-start | bytes 2097152 | tf_op jit(solution)/shard_map/all_to_all | solution.py:468
  11.7 52.9 %collective-permute-start.4 = (f32[1,4096]{1,0:T(1,128)}, f32[1,4096]{1,0:T(1,128)S(1)}, u32[]{:S(2)}, u32[]{:S(2)}) collective-permute-start(f32[1,4096]{1,0:T(1,128)} %refs_13_.1), channel_id=1, source_target_pairs={{4,0},{8,4},{12,8},{16,12},{20,16},{24,20},{28,24},{0,28},{5,1},{9... | collective-permute-start | bytes 49160 | tf_op jit(solution)/shard_map/ppermute | solution.py:374
  70.5 15.1 %collective-permute-start = (bf16[64,4736]{1,0:T(8,128)(2,1)S(1)}, bf16[64,4736]{1,0:T(8,128)(2,1)S(1)}, u32[]{:S(2)}, u32[]{:S(2)}) collective-permute-start(bf16[64,4736]{1,0:T(8,128)(2,1)S(1)} %get-tuple-element.771), channel_id=1, source_target_pairs={{0,4},{1,5},{2,6},{3,7},{4,8},{5,9},{6,10},{7,11},{8,12},{9,13},{1... | collective-permute-start | bytes 1818632 | tf_op jit(solution)/shard_map/while/body/eval_jaxpr/ppermute | solution.py:464
  70.6 10.4 %collective-permute-start.1 = (bf16[64,640]{1,0:T(8,128)(2,1)S(1)}, bf16[64,640]{1,0:T(8,128)(2,1)S(1)}, u32[]{:S(2)}, u32[]{:S(2)}) collective-permute-start(bf16[64,640]{1,0:T(8,128)(2,1)S(1)} %get-tuple-element.772), channel_id=1, source_target_pairs={{0,5},{1,6},{2,7},{3,4},{4,9},{5,10},{6,11},{7,8},{8,13},{9,14},{1... | collective-permute-start | bytes 245768 | tf_op jit(solution)/shard_map/while/body/eval_jaxpr/ppermute | solution.py:464
  73.4 10.5 %collective-permute-start.2 = (bf16[64,640]{1,0:T(8,128)(2,1)S(1)}, bf16[64,640]{1,0:T(8,128)(2,1)}, u32[]{:S(2)}, u32[]{:S(2)}) collective-permute-start(bf16[64,640]{1,0:T(8,128)(2,1)S(1)} %get-tuple-element.772), channel_id=1, source_target_pairs={{0,6},{1,7},{2,4},{3,5},{4,10},{5,11},{6,8},{7,9},{8,14},{9,15},{1... | collective-permute-start | bytes 245768 | tf_op jit(solution)/shard_map/while/body/eval_jaxpr/ppermute | solution.py:464
  75.5 8.4 %collective-permute-start.3 = (bf16[64,640]{1,0:T(8,128)(2,1)S(1)}, bf16[64,640]{1,0:T(8,128)(2,1)}, u32[]{:S(2)}, u32[]{:S(2)}) collective-permute-start(bf16[64,640]{1,0:T(8,128)(2,1)S(1)} %get-tuple-element.772), channel_id=1, source_target_pairs={{0,7},{1,4},{2,5},{3,6},{4,11},{5,8},{6,9},{7,10},{8,15},{9,12},{1... | collective-permute-start | bytes 245768 | tf_op jit(solution)/shard_map/while/body/eval_jaxpr/ppermute | solution.py:464
  101.1 13.1 %collective-permute-start = (bf16[64,4736]{1,0:T(8,128)(2,1)S(1)}, bf16[64,4736]{1,0:T(8,128)(2,1)S(1)}, u32[]{:S(2)}, u32[]{:S(2)}) collective-permute-start(bf16[64,4736]{1,0:T(8,128)(2,1)S(1)} %get-tuple-element.771), channel_id=1, source_target_pairs={{0,4},{1,5},{2,6},{3,7},{4,8},{5,9},{6,10},{7,11},{8,12},{9,13},{1... | collective-permute-start | bytes 1818632 | tf_op jit(solution)/shard_map/while/body/eval_jaxpr/ppermute | solution.py:464
  101.2 8.3 %collective-permute-start.1 = (bf16[64,640]{1,0:T(8,128)(2,1)S(1)}, bf16[64,640]{1,0:T(8,128)(2,1)S(1)}, u32[]{:S(2)}, u32[]{:S(2)}) collective-permute-start(bf16[64,640]{1,0:T(8,128)(2,1)S(1)} %get-tuple-element.772), channel_id=1, source_target_pairs={{0,5},{1,6},{2,7},{3,4},{4,9},{5,10},{6,11},{7,8},{8,13},{9,14},{1... | collective-permute-start | bytes 245768 | tf_op jit(solution)/shard_map/while/body/eval_jaxpr/ppermute | solution.py:464
  101.2 12.1 %collective-permute-start.2 = (bf16[64,640]{1,0:T(8,128)(2,1)S(1)}, bf16[64,640]{1,0:T(8,128)(2,1)}, u32[]{:S(2)}, u32[]{:S(2)}) collective-permute-start(bf16[64,640]{1,0:T(8,128)(2,1)S(1)} %get-tuple-element.772), channel_id=1, source_target_pairs={{0,6},{1,7},{2,4},{3,5},{4,10},{5,11},{6,8},{7,9},{8,14},{9,15},{1... | collective-permute-start | bytes 245768 | tf_op jit(solution)/shard_map/while/body/eval_jaxpr/ppermute | solution.py:464
  101.3 12.0 %collective-permute-start.3 = (bf16[64,640]{1,0:T(8,128)(2,1)S(1)}, bf16[64,640]{1,0:T(8,128)(2,1)}, u32[]{:S(2)}, u32[]{:S(2)}) collective-permute-start(bf16[64,640]{1,0:T(8,128)(2,1)S(1)} %get-tuple-element.772), channel_id=1, source_target_pairs={{0,7},{1,4},{2,5},{3,6},{4,11},{5,8},{6,9},{7,10},{8,15},{9,12},{1... | collective-permute-start | bytes 245768 | tf_op jit(solution)/shard_map/while/body/eval_jaxpr/ppermute | solution.py:464
  129.7 13.1 %collective-permute-start = (bf16[64,4736]{1,0:T(8,128)(2,1)S(1)}, bf16[64,4736]{1,0:T(8,128)(2,1)S(1)}, u32[]{:S(2)}, u32[]{:S(2)}) collective-permute-start(bf16[64,4736]{1,0:T(8,128)(2,1)S(1)} %get-tuple-element.771), channel_id=1, source_target_pairs={{0,4},{1,5},{2,6},{3,7},{4,8},{5,9},{6,10},{7,11},{8,12},{9,13},{1... | collective-permute-start | bytes 1818632 | tf_op jit(solution)/shard_map/while/body/eval_jaxpr/ppermute | solution.py:464
  129.8 8.3 %collective-permute-start.1 = (bf16[64,640]{1,0:T(8,128)(2,1)S(1)}, bf16[64,640]{1,0:T(8,128)(2,1)S(1)}, u32[]{:S(2)}, u32[]{:S(2)}) collective-permute-start(bf16[64,640]{1,0:T(8,128)(2,1)S(1)} %get-tuple-element.772), channel_id=1, source_target_pairs={{0,5},{1,6},{2,7},{3,4},{4,9},{5,10},{6,11},{7,8},{8,13},{9,14},{1... | collective-permute-start | bytes 245768 | tf_op jit(solution)/shard_map/while/body/eval_jaxpr/ppermute | solution.py:464
  129.8 12.1 %collective-permute-start.2 = (bf16[64,640]{1,0:T(8,128)(2,1)S(1)}, bf16[64,640]{1,0:T(8,128)(2,1)}, u32[]{:S(2)}, u32[]{:S(2)}) collective-permute-start(bf16[64,640]{1,0:T(8,128)(2,1)S(1)} %get-tuple-element.772), channel_id=1, source_target_pairs={{0,6},{1,7},{2,4},{3,5},{4,10},{5,11},{6,8},{7,9},{8,14},{9,15},{1... | collective-permute-start | bytes 245768 | tf_op jit(solution)/shard_map/while/body/eval_jaxpr/ppermute | solution.py:464
  129.9 12.0 %collective-permute-start.3 = (bf16[64,640]{1,0:T(8,128)(2,1)S(1)}, bf16[64,640]{1,0:T(8,128)(2,1)}, u32[]{:S(2)}, u32[]{:S(2)}) collective-permute-start(bf16[64,640]{1,0:T(8,128)(2,1)S(1)} %get-tuple-element.772), channel_id=1, source_target_pairs={{0,7},{1,4},{2,5},{3,6},{4,11},{5,8},{6,9},{7,10},{8,15},{9,12},{1... | collective-permute-start | bytes 245768 | tf_op jit(solution)/shard_map/while/body/eval_jaxpr/ppermute | solution.py:464
  158.5 13.1 %collective-permute-start = (bf16[64,4736]{1,0:T(8,128)(2,1)S(1)}, bf16[64,4736]{1,0:T(8,128)(2,1)S(1)}, u32[]{:S(2)}, u32[]{:S(2)}) collective-permute-start(bf16[64,4736]{1,0:T(8,128)(2,1)S(1)} %get-tuple-element.771), channel_id=1, source_target_pairs={{0,4},{1,5},{2,6},{3,7},{4,8},{5,9},{6,10},{7,11},{8,12},{9,13},{1... | collective-permute-start | bytes 1818632 | tf_op jit(solution)/shard_map/while/body/eval_jaxpr/ppermute | solution.py:464
  158.5 8.3 %collective-permute-start.1 = (bf16[64,640]{1,0:T(8,128)(2,1)S(1)}, bf16[64,640]{1,0:T(8,128)(2,1)S(1)}, u32[]{:S(2)}, u32[]{:S(2)}) collective-permute-start(bf16[64,640]{1,0:T(8,128)(2,1)S(1)} %get-tuple-element.772), channel_id=1, source_target_pairs={{0,5},{1,6},{2,7},{3,4},{4,9},{5,10},{6,11},{7,8},{8,13},{9,14},{1... | collective-permute-start | bytes 245768 | tf_op jit(solution)/shard_map/while/body/eval_jaxpr/ppermute | solution.py:464
  158.6 12.1 %collective-permute-start.2 = (bf16[64,640]{1,0:T(8,128)(2,1)S(1)}, bf16[64,640]{1,0:T(8,128)(2,1)}, u32[]{:S(2)}, u32[]{:S(2)}) collective-permute-start(bf16[64,640]{1,0:T(8,128)(2,1)S(1)} %get-tuple-element.772), channel_id=1, source_target_pairs={{0,6},{1,7},{2,4},{3,5},{4,10},{5,11},{6,8},{7,9},{8,14},{9,15},{1... | collective-permute-start | bytes 245768 | tf_op jit(solution)/shard_map/while/body/eval_jaxpr/ppermute | solution.py:464
  158.7 12.0 %collective-permute-start.3 = (bf16[64,640]{1,0:T(8,128)(2,1)S(1)}, bf16[64,640]{1,0:T(8,128)(2,1)}, u32[]{:S(2)}, u32[]{:S(2)}) collective-permute-start(bf16[64,640]{1,0:T(8,128)(2,1)S(1)} %get-tuple-element.772), channel_id=1, source_target_pairs={{0,7},{1,4},{2,5},{3,6},{4,11},{5,8},{6,9},{7,10},{8,15},{9,12},{1... | collective-permute-start | bytes 245768 | tf_op jit(solution)/shard_map/while/body/eval_jaxpr/ppermute | solution.py:464
  187.1 13.1 %collective-permute-start = (bf16[64,4736]{1,0:T(8,128)(2,1)S(1)}, bf16[64,4736]{1,0:T(8,128)(2,1)S(1)}, u32[]{:S(2)}, u32[]{:S(2)}) collective-permute-start(bf16[64,4736]{1,0:T(8,128)(2,1)S(1)} %get-tuple-element.771), channel_id=1, source_target_pairs={{0,4},{1,5},{2,6},{3,7},{4,8},{5,9},{6,10},{7,11},{8,12},{9,13},{1... | collective-permute-start | bytes 1818632 | tf_op jit(solution)/shard_map/while/body/eval_jaxpr/ppermute | solution.py:464
  187.1 8.3 %collective-permute-start.1 = (bf16[64,640]{1,0:T(8,128)(2,1)S(1)}, bf16[64,640]{1,0:T(8,128)(2,1)S(1)}, u32[]{:S(2)}, u32[]{:S(2)}) collective-permute-start(bf16[64,640]{1,0:T(8,128)(2,1)S(1)} %get-tuple-element.772), channel_id=1, source_target_pairs={{0,5},{1,6},{2,7},{3,4},{4,9},{5,10},{6,11},{7,8},{8,13},{9,14},{1... | collective-permute-start | bytes 245768 | tf_op jit(solution)/shard_map/while/body/eval_jaxpr/ppermute | solution.py:464
  187.2 12.1 %collective-permute-start.2 = (bf16[64,640]{1,0:T(8,128)(2,1)S(1)}, bf16[64,640]{1,0:T(8,128)(2,1)}, u32[]{:S(2)}, u32[]{:S(2)}) collective-permute-start(bf16[64,640]{1,0:T(8,128)(2,1)S(1)} %get-tuple-element.772), channel_id=1, source_target_pairs={{0,6},{1,7},{2,4},{3,5},{4,10},{5,11},{6,8},{7,9},{8,14},{9,15},{1... | collective-permute-start | bytes 245768 | tf_op jit(solution)/shard_map/while/body/eval_jaxpr/ppermute | solution.py:464
  187.3 12.0 %collective-permute-start.3 = (bf16[64,640]{1,0:T(8,128)(2,1)S(1)}, bf16[64,640]{1,0:T(8,128)(2,1)}, u32[]{:S(2)}, u32[]{:S(2)}) collective-permute-start(bf16[64,640]{1,0:T(8,128)(2,1)S(1)} %get-tuple-element.772), channel_id=1, source_target_pairs={{0,7},{1,4},{2,5},{3,6},{4,11},{5,8},{6,9},{7,10},{8,15},{9,12},{1... | collective-permute-start | bytes 245768 | tf_op jit(solution)/shard_map/while/body/eval_jaxpr/ppermute | solution.py:464
  215.7 13.1 %collective-permute-start = (bf16[64,4736]{1,0:T(8,128)(2,1)S(1)}, bf16[64,4736]{1,0:T(8,128)(2,1)S(1)}, u32[]{:S(2)}, u32[]{:S(2)}) collective-permute-start(bf16[64,4736]{1,0:T(8,128)(2,1)S(1)} %get-tuple-element.771), channel_id=1, source_target_pairs={{0,4},{1,5},{2,6},{3,7},{4,8},{5,9},{6,10},{7,11},{8,12},{9,13},{1... | collective-permute-start | bytes 1818632 | tf_op jit(solution)/shard_map/while/body/eval_jaxpr/ppermute | solution.py:464
  215.7 8.3 %collective-permute-start.1 = (bf16[64,640]{1,0:T(8,128)(2,1)S(1)}, bf16[64,640]{1,0:T(8,128)(2,1)S(1)}, u32[]{:S(2)}, u32[]{:S(2)}) collective-permute-start(bf16[64,640]{1,0:T(8,128)(2,1)S(1)} %get-tuple-element.772), channel_id=1, source_target_pairs={{0,5},{1,6},{2,7},{3,4},{4,9},{5,10},{6,11},{7,8},{8,13},{9,14},{1... | collective-permute-start | bytes 245768 | tf_op jit(solution)/shard_map/while/body/eval_jaxpr/ppermute | solution.py:464
  215.8 12.1 %collective-permute-start.2 = (bf16[64,640]{1,0:T(8,128)(2,1)S(1)}, bf16[64,640]{1,0:T(8,128)(2,1)}, u32[]{:S(2)}, u32[]{:S(2)}) collective-permute-start(bf16[64,640]{1,0:T(8,128)(2,1)S(1)} %get-tuple-element.772), channel_id=1, source_target_pairs={{0,6},{1,7},{2,4},{3,5},{4,10},{5,11},{6,8},{7,9},{8,14},{9,15},{1... | collective-permute-start | bytes 245768 | tf_op jit(solution)/shard_map/while/body/eval_jaxpr/ppermute | solution.py:464
  215.9 12.0 %collective-permute-start.3 = (bf16[64,640]{1,0:T(8,128)(2,1)S(1)}, bf16[64,640]{1,0:T(8,128)(2,1)}, u32[]{:S(2)}, u32[]{:S(2)}) collective-permute-start(bf16[64,640]{1,0:T(8,128)(2,1)S(1)} %get-tuple-element.772), channel_id=1, source_target_pairs={{0,7},{1,4},{2,5},{3,6},{4,11},{5,8},{6,9},{7,10},{8,15},{9,12},{1... | collective-permute-start | bytes 245768 | tf_op jit(solution)/shard_map/while/body/eval_jaxpr/ppermute | solution.py:464
  244.3 13.1 %collective-permute-start = (bf16[64,4736]{1,0:T(8,128)(2,1)S(1)}, bf16[64,4736]{1,0:T(8,128)(2,1)S(1)}, u32[]{:S(2)}, u32[]{:S(2)}) collective-permute-start(bf16[64,4736]{1,0:T(8,128)(2,1)S(1)} %get-tuple-element.771), channel_id=1, source_target_pairs={{0,4},{1,5},{2,6},{3,7},{4,8},{5,9},{6,10},{7,11},{8,12},{9,13},{1... | collective-permute-start | bytes 1818632 | tf_op jit(solution)/shard_map/while/body/eval_jaxpr/ppermute | solution.py:464
  244.3 8.3 %collective-permute-start.1 = (bf16[64,640]{1,0:T(8,128)(2,1)S(1)}, bf16[64,640]{1,0:T(8,128)(2,1)S(1)}, u32[]{:S(2)}, u32[]{:S(2)}) collective-permute-start(bf16[64,640]{1,0:T(8,128)(2,1)S(1)} %get-tuple-element.772), channel_id=1, source_target_pairs={{0,5},{1,6},{2,7},{3,4},{4,9},{5,10},{6,11},{7,8},{8,13},{9,14},{1... | collective-permute-start | bytes 245768 | tf_op jit(solution)/shard_map/while/body/eval_jaxpr/ppermute | solution.py:464
  244.4 12.1 %collective-permute-start.2 = (bf16[64,640]{1,0:T(8,128)(2,1)S(1)}, bf16[64,640]{1,0:T(8,128)(2,1)}, u32[]{:S(2)}, u32[]{:S(2)}) collective-permute-start(bf16[64,640]{1,0:T(8,128)(2,1)S(1)} %get-tuple-element.772), channel_id=1, source_target_pairs={{0,6},{1,7},{2,4},{3,5},{4,10},{5,11},{6,8},{7,9},{8,14},{9,15},{1... | collective-permute-start | bytes 245768 | tf_op jit(solution)/shard_map/while/body/eval_jaxpr/ppermute | solution.py:464
  244.5 12.0 %collective-permute-start.3 = (bf16[64,640]{1,0:T(8,128)(2,1)S(1)}, bf16[64,640]{1,0:T(8,128)(2,1)}, u32[]{:S(2)}, u32[]{:S(2)}) collective-permute-start(bf16[64,640]{1,0:T(8,128)(2,1)S(1)} %get-tuple-element.772), channel_id=1, source_target_pairs={{0,7},{1,4},{2,5},{3,6},{4,11},{5,8},{6,9},{7,10},{8,15},{9,12},{1... | collective-permute-start | bytes 245768 | tf_op jit(solution)/shard_map/while/body/eval_jaxpr/ppermute | solution.py:464
  273.1 13.1 %collective-permute-start = (bf16[64,4736]{1,0:T(8,128)(2,1)S(1)}, bf16[64,4736]{1,0:T(8,128)(2,1)S(1)}, u32[]{:S(2)}, u32[]{:S(2)}) collective-permute-start(bf16[64,4736]{1,0:T(8,128)(2,1)S(1)} %get-tuple-element.771), channel_id=1, source_target_pairs={{0,4},{1,5},{2,6},{3,7},{4,8},{5,9},{6,10},{7,11},{8,12},{9,13},{1... | collective-permute-start | bytes 1818632 | tf_op jit(solution)/shard_map/while/body/eval_jaxpr/ppermute | solution.py:464
  273.1 8.3 %collective-permute-start.1 = (bf16[64,640]{1,0:T(8,128)(2,1)S(1)}, bf16[64,640]{1,0:T(8,128)(2,1)S(1)}, u32[]{:S(2)}, u32[]{:S(2)}) collective-permute-start(bf16[64,640]{1,0:T(8,128)(2,1)S(1)} %get-tuple-element.772), channel_id=1, source_target_pairs={{0,5},{1,6},{2,7},{3,4},{4,9},{5,10},{6,11},{7,8},{8,13},{9,14},{1... | collective-permute-start | bytes 245768 | tf_op jit(solution)/shard_map/while/body/eval_jaxpr/ppermute | solution.py:464
  273.2 12.1 %collective-permute-start.2 = (bf16[64,640]{1,0:T(8,128)(2,1)S(1)}, bf16[64,640]{1,0:T(8,128)(2,1)}, u32[]{:S(2)}, u32[]{:S(2)}) collective-permute-start(bf16[64,640]{1,0:T(8,128)(2,1)S(1)} %get-tuple-element.772), channel_id=1, source_target_pairs={{0,6},{1,7},{2,4},{3,5},{4,10},{5,11},{6,8},{7,9},{8,14},{9,15},{1... | collective-permute-start | bytes 245768 | tf_op jit(solution)/shard_map/while/body/eval_jaxpr/ppermute | solution.py:464
  273.3 12.0 %collective-permute-start.3 = (bf16[64,640]{1,0:T(8,128)(2,1)S(1)}, bf16[64,640]{1,0:T(8,128)(2,1)}, u32[]{:S(2)}, u32[]{:S(2)}) collective-permute-start(bf16[64,640]{1,0:T(8,128)(2,1)S(1)} %get-tuple-element.772), channel_id=1, source_target_pairs={{0,7},{1,4},{2,5},{3,6},{4,11},{5,8},{6,9},{7,10},{8,15},{9,12},{1... | collective-permute-start | bytes 245768 | tf_op jit(solution)/shard_map/while/body/eval_jaxpr/ppermute | solution.py:464
  301.8 13.1 %collective-permute-start = (bf16[64,4736]{1,0:T(8,128)(2,1)S(1)}, bf16[64,4736]{1,0:T(8,128)(2,1)S(1)}, u32[]{:S(2)}, u32[]{:S(2)}) collective-permute-start(bf16[64,4736]{1,0:T(8,128)(2,1)S(1)} %get-tuple-element.771), channel_id=1, source_target_pairs={{0,4},{1,5},{2,6},{3,7},{4,8},{5,9},{6,10},{7,11},{8,12},{9,13},{1... | collective-permute-start | bytes 1818632 | tf_op jit(solution)/shard_map/while/body/eval_jaxpr/ppermute | solution.py:464
  301.9 8.4 %collective-permute-start.1 = (bf16[64,640]{1,0:T(8,128)(2,1)S(1)}, bf16[64,640]{1,0:T(8,128)(2,1)S(1)}, u32[]{:S(2)}, u32[]{:S(2)}) collective-permute-start(bf16[64,640]{1,0:T(8,128)(2,1)S(1)} %get-tuple-element.772), channel_id=1, source_target_pairs={{0,5},{1,6},{2,7},{3,4},{4,9},{5,10},{6,11},{7,8},{8,13},{9,14},{1... | collective-permute-start | bytes 245768 | tf_op jit(solution)/shard_map/while/body/eval_jaxpr/ppermute | solution.py:464
  302.0 12.1 %collective-permute-start.2 = (bf16[64,640]{1,0:T(8,128)(2,1)S(1)}, bf16[64,640]{1,0:T(8,128)(2,1)}, u32[]{:S(2)}, u32[]{:S(2)}) collective-permute-start(bf16[64,640]{1,0:T(8,128)(2,1)S(1)} %get-tuple-element.772), channel_id=1, source_target_pairs={{0,6},{1,7},{2,4},{3,5},{4,10},{5,11},{6,8},{7,9},{8,14},{9,15},{1... | collective-permute-start | bytes 245768 | tf_op jit(solution)/shard_map/while/body/eval_jaxpr/ppermute | solution.py:464
  302.0 12.1 %collective-permute-start.3 = (bf16[64,640]{1,0:T(8,128)(2,1)S(1)}, bf16[64,640]{1,0:T(8,128)(2,1)}, u32[]{:S(2)}, u32[]{:S(2)}) collective-permute-start(bf16[64,640]{1,0:T(8,128)(2,1)S(1)} %get-tuple-element.772), channel_id=1, source_target_pairs={{0,7},{1,4},{2,5},{3,6},{4,11},{5,8},{6,9},{7,10},{8,15},{9,12},{1... | collective-permute-start | bytes 245768 | tf_op jit(solution)/shard_map/while/body/eval_jaxpr/ppermute | solution.py:464
  320.0 19.4 %collective-permute-start = (bf16[64,4736]{1,0:T(8,128)(2,1)S(1)}, bf16[64,4736]{1,0:T(8,128)(2,1)S(1)}, u32[]{:S(2)}, u32[]{:S(2)}) collective-permute-start(bf16[64,4736]{1,0:T(8,128)(2,1)S(1)} %get-tuple-element.771), channel_id=1, source_target_pairs={{0,4},{1,5},{2,6},{3,7},{4,8},{5,9},{6,10},{7,11},{8,12},{9,13},{1... | collective-permute-start | bytes 1818632 | tf_op jit(solution)/shard_map/while/body/eval_jaxpr/ppermute | solution.py:464
  325.9 8.7 %collective-permute-start.1 = (bf16[64,640]{1,0:T(8,128)(2,1)S(1)}, bf16[64,640]{1,0:T(8,128)(2,1)S(1)}, u32[]{:S(2)}, u32[]{:S(2)}) collective-permute-start(bf16[64,640]{1,0:T(8,128)(2,1)S(1)} %get-tuple-element.772), channel_id=1, source_target_pairs={{0,5},{1,6},{2,7},{3,4},{4,9},{5,10},{6,11},{7,8},{8,13},{9,14},{1... | collective-permute-start | bytes 245768 | tf_op jit(solution)/shard_map/while/body/eval_jaxpr/ppermute | solution.py:464
  327.7 10.9 %collective-permute-start.2 = (bf16[64,640]{1,0:T(8,128)(2,1)S(1)}, bf16[64,640]{1,0:T(8,128)(2,1)}, u32[]{:S(2)}, u32[]{:S(2)}) collective-permute-start(bf16[64,640]{1,0:T(8,128)(2,1)S(1)} %get-tuple-element.772), channel_id=1, source_target_pairs={{0,6},{1,7},{2,4},{3,5},{4,10},{5,11},{6,8},{7,9},{8,14},{9,15},{1... | collective-permute-start | bytes 245768 | tf_op jit(solution)/shard_map/while/body/eval_jaxpr/ppermute | solution.py:464
  329.1 9.5 %collective-permute-start.3 = (bf16[64,640]{1,0:T(8,128)(2,1)S(1)}, bf16[64,640]{1,0:T(8,128)(2,1)}, u32[]{:S(2)}, u32[]{:S(2)}) collective-permute-start(bf16[64,640]{1,0:T(8,128)(2,1)S(1)} %get-tuple-element.772), channel_id=1, source_target_pairs={{0,7},{1,4},{2,5},{3,6},{4,11},{5,8},{6,9},{7,10},{8,15},{9,12},{1... | collective-permute-start | bytes 245768 | tf_op jit(solution)/shard_map/while/body/eval_jaxpr/ppermute | solution.py:464
  344.5 21.2 %collective-permute-start = (bf16[64,4736]{1,0:T(8,128)(2,1)S(1)}, bf16[64,4736]{1,0:T(8,128)(2,1)S(1)}, u32[]{:S(2)}, u32[]{:S(2)}) collective-permute-start(bf16[64,4736]{1,0:T(8,128)(2,1)S(1)} %get-tuple-element.771), channel_id=1, source_target_pairs={{0,4},{1,5},{2,6},{3,7},{4,8},{5,9},{6,10},{7,11},{8,12},{9,13},{1... | collective-permute-start | bytes 1818632 | tf_op jit(solution)/shard_map/while/body/eval_jaxpr/ppermute | solution.py:464
  344.6 16.1 %collective-permute-start.1 = (bf16[64,640]{1,0:T(8,128)(2,1)S(1)}, bf16[64,640]{1,0:T(8,128)(2,1)S(1)}, u32[]{:S(2)}, u32[]{:S(2)}) collective-permute-start(bf16[64,640]{1,0:T(8,128)(2,1)S(1)} %get-tuple-element.772), channel_id=1, source_target_pairs={{0,5},{1,6},{2,7},{3,4},{4,9},{5,10},{6,11},{7,8},{8,13},{9,14},{1... | collective-permute-start | bytes 245768 | tf_op jit(solution)/shard_map/while/body/eval_jaxpr/ppermute | solution.py:464
  356.3 9.2 %collective-permute-start.2 = (bf16[64,640]{1,0:T(8,128)(2,1)S(1)}, bf16[64,640]{1,0:T(8,128)(2,1)}, u32[]{:S(2)}, u32[]{:S(2)}) collective-permute-start(bf16[64,640]{1,0:T(8,128)(2,1)S(1)} %get-tuple-element.772), channel_id=1, source_target_pairs={{0,6},{1,7},{2,4},{3,5},{4,10},{5,11},{6,8},{7,9},{8,14},{9,15},{1... | collective-permute-start | bytes 245768 | tf_op jit(solution)/shard_map/while/body/eval_jaxpr/ppermute | solution.py:464
  357.7 8.0 %collective-permute-start.3 = (bf16[64,640]{1,0:T(8,128)(2,1)S(1)}, bf16[64,640]{1,0:T(8,128)(2,1)}, u32[]{:S(2)}, u32[]{:S(2)}) collective-permute-start(bf16[64,640]{1,0:T(8,128)(2,1)S(1)} %get-tuple-element.772), channel_id=1, source_target_pairs={{0,7},{1,4},{2,5},{3,6},{4,11},{5,8},{6,9},{7,10},{8,15},{9,12},{1... | collective-permute-start | bytes 245768 | tf_op jit(solution)/shard_map/while/body/eval_jaxpr/ppermute | solution.py:464
  370.8 21.2 %collective-permute-start = (bf16[64,4736]{1,0:T(8,128)(2,1)S(1)}, bf16[64,4736]{1,0:T(8,128)(2,1)S(1)}, u32[]{:S(2)}, u32[]{:S(2)}) collective-permute-start(bf16[64,4736]{1,0:T(8,128)(2,1)S(1)} %get-tuple-element.771), channel_id=1, source_target_pairs={{0,4},{1,5},{2,6},{3,7},{4,8},{5,9},{6,10},{7,11},{8,12},{9,13},{1... | collective-permute-start | bytes 1818632 | tf_op jit(solution)/shard_map/while/body/eval_jaxpr/ppermute | solution.py:464
  371.3 17.9 %collective-permute-start.1 = (bf16[64,640]{1,0:T(8,128)(2,1)S(1)}, bf16[64,640]{1,0:T(8,128)(2,1)S(1)}, u32[]{:S(2)}, u32[]{:S(2)}) collective-permute-start(bf16[64,640]{1,0:T(8,128)(2,1)S(1)} %get-tuple-element.772), channel_id=1, source_target_pairs={{0,5},{1,6},{2,7},{3,4},{4,9},{5,10},{6,11},{7,8},{8,13},{9,14},{1... | collective-permute-start | bytes 245768 | tf_op jit(solution)/shard_map/while/body/eval_jaxpr/ppermute | solution.py:464
  374.1 15.1 %collective-permute-start.2 = (bf16[64,640]{1,0:T(8,128)(2,1)S(1)}, bf16[64,640]{1,0:T(8,128)(2,1)}, u32[]{:S(2)}, u32[]{:S(2)}) collective-permute-start(bf16[64,640]{1,0:T(8,128)(2,1)S(1)} %get-tuple-element.772), channel_id=1, source_target_pairs={{0,6},{1,7},{2,4},{3,5},{4,10},{5,11},{6,8},{7,9},{8,14},{9,15},{1... | collective-permute-start | bytes 245768 | tf_op jit(solution)/shard_map/while/body/eval_jaxpr/ppermute | solution.py:464
  386.2 5.8 %collective-permute-start.3 = (bf16[64,640]{1,0:T(8,128)(2,1)S(1)}, bf16[64,640]{1,0:T(8,128)(2,1)}, u32[]{:S(2)}, u32[]{:S(2)}) collective-permute-start(bf16[64,640]{1,0:T(8,128)(2,1)S(1)} %get-tuple-element.772), channel_id=1, source_target_pairs={{0,7},{1,4},{2,5},{3,6},{4,11},{5,8},{6,9},{7,10},{8,15},{9,12},{1... | collective-permute-start | bytes 245768 | tf_op jit(solution)/shard_map/while/body/eval_jaxpr/ppermute | solution.py:464
  397.1 23.9 %collective-permute-start = (bf16[64,4736]{1,0:T(8,128)(2,1)S(1)}, bf16[64,4736]{1,0:T(8,128)(2,1)S(1)}, u32[]{:S(2)}, u32[]{:S(2)}) collective-permute-start(bf16[64,4736]{1,0:T(8,128)(2,1)S(1)} %get-tuple-element.771), channel_id=1, source_target_pairs={{0,4},{1,5},{2,6},{3,7},{4,8},{5,9},{6,10},{7,11},{8,12},{9,13},{1... | collective-permute-start | bytes 1818632 | tf_op jit(solution)/shard_map/while/body/eval_jaxpr/ppermute | solution.py:464
  399.3 18.9 %collective-permute-start.1 = (bf16[64,640]{1,0:T(8,128)(2,1)S(1)}, bf16[64,640]{1,0:T(8,128)(2,1)S(1)}, u32[]{:S(2)}, u32[]{:S(2)}) collective-permute-start(bf16[64,640]{1,0:T(8,128)(2,1)S(1)} %get-tuple-element.772), channel_id=1, source_target_pairs={{0,5},{1,6},{2,7},{3,4},{4,9},{5,10},{6,11},{7,8},{8,13},{9,14},{1... | collective-permute-start | bytes 245768 | tf_op jit(solution)/shard_map/while/body/eval_jaxpr/ppermute | solution.py:464
  400.7 17.5 %collective-permute-start.2 = (bf16[64,640]{1,0:T(8,128)(2,1)S(1)}, bf16[64,640]{1,0:T(8,128)(2,1)}, u32[]{:S(2)}, u32[]{:S(2)}) collective-permute-start(bf16[64,640]{1,0:T(8,128)(2,1)S(1)} %get-tuple-element.772), channel_id=1, source_target_pairs={{0,6},{1,7},{2,4},{3,5},{4,10},{5,11},{6,8},{7,9},{8,14},{9,15},{1... | collective-permute-start | bytes 245768 | tf_op jit(solution)/shard_map/while/body/eval_jaxpr/ppermute | solution.py:464
  403.9 17.1 %collective-permute-start.3 = (bf16[64,640]{1,0:T(8,128)(2,1)S(1)}, bf16[64,640]{1,0:T(8,128)(2,1)}, u32[]{:S(2)}, u32[]{:S(2)}) collective-permute-start(bf16[64,640]{1,0:T(8,128)(2,1)S(1)} %get-tuple-element.772), channel_id=1, source_target_pairs={{0,7},{1,4},{2,5},{3,6},{4,11},{5,8},{6,9},{7,10},{8,15},{9,12},{1... | collective-permute-start | bytes 245768 | tf_op jit(solution)/shard_map/while/body/eval_jaxpr/ppermute | solution.py:464
  426.1 18.0 %collective-permute-start = (bf16[64,4736]{1,0:T(8,128)(2,1)S(1)}, bf16[64,4736]{1,0:T(8,128)(2,1)S(1)}, u32[]{:S(2)}, u32[]{:S(2)}) collective-permute-start(bf16[64,4736]{1,0:T(8,128)(2,1)S(1)} %get-tuple-element.771), channel_id=1, source_target_pairs={{0,4},{1,5},{2,6},{3,7},{4,8},{5,9},{6,10},{7,11},{8,12},{9,13},{1... | collective-permute-start | bytes 1818632 | tf_op jit(solution)/shard_map/while/body/eval_jaxpr/ppermute | solution.py:464
  428.1 9.6 %collective-permute-start.1 = (bf16[64,640]{1,0:T(8,128)(2,1)S(1)}, bf16[64,640]{1,0:T(8,128)(2,1)S(1)}, u32[]{:S(2)}, u32[]{:S(2)}) collective-permute-start(bf16[64,640]{1,0:T(8,128)(2,1)S(1)} %get-tuple-element.772), channel_id=1, source_target_pairs={{0,5},{1,6},{2,7},{3,4},{4,9},{5,10},{6,11},{7,8},{8,13},{9,14},{1... | collective-permute-start | bytes 245768 | tf_op jit(solution)/shard_map/while/body/eval_jaxpr/ppermute | solution.py:464
  429.7 8.1 %collective-permute-start.2 = (bf16[64,640]{1,0:T(8,128)(2,1)S(1)}, bf16[64,640]{1,0:T(8,128)(2,1)}, u32[]{:S(2)}, u32[]{:S(2)}) collective-permute-start(bf16[64,640]{1,0:T(8,128)(2,1)S(1)} %get-tuple-element.772), channel_id=1, source_target_pairs={{0,6},{1,7},{2,4},{3,5},{4,10},{5,11},{6,8},{7,9},{8,14},{9,15},{1... | collective-permute-start | bytes 245768 | tf_op jit(solution)/shard_map/while/body/eval_jaxpr/ppermute | solution.py:464
  432.8 5.9 %collective-permute-start.3 = (bf16[64,640]{1,0:T(8,128)(2,1)S(1)}, bf16[64,640]{1,0:T(8,128)(2,1)}, u32[]{:S(2)}, u32[]{:S(2)}) collective-permute-start(bf16[64,640]{1,0:T(8,128)(2,1)S(1)} %get-tuple-element.772), channel_id=1, source_target_pairs={{0,7},{1,4},{2,5},{3,6},{4,11},{5,8},{6,9},{7,10},{8,15},{9,12},{1... | collective-permute-start | bytes 245768 | tf_op jit(solution)/shard_map/while/body/eval_jaxpr/ppermute | solution.py:464
  449.2 22.6 %collective-permute-start = (bf16[64,4736]{1,0:T(8,128)(2,1)S(1)}, bf16[64,4736]{1,0:T(8,128)(2,1)S(1)}, u32[]{:S(2)}, u32[]{:S(2)}) collective-permute-start(bf16[64,4736]{1,0:T(8,128)(2,1)S(1)} %get-tuple-element.771), channel_id=1, source_target_pairs={{0,4},{1,5},{2,6},{3,7},{4,8},{5,9},{6,10},{7,11},{8,12},{9,13},{1... | collective-permute-start | bytes 1818632 | tf_op jit(solution)/shard_map/while/body/eval_jaxpr/ppermute | solution.py:464
  450.6 15.0 %collective-permute-start.1 = (bf16[64,640]{1,0:T(8,128)(2,1)S(1)}, bf16[64,640]{1,0:T(8,128)(2,1)S(1)}, u32[]{:S(2)}, u32[]{:S(2)}) collective-permute-start(bf16[64,640]{1,0:T(8,128)(2,1)S(1)} %get-tuple-element.772), channel_id=1, source_target_pairs={{0,5},{1,6},{2,7},{3,4},{4,9},{5,10},{6,11},{7,8},{8,13},{9,14},{1... | collective-permute-start | bytes 245768 | tf_op jit(solution)/shard_map/while/body/eval_jaxpr/ppermute | solution.py:464
  454.3 11.3 %collective-permute-start.2 = (bf16[64,640]{1,0:T(8,128)(2,1)S(1)}, bf16[64,640]{1,0:T(8,128)(2,1)}, u32[]{:S(2)}, u32[]{:S(2)}) collective-permute-start(bf16[64,640]{1,0:T(8,128)(2,1)S(1)} %get-tuple-element.772), channel_id=1, source_target_pairs={{0,6},{1,7},{2,4},{3,5},{4,10},{5,11},{6,8},{7,9},{8,14},{9,15},{1... | collective-permute-start | bytes 245768 | tf_op jit(solution)/shard_map/while/body/eval_jaxpr/ppermute | solution.py:464
  457.5 8.5 %collective-permute-start.3 = (bf16[64,640]{1,0:T(8,128)(2,1)S(1)}, bf16[64,640]{1,0:T(8,128)(2,1)}, u32[]{:S(2)}, u32[]{:S(2)}) collective-permute-start(bf16[64,640]{1,0:T(8,128)(2,1)S(1)} %get-tuple-element.772), channel_id=1, source_target_pairs={{0,7},{1,4},{2,5},{3,6},{4,11},{5,8},{6,9},{7,10},{8,15},{9,12},{1... | collective-permute-start | bytes 245768 | tf_op jit(solution)/shard_map/while/body/eval_jaxpr/ppermute | solution.py:464
  (18 other events, 164.5 us)

commit v5 on v3

--- a/solution.py
+++ b/solution.py
@@ -9,7 +9,7 @@
 
 ROWS = 16
 LANES = 128
-COLS = 512
+COLS = 1024
 DEPTH = 1024
 ANY = pl.BlockSpec(memory_space=pl.ANY)
 HBM = pl.BlockSpec(memory_space=pltpu.HBM)
@@ -35,14 +35,6 @@
     )
     tail = jnp.where(lane == extra, high, jnp.where(lane == extra + 1, squares - high, tail))
     return total[:, :rank].astype(jnp.bfloat16), tail.astype(jnp.bfloat16)
-
-
-def merge(even, odd, sublane, distance):
-    clear = (sublane & distance) == 0
-    size = sublane.shape[0]
-    near = jnp.where(clear, even, pltpu.roll(odd, distance, 0))
-    far = jnp.where(clear, pltpu.roll(even, size - distance, 0), odd)
-    return near + far
 
 
 def step_kernel(width, layers, peers, *refs):
@@ -78,9 +70,8 @@
         size_rows,
         drive_rows,
         base_rows,
-        totals,
-        spread_in,
-        spread_out,
+        product,
+        spread,
         input_sem,
         gate_sem,
         state_sem,
@@ -99,7 +90,6 @@
     cols = min(COLS, channels)
     parts = channels // cols
     depth = min(DEPTH, channels)
-    wide_lanes = min(2 * LANES, cols)
     layer = meta[2]
     ahead = (meta[3] == 1) & (layer == layers - 1)
     first = pl.multiple_of(meta[1], ROWS)
@@ -192,13 +182,24 @@
         squares = tail[:, 2 * states : 2 * states + 1] + tail[:, 2 * states + 1 : 2 * states + 2]
         inverse = 1.0 / jnp.sqrt(squares / width + 1e-05)
         low = (total[:, :rank] * inverse).astype(jnp.bfloat16)
-        turned = (tail * inverse).T
+        tail = tail * inverse
+        turned = tail.T
         for row in range(units):
-            column = turned[: 2 * states, row : row + 1]
-            wide = jnp.broadcast_to(column, (2 * states, LANES)).astype(jnp.bfloat16)
-            spread_in[row] = wide[:states]
-            spread_out[row] = wide[states:]
-        sublane = lax.broadcasted_iota(jnp.int32, (states // 2, wide_lanes), 0)
+            column = turned[:states, row : row + 1]
+            spread[row] = jnp.broadcast_to(column, (states, LANES)).astype(jnp.bfloat16)
+        span = (states, rows * states)
+        lane = lax.broadcasted_iota(jnp.int32, span, 1)
+        repeat = (lane % states == lax.broadcasted_iota(jnp.int32, span, 0)).astype(jnp.bfloat16)
+        span = (rows, rows * states)
+        own = lax.broadcasted_iota(jnp.int32, span, 1) // states == lax.broadcasted_iota(
+            jnp.int32, span, 0
+        )
+        outer = tail[:, states : 2 * states].astype(jnp.bfloat16)
+        outer = jnp.dot(outer, repeat, preferred_element_type=jnp.float32)
+        picks = [
+            jnp.where(own, outer[t * rows : (t + 1) * rows], 0.0).astype(jnp.bfloat16)
+            for t in range(steps)
+        ]
         for k in range(swaps):
 
             @pl.when(inside(0, k))
@@ -230,6 +231,7 @@
             def _():
                 held_copy(j + 1).wait()
 
+
             for k in range(swaps):
                 place = planned(0, 0, k) - first
 
@@ -237,39 +239,30 @@
                 def _():
                     hold[place, :, here] = coming[k, :, here].astype(jnp.float32)
 
-            for strip in range(cols // wide_lanes):
-                lanes = pl.ds(strip * wide_lanes, wide_lanes)
-                full = pl.ds(pl.multiple_of(j * cols + strip * wide_lanes, LANES), wide_lanes)
-                rate = rates[:, full]
-                pending = {}
-                for r in range(rows):
-                    h = hold[r, :, full].astype(jnp.bfloat16)
-                    for t in range(steps):
-                        row = t * rows + r
-                        size_row = jnp.broadcast_to(
-                            size_rows[slot, row : row + 1, lanes], (states, wide_lanes)
-                        ).astype(jnp.bfloat16)
-                        drive_row = jnp.broadcast_to(
-                            drive_rows[slot, row : row + 1, lanes], (states, wide_lanes)
-                        ).astype(jnp.bfloat16)
-                        b = jnp.concatenate([spread_in[row]] * (wide_lanes // LANES), axis=1)
-                        c = jnp.concatenate([spread_out[row]] * (wide_lanes // LANES), axis=1)
-                        h = jnp.exp2(size_row * rate) * h + drive_row * b
-                        term = (h * c).astype(jnp.float32)
-                        term = term[: states // 2] + term[states // 2 :]
-                        distance = 1
-                        while (t, distance) in pending:
-                            term = merge(pending.pop((t, distance)), term, sublane, distance)
-                            distance *= 2
-                        if distance == states // 2:
-                            start = row - row % (states // 2)
-                            totals[start : start + states // 2, lanes] = term
-                        else:
-                            pending[t, distance] = term
-                    hold[r, :, full] = h.astype(jnp.float32)
-
+            rate = rates[:, here]
+            for r in range(rows):
+                h = hold[r, :, here].astype(jnp.bfloat16)
+                for t in range(steps):
+                    row = t * rows + r
+                    size_row = jnp.broadcast_to(
+                        size_rows[slot, row : row + 1, :], (states, cols)
+                    ).astype(jnp.bfloat16)
+                    drive_row = jnp.broadcast_to(
+                        drive_rows[slot, row : row + 1, :], (states, cols)
+                    ).astype(jnp.bfloat16)
+                    b = jnp.concatenate([spread[row]] * (cols // LANES), axis=1)
+                    h = jnp.exp2(size_row * rate) * h + drive_row * b
+                    product[t, r * states : (r + 1) * states, :] = h
+                hold[r, :, here] = h.astype(jnp.float32)
+            summed = jnp.concatenate(
+                [
+                    jnp.dot(picks[t], product[t], preferred_element_type=jnp.float32)
+                    for t in range(steps)
+                ],
+                axis=0,
+            )
             opened = gates[:, :, here].astype(jnp.float32).reshape(units, cols)
-            value = (totals[...] + base_rows[slot]) * (opened * jax.nn.sigmoid(opened))
+            value = (summed + base_rows[slot]) * (opened * jax.nn.sigmoid(opened))
             value = value.astype(jnp.bfloat16)
             result[:, :, here] = value.reshape(steps, rows, cols)
             passed = arrived[:, here].astype(jnp.float32) + value.astype(jnp.float32)
@@ -392,12 +385,12 @@
     requests = state.shape[1]
     steps = inputs.shape[0]
     swaps = swap_plan.shape[2]
-    pairs = requests // (2 * ROWS)
+    units = requests // ROWS
     rows = steps * ROWS
     cols = min(COLS, channels)
     parts = channels // cols
     depth = min(DEPTH, channels)
-    turns = pairs + holders - 1
+    turns = units + holders - 1
     plan = jnp.concatenate([swap_plan.reshape(-1), evict_plan.reshape(-1)])
     down = [((i + 1) % holders, i) for i in range(holders)]
     weight = lax.ppermute(jnp.swapaxes(x_weight[0], 0, 1), "section", down)
@@ -412,14 +405,14 @@
     mixed_shape = jax.ShapeDtypeStruct(gate_input.shape, gate_input.dtype)
     moved_shape = jax.ShapeDtypeStruct((holders, states, channels), jnp.bfloat16)
 
-    def meta_of(turn, half):
-        pair = turn - section
-        valid = (pair >= 0) & (pair < pairs)
+    def meta_of(turn):
+        unit = turn - section
+        valid = (unit >= 0) & (unit < units)
         last = section == holders - 1
         following = turn + 1
-        ahead = jnp.where(last, (following >= 0) & (following < pairs), valid)
-        first = (jnp.clip(pair, 0, pairs - 1) * 2 + half) * ROWS
-        then = (jnp.clip(following, 0, pairs - 1) * 2 + half) * ROWS
+        ahead = jnp.where(last, following < units, valid)
+        first = jnp.clip(unit, 0, units - 1) * ROWS
+        then = jnp.clip(following, 0, units - 1) * ROWS
         return jnp.stack([valid, first, section, ahead, then]).astype(jnp.int32)
 
     def step(meta, blocks, final, mixed, leaving):
@@ -429,9 +422,9 @@
             out_shape=[block_shape, partial_shape, state_shape, mixed_shape, moved_shape],
             in_specs=[SMEM, SMEM]
             + [VMEM] * peers
-            + [HBM, HBM, ANY, ANY]
+            + [HBM, HBM, ANY, HBM]
             + [VMEM] * 5
-            + [HBM, ANY]
+            + [HBM, HBM]
             + [HBM] * 3,
             out_specs=[VMEM, VMEM, HBM, HBM, HBM],
             scratch_shapes=[
@@ -445,8 +438,7 @@
                 pltpu.VMEM((2, rows, cols), jnp.float32),
                 pltpu.VMEM((2, rows, cols), jnp.float32),
                 pltpu.VMEM((2, rows, cols), jnp.float32),
-                pltpu.VMEM((rows, cols), jnp.float32),
-                pltpu.VMEM((rows, states, LANES), jnp.bfloat16),
+                pltpu.VMEM((steps, ROWS * states, cols), jnp.bfloat16),
                 pltpu.VMEM((rows, states, LANES), jnp.bfloat16),
                 pltpu.SemaphoreType.DMA((steps,)),
                 pltpu.SemaphoreType.DMA,
@@ -459,7 +451,7 @@
                 pltpu.SemaphoreType.DMA((swaps,)),
             ],
             input_output_aliases={given + 11 + k: 2 + k for k in range(3)},
-            compiler_params=pltpu.CompilerParams(vmem_limit_bytes=28 * 2**20),
+            compiler_params=pltpu.CompilerParams(vmem_limit_bytes=24 * 2**20),
             cost_estimate=pl.CostEstimate(
                 flops=4 * rows * channels * (rank + LANES) + 8 * rows * states * channels,
                 bytes_accessed=4 * channels * rank + 8 * ROWS * states * channels,
@@ -502,12 +494,9 @@
         return lax.all_to_all(block, "section", split_axis=0, concat_axis=0, tiled=True)
 
     def turn(index, carry):
-        out, late, kept = carry
-        early = send(*out)
-        *out, final, mixed, leaving = step(meta_of(index - 1, 1), late, *kept)
-        late = send(*out)
-        *out, final, mixed, leaving = step(meta_of(index, 0), early, final, mixed, leaving)
-        return tuple(out), tuple(late), (final, mixed, leaving)
+        blocks, kept = carry
+        block, partial, *kept = step(meta_of(index), blocks, *kept)
+        return send(block, partial), kept
 
     picked = pl.pallas_call(
         pick_kernel, out_shape=moved_shape, in_specs=[SMEM, SMEM, VMEM], out_specs=VMEM, name="pick"
@@ -516,12 +505,9 @@
     *kept, block, partial = empty(
         [state_shape, mixed_shape, moved_shape, block_shape, partial_shape]
     )
-    late = (block,) + (partial,) * (peers - 1)
-    *out, final, mixed, leaving = step(meta_of(-1, 0), late, *kept)
-    out, late, kept = lax.fori_loop(
-        0, turns, turn, (tuple(out), late, (final, mixed, leaving))
-    )
-    _, _, final, mixed, leaving = step(meta_of(turns - 1, 1), late, *kept)
+    blocks = [block] + [partial] * (peers - 1)
+    blocks, kept = lax.fori_loop(-1, turns - 1, turn, (blocks, kept))
+    _, _, final, mixed, leaving = step(meta_of(turns - 1), blocks, *kept)
     stored = pl.pallas_call(
         keep_kernel,
         out_shape=jax.ShapeDtypeStruct(pool.shape, pool.dtype),

time: 528 us -> 441 us (0.84)
  starting transfers between devices: 215 us -> 112 us
  waiting for transfers between devices: 129 us -> 186 us
  Pallas kernels: 137 us -> 105 us
  blocking collectives: 37.6 us -> 28.5 us
    ppermute x88 -> x60, starting transfers between devices: 206 us -> 102 us  [send(): blocks.append(lax.ppermute(partial if shift else block, axes, route))]
    ppermute x88 -> x60, waiting for transfers between devices: 79.6 us -> 139 us  [send(): blocks.append(lax.ppermute(partial if shift else block, axes, route))]
    pallas_call x24 -> x16, Pallas kernels: 132 us -> 100 us  [step(): pl.pallas_call(functools.partial(step_kernel, width, holders, peers), out...]
    all_to_all x1, blocking collectives: 37.6 us -> 28.5 us  [swap(): lax.all_to_all(block, 'section', split_axis=0, concat_axis=0, tiled=True)]
  transfers between devices with their start and end apart: 91 -> 63, of which waited for: 29 -> 42; matrix products, arithmetic and copies ran while one was open for 1% -> 1% of each run, Pallas kernels for 25% -> 1%
where the time goes in v5:
time: 441 us; the launch traced here: 440 us
  waiting for transfers between devices  186 us (42%)
  starting transfers between devices  112 us (25%)
  Pallas kernels  105 us (24%)
  blocking collectives  28.5 us (6%)
  local copies, waits for them, and re-layouts  6.14 us (1%)
    ppermute x60, waiting for transfers between devices, send(): blocks.append(lax.ppermute(partial if shift else block, axes, route))  139 us
    ppermute x60, starting transfers between devices, send(): blocks.append(lax.ppermute(partial if shift else block, axes, route))  102 us
    pallas_call x16, Pallas kernels, step(): pl.pallas_call(functools.partial(step_kernel, width, holders, peers), out...  100 us
    ppermute x1, waiting for transfers between devices, shards(): next_gain = lax.ppermute(gain, 'section', down)  46.1 us
    all_to_all x1, blocking collectives, swap(): lax.all_to_all(block, 'section', split_axis=0, concat_axis=0, tiled=True)  28.5 us
  transfers between devices with their start and end apart: 63, of which 42 were waited for; matrix products, arithmetic and copies ran while one was open for 1% of the time, Pallas kernels for 1%

profile of v5, /device:TPU:0, one launch (start us, length us, event | category | flops | bytes accessed | tf_op | source)
XLA Modules:
  0.0 440.3 jit_solution(14228046568151599333)
XLA Ops:
  0.6 3.4 collective-permute-start.5
  5.9 2.3 pick.1
  8.1 3.6 all-to-all-start
  11.7 2.6 collective-permute-start.4
  18.4 46.1 %collective-permute-done.4.refs_14_ = f32[1,4096]{1,0:T(1,128)} collective-permute-done((f32[1,4096]{1,0:T(1,128)}, f32[1,4096]{1,0:T(1,128)}, u32[]{:S(2)}, u32[]{:S(2)}) %collective-permute-start.4) | collective-permute-done | bytes 16416 | tf_op jit(solution)/shard_map/ppermute | solution.py:397
  65.3 341.7 %while.28 = (s32[]{:T(128)}, bf16[64,4736]{1,0:T(8,128)(2,1)S(1)}, bf16[64,640]{1,0:T(8,128)(2,1)}, bf16[64,640]{1,0:T(8,128)(2,1)}, bf16[64,640]{1,0:T(8,128)(2...) while((s32[]{:T(128)}, bf16[64,4736]{1,0:T(8,128)(2,1)S(1)}, ...), condition=%wide.region_1.2_spmd, body=%wide.region_0.1_spmd.sunk | while | flops 704643072 | bytes 20185672 | solution.py:509
  66.8 2.8 collective-permute-start.1
  69.6 2.1 collective-permute-start.2
  73.2 5.6 %collective-permute-done.1 = bf16[64,640]{1,0:T(8,128)(2,1)} collective-permute-done((bf16[64,640]{1,0:T(8,128)(2,1)S(1)}, bf16[64,640]{1,0:T(8,128)(2,1)}, u32[]{:S(2)}, u32[]{:S(2)}) %collective-permute-start.1) | collective-permute-done | bytes 81952 | tf_op jit(solution)/shard_map/while/body/eval_jaxpr/ppermute | solution.py:490
  78.8 2.1 collective-permute-done.3
  80.9 2.5 collective-permute-done
  83.5 11.0 %step.11 = (bf16[64,4736]{1,0:T(8,128)(2,1)S(1)}, bf16[64,640]{1,0:T(8,128)(2,1)S(1)}, f32[1,128,16,4096]{3,2,1,0:T(8,128)}, bf16[1,4,128,4096]{3,2,1,0:T(8,128)(2,1)}, bf16[8,16,4096]{2,1,0:T(8,128)(2,1)S(1)}) custom-call(s32[5]{0:T(128)S(1)} %stack.102.refs_0_, ...), custom_call_target="tpu_custom_call", output_to_operand_aliasing={{2}: (17, {}), {3}: (18, {}), {4}: (19, {})} | custom-call | flops 704643072 | bytes 16777216 | tf_op jit(solution)/shard_map/while/body/eval_jaxpr/step/pallas_call | solution.py:420
  94.8 8.2 %collective-permute-done.1 = bf16[64,640]{1,0:T(8,128)(2,1)} collective-permute-done((bf16[64,640]{1,0:T(8,128)(2,1)S(1)}, bf16[64,640]{1,0:T(8,128)(2,1)}, u32[]{:S(2)}, u32[]{:S(2)}) %collective-permute-start.1) | collective-permute-done | bytes 81952 | tf_op jit(solution)/shard_map/while/body/eval_jaxpr/ppermute | solution.py:490
  103.0 3.7 collective-permute-done.2
  107.7 11.2 %step.11 = (bf16[64,4736]{1,0:T(8,128)(2,1)S(1)}, bf16[64,640]{1,0:T(8,128)(2,1)S(1)}, f32[1,128,16,4096]{3,2,1,0:T(8,128)}, bf16[1,4,128,4096]{3,2,1,0:T(8,128)(2,1)}, bf16[8,16,4096]{2,1,0:T(8,128)(2,1)S(1)}) custom-call(s32[5]{0:T(128)S(1)} %stack.102.refs_0_, ...), custom_call_target="tpu_custom_call", output_to_operand_aliasing={{2}: (17, {}), {3}: (18, {}), {4}: (19, {})} | custom-call | flops 704643072 | bytes 16777216 | tf_op jit(solution)/shard_map/while/body/eval_jaxpr/step/pallas_call | solution.py:420
  119.1 8.3 %collective-permute-done.1 = bf16[64,640]{1,0:T(8,128)(2,1)} collective-permute-done((bf16[64,640]{1,0:T(8,128)(2,1)S(1)}, bf16[64,640]{1,0:T(8,128)(2,1)}, u32[]{:S(2)}, u32[]{:S(2)}) %collective-permute-start.1) | collective-permute-done | bytes 81952 | tf_op jit(solution)/shard_map/while/body/eval_jaxpr/ppermute | solution.py:490
  127.4 3.7 collective-permute-done.2
  132.0 11.0 %step.11 = (bf16[64,4736]{1,0:T(8,128)(2,1)S(1)}, bf16[64,640]{1,0:T(8,128)(2,1)S(1)}, f32[1,128,16,4096]{3,2,1,0:T(8,128)}, bf16[1,4,128,4096]{3,2,1,0:T(8,128)(2,1)}, bf16[8,16,4096]{2,1,0:T(8,128)(2,1)S(1)}) custom-call(s32[5]{0:T(128)S(1)} %stack.102.refs_0_, ...), custom_call_target="tpu_custom_call", output_to_operand_aliasing={{2}: (17, {}), {3}: (18, {}), {4}: (19, {})} | custom-call | flops 704643072 | bytes 16777216 | tf_op jit(solution)/shard_map/while/body/eval_jaxpr/step/pallas_call | solution.py:420
  143.3 8.3 %collective-permute-done.1 = bf16[64,640]{1,0:T(8,128)(2,1)} collective-permute-done((bf16[64,640]{1,0:T(8,128)(2,1)S(1)}, bf16[64,640]{1,0:T(8,128)(2,1)}, u32[]{:S(2)}, u32[]{:S(2)}) %collective-permute-start.1) | collective-permute-done | bytes 81952 | tf_op jit(solution)/shard_map/while/body/eval_jaxpr/ppermute | solution.py:490
  151.6 3.7 collective-permute-done.2
  156.2 11.1 %step.11 = (bf16[64,4736]{1,0:T(8,128)(2,1)S(1)}, bf16[64,640]{1,0:T(8,128)(2,1)S(1)}, f32[1,128,16,4096]{3,2,1,0:T(8,128)}, bf16[1,4,128,4096]{3,2,1,0:T(8,128)(2,1)}, bf16[8,16,4096]{2,1,0:T(8,128)(2,1)S(1)}) custom-call(s32[5]{0:T(128)S(1)} %stack.102.refs_0_, ...), custom_call_target="tpu_custom_call", output_to_operand_aliasing={{2}: (17, {}), {3}: (18, {}), {4}: (19, {})} | custom-call | flops 704643072 | bytes 16777216 | tf_op jit(solution)/shard_map/while/body/eval_jaxpr/step/pallas_call | solution.py:420
  167.5 8.3 %collective-permute-done.1 = bf16[64,640]{1,0:T(8,128)(2,1)} collective-permute-done((bf16[64,640]{1,0:T(8,128)(2,1)S(1)}, bf16[64,640]{1,0:T(8,128)(2,1)}, u32[]{:S(2)}, u32[]{:S(2)}) %collective-permute-start.1) | collective-permute-done | bytes 81952 | tf_op jit(solution)/shard_map/while/body/eval_jaxpr/ppermute | solution.py:490
  175.9 3.7 collective-permute-done.2
  180.4 11.0 %step.11 = (bf16[64,4736]{1,0:T(8,128)(2,1)S(1)}, bf16[64,640]{1,0:T(8,128)(2,1)S(1)}, f32[1,128,16,4096]{3,2,1,0:T(8,128)}, bf16[1,4,128,4096]{3,2,1,0:T(8,128)(2,1)}, bf16[8,16,4096]{2,1,0:T(8,128)(2,1)S(1)}) custom-call(s32[5]{0:T(128)S(1)} %stack.102.refs_0_, ...), custom_call_target="tpu_custom_call", output_to_operand_aliasing={{2}: (17, {}), {3}: (18, {}), {4}: (19, {})} | custom-call | flops 704643072 | bytes 16777216 | tf_op jit(solution)/shard_map/while/body/eval_jaxpr/step/pallas_call | solution.py:420
  193.1 7.0 %collective-permute-done.1 = bf16[64,640]{1,0:T(8,128)(2,1)} collective-permute-done((bf16[64,640]{1,0:T(8,128)(2,1)S(1)}, bf16[64,640]{1,0:T(8,128)(2,1)}, u32[]{:S(2)}, u32[]{:S(2)}) %collective-permute-start.1) | collective-permute-done | bytes 81952 | tf_op jit(solution)/shard_map/while/body/eval_jaxpr/ppermute | solution.py:490
  200.1 3.7 collective-permute-done.2
  204.6 11.0 %step.11 = (bf16[64,4736]{1,0:T(8,128)(2,1)S(1)}, bf16[64,640]{1,0:T(8,128)(2,1)S(1)}, f32[1,128,16,4096]{3,2,1,0:T(8,128)}, bf16[1,4,128,4096]{3,2,1,0:T(8,128)(2,1)}, bf16[8,16,4096]{2,1,0:T(8,128)(2,1)S(1)}) custom-call(s32[5]{0:T(128)S(1)} %stack.102.refs_0_, ...), custom_call_target="tpu_custom_call", output_to_operand_aliasing={{2}: (17, {}), {3}: (18, {}), {4}: (19, {})} | custom-call | flops 704643072 | bytes 16777216 | tf_op jit(solution)/shard_map/while/body/eval_jaxpr/step/pallas_call | solution.py:420
  217.4 6.8 %collective-permute-done.1 = bf16[64,640]{1,0:T(8,128)(2,1)} collective-permute-done((bf16[64,640]{1,0:T(8,128)(2,1)S(1)}, bf16[64,640]{1,0:T(8,128)(2,1)}, u32[]{:S(2)}, u32[]{:S(2)}) %collective-permute-start.1) | collective-permute-done | bytes 81952 | tf_op jit(solution)/shard_map/while/body/eval_jaxpr/ppermute | solution.py:490
  224.3 3.6 collective-permute-done.2
  228.7 11.1 %step.11 = (bf16[64,4736]{1,0:T(8,128)(2,1)S(1)}, bf16[64,640]{1,0:T(8,128)(2,1)S(1)}, f32[1,128,16,4096]{3,2,1,0:T(8,128)}, bf16[1,4,128,4096]{3,2,1,0:T(8,128)(2,1)}, bf16[8,16,4096]{2,1,0:T(8,128)(2,1)S(1)}) custom-call(s32[5]{0:T(128)S(1)} %stack.102.refs_0_, ...), custom_call_target="tpu_custom_call", output_to_operand_aliasing={{2}: (17, {}), {3}: (18, {}), {4}: (19, {})} | custom-call | flops 704643072 | bytes 16777216 | tf_op jit(solution)/shard_map/while/body/eval_jaxpr/step/pallas_call | solution.py:420
  241.8 6.8 %collective-permute-done.1 = bf16[64,640]{1,0:T(8,128)(2,1)} collective-permute-done((bf16[64,640]{1,0:T(8,128)(2,1)S(1)}, bf16[64,640]{1,0:T(8,128)(2,1)}, u32[]{:S(2)}, u32[]{:S(2)}) %collective-permute-start.1) | collective-permute-done | bytes 81952 | tf_op jit(solution)/shard_map/while/body/eval_jaxpr/ppermute | solution.py:490
  248.5 3.6 collective-permute-done.2
  253.0 11.5 %step.11 = (bf16[64,4736]{1,0:T(8,128)(2,1)S(1)}, bf16[64,640]{1,0:T(8,128)(2,1)S(1)}, f32[1,128,16,4096]{3,2,1,0:T(8,128)}, bf16[1,4,128,4096]{3,2,1,0:T(8,128)(2,1)}, bf16[8,16,4096]{2,1,0:T(8,128)(2,1)S(1)}) custom-call(s32[5]{0:T(128)S(1)} %stack.102.refs_0_, ...), custom_call_target="tpu_custom_call", output_to_operand_aliasing={{2}: (17, {}), {3}: (18, {}), {4}: (19, {})} | custom-call | flops 704643072 | bytes 16777216 | tf_op jit(solution)/shard_map/while/body/eval_jaxpr/step/pallas_call | solution.py:420
  265.9 7.2 %collective-permute-done.1 = bf16[64,640]{1,0:T(8,128)(2,1)} collective-permute-done((bf16[64,640]{1,0:T(8,128)(2,1)S(1)}, bf16[64,640]{1,0:T(8,128)(2,1)}, u32[]{:S(2)}, u32[]{:S(2)}) %collective-permute-start.1) | collective-permute-done | bytes 81952 | tf_op jit(solution)/shard_map/while/body/eval_jaxpr/ppermute | solution.py:490
  273.2 3.6 collective-permute-done.2
  279.0 5.1 %collective-permute-start = (bf16[64,4736]{1,0:T(8,128)(2,1)S(1)}, bf16[64,4736]{1,0:T(8,128)(2,1)S(1)}, u32[]{:S(2)}, u32[]{:S(2)}) collective-permute-start(bf16[64,4736]{1,0:T(8,128)(2,1)S(1)} %get-tuple-element.771), channel_id=1, source_target_pairs={{0,4},{1,5},{2,6},{3,7},{4,8},{5,9},{6,10},{7,11},{8,12},{9,13},{1... | collective-permute-start | bytes 1818632 | tf_op jit(solution)/shard_map/while/body/eval_jaxpr/ppermute | solution.py:490
  287.0 3.4 collective-permute-start.3
  292.1 4.0 collective-permute-done.2
  298.2 11.6 %collective-permute-start.1 = (bf16[64,640]{1,0:T(8,128)(2,1)S(1)}, bf16[64,640]{1,0:T(8,128)(2,1)}, u32[]{:S(2)}, u32[]{:S(2)}) collective-permute-start(bf16[64,640]{1,0:T(8,128)(2,1)S(1)} %get-tuple-element.772), channel_id=1, source_target_pairs={{0,5},{1,6},{2,7},{3,4},{4,9},{5,10},{6,11},{7,8},{8,13},{9,14},{1... | collective-permute-start | bytes 245768 | tf_op jit(solution)/shard_map/while/body/eval_jaxpr/ppermute | solution.py:490
  309.8 1.9 collective-permute-start.2
  311.7 2.9 collective-permute-start.3
  314.6 4.5 %collective-permute-done.2 = bf16[64,640]{1,0:T(8,128)(2,1)} collective-permute-done((bf16[64,640]{1,0:T(8,128)(2,1)S(1)}, bf16[64,640]{1,0:T(8,128)(2,1)}, u32[]{:S(2)}, u32[]{:S(2)}) %collective-permute-start.2) | collective-permute-done | bytes 81952 | tf_op jit(solution)/shard_map/while/body/eval_jaxpr/ppermute | solution.py:490
  321.7 2.4 collective-permute-start.1
  324.1 11.4 %collective-permute-start.2 = (bf16[64,640]{1,0:T(8,128)(2,1)S(1)}, bf16[64,640]{1,0:T(8,128)(2,1)}, u32[]{:S(2)}, u32[]{:S(2)}) collective-permute-start(bf16[64,640]{1,0:T(8,128)(2,1)S(1)} %get-tuple-element.772), channel_id=1, source_target_pairs={{0,6},{1,7},{2,4},{3,5},{4,10},{5,11},{6,8},{7,9},{8,14},{9,15},{1... | collective-permute-start | bytes 245768 | tf_op jit(solution)/shard_map/while/body/eval_jaxpr/ppermute | solution.py:490
  335.6 3.2 collective-permute-start.3
  338.8 2.8 collective-permute-done.3
  343.0 1.9 collective-permute-start
  344.9 1.9 collective-permute-start.1
  346.8 3.0 collective-permute-start.2
  349.8 13.6 %collective-permute-start.3 = (bf16[64,640]{1,0:T(8,128)(2,1)S(1)}, bf16[64,640]{1,0:T(8,128)(2,1)}, u32[]{:S(2)}, u32[]{:S(2)}) collective-permute-start(bf16[64,640]{1,0:T(8,128)(2,1)S(1)} %get-tuple-element.772), channel_id=1, source_target_pairs={{0,7},{1,4},{2,5},{3,6},{4,11},{5,8},{6,9},{7,10},{8,15},{9,12},{1... | collective-permute-start | bytes 245768 | tf_op jit(solution)/shard_map/while/body/eval_jaxpr/ppermute | solution.py:490
  363.4 2.8 collective-permute-done.3
  367.6 1.9 collective-permute-start
  371.4 3.0 collective-permute-start.2
  374.4 3.4 collective-permute-start.3
  380.2 3.4 collective-permute-done
  385.0 2.6 collective-permute-start
  387.6 3.6 collective-permute-start.1
  391.1 3.3 collective-permute-start.2
  394.4 2.6 collective-permute-start.3
  397.0 3.9 collective-permute-done.1
  401.2 5.8 %collective-permute-done = bf16[64,4736]{1,0:T(8,128)(2,1)S(1)} collective-permute-done((bf16[64,4736]{1,0:T(8,128)(2,1)S(1)}, bf16[64,4736]{1,0:T(8,128)(2,1)S(1)}, u32[]{:S(2)}, u32[]{:S(2)}) %collective-permute-start) | collective-permute-done | bytes 606240 | tf_op jit(solution)/shard_map/while/body/eval_jaxpr/ppermute | solution.py:490
  407.1 2.2 step.10
  409.2 28.5 %all_to_all.10.returned = bf16[8,16,4096]{2,1,0:T(8,128)(2,1)} all-to-all(bf16[8,16,4096]{2,1,0:T(8,128)(2,1)S(1)} %get-tuple-element.588), channel_id=1, replica_groups=mesh['section'=8,'tensor'=4] {'section'}, dimensions={0} | all-to-all | bytes 2097152 | tf_op jit(solution)/shard_map/all_to_all | solution.py:494
  437.8 2.6 keep.1
  (109 shorter events, 43.6 us)
Async XLA Ops:
  0.6 64.7 %copy-start = (f32[1,4096]{1,0:T(1,128)S(1)}, f32[1,4096]{1,0:T(1,128)}, u32[]{:S(2)}) copy-start(f32[1,4096]{1,0:T(1,128)} %refs_10_.1) | copy-start | bytes 49156
  0.6 64.7 %collective-permute-start.5 = (bf16[544,4096]{1,0:T(8,128)(2,1)}, bf16[544,4096]{1,0:T(8,128)(2,1)}, u32[]{:S(2)}, u32[]{:S(2)}) collective-permute-start(bf16[544,4096]{1,0:T(8,128)(2,1)} %bitcast.24), channel_id=1, source_target_pairs={{4,0},{8,4},{12,8},{16,12},{20,16},{24,20},{28,24},{0,28},{5,1},{9... | collective-permute-start | bytes 13369352 | tf_op jit(solution)/shard_map/ppermute | solution.py:396
  8.1 57.2 %all-to-all-start = ((bf16[8,16,4096]{2,1,0:T(8,128)(2,1)}), bf16[8,16,4096]{2,1,0:T(8,128)(2,1)S(1)}, u32[]{:S(2)}, u32[]{:S(2)}) async-start(bf16[8,16,4096]{2,1,0:T(8,128)(2,1)} %pick.1), calls=%async_computation | async-start | bytes 2097152 | tf_op jit(solution)/shard_map/all_to_all | solution.py:494
  11.7 52.9 %collective-permute-start.4 = (f32[1,4096]{1,0:T(1,128)}, f32[1,4096]{1,0:T(1,128)}, u32[]{:S(2)}, u32[]{:S(2)}) collective-permute-start(f32[1,4096]{1,0:T(1,128)} %refs_13_.1), channel_id=1, source_target_pairs={{4,0},{8,4},{12,8},{16,12},{20,16},{24,20},{28,24},{0,28},{5,1},{9... | collective-permute-start | bytes 49160 | tf_op jit(solution)/shard_map/ppermute | solution.py:397
  66.7 16.7 %collective-permute-start = (bf16[64,4736]{1,0:T(8,128)(2,1)S(1)}, bf16[64,4736]{1,0:T(8,128)(2,1)S(1)}, u32[]{:S(2)}, u32[]{:S(2)}) collective-permute-start(bf16[64,4736]{1,0:T(8,128)(2,1)S(1)} %get-tuple-element.771), channel_id=1, source_target_pairs={{0,4},{1,5},{2,6},{3,7},{4,8},{5,9},{6,10},{7,11},{8,12},{9,13},{1... | collective-permute-start | bytes 1818632 | tf_op jit(solution)/shard_map/while/body/eval_jaxpr/ppermute | solution.py:490
  66.8 12.0 %collective-permute-start.1 = (bf16[64,640]{1,0:T(8,128)(2,1)S(1)}, bf16[64,640]{1,0:T(8,128)(2,1)}, u32[]{:S(2)}, u32[]{:S(2)}) collective-permute-start(bf16[64,640]{1,0:T(8,128)(2,1)S(1)} %get-tuple-element.772), channel_id=1, source_target_pairs={{0,5},{1,6},{2,7},{3,4},{4,9},{5,10},{6,11},{7,8},{8,13},{9,14},{1... | collective-permute-start | bytes 245768 | tf_op jit(solution)/shard_map/while/body/eval_jaxpr/ppermute | solution.py:490
  69.6 9.1 %collective-permute-start.2 = (bf16[64,640]{1,0:T(8,128)(2,1)S(1)}, bf16[64,640]{1,0:T(8,128)(2,1)}, u32[]{:S(2)}, u32[]{:S(2)}) collective-permute-start(bf16[64,640]{1,0:T(8,128)(2,1)S(1)} %get-tuple-element.772), channel_id=1, source_target_pairs={{0,6},{1,7},{2,4},{3,5},{4,10},{5,11},{6,8},{7,9},{8,14},{9,15},{1... | collective-permute-start | bytes 245768 | tf_op jit(solution)/shard_map/while/body/eval_jaxpr/ppermute | solution.py:490
  71.8 9.1 %collective-permute-start.3 = (bf16[64,640]{1,0:T(8,128)(2,1)S(1)}, bf16[64,640]{1,0:T(8,128)(2,1)}, u32[]{:S(2)}, u32[]{:S(2)}) collective-permute-start(bf16[64,640]{1,0:T(8,128)(2,1)S(1)} %get-tuple-element.772), channel_id=1, source_target_pairs={{0,7},{1,4},{2,5},{3,6},{4,11},{5,8},{6,9},{7,10},{8,15},{9,12},{1... | collective-permute-start | bytes 245768 | tf_op jit(solution)/shard_map/while/body/eval_jaxpr/ppermute | solution.py:490
  94.5 13.1 %collective-permute-start = (bf16[64,4736]{1,0:T(8,128)(2,1)S(1)}, bf16[64,4736]{1,0:T(8,128)(2,1)S(1)}, u32[]{:S(2)}, u32[]{:S(2)}) collective-permute-start(bf16[64,4736]{1,0:T(8,128)(2,1)S(1)} %get-tuple-element.771), channel_id=1, source_target_pairs={{0,4},{1,5},{2,6},{3,7},{4,8},{5,9},{6,10},{7,11},{8,12},{9,13},{1... | collective-permute-start | bytes 1818632 | tf_op jit(solution)/shard_map/while/body/eval_jaxpr/ppermute | solution.py:490
  94.6 8.4 %collective-permute-start.1 = (bf16[64,640]{1,0:T(8,128)(2,1)S(1)}, bf16[64,640]{1,0:T(8,128)(2,1)}, u32[]{:S(2)}, u32[]{:S(2)}) collective-permute-start(bf16[64,640]{1,0:T(8,128)(2,1)S(1)} %get-tuple-element.772), channel_id=1, source_target_pairs={{0,5},{1,6},{2,7},{3,4},{4,9},{5,10},{6,11},{7,8},{8,13},{9,14},{1... | collective-permute-start | bytes 245768 | tf_op jit(solution)/shard_map/while/body/eval_jaxpr/ppermute | solution.py:490
  94.6 12.1 %collective-permute-start.2 = (bf16[64,640]{1,0:T(8,128)(2,1)S(1)}, bf16[64,640]{1,0:T(8,128)(2,1)}, u32[]{:S(2)}, u32[]{:S(2)}) collective-permute-start(bf16[64,640]{1,0:T(8,128)(2,1)S(1)} %get-tuple-element.772), channel_id=1, source_target_pairs={{0,6},{1,7},{2,4},{3,5},{4,10},{5,11},{6,8},{7,9},{8,14},{9,15},{1... | collective-permute-start | bytes 245768 | tf_op jit(solution)/shard_map/while/body/eval_jaxpr/ppermute | solution.py:490
  94.7 12.0 %collective-permute-start.3 = (bf16[64,640]{1,0:T(8,128)(2,1)S(1)}, bf16[64,640]{1,0:T(8,128)(2,1)}, u32[]{:S(2)}, u32[]{:S(2)}) collective-permute-start(bf16[64,640]{1,0:T(8,128)(2,1)S(1)} %get-tuple-element.772), channel_id=1, source_target_pairs={{0,7},{1,4},{2,5},{3,6},{4,11},{5,8},{6,9},{7,10},{8,15},{9,12},{1... | collective-permute-start | bytes 245768 | tf_op jit(solution)/shard_map/while/body/eval_jaxpr/ppermute | solution.py:490
  118.9 13.1 %collective-permute-start = (bf16[64,4736]{1,0:T(8,128)(2,1)S(1)}, bf16[64,4736]{1,0:T(8,128)(2,1)S(1)}, u32[]{:S(2)}, u32[]{:S(2)}) collective-permute-start(bf16[64,4736]{1,0:T(8,128)(2,1)S(1)} %get-tuple-element.771), channel_id=1, source_target_pairs={{0,4},{1,5},{2,6},{3,7},{4,8},{5,9},{6,10},{7,11},{8,12},{9,13},{1... | collective-permute-start | bytes 1818632 | tf_op jit(solution)/shard_map/while/body/eval_jaxpr/ppermute | solution.py:490
  118.9 8.5 %collective-permute-start.1 = (bf16[64,640]{1,0:T(8,128)(2,1)S(1)}, bf16[64,640]{1,0:T(8,128)(2,1)}, u32[]{:S(2)}, u32[]{:S(2)}) collective-permute-start(bf16[64,640]{1,0:T(8,128)(2,1)S(1)} %get-tuple-element.772), channel_id=1, source_target_pairs={{0,5},{1,6},{2,7},{3,4},{4,9},{5,10},{6,11},{7,8},{8,13},{9,14},{1... | collective-permute-start | bytes 245768 | tf_op jit(solution)/shard_map/while/body/eval_jaxpr/ppermute | solution.py:490
  119.0 12.1 %collective-permute-start.2 = (bf16[64,640]{1,0:T(8,128)(2,1)S(1)}, bf16[64,640]{1,0:T(8,128)(2,1)}, u32[]{:S(2)}, u32[]{:S(2)}) collective-permute-start(bf16[64,640]{1,0:T(8,128)(2,1)S(1)} %get-tuple-element.772), channel_id=1, source_target_pairs={{0,6},{1,7},{2,4},{3,5},{4,10},{5,11},{6,8},{7,9},{8,14},{9,15},{1... | collective-permute-start | bytes 245768 | tf_op jit(solution)/shard_map/while/body/eval_jaxpr/ppermute | solution.py:490
  119.1 12.0 %collective-permute-start.3 = (bf16[64,640]{1,0:T(8,128)(2,1)S(1)}, bf16[64,640]{1,0:T(8,128)(2,1)}, u32[]{:S(2)}, u32[]{:S(2)}) collective-permute-start(bf16[64,640]{1,0:T(8,128)(2,1)S(1)} %get-tuple-element.772), channel_id=1, source_target_pairs={{0,7},{1,4},{2,5},{3,6},{4,11},{5,8},{6,9},{7,10},{8,15},{9,12},{1... | collective-permute-start | bytes 245768 | tf_op jit(solution)/shard_map/while/body/eval_jaxpr/ppermute | solution.py:490
  143.0 13.1 %collective-permute-start = (bf16[64,4736]{1,0:T(8,128)(2,1)S(1)}, bf16[64,4736]{1,0:T(8,128)(2,1)S(1)}, u32[]{:S(2)}, u32[]{:S(2)}) collective-permute-start(bf16[64,4736]{1,0:T(8,128)(2,1)S(1)} %get-tuple-element.771), channel_id=1, source_target_pairs={{0,4},{1,5},{2,6},{3,7},{4,8},{5,9},{6,10},{7,11},{8,12},{9,13},{1... | collective-permute-start | bytes 1818632 | tf_op jit(solution)/shard_map/while/body/eval_jaxpr/ppermute | solution.py:490
  143.1 8.5 %collective-permute-start.1 = (bf16[64,640]{1,0:T(8,128)(2,1)S(1)}, bf16[64,640]{1,0:T(8,128)(2,1)}, u32[]{:S(2)}, u32[]{:S(2)}) collective-permute-start(bf16[64,640]{1,0:T(8,128)(2,1)S(1)} %get-tuple-element.772), channel_id=1, source_target_pairs={{0,5},{1,6},{2,7},{3,4},{4,9},{5,10},{6,11},{7,8},{8,13},{9,14},{1... | collective-permute-start | bytes 245768 | tf_op jit(solution)/shard_map/while/body/eval_jaxpr/ppermute | solution.py:490
  143.1 12.1 %collective-permute-start.2 = (bf16[64,640]{1,0:T(8,128)(2,1)S(1)}, bf16[64,640]{1,0:T(8,128)(2,1)}, u32[]{:S(2)}, u32[]{:S(2)}) collective-permute-start(bf16[64,640]{1,0:T(8,128)(2,1)S(1)} %get-tuple-element.772), channel_id=1, source_target_pairs={{0,6},{1,7},{2,4},{3,5},{4,10},{5,11},{6,8},{7,9},{8,14},{9,15},{1... | collective-permute-start | bytes 245768 | tf_op jit(solution)/shard_map/while/body/eval_jaxpr/ppermute | solution.py:490
  143.2 12.1 %collective-permute-start.3 = (bf16[64,640]{1,0:T(8,128)(2,1)S(1)}, bf16[64,640]{1,0:T(8,128)(2,1)}, u32[]{:S(2)}, u32[]{:S(2)}) collective-permute-start(bf16[64,640]{1,0:T(8,128)(2,1)S(1)} %get-tuple-element.772), channel_id=1, source_target_pairs={{0,7},{1,4},{2,5},{3,6},{4,11},{5,8},{6,9},{7,10},{8,15},{9,12},{1... | collective-permute-start | bytes 245768 | tf_op jit(solution)/shard_map/while/body/eval_jaxpr/ppermute | solution.py:490
  167.3 13.1 %collective-permute-start = (bf16[64,4736]{1,0:T(8,128)(2,1)S(1)}, bf16[64,4736]{1,0:T(8,128)(2,1)S(1)}, u32[]{:S(2)}, u32[]{:S(2)}) collective-permute-start(bf16[64,4736]{1,0:T(8,128)(2,1)S(1)} %get-tuple-element.771), channel_id=1, source_target_pairs={{0,4},{1,5},{2,6},{3,7},{4,8},{5,9},{6,10},{7,11},{8,12},{9,13},{1... | collective-permute-start | bytes 1818632 | tf_op jit(solution)/shard_map/while/body/eval_jaxpr/ppermute | solution.py:490
  167.3 8.5 %collective-permute-start.1 = (bf16[64,640]{1,0:T(8,128)(2,1)S(1)}, bf16[64,640]{1,0:T(8,128)(2,1)}, u32[]{:S(2)}, u32[]{:S(2)}) collective-permute-start(bf16[64,640]{1,0:T(8,128)(2,1)S(1)} %get-tuple-element.772), channel_id=1, source_target_pairs={{0,5},{1,6},{2,7},{3,4},{4,9},{5,10},{6,11},{7,8},{8,13},{9,14},{1... | collective-permute-start | bytes 245768 | tf_op jit(solution)/shard_map/while/body/eval_jaxpr/ppermute | solution.py:490
  167.4 12.1 %collective-permute-start.2 = (bf16[64,640]{1,0:T(8,128)(2,1)S(1)}, bf16[64,640]{1,0:T(8,128)(2,1)}, u32[]{:S(2)}, u32[]{:S(2)}) collective-permute-start(bf16[64,640]{1,0:T(8,128)(2,1)S(1)} %get-tuple-element.772), channel_id=1, source_target_pairs={{0,6},{1,7},{2,4},{3,5},{4,10},{5,11},{6,8},{7,9},{8,14},{9,15},{1... | collective-permute-start | bytes 245768 | tf_op jit(solution)/shard_map/while/body/eval_jaxpr/ppermute | solution.py:490
  167.5 12.1 %collective-permute-start.3 = (bf16[64,640]{1,0:T(8,128)(2,1)S(1)}, bf16[64,640]{1,0:T(8,128)(2,1)}, u32[]{:S(2)}, u32[]{:S(2)}) collective-permute-start(bf16[64,640]{1,0:T(8,128)(2,1)S(1)} %get-tuple-element.772), channel_id=1, source_target_pairs={{0,7},{1,4},{2,5},{3,6},{4,11},{5,8},{6,9},{7,10},{8,15},{9,12},{1... | collective-permute-start | bytes 245768 | tf_op jit(solution)/shard_map/while/body/eval_jaxpr/ppermute | solution.py:490
  191.4 13.1 %collective-permute-start = (bf16[64,4736]{1,0:T(8,128)(2,1)S(1)}, bf16[64,4736]{1,0:T(8,128)(2,1)S(1)}, u32[]{:S(2)}, u32[]{:S(2)}) collective-permute-start(bf16[64,4736]{1,0:T(8,128)(2,1)S(1)} %get-tuple-element.771), channel_id=1, source_target_pairs={{0,4},{1,5},{2,6},{3,7},{4,8},{5,9},{6,10},{7,11},{8,12},{9,13},{1... | collective-permute-start | bytes 1818632 | tf_op jit(solution)/shard_map/while/body/eval_jaxpr/ppermute | solution.py:490
  191.5 8.6 %collective-permute-start.1 = (bf16[64,640]{1,0:T(8,128)(2,1)S(1)}, bf16[64,640]{1,0:T(8,128)(2,1)}, u32[]{:S(2)}, u32[]{:S(2)}) collective-permute-start(bf16[64,640]{1,0:T(8,128)(2,1)S(1)} %get-tuple-element.772), channel_id=1, source_target_pairs={{0,5},{1,6},{2,7},{3,4},{4,9},{5,10},{6,11},{7,8},{8,13},{9,14},{1... | collective-permute-start | bytes 245768 | tf_op jit(solution)/shard_map/while/body/eval_jaxpr/ppermute | solution.py:490
  191.6 12.2 %collective-permute-start.2 = (bf16[64,640]{1,0:T(8,128)(2,1)S(1)}, bf16[64,640]{1,0:T(8,128)(2,1)}, u32[]{:S(2)}, u32[]{:S(2)}) collective-permute-start(bf16[64,640]{1,0:T(8,128)(2,1)S(1)} %get-tuple-element.772), channel_id=1, source_target_pairs={{0,6},{1,7},{2,4},{3,5},{4,10},{5,11},{6,8},{7,9},{8,14},{9,15},{1... | collective-permute-start | bytes 245768 | tf_op jit(solution)/shard_map/while/body/eval_jaxpr/ppermute | solution.py:490
  191.6 12.1 %collective-permute-start.3 = (bf16[64,640]{1,0:T(8,128)(2,1)S(1)}, bf16[64,640]{1,0:T(8,128)(2,1)}, u32[]{:S(2)}, u32[]{:S(2)}) collective-permute-start(bf16[64,640]{1,0:T(8,128)(2,1)S(1)} %get-tuple-element.772), channel_id=1, source_target_pairs={{0,7},{1,4},{2,5},{3,6},{4,11},{5,8},{6,9},{7,10},{8,15},{9,12},{1... | collective-permute-start | bytes 245768 | tf_op jit(solution)/shard_map/while/body/eval_jaxpr/ppermute | solution.py:490
  215.6 13.1 %collective-permute-start = (bf16[64,4736]{1,0:T(8,128)(2,1)S(1)}, bf16[64,4736]{1,0:T(8,128)(2,1)S(1)}, u32[]{:S(2)}, u32[]{:S(2)}) collective-permute-start(bf16[64,4736]{1,0:T(8,128)(2,1)S(1)} %get-tuple-element.771), channel_id=1, source_target_pairs={{0,4},{1,5},{2,6},{3,7},{4,8},{5,9},{6,10},{7,11},{8,12},{9,13},{1... | collective-permute-start | bytes 1818632 | tf_op jit(solution)/shard_map/while/body/eval_jaxpr/ppermute | solution.py:490
  215.7 8.6 %collective-permute-start.1 = (bf16[64,640]{1,0:T(8,128)(2,1)S(1)}, bf16[64,640]{1,0:T(8,128)(2,1)}, u32[]{:S(2)}, u32[]{:S(2)}) collective-permute-start(bf16[64,640]{1,0:T(8,128)(2,1)S(1)} %get-tuple-element.772), channel_id=1, source_target_pairs={{0,5},{1,6},{2,7},{3,4},{4,9},{5,10},{6,11},{7,8},{8,13},{9,14},{1... | collective-permute-start | bytes 245768 | tf_op jit(solution)/shard_map/while/body/eval_jaxpr/ppermute | solution.py:490
  215.7 12.2 %collective-permute-start.2 = (bf16[64,640]{1,0:T(8,128)(2,1)S(1)}, bf16[64,640]{1,0:T(8,128)(2,1)}, u32[]{:S(2)}, u32[]{:S(2)}) collective-permute-start(bf16[64,640]{1,0:T(8,128)(2,1)S(1)} %get-tuple-element.772), channel_id=1, source_target_pairs={{0,6},{1,7},{2,4},{3,5},{4,10},{5,11},{6,8},{7,9},{8,14},{9,15},{1... | collective-permute-start | bytes 245768 | tf_op jit(solution)/shard_map/while/body/eval_jaxpr/ppermute | solution.py:490
  215.8 12.1 %collective-permute-start.3 = (bf16[64,640]{1,0:T(8,128)(2,1)S(1)}, bf16[64,640]{1,0:T(8,128)(2,1)}, u32[]{:S(2)}, u32[]{:S(2)}) collective-permute-start(bf16[64,640]{1,0:T(8,128)(2,1)S(1)} %get-tuple-element.772), channel_id=1, source_target_pairs={{0,7},{1,4},{2,5},{3,6},{4,11},{5,8},{6,9},{7,10},{8,15},{9,12},{1... | collective-permute-start | bytes 245768 | tf_op jit(solution)/shard_map/while/body/eval_jaxpr/ppermute | solution.py:490
  239.9 13.1 %collective-permute-start = (bf16[64,4736]{1,0:T(8,128)(2,1)S(1)}, bf16[64,4736]{1,0:T(8,128)(2,1)S(1)}, u32[]{:S(2)}, u32[]{:S(2)}) collective-permute-start(bf16[64,4736]{1,0:T(8,128)(2,1)S(1)} %get-tuple-element.771), channel_id=1, source_target_pairs={{0,4},{1,5},{2,6},{3,7},{4,8},{5,9},{6,10},{7,11},{8,12},{9,13},{1... | collective-permute-start | bytes 1818632 | tf_op jit(solution)/shard_map/while/body/eval_jaxpr/ppermute | solution.py:490
  239.9 8.6 %collective-permute-start.1 = (bf16[64,640]{1,0:T(8,128)(2,1)S(1)}, bf16[64,640]{1,0:T(8,128)(2,1)}, u32[]{:S(2)}, u32[]{:S(2)}) collective-permute-start(bf16[64,640]{1,0:T(8,128)(2,1)S(1)} %get-tuple-element.772), channel_id=1, source_target_pairs={{0,5},{1,6},{2,7},{3,4},{4,9},{5,10},{6,11},{7,8},{8,13},{9,14},{1... | collective-permute-start | bytes 245768 | tf_op jit(solution)/shard_map/while/body/eval_jaxpr/ppermute | solution.py:490
  240.0 12.2 %collective-permute-start.2 = (bf16[64,640]{1,0:T(8,128)(2,1)S(1)}, bf16[64,640]{1,0:T(8,128)(2,1)}, u32[]{:S(2)}, u32[]{:S(2)}) collective-permute-start(bf16[64,640]{1,0:T(8,128)(2,1)S(1)} %get-tuple-element.772), channel_id=1, source_target_pairs={{0,6},{1,7},{2,4},{3,5},{4,10},{5,11},{6,8},{7,9},{8,14},{9,15},{1... | collective-permute-start | bytes 245768 | tf_op jit(solution)/shard_map/while/body/eval_jaxpr/ppermute | solution.py:490
  240.1 12.1 %collective-permute-start.3 = (bf16[64,640]{1,0:T(8,128)(2,1)S(1)}, bf16[64,640]{1,0:T(8,128)(2,1)}, u32[]{:S(2)}, u32[]{:S(2)}) collective-permute-start(bf16[64,640]{1,0:T(8,128)(2,1)S(1)} %get-tuple-element.772), channel_id=1, source_target_pairs={{0,7},{1,4},{2,5},{3,6},{4,11},{5,8},{6,9},{7,10},{8,15},{9,12},{1... | collective-permute-start | bytes 245768 | tf_op jit(solution)/shard_map/while/body/eval_jaxpr/ppermute | solution.py:490
  264.5 13.1 %collective-permute-start = (bf16[64,4736]{1,0:T(8,128)(2,1)S(1)}, bf16[64,4736]{1,0:T(8,128)(2,1)S(1)}, u32[]{:S(2)}, u32[]{:S(2)}) collective-permute-start(bf16[64,4736]{1,0:T(8,128)(2,1)S(1)} %get-tuple-element.771), channel_id=1, source_target_pairs={{0,4},{1,5},{2,6},{3,7},{4,8},{5,9},{6,10},{7,11},{8,12},{9,13},{1... | collective-permute-start | bytes 1818632 | tf_op jit(solution)/shard_map/while/body/eval_jaxpr/ppermute | solution.py:490
  264.5 8.6 %collective-permute-start.1 = (bf16[64,640]{1,0:T(8,128)(2,1)S(1)}, bf16[64,640]{1,0:T(8,128)(2,1)}, u32[]{:S(2)}, u32[]{:S(2)}) collective-permute-start(bf16[64,640]{1,0:T(8,128)(2,1)S(1)} %get-tuple-element.772), channel_id=1, source_target_pairs={{0,5},{1,6},{2,7},{3,4},{4,9},{5,10},{6,11},{7,8},{8,13},{9,14},{1... | collective-permute-start | bytes 245768 | tf_op jit(solution)/shard_map/while/body/eval_jaxpr/ppermute | solution.py:490
  264.6 12.2 %collective-permute-start.2 = (bf16[64,640]{1,0:T(8,128)(2,1)S(1)}, bf16[64,640]{1,0:T(8,128)(2,1)}, u32[]{:S(2)}, u32[]{:S(2)}) collective-permute-start(bf16[64,640]{1,0:T(8,128)(2,1)S(1)} %get-tuple-element.772), channel_id=1, source_target_pairs={{0,6},{1,7},{2,4},{3,5},{4,10},{5,11},{6,8},{7,9},{8,14},{9,15},{1... | collective-permute-start | bytes 245768 | tf_op jit(solution)/shard_map/while/body/eval_jaxpr/ppermute | solution.py:490
  264.7 12.1 %collective-permute-start.3 = (bf16[64,640]{1,0:T(8,128)(2,1)S(1)}, bf16[64,640]{1,0:T(8,128)(2,1)}, u32[]{:S(2)}, u32[]{:S(2)}) collective-permute-start(bf16[64,640]{1,0:T(8,128)(2,1)S(1)} %get-tuple-element.772), channel_id=1, source_target_pairs={{0,7},{1,4},{2,5},{3,6},{4,11},{5,8},{6,9},{7,10},{8,15},{9,12},{1... | collective-permute-start | bytes 245768 | tf_op jit(solution)/shard_map/while/body/eval_jaxpr/ppermute | solution.py:490
  279.0 17.8 %collective-permute-start = (bf16[64,4736]{1,0:T(8,128)(2,1)S(1)}, bf16[64,4736]{1,0:T(8,128)(2,1)S(1)}, u32[]{:S(2)}, u32[]{:S(2)}) collective-permute-start(bf16[64,4736]{1,0:T(8,128)(2,1)S(1)} %get-tuple-element.771), channel_id=1, source_target_pairs={{0,4},{1,5},{2,6},{3,7},{4,8},{5,9},{6,10},{7,11},{8,12},{9,13},{1... | collective-permute-start | bytes 1818632 | tf_op jit(solution)/shard_map/while/body/eval_jaxpr/ppermute | solution.py:490
  284.1 8.0 %collective-permute-start.1 = (bf16[64,640]{1,0:T(8,128)(2,1)S(1)}, bf16[64,640]{1,0:T(8,128)(2,1)}, u32[]{:S(2)}, u32[]{:S(2)}) collective-permute-start(bf16[64,640]{1,0:T(8,128)(2,1)S(1)} %get-tuple-element.772), channel_id=1, source_target_pairs={{0,5},{1,6},{2,7},{3,4},{4,9},{5,10},{6,11},{7,8},{8,13},{9,14},{1... | collective-permute-start | bytes 245768 | tf_op jit(solution)/shard_map/while/body/eval_jaxpr/ppermute | solution.py:490
  285.6 10.5 %collective-permute-start.2 = (bf16[64,640]{1,0:T(8,128)(2,1)S(1)}, bf16[64,640]{1,0:T(8,128)(2,1)}, u32[]{:S(2)}, u32[]{:S(2)}) collective-permute-start(bf16[64,640]{1,0:T(8,128)(2,1)S(1)} %get-tuple-element.772), channel_id=1, source_target_pairs={{0,6},{1,7},{2,4},{3,5},{4,10},{5,11},{6,8},{7,9},{8,14},{9,15},{1... | collective-permute-start | bytes 245768 | tf_op jit(solution)/shard_map/while/body/eval_jaxpr/ppermute | solution.py:490
  287.0 9.0 %collective-permute-start.3 = (bf16[64,640]{1,0:T(8,128)(2,1)S(1)}, bf16[64,640]{1,0:T(8,128)(2,1)}, u32[]{:S(2)}, u32[]{:S(2)}) collective-permute-start(bf16[64,640]{1,0:T(8,128)(2,1)S(1)} %get-tuple-element.772), channel_id=1, source_target_pairs={{0,7},{1,4},{2,5},{3,6},{4,11},{5,8},{6,9},{7,10},{8,15},{9,12},{1... | collective-permute-start | bytes 245768 | tf_op jit(solution)/shard_map/while/body/eval_jaxpr/ppermute | solution.py:490
  298.1 21.3 %collective-permute-start = (bf16[64,4736]{1,0:T(8,128)(2,1)S(1)}, bf16[64,4736]{1,0:T(8,128)(2,1)S(1)}, u32[]{:S(2)}, u32[]{:S(2)}) collective-permute-start(bf16[64,4736]{1,0:T(8,128)(2,1)S(1)} %get-tuple-element.771), channel_id=1, source_target_pairs={{0,4},{1,5},{2,6},{3,7},{4,8},{5,9},{6,10},{7,11},{8,12},{9,13},{1... | collective-permute-start | bytes 1818632 | tf_op jit(solution)/shard_map/while/body/eval_jaxpr/ppermute | solution.py:490
  298.2 16.4 %collective-permute-start.1 = (bf16[64,640]{1,0:T(8,128)(2,1)S(1)}, bf16[64,640]{1,0:T(8,128)(2,1)}, u32[]{:S(2)}, u32[]{:S(2)}) collective-permute-start(bf16[64,640]{1,0:T(8,128)(2,1)S(1)} %get-tuple-element.772), channel_id=1, source_target_pairs={{0,5},{1,6},{2,7},{3,4},{4,9},{5,10},{6,11},{7,8},{8,13},{9,14},{1... | collective-permute-start | bytes 245768 | tf_op jit(solution)/shard_map/while/body/eval_jaxpr/ppermute | solution.py:490
  309.8 9.3 %collective-permute-start.2 = (bf16[64,640]{1,0:T(8,128)(2,1)S(1)}, bf16[64,640]{1,0:T(8,128)(2,1)}, u32[]{:S(2)}, u32[]{:S(2)}) collective-permute-start(bf16[64,640]{1,0:T(8,128)(2,1)S(1)} %get-tuple-element.772), channel_id=1, source_target_pairs={{0,6},{1,7},{2,4},{3,5},{4,10},{5,11},{6,8},{7,9},{8,14},{9,15},{1... | collective-permute-start | bytes 245768 | tf_op jit(solution)/shard_map/while/body/eval_jaxpr/ppermute | solution.py:490
  311.7 7.7 %collective-permute-start.3 = (bf16[64,640]{1,0:T(8,128)(2,1)S(1)}, bf16[64,640]{1,0:T(8,128)(2,1)}, u32[]{:S(2)}, u32[]{:S(2)}) collective-permute-start(bf16[64,640]{1,0:T(8,128)(2,1)S(1)} %get-tuple-element.772), channel_id=1, source_target_pairs={{0,7},{1,4},{2,5},{3,6},{4,11},{5,8},{6,9},{7,10},{8,15},{9,12},{1... | collective-permute-start | bytes 245768 | tf_op jit(solution)/shard_map/while/body/eval_jaxpr/ppermute | solution.py:490
  320.9 20.7 %collective-permute-start = (bf16[64,4736]{1,0:T(8,128)(2,1)S(1)}, bf16[64,4736]{1,0:T(8,128)(2,1)S(1)}, u32[]{:S(2)}, u32[]{:S(2)}) collective-permute-start(bf16[64,4736]{1,0:T(8,128)(2,1)S(1)} %get-tuple-element.771), channel_id=1, source_target_pairs={{0,4},{1,5},{2,6},{3,7},{4,8},{5,9},{6,10},{7,11},{8,12},{9,13},{1... | collective-permute-start | bytes 1818632 | tf_op jit(solution)/shard_map/while/body/eval_jaxpr/ppermute | solution.py:490
  321.7 17.1 %collective-permute-start.1 = (bf16[64,640]{1,0:T(8,128)(2,1)S(1)}, bf16[64,640]{1,0:T(8,128)(2,1)}, u32[]{:S(2)}, u32[]{:S(2)}) collective-permute-start(bf16[64,640]{1,0:T(8,128)(2,1)S(1)} %get-tuple-element.772), channel_id=1, source_target_pairs={{0,5},{1,6},{2,7},{3,4},{4,9},{5,10},{6,11},{7,8},{8,13},{9,14},{1... | collective-permute-start | bytes 245768 | tf_op jit(solution)/shard_map/while/body/eval_jaxpr/ppermute | solution.py:490
  324.1 14.6 %collective-permute-start.2 = (bf16[64,640]{1,0:T(8,128)(2,1)S(1)}, bf16[64,640]{1,0:T(8,128)(2,1)}, u32[]{:S(2)}, u32[]{:S(2)}) collective-permute-start(bf16[64,640]{1,0:T(8,128)(2,1)S(1)} %get-tuple-element.772), channel_id=1, source_target_pairs={{0,6},{1,7},{2,4},{3,5},{4,10},{5,11},{6,8},{7,9},{8,14},{9,15},{1... | collective-permute-start | bytes 245768 | tf_op jit(solution)/shard_map/while/body/eval_jaxpr/ppermute | solution.py:490
  335.6 6.0 %collective-permute-start.3 = (bf16[64,640]{1,0:T(8,128)(2,1)S(1)}, bf16[64,640]{1,0:T(8,128)(2,1)}, u32[]{:S(2)}, u32[]{:S(2)}) collective-permute-start(bf16[64,640]{1,0:T(8,128)(2,1)S(1)} %get-tuple-element.772), channel_id=1, source_target_pairs={{0,7},{1,4},{2,5},{3,6},{4,11},{5,8},{6,9},{7,10},{8,15},{9,12},{1... | collective-permute-start | bytes 245768 | tf_op jit(solution)/shard_map/while/body/eval_jaxpr/ppermute | solution.py:490
  343.0 23.2 %collective-permute-start = (bf16[64,4736]{1,0:T(8,128)(2,1)S(1)}, bf16[64,4736]{1,0:T(8,128)(2,1)S(1)}, u32[]{:S(2)}, u32[]{:S(2)}) collective-permute-start(bf16[64,4736]{1,0:T(8,128)(2,1)S(1)} %get-tuple-element.771), channel_id=1, source_target_pairs={{0,4},{1,5},{2,6},{3,7},{4,8},{5,9},{6,10},{7,11},{8,12},{9,13},{1... | collective-permute-start | bytes 1818632 | tf_op jit(solution)/shard_map/while/body/eval_jaxpr/ppermute | solution.py:490
  344.9 18.5 %collective-permute-start.1 = (bf16[64,640]{1,0:T(8,128)(2,1)S(1)}, bf16[64,640]{1,0:T(8,128)(2,1)}, u32[]{:S(2)}, u32[]{:S(2)}) collective-permute-start(bf16[64,640]{1,0:T(8,128)(2,1)S(1)} %get-tuple-element.772), channel_id=1, source_target_pairs={{0,5},{1,6},{2,7},{3,4},{4,9},{5,10},{6,11},{7,8},{8,13},{9,14},{1... | collective-permute-start | bytes 245768 | tf_op jit(solution)/shard_map/while/body/eval_jaxpr/ppermute | solution.py:490
  346.8 16.6 %collective-permute-start.2 = (bf16[64,640]{1,0:T(8,128)(2,1)S(1)}, bf16[64,640]{1,0:T(8,128)(2,1)}, u32[]{:S(2)}, u32[]{:S(2)}) collective-permute-start(bf16[64,640]{1,0:T(8,128)(2,1)S(1)} %get-tuple-element.772), channel_id=1, source_target_pairs={{0,6},{1,7},{2,4},{3,5},{4,10},{5,11},{6,8},{7,9},{8,14},{9,15},{1... | collective-permute-start | bytes 245768 | tf_op jit(solution)/shard_map/while/body/eval_jaxpr/ppermute | solution.py:490
  349.8 16.4 %collective-permute-start.3 = (bf16[64,640]{1,0:T(8,128)(2,1)S(1)}, bf16[64,640]{1,0:T(8,128)(2,1)}, u32[]{:S(2)}, u32[]{:S(2)}) collective-permute-start(bf16[64,640]{1,0:T(8,128)(2,1)S(1)} %get-tuple-element.772), channel_id=1, source_target_pairs={{0,7},{1,4},{2,5},{3,6},{4,11},{5,8},{6,9},{7,10},{8,15},{9,12},{1... | collective-permute-start | bytes 245768 | tf_op jit(solution)/shard_map/while/body/eval_jaxpr/ppermute | solution.py:490
  367.6 16.0 %collective-permute-start = (bf16[64,4736]{1,0:T(8,128)(2,1)S(1)}, bf16[64,4736]{1,0:T(8,128)(2,1)S(1)}, u32[]{:S(2)}, u32[]{:S(2)}) collective-permute-start(bf16[64,4736]{1,0:T(8,128)(2,1)S(1)} %get-tuple-element.771), channel_id=1, source_target_pairs={{0,4},{1,5},{2,6},{3,7},{4,8},{5,9},{6,10},{7,11},{8,12},{9,13},{1... | collective-permute-start | bytes 1818632 | tf_op jit(solution)/shard_map/while/body/eval_jaxpr/ppermute | solution.py:490
  369.6 8.3 %collective-permute-start.1 = (bf16[64,640]{1,0:T(8,128)(2,1)S(1)}, bf16[64,640]{1,0:T(8,128)(2,1)}, u32[]{:S(2)}, u32[]{:S(2)}) collective-permute-start(bf16[64,640]{1,0:T(8,128)(2,1)S(1)} %get-tuple-element.772), channel_id=1, source_target_pairs={{0,5},{1,6},{2,7},{3,4},{4,9},{5,10},{6,11},{7,8},{8,13},{9,14},{1... | collective-permute-start | bytes 245768 | tf_op jit(solution)/shard_map/while/body/eval_jaxpr/ppermute | solution.py:490
  371.4 7.8 %collective-permute-start.2 = (bf16[64,640]{1,0:T(8,128)(2,1)S(1)}, bf16[64,640]{1,0:T(8,128)(2,1)}, u32[]{:S(2)}, u32[]{:S(2)}) collective-permute-start(bf16[64,640]{1,0:T(8,128)(2,1)S(1)} %get-tuple-element.772), channel_id=1, source_target_pairs={{0,6},{1,7},{2,4},{3,5},{4,10},{5,11},{6,8},{7,9},{8,14},{9,15},{1... | collective-permute-start | bytes 245768 | tf_op jit(solution)/shard_map/while/body/eval_jaxpr/ppermute | solution.py:490
  374.4 5.8 %collective-permute-start.3 = (bf16[64,640]{1,0:T(8,128)(2,1)S(1)}, bf16[64,640]{1,0:T(8,128)(2,1)}, u32[]{:S(2)}, u32[]{:S(2)}) collective-permute-start(bf16[64,640]{1,0:T(8,128)(2,1)S(1)} %get-tuple-element.772), channel_id=1, source_target_pairs={{0,7},{1,4},{2,5},{3,6},{4,11},{5,8},{6,9},{7,10},{8,15},{9,12},{1... | collective-permute-start | bytes 245768 | tf_op jit(solution)/shard_map/while/body/eval_jaxpr/ppermute | solution.py:490
  385.0 22.0 %collective-permute-start = (bf16[64,4736]{1,0:T(8,128)(2,1)S(1)}, bf16[64,4736]{1,0:T(8,128)(2,1)S(1)}, u32[]{:S(2)}, u32[]{:S(2)}) collective-permute-start(bf16[64,4736]{1,0:T(8,128)(2,1)S(1)} %get-tuple-element.771), channel_id=1, source_target_pairs={{0,4},{1,5},{2,6},{3,7},{4,8},{5,9},{6,10},{7,11},{8,12},{9,13},{1... | collective-permute-start | bytes 1818632 | tf_op jit(solution)/shard_map/while/body/eval_jaxpr/ppermute | solution.py:490
  387.6 13.3 %collective-permute-start.1 = (bf16[64,640]{1,0:T(8,128)(2,1)S(1)}, bf16[64,640]{1,0:T(8,128)(2,1)}, u32[]{:S(2)}, u32[]{:S(2)}) collective-permute-start(bf16[64,640]{1,0:T(8,128)(2,1)S(1)} %get-tuple-element.772), channel_id=1, source_target_pairs={{0,5},{1,6},{2,7},{3,4},{4,9},{5,10},{6,11},{7,8},{8,13},{9,14},{1... | collective-permute-start | bytes 245768 | tf_op jit(solution)/shard_map/while/body/eval_jaxpr/ppermute | solution.py:490
  391.1 9.8 %collective-permute-start.2 = (bf16[64,640]{1,0:T(8,128)(2,1)S(1)}, bf16[64,640]{1,0:T(8,128)(2,1)}, u32[]{:S(2)}, u32[]{:S(2)}) collective-permute-start(bf16[64,640]{1,0:T(8,128)(2,1)S(1)} %get-tuple-element.772), channel_id=1, source_target_pairs={{0,6},{1,7},{2,4},{3,5},{4,10},{5,11},{6,8},{7,9},{8,14},{9,15},{1... | collective-permute-start | bytes 245768 | tf_op jit(solution)/shard_map/while/body/eval_jaxpr/ppermute | solution.py:490
  394.4 6.8 %collective-permute-start.3 = (bf16[64,640]{1,0:T(8,128)(2,1)S(1)}, bf16[64,640]{1,0:T(8,128)(2,1)}, u32[]{:S(2)}, u32[]{:S(2)}) collective-permute-start(bf16[64,640]{1,0:T(8,128)(2,1)S(1)} %get-tuple-element.772), channel_id=1, source_target_pairs={{0,7},{1,4},{2,5},{3,6},{4,11},{5,8},{6,9},{7,10},{8,15},{9,12},{1... | collective-permute-start | bytes 245768 | tf_op jit(solution)/shard_map/while/body/eval_jaxpr/ppermute | solution.py:490

commit v6 on v5

--- a/solution.py
+++ b/solution.py
@@ -9,7 +9,7 @@
 
 ROWS = 16
 LANES = 128
-COLS = 1024
+COLS = 512
 DEPTH = 1024
 ANY = pl.BlockSpec(memory_space=pl.ANY)
 HBM = pl.BlockSpec(memory_space=pltpu.HBM)
@@ -35,6 +35,59 @@
     )
     tail = jnp.where(lane == extra, high, jnp.where(lane == extra + 1, squares - high, tail))
     return total[:, :rank].astype(jnp.bfloat16), tail.astype(jnp.bfloat16)
+
+
+def project(onward, partial, gain, weight, copy):
+    units = onward.shape[0]
+    rank = partial.shape[1] - LANES
+    channels = weight.shape[1]
+    depth = min(DEPTH, channels)
+    total = jnp.zeros((units, weight.shape[0]), jnp.float32)
+    squares = jnp.zeros((units, 1), jnp.float32)
+    for k in range(channels // depth):
+        span = pl.ds(k * depth, depth)
+        wide = onward[:, span].astype(jnp.float32)
+        squares += jnp.sum(wide * wide, axis=1, keepdims=True)
+        scaled = (wide * gain[:, span]).astype(jnp.bfloat16)
+        copy(k).wait()
+        total += lax.dot_general(
+            scaled,
+            weight[:, span],
+            (((1,), (1,)), ((), ())),
+            preferred_element_type=jnp.float32,
+        )
+    low, tail = finish(total, squares, rank)
+    onward[:, channels : channels + rank] = low
+    onward[:, channels + rank :] = tail
+    partial[:, :rank] = low
+    partial[:, rank:] = tail
+
+
+def open_kernel(place, inputs, gain, own_weight, onward, partial, weight, input_sem, weight_sem):
+    steps = inputs.shape[0]
+    channels = weight.shape[1]
+    depth = min(DEPTH, channels)
+
+    def weight_copy(k):
+        span = pl.ds(k * depth, depth)
+        return pltpu.make_async_copy(own_weight.at[:, span], weight.at[:, span], weight_sem.at[k])
+
+    def input_copy(t):
+        return pltpu.make_async_copy(
+            inputs.at[t, pl.ds(0, ROWS)],
+            onward.at[pl.ds(t * ROWS, ROWS), pl.ds(0, channels)],
+            input_sem.at[t],
+        )
+
+    @pl.when(place[0] == 0)
+    def _():
+        for t in range(steps):
+            input_copy(t).start()
+        for k in range(channels // depth):
+            weight_copy(k).start()
+        for t in range(steps):
+            input_copy(t).wait()
+        project(onward, partial, gain, weight, weight_copy)
 
 
 def step_kernel(width, layers, peers, *refs):
@@ -294,25 +347,7 @@
 
     @pl.when(meta[3] == 1)
     def _():
-        total = jnp.zeros((units, weight.shape[0]), jnp.float32)
-        squares = jnp.zeros((units, 1), jnp.float32)
-        for k in range(channels // depth):
-            span = pl.ds(k * depth, depth)
-            wide = onward[:, span].astype(jnp.float32)
-            squares += jnp.sum(wide * wide, axis=1, keepdims=True)
-            scaled = (wide * next_gain[:, span]).astype(jnp.bfloat16)
-            weight_copy(k).wait()
-            total += lax.dot_general(
-                scaled,
-                weight[:, span],
-                (((1,), (1,)), ((), ())),
-                preferred_element_type=jnp.float32,
-            )
-        low, tail = finish(total, squares, rank)
-        onward[:, channels : channels + rank] = low
-        onward[:, channels + rank :] = tail
-        partial[:, :rank] = low
-        partial[:, rank:] = tail
+        project(onward, partial, next_gain, weight, weight_copy)
 
     @pl.when(meta[0] == 1)
     def _():
@@ -393,7 +428,8 @@
     turns = units + holders - 1
     plan = jnp.concatenate([swap_plan.reshape(-1), evict_plan.reshape(-1)])
     down = [((i + 1) % holders, i) for i in range(holders)]
-    weight = lax.ppermute(jnp.swapaxes(x_weight[0], 0, 1), "section", down)
+    own_weight = jnp.swapaxes(x_weight[0], 0, 1)
+    weight = lax.ppermute(own_weight, "section", down)
     next_gain = lax.ppermute(gain, "section", down)
     rates = (-LOG2E * jnp.exp(a_log[0])).astype(jnp.bfloat16)
     place = section.astype(jnp.int32)[None]
@@ -502,11 +538,25 @@
         pick_kernel, out_shape=moved_shape, in_specs=[SMEM, SMEM, VMEM], out_specs=VMEM, name="pick"
     )(place, plan, pool)
     landed = swap(picked)
-    *kept, block, partial = empty(
-        [state_shape, mixed_shape, moved_shape, block_shape, partial_shape]
-    )
-    blocks = [block] + [partial] * (peers - 1)
-    blocks, kept = lax.fori_loop(-1, turns - 1, turn, (blocks, kept))
+    block, partial = pl.pallas_call(
+        open_kernel,
+        out_shape=[block_shape, partial_shape],
+        in_specs=[SMEM, HBM, VMEM, HBM],
+        out_specs=[VMEM, VMEM],
+        scratch_shapes=[
+            pltpu.VMEM(weight.shape, jnp.bfloat16),
+            pltpu.SemaphoreType.DMA((steps,)),
+            pltpu.SemaphoreType.DMA((channels // depth,)),
+        ],
+        compiler_params=pltpu.CompilerParams(vmem_limit_bytes=24 * 2**20),
+        name="open",
+    )(place, inputs, gain, own_weight)
+    blocks = [block]
+    for shift in range(1, peers):
+        route = [(i, (i + shift) % peers) for i in range(peers)]
+        blocks.append(lax.ppermute(partial, "tensor", route))
+    kept = list(empty([state_shape, mixed_shape, moved_shape]))
+    blocks, kept = lax.fori_loop(0, turns - 1, turn, (blocks, kept))
     _, _, final, mixed, leaving = step(meta_of(turns - 1), blocks, *kept)
     stored = pl.pallas_call(
         keep_kernel,

time: 441 us -> 414 us (0.939)
  waiting for transfers between devices: 186 us -> 173 us
  starting transfers between devices: 112 us -> 106 us
    ppermute x60 -> x56, starting transfers between devices: 102 us -> 93 us  [send(): blocks.append(lax.ppermute(partial if shift else block, axes, route))]
    ppermute x60 -> x56, waiting for transfers between devices: 139 us -> 131 us  [send(): blocks.append(lax.ppermute(partial if shift else block, axes, route))]
    pallas_call x16 -> x15, Pallas kernels: 100 us -> 92 us  [step(): pl.pallas_call(functools.partial(step_kernel, width, holders, peers), out...]
    ppermute x1 -> x4, starting transfers between devices: 3.39 us -> 8.95 us  [the longest x3 5.57 us: shards(): blocks.append(lax.ppermute(partial, 'tensor', route))]
    ppermute x1, waiting for transfers between devices: 46.1 us -> 40.9 us  [shards(): next_gain = lax.ppermute(gain, 'section', down)]
  transfers between devices with their start and end apart: 63 -> 62, of which waited for: 42 -> 39; matrix products, arithmetic and copies ran while one was open for 1% -> 0% of each run, Pallas kernels for 1% -> 1%
where the time goes in v6:
time: 414 us
  waiting for transfers between devices  173 us (42%)
  starting transfers between devices  106 us (26%)
  Pallas kernels  101 us (24%)
  blocking collectives  27.9 us (7%)
  local copies, waits for them, and re-layouts  5.28 us (1%)
    ppermute x56, waiting for transfers between devices, send(): blocks.append(lax.ppermute(partial if shift else block, axes, route))  131 us
    ppermute x56, starting transfers between devices, send(): blocks.append(lax.ppermute(partial if shift else block, axes, route))  93 us
    pallas_call x15, Pallas kernels, step(): pl.pallas_call(functools.partial(step_kernel, width, holders, peers), out...  92 us
    ppermute x1, waiting for transfers between devices, shards(): next_gain = lax.ppermute(gain, 'section', down)  40.9 us
    all_to_all x1, blocking collectives, swap(): lax.all_to_all(block, 'section', split_axis=0, concat_axis=0, tiled=True)  27.9 us
  transfers between devices with their start and end apart: 62, of which 39 were waited for; matrix products, arithmetic and copies ran while one was open for 0% of the time, Pallas kernels for 1%

profile of v6, /device:TPU:0, one launch (start us, length us, event | category | flops | bytes accessed | tf_op | source)
XLA Modules:
  0.0 413.6 jit_solution(8126901557128106019)
XLA Ops:
  0.6 3.4 collective-permute-start.8
  5.8 2.3 pick.1
  8.1 3.6 all-to-all-start
  11.7 2.3 copy-done
  14.0 3.9 open.1
  17.9 1.6 collective-permute-start.4
  19.5 2.6 collective-permute-start.5
  23.6 40.9 %collective-permute-done.7.refs_14_ = f32[1,4096]{1,0:T(1,128)S(1)} collective-permute-done((f32[1,4096]{1,0:T(1,128)S(1)}, f32[1,4096]{1,0:T(1,128)S(1)}, u32[]{:S(2)}, u32[]{:S(2)}) %collective-permute-start.7) | collective-permute-done | bytes 16416 | tf_op jit(solution)/shard_map/ppermute | solution.py:433
  65.3 315.9 %while.26 = (s32[]{:T(128)}, bf16[64,4736]{1,0:T(8,128)(2,1)S(1)}, bf16[64,640]{1,0:T(8,128)(2,1)S(1)}, bf16[64,640]{1,0:T(8,128)(2,1)S(1)}, bf16[64,640]{1,0:T(...) while((s32[]{:T(128)}, bf16[64,4736]{1,0:T(8,128)(2,1)S(1)}, ...), condition=%wide.region_1.2_spmd, body=%wide.region_0.1_spmd.sunk | while | flops 704643072 | bytes 20185652 | solution.py:559
  65.5 10.4 %step.8 = (bf16[64,4736]{1,0:T(8,128)(2,1)S(1)}, bf16[64,640]{1,0:T(8,128)(2,1)S(1)}, f32[1,128,16,4096]{3,2,1,0:T(8,128)}, bf16[1,4,128,4096]{3,2,1,0:T(8,128)(2,1)}, bf16[8,16,4096]{2,1,0:T(8,128)(2,1)S(1)}) custom-call(s32[5]{0:T(128)S(1)} %stack.87.refs_0_, ...), custom_call_target="tpu_custom_call", output_to_operand_aliasing={{2}: (17, {}), {3}: (18, {}), {4}: (19, {})} | custom-call | flops 704643072 | bytes 16777216 | tf_op jit(solution)/shard_map/while/body/eval_jaxpr/step/pallas_call | solution.py:456
  76.1 8.2 %collective-permute-done.1 = bf16[64,640]{1,0:T(8,128)(2,1)S(1)} collective-permute-done((bf16[64,640]{1,0:T(8,128)(2,1)S(1)}, bf16[64,640]{1,0:T(8,128)(2,1)S(1)}, u32[]{:S(2)}, u32[]{:S(2)}) %collective-permute-start.1) | collective-permute-done | bytes 81952 | tf_op jit(solution)/shard_map/while/body/eval_jaxpr/ppermute | solution.py:526
  84.4 3.7 collective-permute-done.2
  89.0 10.4 %step.8 = (bf16[64,4736]{1,0:T(8,128)(2,1)S(1)}, bf16[64,640]{1,0:T(8,128)(2,1)S(1)}, f32[1,128,16,4096]{3,2,1,0:T(8,128)}, bf16[1,4,128,4096]{3,2,1,0:T(8,128)(2,1)}, bf16[8,16,4096]{2,1,0:T(8,128)(2,1)S(1)}) custom-call(s32[5]{0:T(128)S(1)} %stack.87.refs_0_, ...), custom_call_target="tpu_custom_call", output_to_operand_aliasing={{2}: (17, {}), {3}: (18, {}), {4}: (19, {})} | custom-call | flops 704643072 | bytes 16777216 | tf_op jit(solution)/shard_map/while/body/eval_jaxpr/step/pallas_call | solution.py:456
  99.7 8.3 %collective-permute-done.1 = bf16[64,640]{1,0:T(8,128)(2,1)S(1)} collective-permute-done((bf16[64,640]{1,0:T(8,128)(2,1)S(1)}, bf16[64,640]{1,0:T(8,128)(2,1)S(1)}, u32[]{:S(2)}, u32[]{:S(2)}) %collective-permute-start.1) | collective-permute-done | bytes 81952 | tf_op jit(solution)/shard_map/while/body/eval_jaxpr/ppermute | solution.py:526
  107.9 3.7 collective-permute-done.2
  112.6 10.5 %step.8 = (bf16[64,4736]{1,0:T(8,128)(2,1)S(1)}, bf16[64,640]{1,0:T(8,128)(2,1)S(1)}, f32[1,128,16,4096]{3,2,1,0:T(8,128)}, bf16[1,4,128,4096]{3,2,1,0:T(8,128)(2,1)}, bf16[8,16,4096]{2,1,0:T(8,128)(2,1)S(1)}) custom-call(s32[5]{0:T(128)S(1)} %stack.87.refs_0_, ...), custom_call_target="tpu_custom_call", output_to_operand_aliasing={{2}: (17, {}), {3}: (18, {}), {4}: (19, {})} | custom-call | flops 704643072 | bytes 16777216 | tf_op jit(solution)/shard_map/while/body/eval_jaxpr/step/pallas_call | solution.py:456
  123.3 8.2 %collective-permute-done.1 = bf16[64,640]{1,0:T(8,128)(2,1)S(1)} collective-permute-done((bf16[64,640]{1,0:T(8,128)(2,1)S(1)}, bf16[64,640]{1,0:T(8,128)(2,1)S(1)}, u32[]{:S(2)}, u32[]{:S(2)}) %collective-permute-start.1) | collective-permute-done | bytes 81952 | tf_op jit(solution)/shard_map/while/body/eval_jaxpr/ppermute | solution.py:526
  131.6 3.7 collective-permute-done.2
  136.2 10.4 %step.8 = (bf16[64,4736]{1,0:T(8,128)(2,1)S(1)}, bf16[64,640]{1,0:T(8,128)(2,1)S(1)}, f32[1,128,16,4096]{3,2,1,0:T(8,128)}, bf16[1,4,128,4096]{3,2,1,0:T(8,128)(2,1)}, bf16[8,16,4096]{2,1,0:T(8,128)(2,1)S(1)}) custom-call(s32[5]{0:T(128)S(1)} %stack.87.refs_0_, ...), custom_call_target="tpu_custom_call", output_to_operand_aliasing={{2}: (17, {}), {3}: (18, {}), {4}: (19, {})} | custom-call | flops 704643072 | bytes 16777216 | tf_op jit(solution)/shard_map/while/body/eval_jaxpr/step/pallas_call | solution.py:456
  146.9 8.3 %collective-permute-done.1 = bf16[64,640]{1,0:T(8,128)(2,1)S(1)} collective-permute-done((bf16[64,640]{1,0:T(8,128)(2,1)S(1)}, bf16[64,640]{1,0:T(8,128)(2,1)S(1)}, u32[]{:S(2)}, u32[]{:S(2)}) %collective-permute-start.1) | collective-permute-done | bytes 81952 | tf_op jit(solution)/shard_map/while/body/eval_jaxpr/ppermute | solution.py:526
  155.2 3.7 collective-permute-done.2
  159.8 10.4 %step.8 = (bf16[64,4736]{1,0:T(8,128)(2,1)S(1)}, bf16[64,640]{1,0:T(8,128)(2,1)S(1)}, f32[1,128,16,4096]{3,2,1,0:T(8,128)}, bf16[1,4,128,4096]{3,2,1,0:T(8,128)(2,1)}, bf16[8,16,4096]{2,1,0:T(8,128)(2,1)S(1)}) custom-call(s32[5]{0:T(128)S(1)} %stack.87.refs_0_, ...), custom_call_target="tpu_custom_call", output_to_operand_aliasing={{2}: (17, {}), {3}: (18, {}), {4}: (19, {})} | custom-call | flops 704643072 | bytes 16777216 | tf_op jit(solution)/shard_map/while/body/eval_jaxpr/step/pallas_call | solution.py:456
  171.8 6.9 %collective-permute-done.1 = bf16[64,640]{1,0:T(8,128)(2,1)S(1)} collective-permute-done((bf16[64,640]{1,0:T(8,128)(2,1)S(1)}, bf16[64,640]{1,0:T(8,128)(2,1)S(1)}, u32[]{:S(2)}, u32[]{:S(2)}) %collective-permute-start.1) | collective-permute-done | bytes 81952 | tf_op jit(solution)/shard_map/while/body/eval_jaxpr/ppermute | solution.py:526
  178.7 3.7 collective-permute-done.2
  183.4 10.6 %step.8 = (bf16[64,4736]{1,0:T(8,128)(2,1)S(1)}, bf16[64,640]{1,0:T(8,128)(2,1)S(1)}, f32[1,128,16,4096]{3,2,1,0:T(8,128)}, bf16[1,4,128,4096]{3,2,1,0:T(8,128)(2,1)}, bf16[8,16,4096]{2,1,0:T(8,128)(2,1)S(1)}) custom-call(s32[5]{0:T(128)S(1)} %stack.87.refs_0_, ...), custom_call_target="tpu_custom_call", output_to_operand_aliasing={{2}: (17, {}), {3}: (18, {}), {4}: (19, {})} | custom-call | flops 704643072 | bytes 16777216 | tf_op jit(solution)/shard_map/while/body/eval_jaxpr/step/pallas_call | solution.py:456
  195.6 6.9 %collective-permute-done.1 = bf16[64,640]{1,0:T(8,128)(2,1)S(1)} collective-permute-done((bf16[64,640]{1,0:T(8,128)(2,1)S(1)}, bf16[64,640]{1,0:T(8,128)(2,1)S(1)}, u32[]{:S(2)}, u32[]{:S(2)}) %collective-permute-start.1) | collective-permute-done | bytes 81952 | tf_op jit(solution)/shard_map/while/body/eval_jaxpr/ppermute | solution.py:526
  202.5 3.6 collective-permute-done.2
  207.1 10.7 %step.8 = (bf16[64,4736]{1,0:T(8,128)(2,1)S(1)}, bf16[64,640]{1,0:T(8,128)(2,1)S(1)}, f32[1,128,16,4096]{3,2,1,0:T(8,128)}, bf16[1,4,128,4096]{3,2,1,0:T(8,128)(2,1)}, bf16[8,16,4096]{2,1,0:T(8,128)(2,1)S(1)}) custom-call(s32[5]{0:T(128)S(1)} %stack.87.refs_0_, ...), custom_call_target="tpu_custom_call", output_to_operand_aliasing={{2}: (17, {}), {3}: (18, {}), {4}: (19, {})} | custom-call | flops 704643072 | bytes 16777216 | tf_op jit(solution)/shard_map/while/body/eval_jaxpr/step/pallas_call | solution.py:456
  219.2 7.2 %collective-permute-done.1 = bf16[64,640]{1,0:T(8,128)(2,1)S(1)} collective-permute-done((bf16[64,640]{1,0:T(8,128)(2,1)S(1)}, bf16[64,640]{1,0:T(8,128)(2,1)S(1)}, u32[]{:S(2)}, u32[]{:S(2)}) %collective-permute-start.1) | collective-permute-done | bytes 81952 | tf_op jit(solution)/shard_map/while/body/eval_jaxpr/ppermute | solution.py:526
  226.3 3.6 collective-permute-done.2
  230.9 10.7 %step.8 = (bf16[64,4736]{1,0:T(8,128)(2,1)S(1)}, bf16[64,640]{1,0:T(8,128)(2,1)S(1)}, f32[1,128,16,4096]{3,2,1,0:T(8,128)}, bf16[1,4,128,4096]{3,2,1,0:T(8,128)(2,1)}, bf16[8,16,4096]{2,1,0:T(8,128)(2,1)S(1)}) custom-call(s32[5]{0:T(128)S(1)} %stack.87.refs_0_, ...), custom_call_target="tpu_custom_call", output_to_operand_aliasing={{2}: (17, {}), {3}: (18, {}), {4}: (19, {})} | custom-call | flops 704643072 | bytes 16777216 | tf_op jit(solution)/shard_map/while/body/eval_jaxpr/step/pallas_call | solution.py:456
  243.0 7.2 %collective-permute-done.1 = bf16[64,640]{1,0:T(8,128)(2,1)S(1)} collective-permute-done((bf16[64,640]{1,0:T(8,128)(2,1)S(1)}, bf16[64,640]{1,0:T(8,128)(2,1)S(1)}, u32[]{:S(2)}, u32[]{:S(2)}) %collective-permute-start.1) | collective-permute-done | bytes 81952 | tf_op jit(solution)/shard_map/while/body/eval_jaxpr/ppermute | solution.py:526
  250.2 3.6 collective-permute-done.2
  255.8 4.7 %collective-permute-start = (bf16[64,4736]{1,0:T(8,128)(2,1)S(1)}, bf16[64,4736]{1,0:T(8,128)(2,1)S(1)}, u32[]{:S(2)}, u32[]{:S(2)}) collective-permute-start(bf16[64,4736]{1,0:T(8,128)(2,1)S(1)} %get-tuple-element.606), channel_id=1, source_target_pairs={{0,4},{1,5},{2,6},{3,7},{4,8},{5,9},{6,10},{7,11},{8,12},{9,13},{1... | collective-permute-start | bytes 1818632 | tf_op jit(solution)/shard_map/while/body/eval_jaxpr/ppermute | solution.py:526
  260.6 1.7 collective-permute-start.1
  262.3 1.6 collective-permute-start.2
  263.9 3.0 collective-permute-start.3
  266.9 2.2 collective-permute-done.1
  269.1 3.9 collective-permute-done.2
  274.9 10.7 %collective-permute-start.1 = (bf16[64,640]{1,0:T(8,128)(2,1)S(1)}, bf16[64,640]{1,0:T(8,128)(2,1)S(1)}, u32[]{:S(2)}, u32[]{:S(2)}) collective-permute-start(bf16[64,640]{1,0:T(8,128)(2,1)S(1)} %get-tuple-element.607), channel_id=1, source_target_pairs={{0,5},{1,6},{2,7},{3,4},{4,9},{5,10},{6,11},{7,8},{8,13},{9,14},{1... | collective-permute-start | bytes 245768 | tf_op jit(solution)/shard_map/while/body/eval_jaxpr/ppermute | solution.py:526
  287.1 3.3 collective-permute-start.3
  290.4 4.8 %collective-permute-done.2 = bf16[64,640]{1,0:T(8,128)(2,1)S(1)} collective-permute-done((bf16[64,640]{1,0:T(8,128)(2,1)S(1)}, bf16[64,640]{1,0:T(8,128)(2,1)S(1)}, u32[]{:S(2)}, u32[]{:S(2)}) %collective-permute-start.2) | collective-permute-done | bytes 81952 | tf_op jit(solution)/shard_map/while/body/eval_jaxpr/ppermute | solution.py:526
  296.9 2.7 collective-permute-start.1
  299.6 11.4 %collective-permute-start.2 = (bf16[64,640]{1,0:T(8,128)(2,1)S(1)}, bf16[64,640]{1,0:T(8,128)(2,1)S(1)}, u32[]{:S(2)}, u32[]{:S(2)}) collective-permute-start(bf16[64,640]{1,0:T(8,128)(2,1)S(1)} %get-tuple-element.607), channel_id=1, source_target_pairs={{0,6},{1,7},{2,4},{3,5},{4,10},{5,11},{6,8},{7,9},{8,14},{9,15},{1... | collective-permute-start | bytes 245768 | tf_op jit(solution)/shard_map/while/body/eval_jaxpr/ppermute | solution.py:526
  311.0 3.1 collective-permute-start.3
  314.1 2.8 collective-permute-done.3
  318.0 1.8 collective-permute-start
  321.5 3.1 collective-permute-start.2
  324.6 13.6 %collective-permute-start.3 = (bf16[64,640]{1,0:T(8,128)(2,1)S(1)}, bf16[64,640]{1,0:T(8,128)(2,1)S(1)}, u32[]{:S(2)}, u32[]{:S(2)}) collective-permute-start(bf16[64,640]{1,0:T(8,128)(2,1)S(1)} %get-tuple-element.607), channel_id=1, source_target_pairs={{0,7},{1,4},{2,5},{3,6},{4,11},{5,8},{6,9},{7,10},{8,15},{9,12},{1... | collective-permute-start | bytes 245768 | tf_op jit(solution)/shard_map/while/body/eval_jaxpr/ppermute | solution.py:526
  338.3 2.8 collective-permute-done.3
  342.2 1.8 collective-permute-start
  344.0 1.6 collective-permute-start.1
  345.7 3.2 collective-permute-start.2
  348.8 3.6 collective-permute-start.3
  354.8 3.7 collective-permute-done
  359.6 2.1 collective-permute-start
  361.7 3.4 collective-permute-start.1
  365.1 3.3 collective-permute-start.2
  368.3 2.7 collective-permute-start.3
  371.1 3.9 collective-permute-done.1
  375.2 6.1 %collective-permute-done = bf16[64,4736]{1,0:T(8,128)(2,1)S(1)} collective-permute-done((bf16[64,4736]{1,0:T(8,128)(2,1)S(1)}, bf16[64,4736]{1,0:T(8,128)(2,1)S(1)}, u32[]{:S(2)}, u32[]{:S(2)}) %collective-permute-start) | collective-permute-done | bytes 606240 | tf_op jit(solution)/shard_map/while/body/eval_jaxpr/ppermute | solution.py:526
  381.3 1.9 step.7
  383.1 27.9 %all_to_all.10.returned = bf16[8,16,4096]{2,1,0:T(8,128)(2,1)} all-to-all(bf16[8,16,4096]{2,1,0:T(8,128)(2,1)S(1)} %get-tuple-element.423), channel_id=1, replica_groups=mesh['section'=8,'tensor'=4] {'section'}, dimensions={0} | all-to-all | bytes 2097152 | tf_op jit(solution)/shard_map/all_to_all | solution.py:530
  411.0 2.6 keep.1
  (112 shorter events, 32.4 us)
Async XLA Ops:
  0.6 64.7 %collective-permute-start.8 = (bf16[544,4096]{1,0:T(8,128)(2,1)}, bf16[544,4096]{1,0:T(8,128)(2,1)}, u32[]{:S(2)}, u32[]{:S(2)}) collective-permute-start(bf16[544,4096]{1,0:T(8,128)(2,1)} %bitcast.24), channel_id=1, source_target_pairs={{4,0},{8,4},{12,8},{16,12},{20,16},{24,20},{28,24},{0,28},{5,1},{9... | collective-permute-start | bytes 13369352 | tf_op jit(solution)/shard_map/ppermute | solution.py:432
  8.1 57.2 %all-to-all-start = ((bf16[8,16,4096]{2,1,0:T(8,128)(2,1)}), bf16[8,16,4096]{2,1,0:T(8,128)(2,1)S(1)}, u32[]{:S(2)}, u32[]{:S(2)}) async-start(bf16[8,16,4096]{2,1,0:T(8,128)(2,1)} %pick.1), calls=%async_computation | async-start | bytes 2097152 | tf_op jit(solution)/shard_map/all_to_all | solution.py:530
  14.0 51.4 %copy-start.2 = (f32[1,4096]{1,0:T(1,128)S(1)}, f32[1,4096]{1,0:T(1,128)}, u32[]{:S(2)}) copy-start(f32[1,4096]{1,0:T(1,128)} %refs_10_.1) | copy-start | bytes 49156
  14.0 51.4 %copy-start.3 = (f32[1,4096]{1,0:T(1,128)S(1)}, f32[1,4096]{1,0:T(1,128)}, u32[]{:S(2)}) copy-start(f32[1,4096]{1,0:T(1,128)} %refs_12_.1) | copy-start | bytes 49156
  17.9 46.7 %collective-permute-start.4 = (bf16[64,640]{1,0:T(8,128)(2,1)S(1)}, bf16[64,640]{1,0:T(8,128)(2,1)S(1)}, u32[]{:S(2)}, u32[]{:S(2)}) collective-permute-start(bf16[64,640]{1,0:T(8,128)(2,1)S(1)} %get-tuple-element.410), channel_id=1, source_target_pairs={{0,1},{1,2},{2,3},{3,0},{4,5},{5,6},{6,7},{7,4},{8,9},{9,10},{10,1... | collective-permute-start | bytes 245768 | tf_op jit(solution)/shard_map/ppermute | solution.py:557
  19.5 45.0 %collective-permute-start.5 = (bf16[64,640]{1,0:T(8,128)(2,1)S(1)}, bf16[64,640]{1,0:T(8,128)(2,1)S(1)}, u32[]{:S(2)}, u32[]{:S(2)}) collective-permute-start(bf16[64,640]{1,0:T(8,128)(2,1)S(1)} %get-tuple-element.410), channel_id=1, source_target_pairs={{0,2},{1,3},{2,0},{3,1},{4,6},{5,7},{6,4},{7,5},{8,10},{9,11},{10,... | collective-permute-start | bytes 245768 | tf_op jit(solution)/shard_map/ppermute | solution.py:557
  22.1 42.4 %collective-permute-start.6 = (bf16[64,640]{1,0:T(8,128)(2,1)S(1)}, bf16[64,640]{1,0:T(8,128)(2,1)S(1)}, u32[]{:S(2)}, u32[]{:S(2)}) collective-permute-start(bf16[64,640]{1,0:T(8,128)(2,1)S(1)} %get-tuple-element.410), channel_id=1, source_target_pairs={{0,3},{1,0},{2,1},{3,2},{4,7},{5,4},{6,5},{7,6},{8,11},{9,8},{10,9... | collective-permute-start | bytes 245768 | tf_op jit(solution)/shard_map/ppermute | solution.py:557
  23.5 41.1 %collective-permute-start.7 = (f32[1,4096]{1,0:T(1,128)S(1)}, f32[1,4096]{1,0:T(1,128)S(1)}, u32[]{:S(2)}, u32[]{:S(2)}) collective-permute-start(f32[1,4096]{1,0:T(1,128)S(1)} %copy-done.1), channel_id=1, source_target_pairs={{4,0},{8,4},{12,8},{16,12},{20,16},{24,20},{28,24},{0,28},{5,1},{9... | collective-permute-start | bytes 49160 | tf_op jit(solution)/shard_map/ppermute | solution.py:433
  75.9 13.1 %collective-permute-start = (bf16[64,4736]{1,0:T(8,128)(2,1)S(1)}, bf16[64,4736]{1,0:T(8,128)(2,1)S(1)}, u32[]{:S(2)}, u32[]{:S(2)}) collective-permute-start(bf16[64,4736]{1,0:T(8,128)(2,1)S(1)} %get-tuple-element.606), channel_id=1, source_target_pairs={{0,4},{1,5},{2,6},{3,7},{4,8},{5,9},{6,10},{7,11},{8,12},{9,13},{1... | collective-permute-start | bytes 1818632 | tf_op jit(solution)/shard_map/while/body/eval_jaxpr/ppermute | solution.py:526
  75.9 8.4 %collective-permute-start.1 = (bf16[64,640]{1,0:T(8,128)(2,1)S(1)}, bf16[64,640]{1,0:T(8,128)(2,1)S(1)}, u32[]{:S(2)}, u32[]{:S(2)}) collective-permute-start(bf16[64,640]{1,0:T(8,128)(2,1)S(1)} %get-tuple-element.607), channel_id=1, source_target_pairs={{0,5},{1,6},{2,7},{3,4},{4,9},{5,10},{6,11},{7,8},{8,13},{9,14},{1... | collective-permute-start | bytes 245768 | tf_op jit(solution)/shard_map/while/body/eval_jaxpr/ppermute | solution.py:526
  76.0 12.0 %collective-permute-start.2 = (bf16[64,640]{1,0:T(8,128)(2,1)S(1)}, bf16[64,640]{1,0:T(8,128)(2,1)S(1)}, u32[]{:S(2)}, u32[]{:S(2)}) collective-permute-start(bf16[64,640]{1,0:T(8,128)(2,1)S(1)} %get-tuple-element.607), channel_id=1, source_target_pairs={{0,6},{1,7},{2,4},{3,5},{4,10},{5,11},{6,8},{7,9},{8,14},{9,15},{1... | collective-permute-start | bytes 245768 | tf_op jit(solution)/shard_map/while/body/eval_jaxpr/ppermute | solution.py:526
  76.1 12.0 %collective-permute-start.3 = (bf16[64,640]{1,0:T(8,128)(2,1)S(1)}, bf16[64,640]{1,0:T(8,128)(2,1)S(1)}, u32[]{:S(2)}, u32[]{:S(2)}) collective-permute-start(bf16[64,640]{1,0:T(8,128)(2,1)S(1)} %get-tuple-element.607), channel_id=1, source_target_pairs={{0,7},{1,4},{2,5},{3,6},{4,11},{5,8},{6,9},{7,10},{8,15},{9,12},{1... | collective-permute-start | bytes 245768 | tf_op jit(solution)/shard_map/while/body/eval_jaxpr/ppermute | solution.py:526
  99.4 13.1 %collective-permute-start = (bf16[64,4736]{1,0:T(8,128)(2,1)S(1)}, bf16[64,4736]{1,0:T(8,128)(2,1)S(1)}, u32[]{:S(2)}, u32[]{:S(2)}) collective-permute-start(bf16[64,4736]{1,0:T(8,128)(2,1)S(1)} %get-tuple-element.606), channel_id=1, source_target_pairs={{0,4},{1,5},{2,6},{3,7},{4,8},{5,9},{6,10},{7,11},{8,12},{9,13},{1... | collective-permute-start | bytes 1818632 | tf_op jit(solution)/shard_map/while/body/eval_jaxpr/ppermute | solution.py:526
  99.5 8.4 %collective-permute-start.1 = (bf16[64,640]{1,0:T(8,128)(2,1)S(1)}, bf16[64,640]{1,0:T(8,128)(2,1)S(1)}, u32[]{:S(2)}, u32[]{:S(2)}) collective-permute-start(bf16[64,640]{1,0:T(8,128)(2,1)S(1)} %get-tuple-element.607), channel_id=1, source_target_pairs={{0,5},{1,6},{2,7},{3,4},{4,9},{5,10},{6,11},{7,8},{8,13},{9,14},{1... | collective-permute-start | bytes 245768 | tf_op jit(solution)/shard_map/while/body/eval_jaxpr/ppermute | solution.py:526
  99.6 12.1 %collective-permute-start.2 = (bf16[64,640]{1,0:T(8,128)(2,1)S(1)}, bf16[64,640]{1,0:T(8,128)(2,1)S(1)}, u32[]{:S(2)}, u32[]{:S(2)}) collective-permute-start(bf16[64,640]{1,0:T(8,128)(2,1)S(1)} %get-tuple-element.607), channel_id=1, source_target_pairs={{0,6},{1,7},{2,4},{3,5},{4,10},{5,11},{6,8},{7,9},{8,14},{9,15},{1... | collective-permute-start | bytes 245768 | tf_op jit(solution)/shard_map/while/body/eval_jaxpr/ppermute | solution.py:526
  99.6 12.0 %collective-permute-start.3 = (bf16[64,640]{1,0:T(8,128)(2,1)S(1)}, bf16[64,640]{1,0:T(8,128)(2,1)S(1)}, u32[]{:S(2)}, u32[]{:S(2)}) collective-permute-start(bf16[64,640]{1,0:T(8,128)(2,1)S(1)} %get-tuple-element.607), channel_id=1, source_target_pairs={{0,7},{1,4},{2,5},{3,6},{4,11},{5,8},{6,9},{7,10},{8,15},{9,12},{1... | collective-permute-start | bytes 245768 | tf_op jit(solution)/shard_map/while/body/eval_jaxpr/ppermute | solution.py:526
  123.1 13.1 %collective-permute-start = (bf16[64,4736]{1,0:T(8,128)(2,1)S(1)}, bf16[64,4736]{1,0:T(8,128)(2,1)S(1)}, u32[]{:S(2)}, u32[]{:S(2)}) collective-permute-start(bf16[64,4736]{1,0:T(8,128)(2,1)S(1)} %get-tuple-element.606), channel_id=1, source_target_pairs={{0,4},{1,5},{2,6},{3,7},{4,8},{5,9},{6,10},{7,11},{8,12},{9,13},{1... | collective-permute-start | bytes 1818632 | tf_op jit(solution)/shard_map/while/body/eval_jaxpr/ppermute | solution.py:526
  123.2 8.4 %collective-permute-start.1 = (bf16[64,640]{1,0:T(8,128)(2,1)S(1)}, bf16[64,640]{1,0:T(8,128)(2,1)S(1)}, u32[]{:S(2)}, u32[]{:S(2)}) collective-permute-start(bf16[64,640]{1,0:T(8,128)(2,1)S(1)} %get-tuple-element.607), channel_id=1, source_target_pairs={{0,5},{1,6},{2,7},{3,4},{4,9},{5,10},{6,11},{7,8},{8,13},{9,14},{1... | collective-permute-start | bytes 245768 | tf_op jit(solution)/shard_map/while/body/eval_jaxpr/ppermute | solution.py:526
  123.2 12.0 %collective-permute-start.2 = (bf16[64,640]{1,0:T(8,128)(2,1)S(1)}, bf16[64,640]{1,0:T(8,128)(2,1)S(1)}, u32[]{:S(2)}, u32[]{:S(2)}) collective-permute-start(bf16[64,640]{1,0:T(8,128)(2,1)S(1)} %get-tuple-element.607), channel_id=1, source_target_pairs={{0,6},{1,7},{2,4},{3,5},{4,10},{5,11},{6,8},{7,9},{8,14},{9,15},{1... | collective-permute-start | bytes 245768 | tf_op jit(solution)/shard_map/while/body/eval_jaxpr/ppermute | solution.py:526
  123.3 12.0 %collective-permute-start.3 = (bf16[64,640]{1,0:T(8,128)(2,1)S(1)}, bf16[64,640]{1,0:T(8,128)(2,1)S(1)}, u32[]{:S(2)}, u32[]{:S(2)}) collective-permute-start(bf16[64,640]{1,0:T(8,128)(2,1)S(1)} %get-tuple-element.607), channel_id=1, source_target_pairs={{0,7},{1,4},{2,5},{3,6},{4,11},{5,8},{6,9},{7,10},{8,15},{9,12},{1... | collective-permute-start | bytes 245768 | tf_op jit(solution)/shard_map/while/body/eval_jaxpr/ppermute | solution.py:526
  146.6 13.1 %collective-permute-start = (bf16[64,4736]{1,0:T(8,128)(2,1)S(1)}, bf16[64,4736]{1,0:T(8,128)(2,1)S(1)}, u32[]{:S(2)}, u32[]{:S(2)}) collective-permute-start(bf16[64,4736]{1,0:T(8,128)(2,1)S(1)} %get-tuple-element.606), channel_id=1, source_target_pairs={{0,4},{1,5},{2,6},{3,7},{4,8},{5,9},{6,10},{7,11},{8,12},{9,13},{1... | collective-permute-start | bytes 1818632 | tf_op jit(solution)/shard_map/while/body/eval_jaxpr/ppermute | solution.py:526
  146.7 8.4 %collective-permute-start.1 = (bf16[64,640]{1,0:T(8,128)(2,1)S(1)}, bf16[64,640]{1,0:T(8,128)(2,1)S(1)}, u32[]{:S(2)}, u32[]{:S(2)}) collective-permute-start(bf16[64,640]{1,0:T(8,128)(2,1)S(1)} %get-tuple-element.607), channel_id=1, source_target_pairs={{0,5},{1,6},{2,7},{3,4},{4,9},{5,10},{6,11},{7,8},{8,13},{9,14},{1... | collective-permute-start | bytes 245768 | tf_op jit(solution)/shard_map/while/body/eval_jaxpr/ppermute | solution.py:526
  146.8 12.1 %collective-permute-start.2 = (bf16[64,640]{1,0:T(8,128)(2,1)S(1)}, bf16[64,640]{1,0:T(8,128)(2,1)S(1)}, u32[]{:S(2)}, u32[]{:S(2)}) collective-permute-start(bf16[64,640]{1,0:T(8,128)(2,1)S(1)} %get-tuple-element.607), channel_id=1, source_target_pairs={{0,6},{1,7},{2,4},{3,5},{4,10},{5,11},{6,8},{7,9},{8,14},{9,15},{1... | collective-permute-start | bytes 245768 | tf_op jit(solution)/shard_map/while/body/eval_jaxpr/ppermute | solution.py:526
  146.8 12.0 %collective-permute-start.3 = (bf16[64,640]{1,0:T(8,128)(2,1)S(1)}, bf16[64,640]{1,0:T(8,128)(2,1)S(1)}, u32[]{:S(2)}, u32[]{:S(2)}) collective-permute-start(bf16[64,640]{1,0:T(8,128)(2,1)S(1)} %get-tuple-element.607), channel_id=1, source_target_pairs={{0,7},{1,4},{2,5},{3,6},{4,11},{5,8},{6,9},{7,10},{8,15},{9,12},{1... | collective-permute-start | bytes 245768 | tf_op jit(solution)/shard_map/while/body/eval_jaxpr/ppermute | solution.py:526
  170.2 13.1 %collective-permute-start = (bf16[64,4736]{1,0:T(8,128)(2,1)S(1)}, bf16[64,4736]{1,0:T(8,128)(2,1)S(1)}, u32[]{:S(2)}, u32[]{:S(2)}) collective-permute-start(bf16[64,4736]{1,0:T(8,128)(2,1)S(1)} %get-tuple-element.606), channel_id=1, source_target_pairs={{0,4},{1,5},{2,6},{3,7},{4,8},{5,9},{6,10},{7,11},{8,12},{9,13},{1... | collective-permute-start | bytes 1818632 | tf_op jit(solution)/shard_map/while/body/eval_jaxpr/ppermute | solution.py:526
  170.3 8.5 %collective-permute-start.1 = (bf16[64,640]{1,0:T(8,128)(2,1)S(1)}, bf16[64,640]{1,0:T(8,128)(2,1)S(1)}, u32[]{:S(2)}, u32[]{:S(2)}) collective-permute-start(bf16[64,640]{1,0:T(8,128)(2,1)S(1)} %get-tuple-element.607), channel_id=1, source_target_pairs={{0,5},{1,6},{2,7},{3,4},{4,9},{5,10},{6,11},{7,8},{8,13},{9,14},{1... | collective-permute-start | bytes 245768 | tf_op jit(solution)/shard_map/while/body/eval_jaxpr/ppermute | solution.py:526
  170.3 12.1 %collective-permute-start.2 = (bf16[64,640]{1,0:T(8,128)(2,1)S(1)}, bf16[64,640]{1,0:T(8,128)(2,1)S(1)}, u32[]{:S(2)}, u32[]{:S(2)}) collective-permute-start(bf16[64,640]{1,0:T(8,128)(2,1)S(1)} %get-tuple-element.607), channel_id=1, source_target_pairs={{0,6},{1,7},{2,4},{3,5},{4,10},{5,11},{6,8},{7,9},{8,14},{9,15},{1... | collective-permute-start | bytes 245768 | tf_op jit(solution)/shard_map/while/body/eval_jaxpr/ppermute | solution.py:526
  170.4 12.0 %collective-permute-start.3 = (bf16[64,640]{1,0:T(8,128)(2,1)S(1)}, bf16[64,640]{1,0:T(8,128)(2,1)S(1)}, u32[]{:S(2)}, u32[]{:S(2)}) collective-permute-start(bf16[64,640]{1,0:T(8,128)(2,1)S(1)} %get-tuple-element.607), channel_id=1, source_target_pairs={{0,7},{1,4},{2,5},{3,6},{4,11},{5,8},{6,9},{7,10},{8,15},{9,12},{1... | collective-permute-start | bytes 245768 | tf_op jit(solution)/shard_map/while/body/eval_jaxpr/ppermute | solution.py:526
  194.0 13.1 %collective-permute-start = (bf16[64,4736]{1,0:T(8,128)(2,1)S(1)}, bf16[64,4736]{1,0:T(8,128)(2,1)S(1)}, u32[]{:S(2)}, u32[]{:S(2)}) collective-permute-start(bf16[64,4736]{1,0:T(8,128)(2,1)S(1)} %get-tuple-element.606), channel_id=1, source_target_pairs={{0,4},{1,5},{2,6},{3,7},{4,8},{5,9},{6,10},{7,11},{8,12},{9,13},{1... | collective-permute-start | bytes 1818632 | tf_op jit(solution)/shard_map/while/body/eval_jaxpr/ppermute | solution.py:526
  194.0 8.5 %collective-permute-start.1 = (bf16[64,640]{1,0:T(8,128)(2,1)S(1)}, bf16[64,640]{1,0:T(8,128)(2,1)S(1)}, u32[]{:S(2)}, u32[]{:S(2)}) collective-permute-start(bf16[64,640]{1,0:T(8,128)(2,1)S(1)} %get-tuple-element.607), channel_id=1, source_target_pairs={{0,5},{1,6},{2,7},{3,4},{4,9},{5,10},{6,11},{7,8},{8,13},{9,14},{1... | collective-permute-start | bytes 245768 | tf_op jit(solution)/shard_map/while/body/eval_jaxpr/ppermute | solution.py:526
  194.1 12.1 %collective-permute-start.2 = (bf16[64,640]{1,0:T(8,128)(2,1)S(1)}, bf16[64,640]{1,0:T(8,128)(2,1)S(1)}, u32[]{:S(2)}, u32[]{:S(2)}) collective-permute-start(bf16[64,640]{1,0:T(8,128)(2,1)S(1)} %get-tuple-element.607), channel_id=1, source_target_pairs={{0,6},{1,7},{2,4},{3,5},{4,10},{5,11},{6,8},{7,9},{8,14},{9,15},{1... | collective-permute-start | bytes 245768 | tf_op jit(solution)/shard_map/while/body/eval_jaxpr/ppermute | solution.py:526
  194.1 12.0 %collective-permute-start.3 = (bf16[64,640]{1,0:T(8,128)(2,1)S(1)}, bf16[64,640]{1,0:T(8,128)(2,1)S(1)}, u32[]{:S(2)}, u32[]{:S(2)}) collective-permute-start(bf16[64,640]{1,0:T(8,128)(2,1)S(1)} %get-tuple-element.607), channel_id=1, source_target_pairs={{0,7},{1,4},{2,5},{3,6},{4,11},{5,8},{6,9},{7,10},{8,15},{9,12},{1... | collective-permute-start | bytes 245768 | tf_op jit(solution)/shard_map/while/body/eval_jaxpr/ppermute | solution.py:526
  217.8 13.1 %collective-permute-start = (bf16[64,4736]{1,0:T(8,128)(2,1)S(1)}, bf16[64,4736]{1,0:T(8,128)(2,1)S(1)}, u32[]{:S(2)}, u32[]{:S(2)}) collective-permute-start(bf16[64,4736]{1,0:T(8,128)(2,1)S(1)} %get-tuple-element.606), channel_id=1, source_target_pairs={{0,4},{1,5},{2,6},{3,7},{4,8},{5,9},{6,10},{7,11},{8,12},{9,13},{1... | collective-permute-start | bytes 1818632 | tf_op jit(solution)/shard_map/while/body/eval_jaxpr/ppermute | solution.py:526
  217.9 8.5 %collective-permute-start.1 = (bf16[64,640]{1,0:T(8,128)(2,1)S(1)}, bf16[64,640]{1,0:T(8,128)(2,1)S(1)}, u32[]{:S(2)}, u32[]{:S(2)}) collective-permute-start(bf16[64,640]{1,0:T(8,128)(2,1)S(1)} %get-tuple-element.607), channel_id=1, source_target_pairs={{0,5},{1,6},{2,7},{3,4},{4,9},{5,10},{6,11},{7,8},{8,13},{9,14},{1... | collective-permute-start | bytes 245768 | tf_op jit(solution)/shard_map/while/body/eval_jaxpr/ppermute | solution.py:526
  217.9 12.1 %collective-permute-start.2 = (bf16[64,640]{1,0:T(8,128)(2,1)S(1)}, bf16[64,640]{1,0:T(8,128)(2,1)S(1)}, u32[]{:S(2)}, u32[]{:S(2)}) collective-permute-start(bf16[64,640]{1,0:T(8,128)(2,1)S(1)} %get-tuple-element.607), channel_id=1, source_target_pairs={{0,6},{1,7},{2,4},{3,5},{4,10},{5,11},{6,8},{7,9},{8,14},{9,15},{1... | collective-permute-start | bytes 245768 | tf_op jit(solution)/shard_map/while/body/eval_jaxpr/ppermute | solution.py:526
  218.0 12.0 %collective-permute-start.3 = (bf16[64,640]{1,0:T(8,128)(2,1)S(1)}, bf16[64,640]{1,0:T(8,128)(2,1)S(1)}, u32[]{:S(2)}, u32[]{:S(2)}) collective-permute-start(bf16[64,640]{1,0:T(8,128)(2,1)S(1)} %get-tuple-element.607), channel_id=1, source_target_pairs={{0,7},{1,4},{2,5},{3,6},{4,11},{5,8},{6,9},{7,10},{8,15},{9,12},{1... | collective-permute-start | bytes 245768 | tf_op jit(solution)/shard_map/while/body/eval_jaxpr/ppermute | solution.py:526
  241.6 13.1 %collective-permute-start = (bf16[64,4736]{1,0:T(8,128)(2,1)S(1)}, bf16[64,4736]{1,0:T(8,128)(2,1)S(1)}, u32[]{:S(2)}, u32[]{:S(2)}) collective-permute-start(bf16[64,4736]{1,0:T(8,128)(2,1)S(1)} %get-tuple-element.606), channel_id=1, source_target_pairs={{0,4},{1,5},{2,6},{3,7},{4,8},{5,9},{6,10},{7,11},{8,12},{9,13},{1... | collective-permute-start | bytes 1818632 | tf_op jit(solution)/shard_map/while/body/eval_jaxpr/ppermute | solution.py:526
  241.7 8.5 %collective-permute-start.1 = (bf16[64,640]{1,0:T(8,128)(2,1)S(1)}, bf16[64,640]{1,0:T(8,128)(2,1)S(1)}, u32[]{:S(2)}, u32[]{:S(2)}) collective-permute-start(bf16[64,640]{1,0:T(8,128)(2,1)S(1)} %get-tuple-element.607), channel_id=1, source_target_pairs={{0,5},{1,6},{2,7},{3,4},{4,9},{5,10},{6,11},{7,8},{8,13},{9,14},{1... | collective-permute-start | bytes 245768 | tf_op jit(solution)/shard_map/while/body/eval_jaxpr/ppermute | solution.py:526
  241.7 12.1 %collective-permute-start.2 = (bf16[64,640]{1,0:T(8,128)(2,1)S(1)}, bf16[64,640]{1,0:T(8,128)(2,1)S(1)}, u32[]{:S(2)}, u32[]{:S(2)}) collective-permute-start(bf16[64,640]{1,0:T(8,128)(2,1)S(1)} %get-tuple-element.607), channel_id=1, source_target_pairs={{0,6},{1,7},{2,4},{3,5},{4,10},{5,11},{6,8},{7,9},{8,14},{9,15},{1... | collective-permute-start | bytes 245768 | tf_op jit(solution)/shard_map/while/body/eval_jaxpr/ppermute | solution.py:526
  241.8 12.0 %collective-permute-start.3 = (bf16[64,640]{1,0:T(8,128)(2,1)S(1)}, bf16[64,640]{1,0:T(8,128)(2,1)S(1)}, u32[]{:S(2)}, u32[]{:S(2)}) collective-permute-start(bf16[64,640]{1,0:T(8,128)(2,1)S(1)} %get-tuple-element.607), channel_id=1, source_target_pairs={{0,7},{1,4},{2,5},{3,6},{4,11},{5,8},{6,9},{7,10},{8,15},{9,12},{1... | collective-permute-start | bytes 245768 | tf_op jit(solution)/shard_map/while/body/eval_jaxpr/ppermute | solution.py:526
  255.8 17.9 %collective-permute-start = (bf16[64,4736]{1,0:T(8,128)(2,1)S(1)}, bf16[64,4736]{1,0:T(8,128)(2,1)S(1)}, u32[]{:S(2)}, u32[]{:S(2)}) collective-permute-start(bf16[64,4736]{1,0:T(8,128)(2,1)S(1)} %get-tuple-element.606), channel_id=1, source_target_pairs={{0,4},{1,5},{2,6},{3,7},{4,8},{5,9},{6,10},{7,11},{8,12},{9,13},{1... | collective-permute-start | bytes 1818632 | tf_op jit(solution)/shard_map/while/body/eval_jaxpr/ppermute | solution.py:526
  260.6 8.5 %collective-permute-start.1 = (bf16[64,640]{1,0:T(8,128)(2,1)S(1)}, bf16[64,640]{1,0:T(8,128)(2,1)S(1)}, u32[]{:S(2)}, u32[]{:S(2)}) collective-permute-start(bf16[64,640]{1,0:T(8,128)(2,1)S(1)} %get-tuple-element.607), channel_id=1, source_target_pairs={{0,5},{1,6},{2,7},{3,4},{4,9},{5,10},{6,11},{7,8},{8,13},{9,14},{1... | collective-permute-start | bytes 245768 | tf_op jit(solution)/shard_map/while/body/eval_jaxpr/ppermute | solution.py:526
  262.3 10.7 %collective-permute-start.2 = (bf16[64,640]{1,0:T(8,128)(2,1)S(1)}, bf16[64,640]{1,0:T(8,128)(2,1)S(1)}, u32[]{:S(2)}, u32[]{:S(2)}) collective-permute-start(bf16[64,640]{1,0:T(8,128)(2,1)S(1)} %get-tuple-element.607), channel_id=1, source_target_pairs={{0,6},{1,7},{2,4},{3,5},{4,10},{5,11},{6,8},{7,9},{8,14},{9,15},{1... | collective-permute-start | bytes 245768 | tf_op jit(solution)/shard_map/while/body/eval_jaxpr/ppermute | solution.py:526
  263.9 9.1 %collective-permute-start.3 = (bf16[64,640]{1,0:T(8,128)(2,1)S(1)}, bf16[64,640]{1,0:T(8,128)(2,1)S(1)}, u32[]{:S(2)}, u32[]{:S(2)}) collective-permute-start(bf16[64,640]{1,0:T(8,128)(2,1)S(1)} %get-tuple-element.607), channel_id=1, source_target_pairs={{0,7},{1,4},{2,5},{3,6},{4,11},{5,8},{6,9},{7,10},{8,15},{9,12},{1... | collective-permute-start | bytes 245768 | tf_op jit(solution)/shard_map/while/body/eval_jaxpr/ppermute | solution.py:526
  274.9 20.5 %collective-permute-start = (bf16[64,4736]{1,0:T(8,128)(2,1)S(1)}, bf16[64,4736]{1,0:T(8,128)(2,1)S(1)}, u32[]{:S(2)}, u32[]{:S(2)}) collective-permute-start(bf16[64,4736]{1,0:T(8,128)(2,1)S(1)} %get-tuple-element.606), channel_id=1, source_target_pairs={{0,4},{1,5},{2,6},{3,7},{4,8},{5,9},{6,10},{7,11},{8,12},{9,13},{1... | collective-permute-start | bytes 1818632 | tf_op jit(solution)/shard_map/while/body/eval_jaxpr/ppermute | solution.py:526
  274.9 15.5 %collective-permute-start.1 = (bf16[64,640]{1,0:T(8,128)(2,1)S(1)}, bf16[64,640]{1,0:T(8,128)(2,1)S(1)}, u32[]{:S(2)}, u32[]{:S(2)}) collective-permute-start(bf16[64,640]{1,0:T(8,128)(2,1)S(1)} %get-tuple-element.607), channel_id=1, source_target_pairs={{0,5},{1,6},{2,7},{3,4},{4,9},{5,10},{6,11},{7,8},{8,13},{9,14},{1... | collective-permute-start | bytes 245768 | tf_op jit(solution)/shard_map/while/body/eval_jaxpr/ppermute | solution.py:526
  285.6 9.6 %collective-permute-start.2 = (bf16[64,640]{1,0:T(8,128)(2,1)S(1)}, bf16[64,640]{1,0:T(8,128)(2,1)S(1)}, u32[]{:S(2)}, u32[]{:S(2)}) collective-permute-start(bf16[64,640]{1,0:T(8,128)(2,1)S(1)} %get-tuple-element.607), channel_id=1, source_target_pairs={{0,6},{1,7},{2,4},{3,5},{4,10},{5,11},{6,8},{7,9},{8,14},{9,15},{1... | collective-permute-start | bytes 245768 | tf_op jit(solution)/shard_map/while/body/eval_jaxpr/ppermute | solution.py:526
  287.1 8.3 %collective-permute-start.3 = (bf16[64,640]{1,0:T(8,128)(2,1)S(1)}, bf16[64,640]{1,0:T(8,128)(2,1)S(1)}, u32[]{:S(2)}, u32[]{:S(2)}) collective-permute-start(bf16[64,640]{1,0:T(8,128)(2,1)S(1)} %get-tuple-element.607), channel_id=1, source_target_pairs={{0,7},{1,4},{2,5},{3,6},{4,11},{5,8},{6,9},{7,10},{8,15},{9,12},{1... | collective-permute-start | bytes 245768 | tf_op jit(solution)/shard_map/while/body/eval_jaxpr/ppermute | solution.py:526
  296.5 20.4 %collective-permute-start = (bf16[64,4736]{1,0:T(8,128)(2,1)S(1)}, bf16[64,4736]{1,0:T(8,128)(2,1)S(1)}, u32[]{:S(2)}, u32[]{:S(2)}) collective-permute-start(bf16[64,4736]{1,0:T(8,128)(2,1)S(1)} %get-tuple-element.606), channel_id=1, source_target_pairs={{0,4},{1,5},{2,6},{3,7},{4,8},{5,9},{6,10},{7,11},{8,12},{9,13},{1... | collective-permute-start | bytes 1818632 | tf_op jit(solution)/shard_map/while/body/eval_jaxpr/ppermute | solution.py:526
  296.9 17.1 %collective-permute-start.1 = (bf16[64,640]{1,0:T(8,128)(2,1)S(1)}, bf16[64,640]{1,0:T(8,128)(2,1)S(1)}, u32[]{:S(2)}, u32[]{:S(2)}) collective-permute-start(bf16[64,640]{1,0:T(8,128)(2,1)S(1)} %get-tuple-element.607), channel_id=1, source_target_pairs={{0,5},{1,6},{2,7},{3,4},{4,9},{5,10},{6,11},{7,8},{8,13},{9,14},{1... | collective-permute-start | bytes 245768 | tf_op jit(solution)/shard_map/while/body/eval_jaxpr/ppermute | solution.py:526
  299.6 14.4 %collective-permute-start.2 = (bf16[64,640]{1,0:T(8,128)(2,1)S(1)}, bf16[64,640]{1,0:T(8,128)(2,1)S(1)}, u32[]{:S(2)}, u32[]{:S(2)}) collective-permute-start(bf16[64,640]{1,0:T(8,128)(2,1)S(1)} %get-tuple-element.607), channel_id=1, source_target_pairs={{0,6},{1,7},{2,4},{3,5},{4,10},{5,11},{6,8},{7,9},{8,14},{9,15},{1... | collective-permute-start | bytes 245768 | tf_op jit(solution)/shard_map/while/body/eval_jaxpr/ppermute | solution.py:526
  311.0 5.9 %collective-permute-start.3 = (bf16[64,640]{1,0:T(8,128)(2,1)S(1)}, bf16[64,640]{1,0:T(8,128)(2,1)S(1)}, u32[]{:S(2)}, u32[]{:S(2)}) collective-permute-start(bf16[64,640]{1,0:T(8,128)(2,1)S(1)} %get-tuple-element.607), channel_id=1, source_target_pairs={{0,7},{1,4},{2,5},{3,6},{4,11},{5,8},{6,9},{7,10},{8,15},{9,12},{1... | collective-permute-start | bytes 245768 | tf_op jit(solution)/shard_map/while/body/eval_jaxpr/ppermute | solution.py:526
  318.0 23.1 %collective-permute-start = (bf16[64,4736]{1,0:T(8,128)(2,1)S(1)}, bf16[64,4736]{1,0:T(8,128)(2,1)S(1)}, u32[]{:S(2)}, u32[]{:S(2)}) collective-permute-start(bf16[64,4736]{1,0:T(8,128)(2,1)S(1)} %get-tuple-element.606), channel_id=1, source_target_pairs={{0,4},{1,5},{2,6},{3,7},{4,8},{5,9},{6,10},{7,11},{8,12},{9,13},{1... | collective-permute-start | bytes 1818632 | tf_op jit(solution)/shard_map/while/body/eval_jaxpr/ppermute | solution.py:526
  319.9 18.4 %collective-permute-start.1 = (bf16[64,640]{1,0:T(8,128)(2,1)S(1)}, bf16[64,640]{1,0:T(8,128)(2,1)S(1)}, u32[]{:S(2)}, u32[]{:S(2)}) collective-permute-start(bf16[64,640]{1,0:T(8,128)(2,1)S(1)} %get-tuple-element.607), channel_id=1, source_target_pairs={{0,5},{1,6},{2,7},{3,4},{4,9},{5,10},{6,11},{7,8},{8,13},{9,14},{1... | collective-permute-start | bytes 245768 | tf_op jit(solution)/shard_map/while/body/eval_jaxpr/ppermute | solution.py:526
  321.5 16.8 %collective-permute-start.2 = (bf16[64,640]{1,0:T(8,128)(2,1)S(1)}, bf16[64,640]{1,0:T(8,128)(2,1)S(1)}, u32[]{:S(2)}, u32[]{:S(2)}) collective-permute-start(bf16[64,640]{1,0:T(8,128)(2,1)S(1)} %get-tuple-element.607), channel_id=1, source_target_pairs={{0,6},{1,7},{2,4},{3,5},{4,10},{5,11},{6,8},{7,9},{8,14},{9,15},{1... | collective-permute-start | bytes 245768 | tf_op jit(solution)/shard_map/while/body/eval_jaxpr/ppermute | solution.py:526
  324.6 16.5 %collective-permute-start.3 = (bf16[64,640]{1,0:T(8,128)(2,1)S(1)}, bf16[64,640]{1,0:T(8,128)(2,1)S(1)}, u32[]{:S(2)}, u32[]{:S(2)}) collective-permute-start(bf16[64,640]{1,0:T(8,128)(2,1)S(1)} %get-tuple-element.607), channel_id=1, source_target_pairs={{0,7},{1,4},{2,5},{3,6},{4,11},{5,8},{6,9},{7,10},{8,15},{9,12},{1... | collective-permute-start | bytes 245768 | tf_op jit(solution)/shard_map/while/body/eval_jaxpr/ppermute | solution.py:526
  342.2 16.3 %collective-permute-start = (bf16[64,4736]{1,0:T(8,128)(2,1)S(1)}, bf16[64,4736]{1,0:T(8,128)(2,1)S(1)}, u32[]{:S(2)}, u32[]{:S(2)}) collective-permute-start(bf16[64,4736]{1,0:T(8,128)(2,1)S(1)} %get-tuple-element.606), channel_id=1, source_target_pairs={{0,4},{1,5},{2,6},{3,7},{4,8},{5,9},{6,10},{7,11},{8,12},{9,13},{1... | collective-permute-start | bytes 1818632 | tf_op jit(solution)/shard_map/while/body/eval_jaxpr/ppermute | solution.py:526
  344.0 8.4 %collective-permute-start.1 = (bf16[64,640]{1,0:T(8,128)(2,1)S(1)}, bf16[64,640]{1,0:T(8,128)(2,1)S(1)}, u32[]{:S(2)}, u32[]{:S(2)}) collective-permute-start(bf16[64,640]{1,0:T(8,128)(2,1)S(1)} %get-tuple-element.607), channel_id=1, source_target_pairs={{0,5},{1,6},{2,7},{3,4},{4,9},{5,10},{6,11},{7,8},{8,13},{9,14},{1... | collective-permute-start | bytes 245768 | tf_op jit(solution)/shard_map/while/body/eval_jaxpr/ppermute | solution.py:526
  345.7 8.2 %collective-permute-start.2 = (bf16[64,640]{1,0:T(8,128)(2,1)S(1)}, bf16[64,640]{1,0:T(8,128)(2,1)S(1)}, u32[]{:S(2)}, u32[]{:S(2)}) collective-permute-start(bf16[64,640]{1,0:T(8,128)(2,1)S(1)} %get-tuple-element.607), channel_id=1, source_target_pairs={{0,6},{1,7},{2,4},{3,5},{4,10},{5,11},{6,8},{7,9},{8,14},{9,15},{1... | collective-permute-start | bytes 245768 | tf_op jit(solution)/shard_map/while/body/eval_jaxpr/ppermute | solution.py:526
  348.8 5.9 %collective-permute-start.3 = (bf16[64,640]{1,0:T(8,128)(2,1)S(1)}, bf16[64,640]{1,0:T(8,128)(2,1)S(1)}, u32[]{:S(2)}, u32[]{:S(2)}) collective-permute-start(bf16[64,640]{1,0:T(8,128)(2,1)S(1)} %get-tuple-element.607), channel_id=1, source_target_pairs={{0,7},{1,4},{2,5},{3,6},{4,11},{5,8},{6,9},{7,10},{8,15},{9,12},{1... | collective-permute-start | bytes 245768 | tf_op jit(solution)/shard_map/while/body/eval_jaxpr/ppermute | solution.py:526
  359.6 21.7 %collective-permute-start = (bf16[64,4736]{1,0:T(8,128)(2,1)S(1)}, bf16[64,4736]{1,0:T(8,128)(2,1)S(1)}, u32[]{:S(2)}, u32[]{:S(2)}) collective-permute-start(bf16[64,4736]{1,0:T(8,128)(2,1)S(1)} %get-tuple-element.606), channel_id=1, source_target_pairs={{0,4},{1,5},{2,6},{3,7},{4,8},{5,9},{6,10},{7,11},{8,12},{9,13},{1... | collective-permute-start | bytes 1818632 | tf_op jit(solution)/shard_map/while/body/eval_jaxpr/ppermute | solution.py:526
  361.7 13.3 %collective-permute-start.1 = (bf16[64,640]{1,0:T(8,128)(2,1)S(1)}, bf16[64,640]{1,0:T(8,128)(2,1)S(1)}, u32[]{:S(2)}, u32[]{:S(2)}) collective-permute-start(bf16[64,640]{1,0:T(8,128)(2,1)S(1)} %get-tuple-element.607), channel_id=1, source_target_pairs={{0,5},{1,6},{2,7},{3,4},{4,9},{5,10},{6,11},{7,8},{8,13},{9,14},{1... | collective-permute-start | bytes 245768 | tf_op jit(solution)/shard_map/while/body/eval_jaxpr/ppermute | solution.py:526
  365.1 9.9 %collective-permute-start.2 = (bf16[64,640]{1,0:T(8,128)(2,1)S(1)}, bf16[64,640]{1,0:T(8,128)(2,1)S(1)}, u32[]{:S(2)}, u32[]{:S(2)}) collective-permute-start(bf16[64,640]{1,0:T(8,128)(2,1)S(1)} %get-tuple-element.607), channel_id=1, source_target_pairs={{0,6},{1,7},{2,4},{3,5},{4,10},{5,11},{6,8},{7,9},{8,14},{9,15},{1... | collective-permute-start | bytes 245768 | tf_op jit(solution)/shard_map/while/body/eval_jaxpr/ppermute | solution.py:526
  368.3 6.9 %collective-permute-start.3 = (bf16[64,640]{1,0:T(8,128)(2,1)S(1)}, bf16[64,640]{1,0:T(8,128)(2,1)S(1)}, u32[]{:S(2)}, u32[]{:S(2)}) collective-permute-start(bf16[64,640]{1,0:T(8,128)(2,1)S(1)} %get-tuple-element.607), channel_id=1, source_target_pairs={{0,7},{1,4},{2,5},{3,6},{4,11},{5,8},{6,9},{7,10},{8,15},{9,12},{1... | collective-permute-start | bytes 245768 | tf_op jit(solution)/shard_map/while/body/eval_jaxpr/ppermute | solution.py:526
  (3 other events, 21.3 us)
